TPU v7x, 32 devices: a whole 2x2x4 slice. The times are simulated.
32 devices in a mesh: dp: 8 (over y, x, core), tensor: 4 (over z).
Axes of the slice: x: 2, y: 2, z: 4, core: 2. Of those that a mesh axis runs over, the one named last changes fastest.
Arguments:
- clips: bfloat16 [16, 1568, 1024], P('dp', 'tensor'), may hold values from -6 to 6
- w_qkv: bfloat16 [3, 1024, 1024], P(None, 'dp', 'tensor'), may hold values from -0.1875 to 0.1875
- w_out: bfloat16 [1024, 1024], P('tensor', 'dp'), may hold values from -1.25 to 1.25
- w_up: bfloat16 [1024, 4096], P('dp', 'tensor'), may hold values from -0.1875 to 0.1875
- w_down: bfloat16 [4096, 1024], P('tensor', 'dp'), may hold values from -0.09375 to 0.09375
- norm_gain: bfloat16 [2, 1024], P(None, 'dp'), may hold values from 0.5 to 1.5
- shifts: bfloat16 [4, 1024], P(None, 'dp'), may hold values from -3 to 3
- bias_qv: bfloat16 [2, 1024], P(None, ('tensor', 'dp')), may hold values from -3 to 3
- up_bias: bfloat16 [4096], P(('tensor', 'dp')), may hold values from -3 to 3
- teacher: bfloat16 [16, 1568, 1024], P('dp', 'tensor'), may hold values from -6 to 6
Outputs:
- out: bfloat16 [16, 1568, 1024], P('dp', 'tensor')
- grad_in: bfloat16 [16, 1568, 1024], P('dp', 'tensor')
- grad_qkv: float32 [3, 1024, 1024], P(None, 'dp', 'tensor')
- grad_out: float32 [1024, 1024], P('tensor', 'dp')
- grad_up: float32 [1024, 4096], P('dp', 'tensor')
- grad_down: float32 [4096, 1024], P('tensor', 'dp')
- grad_gain: float32 [2, 1024], P(None, ('dp', 'tensor'))
- grad_shift: float32 [4, 1024], P(None, ('dp', 'tensor'))
- grad_bias_qv: float32 [2, 1024], P(None, ('tensor', 'dp'))
- grad_up_bias: float32 [4096], P(('tensor', 'dp'))
All inputs are finite; a program needn't handle non-finite values.
Results may differ from a plain program's by a relative error of at most 0.005.
The roundings to bfloat16 on the way count: a program that leaves them out, or rounds other values in their place, can miss the bound.
Values may be sent and summed in bfloat16 or wider, within the bound.
No kernel may reach another device: no remote copies, remote signals or barrier semaphores. Data moves between devices by JAX's collectives and lax.ppermute only.
A program may use at most 320 MiB of HBM per device.

v0:
```python
import jax
import jax.numpy as jnp
from jax import lax
from jax.sharding import PartitionSpec as P

HEAD_DIM = 64


EPS = 1e-05


def layer_norm(value, gain, shift):
    mean = jnp.mean(value, -1, keepdims=True)
    centred = value - mean
    spread = jnp.mean(centred * centred, -1, keepdims=True)
    return centred * lax.rsqrt(spread + EPS) * gain + shift


def exact_gelu(value):
    return jax.nn.gelu(value, approximate=False)


def attend_clip(query, keys, values, scale):
    scores = jnp.einsum("qhe,khe->hqk", query, keys, preferred_element_type=jnp.float32) * scale
    top = jnp.max(scores, -1, keepdims=True)
    expd = jnp.exp(scores - top)
    total = jnp.sum(expd, -1, keepdims=True)
    prob = (expd / total).astype(jnp.bfloat16)
    mixed = jnp.einsum("hqk,khe->qhe", prob, values, preferred_element_type=jnp.float32)
    return (mixed.astype(jnp.bfloat16), (top + jnp.log(total))[..., 0])


def attend_back(query, keys, values, d_mixed, logsum, scale):
    scores = jnp.einsum("qhe,khe->hqk", query, keys, preferred_element_type=jnp.float32) * scale
    prob = jnp.exp(scores - logsum[:, :, None])
    d_prob = jnp.einsum("qhe,khe->hqk", d_mixed, values, preferred_element_type=jnp.float32)
    delta = jnp.sum(d_prob * prob, -1, keepdims=True)
    d_scores = (prob * (d_prob - delta)).astype(jnp.bfloat16)
    d_values = jnp.einsum(
        "hqk,qhe->khe", prob.astype(jnp.bfloat16), d_mixed, preferred_element_type=jnp.float32
    )
    d_query = jnp.einsum("hqk,khe->qhe", d_scores, keys, preferred_element_type=jnp.float32) * scale
    d_keys = jnp.einsum("hqk,qhe->khe", d_scores, query, preferred_element_type=jnp.float32) * scale
    return jnp.stack([d_query, d_keys, d_values]).astype(jnp.bfloat16)


def local(clips, w_qkv, w_out, w_up, w_down, norm_gain, shifts, bias_qv, up_bias, teacher):
    wq, wo, wu, wd, gains, shift_all, bias_pair, up_shift = (
        lax.all_gather(w_qkv, "dp", axis=1, tiled=True),
        lax.all_gather(w_out, "dp", axis=1, tiled=True),
        lax.all_gather(w_up, "dp", axis=0, tiled=True),
        lax.all_gather(w_down, "dp", axis=1, tiled=True),
        lax.all_gather(norm_gain, "dp", axis=1, tiled=True),
        lax.all_gather(shifts, "dp", axis=1, tiled=True),
        lax.all_gather(bias_qv, "dp", axis=1, tiled=True),
        lax.all_gather(up_bias, "dp", axis=0, tiled=True),
    )
    gains = gains.astype(jnp.float32)
    shift_all = shift_all.astype(jnp.float32)
    bias_pair = bias_pair.astype(jnp.float32)
    up_shift = up_shift.astype(jnp.float32)
    width = wq.shape[2]
    heads_here = width // HEAD_DIM
    scale = HEAD_DIM ** (-0.5)
    inputs = jnp.swapaxes(clips, 0, 1).astype(jnp.float32)
    first = layer_norm(inputs, gains[0], shift_all[0]).astype(jnp.bfloat16)
    whole_first = lax.all_gather(first, "tensor", axis=0, tiled=True)
    seq = whole_first.shape[0]
    count = whole_first.shape[1]
    projected = jnp.einsum("scd,kde->ksce", whole_first, wq, preferred_element_type=jnp.float32)
    qkv_bias = jnp.stack([bias_pair[0], jnp.zeros_like(bias_pair[0]), bias_pair[1]])
    qkv = (projected + qkv_bias[:, None, None, :]).astype(jnp.bfloat16)

    def heads(value):
        return jnp.swapaxes(value, 0, 1).reshape(count, seq, heads_here, HEAD_DIM)

    query_h, keys_h, values_h = (heads(qkv[0]), heads(qkv[1]), heads(qkv[2]))
    attended, logsum = lax.map(
        lambda item: attend_clip(item[0], item[1], item[2], scale), (query_h, keys_h, values_h)
    )
    mixed = jnp.swapaxes(attended.reshape(count, seq, width), 0, 1)
    piece = mixed
    attn = lax.psum_scatter(
        jnp.einsum("scd,de->sce", piece, wo, preferred_element_type=jnp.float32),
        "tensor",
        scatter_dimension=0,
        tiled=True,
    )
    hidden = inputs + attn + shift_all[2]
    second = layer_norm(hidden, gains[1], shift_all[1]).astype(jnp.bfloat16)
    whole_second = lax.all_gather(second, "tensor", axis=0, tiled=True)
    pre = jnp.einsum("scd,df->scf", whole_second, wu, preferred_element_type=jnp.float32) + up_shift
    active = exact_gelu(pre).astype(jnp.bfloat16)
    piece = active
    ffn = lax.psum_scatter(
        jnp.einsum("scf,fe->sce", piece, wd, preferred_element_type=jnp.float32),
        "tensor",
        scatter_dimension=0,
        tiled=True,
    )
    output = hidden + ffn + shift_all[3]
    d_out = output - jnp.swapaxes(teacher, 0, 1).astype(jnp.float32)
    whole_d_ffn = lax.all_gather(d_out.astype(jnp.bfloat16), "tensor", axis=0, tiled=True)
    d_active = jnp.einsum("sce,fe->scf", whole_d_ffn, wd, preferred_element_type=jnp.float32)
    grad_down = jnp.einsum("scf,sce->fe", active, whole_d_ffn, preferred_element_type=jnp.float32)
    gelu_value, gelu_back = jax.vjp(exact_gelu, pre)
    d_pre = gelu_back(d_active)[0].astype(jnp.bfloat16)
    grad_up_shift = jnp.sum(d_pre.astype(jnp.float32), (0, 1))
    grad_up = jnp.einsum("scd,scf->df", whole_second, d_pre, preferred_element_type=jnp.float32)
    piece = d_pre
    d_second = lax.psum_scatter(
        jnp.einsum("scf,df->scd", piece, wu, preferred_element_type=jnp.float32),
        "tensor",
        scatter_dimension=0,
        tiled=True,
    )
    norm_value, second_back = jax.vjp(layer_norm, hidden, gains[1], shift_all[1])
    d_hidden_norm, grad_gain_two, grad_shift_two = second_back(d_second)
    d_hidden = d_out + d_hidden_norm
    whole_d_attn = lax.all_gather(d_hidden.astype(jnp.bfloat16), "tensor", axis=0, tiled=True)
    d_mixed = jnp.einsum(
        "sce,de->scd", whole_d_attn, wo, preferred_element_type=jnp.float32
    ).astype(jnp.bfloat16)
    grad_out = jnp.einsum("scd,sce->de", mixed, whole_d_attn, preferred_element_type=jnp.float32)
    d_heads = jnp.swapaxes(d_mixed, 0, 1).reshape(count, seq, heads_here, HEAD_DIM)
    d_stacked = lax.map(
        lambda item: attend_back(item[0], item[1], item[2], item[3], item[4], scale),
        (query_h, keys_h, values_h, d_heads, logsum),
    )
    d_qkv = jnp.transpose(d_stacked.reshape(count, 3, seq, width), (1, 2, 0, 3))
    bias_sums = jnp.sum(d_qkv.astype(jnp.float32), (1, 2))
    grad_pair = jnp.stack([bias_sums[0], bias_sums[2]])
    grad_qkv = jnp.einsum("scd,ksce->kde", whole_first, d_qkv, preferred_element_type=jnp.float32)
    piece = d_qkv
    d_first = lax.psum_scatter(
        jnp.einsum("ksce,kde->scd", piece, wq, preferred_element_type=jnp.float32),
        "tensor",
        scatter_dimension=0,
        tiled=True,
    )
    first_value, first_back = jax.vjp(layer_norm, inputs, gains[0], shift_all[0])
    d_in_norm, grad_gain_one, grad_shift_one = first_back(d_first)
    d_inputs = d_hidden + d_in_norm
    sums = (
        lax.psum_scatter(grad_qkv, "dp", scatter_dimension=1, tiled=True),
        lax.psum_scatter(grad_out, "dp", scatter_dimension=1, tiled=True),
        lax.psum_scatter(grad_up, "dp", scatter_dimension=0, tiled=True),
        lax.psum_scatter(grad_down, "dp", scatter_dimension=1, tiled=True),
        lax.psum_scatter(grad_pair, "dp", scatter_dimension=1, tiled=True),
        lax.psum_scatter(grad_up_shift, "dp", scatter_dimension=0, tiled=True),
    )
    grad_gain = jnp.stack([grad_gain_one, grad_gain_two])
    grad_shift = jnp.stack(
        [grad_shift_one, grad_shift_two, jnp.sum(d_hidden, (0, 1)), jnp.sum(d_out, (0, 1))]
    )
    norm_sums = (
        lax.psum_scatter(grad_gain, ("dp", "tensor"), scatter_dimension=1, tiled=True),
        lax.psum_scatter(grad_shift, ("dp", "tensor"), scatter_dimension=1, tiled=True),
    )
    result = jnp.swapaxes(output, 0, 1).astype(jnp.bfloat16)
    grad_in = jnp.swapaxes(d_inputs, 0, 1).astype(jnp.bfloat16)
    return (
        result,
        grad_in,
        sums[0],
        sums[1],
        sums[2],
        sums[3],
        norm_sums[0],
        norm_sums[1],
        sums[4],
        sums[5],
    )


def solution(mesh):
    in_specs = (
        P("dp", "tensor", None),
        P(None, "dp", "tensor"),
        P("tensor", "dp"),
        P("dp", "tensor"),
        P("tensor", "dp"),
        P(None, "dp"),
        P(None, "dp"),
        P(None, ("tensor", "dp")),
        P(("tensor", "dp")),
        P("dp", "tensor", None),
    )
    out_specs = (
        P("dp", "tensor", None),
        P("dp", "tensor", None),
        P(None, "dp", "tensor"),
        P("tensor", "dp"),
        P("dp", "tensor"),
        P("tensor", "dp"),
        P(None, ("dp", "tensor")),
        P(None, ("dp", "tensor")),
        P(None, ("tensor", "dp")),
        P(("tensor", "dp")),
    )
    return jax.shard_map(local, mesh=mesh, in_specs=in_specs, out_specs=out_specs, check_vma=False)
```

profile of v0, /device:TPU:0, one launch (start us, length us, event | category | flops | bytes accessed | tf_op | source)
XLA Modules:
  0.0 2427.1 jit_solution(12441748339226214319)
XLA Ops:
  54.9 103.2 %all-gather.10.cloned.1.call-done = bf16[1568,2,1024]{2,0,1:T(8,128)(2,1)} async-done(((bf16[392,2,1024]{2,0,1:T(8,128)(2,1)}), bf16[1568,2,1024]{2,0,1:T(8,128)(2,1)}) %all-gather.10.cloned.1.call-update) | async-done | bytes 6422544 | tf_op jit(solution)/shard_map/all_gather | solution.py:67
  175.6 102.5 %while.22 = (s32[]{:T(128)}, bf16[2,1568,4,64]{1,3,2,0:T(8,128)(2,1)}, f32[2,4,1568]{2,1,0:T(4,128)S(1)}, bf16[2,1568,4,64]{1,3,2,0:T(8,128)(2,1)}, bf16[2,1568,...) while((s32[]{:T(128)}, bf16[2,1568,4,64]{1,3,2,0:T(8,128)(2,1)}, ...), condition=%wide.region_5.6_spmd, body=%wide.region_2.5_spmd.sunk | while | flops 2606536704 | bytes 124037712 | solution.py:78
  175.6 16.1 multiply_reduce_fusion.7
  191.7 16.9 fusion.144
  208.5 18.3 fusion.145
  226.8 16.1 multiply_reduce_fusion.7
  243.0 16.9 fusion.144
  259.8 18.3 fusion.145
  291.2 213.8 %reduce-scatter.18.cloned.1.call-done = f32[392,2,1024]{2,0,1:T(8,128)} async-done(((f32[1568,2,1024]{2,0,1:T(8,128)}), f32[392,2,1024]{2,0,1:T(8,128)}) %reduce-scatter.18.cloned.1.call-update) | async-done | bytes 3211280 | tf_op jit(solution)/shard_map/reduce_scatter | solution.py:83
  519.6 16.1 all-gather.16.cloned.1.call-done
  535.7 119.5 %all-gather.14.cloned.1.call-done = bf16[1568,2,1024]{2,0,1:T(8,128)(2,1)} async-done(((bf16[392,2,1024]{2,0,1:T(8,128)(2,1)}), bf16[1568,2,1024]{2,0,1:T(8,128)(2,1)}) %all-gather.14.cloned.1.call-update) | async-done | bytes 6422544 | tf_op jit(solution)/shard_map/all_gather | solution.py:91
  655.3 18.2 fusion.75
  673.4 32.5 %multiply_convert_fusion.1 = (bf16[1568,2,1024]{2,0,1:T(8,128)(2,1)}, f32[1568,2,1024]{2,0,1:T(8,128)}) fusion(f32[1568,2,1024]{2,0,1:T(8,128)} %get-tuple-element.198, f32[1024]{0:T(1024)S(1)} %bitcast.284, u8[1568,1024]{1,0:T(8,128)(4,1)S(1)} %get-tuple-element.137, u8[1568,1024]{1,0:T(8,128)(4,1)S(1)} %get-tuple-element.136), kind=kLoop, calls=%fused_computation.63 | loop fusion | flops 227999744 | bytes 35328000 | tf_op jit(solution)/shard_map/convert_element_type | solution.py:93
  719.2 214.2 %reduce-scatter.20.cloned.1.call-done = f32[392,2,1024]{2,0,1:T(8,128)} async-done(((f32[1568,2,1024]{2,0,1:T(8,128)}), f32[392,2,1024]{2,0,1:T(8,128)}) %reduce-scatter.20.cloned.1.call-update) | async-done | bytes 3211280 | tf_op jit(solution)/shard_map/reduce_scatter | solution.py:95
  940.8 118.7 %all-gather.20.cloned.1.call-done = bf16[1568,2,1024]{2,0,1:T(8,128)(2,1)} async-done(((bf16[392,2,1024]{2,0,1:T(8,128)(2,1)}), bf16[1568,2,1024]{2,0,1:T(8,128)(2,1)}) %all-gather.20.cloned.1.call-update) | async-done | bytes 6422544 | tf_op jit(solution)/shard_map/all_gather | solution.py:103
  1059.4 20.2 convert_reduce_fusion
  1092.7 214.4 %reduce-scatter.22.cloned.1.call-done = f32[392,2,1024]{2,0,1:T(8,128)} async-done(((f32[1568,2,1024]{2,0,1:T(8,128)}), f32[392,2,1024]{2,0,1:T(8,128)}) %reduce-scatter.22.cloned.1.call-update) | async-done | bytes 3211280 | tf_op jit(solution)/shard_map/reduce_scatter | solution.py:111
  1319.1 118.6 %all-gather.22.cloned.1.call-done = bf16[1568,2,1024]{2,0,1:T(8,128)(2,1)} async-done(((bf16[392,2,1024]{2,0,1:T(8,128)(2,1)}), bf16[1568,2,1024]{2,0,1:T(8,128)(2,1)}) %all-gather.22.cloned.1.call-update) | async-done | bytes 6422544 | tf_op jit(solution)/shard_map/all_gather | solution.py:120
  1447.1 236.9 %while.23 = (s32[]{:T(128)}, bf16[2,3,1568,4,64]{2,4,3,1,0:T(8,128)(2,1)}, bf16[2,1568,4,64]{1,3,2,0:T(8,128)(2,1)S(1)}, bf16[2,1568,4,64]{1,3,2,0:T(8,128)(2,1)...) while((s32[]{:T(128)}, ...), condition=%wide.region_15.16_spmd, body=%wide.region_13.15_spmd.sunk | while | flops 6381979648 | bytes 313366624 | solution.py:126
  1447.5 16.3 subtract_exponential_fusion.3
  1479.8 27.1 %multiply_reduce_fusion.8 = (f32[4,1568]{1,0:T(4,128)S(1)}, f32[4,1568,1568]{1,2,0:T(8,128)}) fusion(f32[4,1568,1568]{1,2,0:T(8,128)} %subtract_exponential_fusion.3, bf16[2,1568,4,64]{1,3,2,0:T(8,128)(2,1)} %get-tuple-element.332, s32[]{:T(128)S(6)} %copy.99, bf16[2,1568,4,64]{1,3,2,0:T(8,128)(2,1)} %get-tuple-element.331), kind=kOutput, calls=%fused_computation.20.clone.1 | convolution fusion | flops 1278478208 | bytes 82814464 | tf_op jit(solution)/shard_map/while/body/eval_jaxpr/qhe,khe->hqk/dot_general | solution.py:36
  1506.9 33.6 %multiply_convert_fusion.3 = bf16[4,1568,1568]{1,2,0:T(8,128)(2,1)} fusion(f32[4,1568,1568]{1,2,0:T(8,128)} %subtract_exponential_fusion.3, f32[4,1568,1568]{1,2,0:T(8,128)} %get-tuple-element.287, f32[4,1568]{1,0:T(4,128)S(1)} %get-tuple-element.288), kind=kLoop, calls=%fused_computation.19.clone.1 | loop fusion | flops 29503488 | bytes 98370048 | tf_op jit(solution)/shard_map/while/body/eval_jaxpr/convert_element_type | solution.py:38
  1565.7 16.2 subtract_exponential_fusion.3
  1597.9 27.1 %multiply_reduce_fusion.8 = (f32[4,1568]{1,0:T(4,128)S(1)}, f32[4,1568,1568]{1,2,0:T(8,128)}) fusion(f32[4,1568,1568]{1,2,0:T(8,128)} %subtract_exponential_fusion.3, bf16[2,1568,4,64]{1,3,2,0:T(8,128)(2,1)} %get-tuple-element.332, s32[]{:T(128)S(6)} %copy.99, bf16[2,1568,4,64]{1,3,2,0:T(8,128)(2,1)} %get-tuple-element.331), kind=kOutput, calls=%fused_computation.20.clone.1 | convolution fusion | flops 1278478208 | bytes 82814464 | tf_op jit(solution)/shard_map/while/body/eval_jaxpr/qhe,khe->hqk/dot_general | solution.py:36
  1625.1 33.6 %multiply_convert_fusion.3 = bf16[4,1568,1568]{1,2,0:T(8,128)(2,1)} fusion(f32[4,1568,1568]{1,2,0:T(8,128)} %subtract_exponential_fusion.3, f32[4,1568,1568]{1,2,0:T(8,128)} %get-tuple-element.287, f32[4,1568]{1,0:T(4,128)S(1)} %get-tuple-element.288), kind=kLoop, calls=%fused_computation.19.clone.1 | loop fusion | flops 29503488 | bytes 98370048 | tf_op jit(solution)/shard_map/while/body/eval_jaxpr/convert_element_type | solution.py:38
  1717.6 199.2 %reduce-scatter.24.cloned.1.call-done = f32[392,2,1024]{2,0,1:T(8,128)} async-done(((f32[1568,2,1024]{2,0,1:T(8,128)}), f32[392,2,1024]{2,0,1:T(8,128)}) %reduce-scatter.24.cloned.1.call-update) | async-done | bytes 3211280 | tf_op jit(solution)/shard_map/reduce_scatter | solution.py:135
  1973.4 31.3 %reduce-scatter.26.cloned.1.call-done = f32[3,128,256]{1,2,0:T(8,128)} async-done(((f32[3,1024,256]{1,2,0:T(8,128)}), f32[3,128,256]{1,2,0:T(8,128)}) %reduce-scatter.26.cloned.1.call-update) | async-done | bytes 393232 | tf_op jit(solution)/shard_map/reduce_scatter | solution.py:145
  2011.0 129.9 %reduce-scatter.34.cloned.1.call-done = f32[32,2]{1,0:T(8,128)} async-done(((f32[1024,2]{1,0:T(8,128)}), f32[32,2]{1,0:T(8,128)}) %reduce-scatter.34.cloned.1.call-update) | async-done | bytes 272
  2142.3 131.2 %reduce-scatter.36.cloned.1.call-done = f32[32,4]{1,0:T(8,128)} async-done(((f32[1024,4]{1,0:T(8,128)}), f32[32,4]{1,0:T(8,128)}) %reduce-scatter.36.cloned.1.call-update) | async-done | bytes 528
  2274.8 50.1 %reduce-scatter.30.cloned.1.call-done = f32[128,1024]{1,0:T(8,128)} async-done(((f32[1024,1024]{1,0:T(8,128)}), f32[128,1024]{1,0:T(8,128)}) %reduce-scatter.30.cloned.1.call-update) | async-done | bytes 524304 | tf_op jit(solution)/shard_map/reduce_scatter | solution.py:147
  2324.9 55.5 %reduce-scatter.32.cloned.1.call-done = f32[1024,128]{1,0:T(8,128)} async-done(((f32[1024,1024]{1,0:T(8,128)}), f32[1024,128]{1,0:T(8,128)}) %reduce-scatter.32.cloned.1.call-update) | async-done | bytes 524304 | tf_op jit(solution)/shard_map/reduce_scatter | solution.py:148
  2380.4 39.7 %reduce-scatter.28.cloned.1.call-done = f32[256,128]{1,0:T(8,128)} async-done(((f32[256,1024]{1,0:T(8,128)}), f32[256,128]{1,0:T(8,128)}) %reduce-scatter.28.cloned.1.call-update) | async-done | bytes 131088 | tf_op jit(solution)/shard_map/reduce_scatter | solution.py:146
  (192 shorter events, 328.4 us)
Async XLA Ops:
  7.2 36.8 %copy-start.20 = (bf16[256,128]{1,0:T(8,128)(2,1)S(1)}, bf16[256,128]{1,0:T(8,128)(2,1)}, u32[]{:S(2)}) copy-start(bf16[256,128]{1,0:T(8,128)(2,1)} %param.16) | copy-start | bytes 196612
  7.2 47.7 %all-gather.12.cloned.1.call-start = ((), (), s32[]{:S(2)}) async-start(), calls=%async_computation.12 | async-start | bytes 1769472 | tf_op jit(solution)/shard_map/all_gather | solution.py:49
  7.9 150.1 %all-gather.10.cloned.1.call-start = ((), (), s32[]{:S(2)}) async-start(), calls=%async_computation.11 | async-start | bytes 8028160 | tf_op jit(solution)/shard_map/all_gather | solution.py:67
  35.9 469.2 %reduce-scatter.18.cloned.1.call-start = ((), (), s32[]{:S(2)}) async-start(), calls=%async_computation.13 | async-start | bytes 16056320 | tf_op jit(solution)/shard_map/reduce_scatter | solution.py:83
  290.6 214.5 %copy-start.29 = (f32[1,1024]{1,0:T(1,128)S(1)}, f32[1,1024]{1,0:T(1,128)}, u32[]{:S(2)}) copy-start(f32[1,1024]{1,0:T(1,128)} %get-tuple-element.189) | copy-start | bytes 12292
  290.6 245.1 %all-gather.16.cloned.1.call-start = ((), (), s32[]{:S(2)}) async-start(), calls=%async_computation.15 | async-start | bytes 2359296 | tf_op jit(solution)/shard_map/all_gather | solution.py:51
  291.2 364.1 %all-gather.14.cloned.1.call-start = ((), (), s32[]{:S(2)}) async-start(), calls=%async_computation.14 | async-start | bytes 8028160 | tf_op jit(solution)/shard_map/all_gather | solution.py:91
  510.2 195.7 %all-gather.18.cloned.1.call-start = ((), (), s32[]{:S(2)}) async-start(), calls=%async_computation.16 | async-start | bytes 2359296 | tf_op jit(solution)/shard_map/all_gather | solution.py:52
  510.8 422.6 %reduce-scatter.20.cloned.1.call-start = ((), (), s32[]{:S(2)}) async-start(), calls=%async_computation.17 | async-start | bytes 16056320 | tf_op jit(solution)/shard_map/reduce_scatter | solution.py:95
  719.0 214.5 %copy-start.25 = (f32[1,1024]{1,0:T(1,128)S(1)}, f32[1,1024]{1,0:T(1,128)}, u32[]{:S(2)}) copy-start(f32[1,1024]{1,0:T(1,128)} %get-tuple-element.191) | copy-start | bytes 12292
  719.0 340.4 %all-gather.20.cloned.1.call-start = ((), (), s32[]{:S(2)}) async-start(), calls=%async_computation.18 | async-start | bytes 8028160 | tf_op jit(solution)/shard_map/all_gather | solution.py:103
  940.7 366.3 %reduce-scatter.22.cloned.1.call-start = ((), (), s32[]{:S(2)}) async-start(), calls=%async_computation.19 | async-start | bytes 16056320 | tf_op jit(solution)/shard_map/reduce_scatter | solution.py:111
  1092.6 345.1 %all-gather.22.cloned.1.call-start = ((), (), s32[]{:S(2)}) async-start(), calls=%async_computation.20 | async-start | bytes 8028160 | tf_op jit(solution)/shard_map/all_gather | solution.py:120
  1319.0 597.8 %reduce-scatter.24.cloned.1.call-start = ((), (), s32[]{:S(2)}) async-start(), calls=%async_computation.21 | async-start | bytes 16056320 | tf_op jit(solution)/shard_map/reduce_scatter | solution.py:135
  1319.0 128.1 %copy-start.1 = (bf16[2,1568,4,64]{1,3,2,0:T(8,128)(2,1)S(1)}, bf16[2,1568,4,64]{1,3,2,0:T(8,128)(2,1)}, u32[]{:S(2)}) copy-start(bf16[2,1568,4,64]{1,3,2,0:T(8,128)(2,1)} %copy-done) | copy-start | bytes 4816900
  1319.0 128.1 %copy-start.3 = (bf16[2,1568,4,64]{1,3,2,0:T(8,128)(2,1)S(1)}, bf16[2,1568,4,64]{1,3,2,0:T(8,128)(2,1)}, u32[]{:S(2)}) copy-start(bf16[2,1568,4,64]{1,3,2,0:T(8,128)(2,1)} %copy-done.2) | copy-start | bytes 4816900
  1702.4 269.7 %reduce-scatter.38.cloned.1.call-start = ((), (), s32[]{:S(2)}) async-start(), calls=%async_computation.28 | async-start | bytes 147456
  1706.3 210.5 %copy-start.4 = (bf16[2,392,1024]{2,1,0:T(8,128)(2,1)S(1)}, bf16[2,392,1024]{2,1,0:T(8,128)(2,1)}, u32[]{:S(2)}) copy-start(bf16[2,392,1024]{2,1,0:T(8,128)(2,1)} %param.14) | copy-start | bytes 4816900
  1706.4 210.4 %copy-start.14 = (f32[392,2]{0,1:T(2,128)S(1)}, f32[392,2]{0,1:T(2,128)}, u32[]{:S(2)}) copy-start(f32[392,2]{0,1:T(2,128)} %copy-done.13) | copy-start | bytes 9412
  1706.4 210.4 %copy-start.16 = (f32[1,1024]{1,0:T(1,128)S(1)}, f32[1,1024]{1,0:T(1,128)}, u32[]{:S(2)}) copy-start(f32[1,1024]{1,0:T(1,128)} %copy-done.15) | copy-start | bytes 12292
  1706.4 298.4 %reduce-scatter.26.cloned.1.call-start = ((), (), s32[]{:S(2)}) async-start(), calls=%async_computation.22 | async-start | bytes 3538944 | tf_op jit(solution)/shard_map/reduce_scatter | solution.py:145
  1717.5 202.2 %copy-start.22 = (f32[392,2]{0,1:T(2,128)S(1)}, f32[392,2]{0,1:T(2,128)}, u32[]{:S(2)}) copy-start(f32[392,2]{0,1:T(2,128)} %copy-done.21) | copy-start | bytes 9412
  1717.5 202.2 %copy-start.19 = (f32[392,2]{0,1:T(2,128)S(1)}, f32[392,2]{0,1:T(2,128)}, u32[]{:S(2)}) copy-start(f32[392,2]{0,1:T(2,128)} %copy-done.18) | copy-start | bytes 9412
  1717.5 203.9 %copy-start.23 = (f32[1024]{0:T(1024)S(1)}, f32[1024]{0:T(1024)}, u32[]{:S(2)}) copy-start(f32[1024]{0:T(1024)} %get-tuple-element.138) | copy-start | bytes 12292
  1717.5 205.1 %copy-start.24 = (f32[1024]{0:T(1024)S(1)}, f32[1024]{0:T(1024)}, u32[]{:S(2)}) copy-start(f32[1024]{0:T(1024)} %get-tuple-element.174) | copy-start | bytes 12292
  1717.6 205.1 %copy-start.26 = (f32[1024]{0:T(1024)S(1)}, f32[1024]{0:T(1024)}, u32[]{:S(2)}) copy-start(f32[1024]{0:T(1024)} %get-tuple-element.144) | copy-start | bytes 12292
  1717.6 205.1 %copy-start.27 = (f32[1024]{0:T(1024)S(1)}, f32[1024]{0:T(1024)}, u32[]{:S(2)}) copy-start(f32[1024]{0:T(1024)} %get-tuple-element.172) | copy-start | bytes 12292
  1717.6 423.3 %reduce-scatter.34.cloned.1.call-start = ((), (), s32[]{:S(2)}) async-start(), calls=%async_computation.26 | async-start | bytes 540672
  1922.6 350.9 %reduce-scatter.36.cloned.1.call-start = ((), (), s32[]{:S(2)}) async-start(), calls=%async_computation.27 | async-start | bytes 540672
  1923.7 401.2 %reduce-scatter.30.cloned.1.call-start = ((), (), s32[]{:S(2)}) async-start(), calls=%async_computation.24 | async-start | bytes 4718592 | tf_op jit(solution)/shard_map/reduce_scatter | solution.py:147
  1936.5 443.9 %reduce-scatter.32.cloned.1.call-start = ((), (), s32[]{:S(2)}) async-start(), calls=%async_computation.25 | async-start | bytes 4718592 | tf_op jit(solution)/shard_map/reduce_scatter | solution.py:148
  1949.4 470.7 %reduce-scatter.28.cloned.1.call-start = ((), (), s32[]{:S(2)}) async-start(), calls=%async_computation.23 | async-start | bytes 1179648 | tf_op jit(solution)/shard_map/reduce_scatter | solution.py:146
  (21 other events, 114.2 us)
Sparse Core Ops, SparseCore 0:
  9.9 28.4 all-gather.11
  40.5 117.4 all-gather.9
  290.7 214.2 reduce-scatter.17
  506.8 28.9 all-gather.15
  537.7 117.4 all-gather.13
  657.0 26.3 all-gather.17
  719.1 214.2 reduce-scatter.19
  940.8 118.5 all-gather.19
  1092.7 214.2 reduce-scatter.21
  1319.1 118.5 all-gather.21
  1702.5 214.2 reduce-scatter.23
  1920.2 34.3 reduce-scatter.37
  1958.4 46.2 reduce-scatter.25
  2006.8 134.0 reduce-scatter.33
  2143.1 130.3 reduce-scatter.35
  2277.2 47.6 reduce-scatter.29
  2329.1 51.2 reduce-scatter.31
  2384.0 36.0 reduce-scatter.27
where the time goes:
time: 2430 us
  waiting for transfers between devices  1760 us (72%)
  matrix products  371 us (15%)
  other arithmetic  179 us (7%)
  blocking collectives  60.2 us (2%)
  local copies, waits for them, and re-layouts  42.5 us (2%)
    unnamed x21, waiting for transfers between devices  263 us
    reduce_scatter x1, waiting for transfers between devices, local(): lax.psum_scatter(jnp.einsum('scf,df->scd', piece, wu, preferred_element_t...  214 us
    reduce_scatter x1, waiting for transfers between devices, local(): lax.psum_scatter(jnp.einsum('scf,fe->sce', piece, wd, preferred_element_t...  214 us
    reduce_scatter x1, waiting for transfers between devices, local(): lax.psum_scatter(jnp.einsum('scd,de->sce', piece, wo, preferred_element_t...  214 us
    reduce_scatter x1, waiting for transfers between devices, local(): lax.psum_scatter(jnp.einsum('ksce,kde->scd', piece, wq, preferred_element...  199 us
    all_gather x1, waiting for transfers between devices, local(): whole_second = lax.all_gather(second, 'tensor', axis=0, tiled=True)  120 us
    all_gather x1, waiting for transfers between devices, local(): lax.all_gather(d_out.astype(jnp.bfloat16), 'tensor', axis=0, tiled=True)  119 us
    all_gather x1, waiting for transfers between devices, local(): lax.all_gather(d_hidden.astype(jnp.bfloat16), 'tensor', axis=0, tiled=True)  119 us
  transfers between devices with their start and end apart: 18, of which 15 were waited for; matrix products, arithmetic and copies ran while one was open for 5% of the time, Pallas kernels for 0%

commit v1 on v0

--- a/solution.py
+++ b/solution.py
@@ -1,7 +1,11 @@
+import functools
+
 import jax
 import jax.numpy as jnp
 from jax import lax
-from jax.sharding import PartitionSpec as P
+from jax.experimental import pallas as pl
+from jax.experimental.pallas import tpu as pltpu
+from jax.sharding import Mesh, PartitionSpec as P
 
 HEAD_DIM = 64
 
@@ -173,7 +177,518 @@
     )
 
 
+BF = jnp.bfloat16
+F32 = jnp.float32
+LOG2E = 1.4426950408889634
+VMEM_LIMIT = 56 * 2**20
+ROW_NN = (((1,), (0,)), ((), ()))
+ROW_NT = (((1,), (1,)), ((), ()))
+ROW_TN = (((0,), (0,)), ((), ()))
+
+
+def dot(left, right, dims=ROW_NN):
+    return lax.dot_general(left, right, dims, preferred_element_type=F32)
+
+
+def three_parts(value):
+    high = value.astype(BF)
+    rest = value - high.astype(F32)
+    middle = rest.astype(BF)
+    return high, middle, (rest - middle.astype(F32)).astype(BF)
+
+
+def query_blocks(seq, step):
+    blocks = []
+    start = 0
+    while start < seq:
+        used = min(step, seq - start)
+        blocks.append((start, -(-used // 128) * 128, used))
+        start += used
+    return blocks
+
+
+def pad_columns(value, width):
+    extra = width - value.shape[1]
+    if extra == 0:
+        return value
+    return jnp.concatenate([value, jnp.zeros((value.shape[0], extra), value.dtype)], 1)
+
+
+def attend_kernel(seq, padded, step, q_ref, k_ref, v_ref, o_ref, wide_ref, lse_ref, key_s, query_s, value_s):
+    key = k_ref[0]
+    key_s[...] = jnp.concatenate([key, key, key, jnp.zeros((HEAD_DIM, seq), BF)], 0).T
+    parts = three_parts(pad_columns(q_ref[0].astype(F32) * (LOG2E * HEAD_DIM**-0.5), padded))
+    query_s[...] = jnp.concatenate([*parts, jnp.zeros((HEAD_DIM, padded), BF)], 0)
+    value_s[0:HEAD_DIM] = v_ref[0]
+    value_s[HEAD_DIM : HEAD_DIM + 16] = jnp.ones((16, seq), BF)
+    for start, width, used in query_blocks(seq, step):
+        scores = dot(key_s[...], query_s[:, start : start + width])
+        top = jnp.max(scores, 0, keepdims=True)
+        prob = jnp.exp2(scores - top).astype(BF)
+        mixed = dot(value_s[...], prob)
+        total = mixed[HEAD_DIM : HEAD_DIM + 1]
+        result = (mixed[0:HEAD_DIM] * (1.0 / total))[:, :used]
+        wide_ref[0, :, start : start + used] = result
+        o_ref[0, :, start : start + used] = result.astype(BF)
+        lse_ref[0, :, start : start + used] = (top + jnp.log2(total))[:, :used]
+
+
+def attend(query, keys, values, step):
+    heads, _, seq = query.shape
+    padded = -(-seq // 128) * 128
+    spec = lambda rows: pl.BlockSpec((1, rows, seq), lambda h: (h, 0, 0))
+    return pl.pallas_call(
+        functools.partial(attend_kernel, seq, padded, step),
+        grid=(heads,),
+        in_specs=[spec(HEAD_DIM)] * 3,
+        out_specs=[spec(HEAD_DIM), spec(HEAD_DIM), spec(1)],
+        out_shape=[
+            jax.ShapeDtypeStruct((heads, HEAD_DIM, seq), BF),
+            jax.ShapeDtypeStruct((heads, HEAD_DIM, seq), F32),
+            jax.ShapeDtypeStruct((heads, 1, seq), F32),
+        ],
+        scratch_shapes=[
+            pltpu.VMEM((seq, 4 * HEAD_DIM), BF),
+            pltpu.VMEM((4 * HEAD_DIM, padded), BF),
+            pltpu.VMEM((HEAD_DIM + 16, seq), BF),
+        ],
+        compiler_params=pltpu.CompilerParams(vmem_limit_bytes=VMEM_LIMIT),
+        cost_estimate=pl.CostEstimate(
+            flops=4 * heads * seq * seq * 256, bytes_accessed=12 * heads * seq * HEAD_DIM, transcendentals=heads * seq * seq
+        ),
+        name="attend",
+    )(query, keys, values)
+
+
+def attend_back_kernel(seq, padded, step, q_ref, k_ref, v_ref, d_ref, lse_ref, delta_ref, out_ref, key_s, query_s, value_s, dmix_s):
+    key = k_ref[0]
+    ones = jnp.ones((16, seq), BF)
+    key_s[...] = jnp.concatenate([key, key, key, ones, jnp.zeros((48, seq), BF)], 0).T
+    value_s[...] = jnp.concatenate([v_ref[0], ones, jnp.zeros((48, seq), BF)], 0).T
+    query = pad_columns(q_ref[0], padded).astype(F32)
+    blank = jnp.zeros((13, padded), BF)
+    tail = jnp.zeros((48, padded), BF)
+    lse = jnp.concatenate([*three_parts(pad_columns(-lse_ref[0], padded)), blank], 0)
+    delta = jnp.concatenate([*three_parts(pad_columns(-delta_ref[0], padded)), blank], 0)
+    query_s[...] = jnp.concatenate([*three_parts(query * (LOG2E * HEAD_DIM**-0.5)), lse, tail], 0)
+    dmix_s[...] = jnp.concatenate([pad_columns(d_ref[0], padded), delta, tail], 0)
+    scaled = (query * HEAD_DIM**-0.5).astype(BF)
+    d_keys = jnp.zeros((HEAD_DIM, seq), F32)
+    d_values = jnp.zeros((HEAD_DIM, seq), F32)
+    for start, width, used in query_blocks(seq, step):
+        prob = jnp.exp2(dot(key_s[...], query_s[:, start : start + width]))
+        d_scores = (prob * dot(value_s[...], dmix_s[:, start : start + width])).astype(BF)
+        d_values = d_values + dot(dmix_s[0:HEAD_DIM, start : start + width], prob.astype(BF), ROW_NT)
+        d_keys = d_keys + dot(scaled[:, start : start + width], d_scores, ROW_NT)
+        d_query = dot(key, d_scores) * HEAD_DIM**-0.5
+        out_ref[0, 0, :, start : start + used] = d_query[:, :used].astype(BF)
+    out_ref[1, 0] = d_keys.astype(BF)
+    out_ref[2, 0] = d_values.astype(BF)
+
+
+def attend_backward(query, keys, values, d_mixed, lse, delta, step):
+    heads, _, seq = query.shape
+    padded = -(-seq // 128) * 128
+    spec = lambda rows: pl.BlockSpec((1, rows, seq), lambda h: (h, 0, 0))
+    return pl.pallas_call(
+        functools.partial(attend_back_kernel, seq, padded, step),
+        grid=(heads,),
+        in_specs=[spec(HEAD_DIM)] * 4 + [spec(1)] * 2,
+        out_specs=pl.BlockSpec((3, 1, HEAD_DIM, seq), lambda h: (0, h, 0, 0)),
+        out_shape=jax.ShapeDtypeStruct((3, heads, HEAD_DIM, seq), BF),
+        scratch_shapes=[
+            pltpu.VMEM((seq, 4 * HEAD_DIM), BF),
+            pltpu.VMEM((4 * HEAD_DIM, padded), BF),
+            pltpu.VMEM((seq, 2 * HEAD_DIM), BF),
+            pltpu.VMEM((2 * HEAD_DIM, padded), BF),
+        ],
+        compiler_params=pltpu.CompilerParams(vmem_limit_bytes=VMEM_LIMIT),
+        cost_estimate=pl.CostEstimate(
+            flops=10 * heads * seq * seq * 256, bytes_accessed=14 * heads * seq * HEAD_DIM, transcendentals=heads * seq * seq
+        ),
+        name="attend_backward",
+    )(query, keys, values, d_mixed, lse, delta)
+
+
+def gelu_pair(value):
+    cdf = 0.5 * (1.0 + lax.erf(value * 0.7071067811865476))
+    slope = cdf + value * (jnp.exp(-0.5 * value * value) * 0.3989422804014327)
+    return value * cdf, slope
+
+
+def ffn_kernel(x_ref, w_ref, b_ref, out_ref, g_ref, slope_ref):
+    width = x_ref.shape[1]
+    units = w_ref.shape[4]
+    pre = dot(x_ref[...], w_ref[:, 0, 0].reshape(width, units)) + b_ref[0]
+    active, slope = gelu_pair(pre)
+    active = active.astype(BF)
+    g_ref[...] = active
+    slope_ref[...] = slope
+    part = dot(active, w_ref[:, 0, 1].reshape(width, units), ROW_NT)
+
+    @pl.when(pl.program_id(0) == 0)
+    def _():
+        out_ref[...] = part
+
+    @pl.when(pl.program_id(0) > 0)
+    def _():
+        out_ref[...] += part
+
+
+def ffn_forward(x, weights, bias):
+    rows, width = x.shape
+    owners, blocks, _, part, units = weights.shape
+    whole = pl.BlockSpec((rows, width), lambda t: (0, 0))
+    column = pl.BlockSpec((rows, units), lambda t: (0, t))
+    return pl.pallas_call(
+        ffn_kernel,
+        grid=(blocks,),
+        in_specs=[
+            whole,
+            pl.BlockSpec((owners, 1, 2, part, units), lambda t: (0, t, 0, 0, 0)),
+            pl.BlockSpec((1, 1, units), lambda t: (t, 0, 0)),
+        ],
+        out_specs=[whole, column, column],
+        out_shape=[
+            jax.ShapeDtypeStruct((rows, width), F32),
+            jax.ShapeDtypeStruct((rows, blocks * units), BF),
+            jax.ShapeDtypeStruct((rows, blocks * units), F32),
+        ],
+        compiler_params=pltpu.CompilerParams(vmem_limit_bytes=VMEM_LIMIT),
+        cost_estimate=pl.CostEstimate(
+            flops=4 * rows * width * blocks * units, bytes_accessed=2 * weights.size + 10 * rows * blocks * units, transcendentals=rows * blocks * units
+        ),
+        name="ffn",
+    )(x, weights, bias)
+
+
+def ffn_back_kernel(d_ref, w_ref, slope_ref, out_ref, dpre_ref, sum_ref):
+    width = d_ref.shape[1]
+    units = w_ref.shape[4]
+    d_active = dot(d_ref[...], w_ref[:, 0, 1].reshape(width, units))
+    d_pre = (d_active * slope_ref[...]).astype(BF)
+    dpre_ref[...] = d_pre
+    sum_ref[0] = jnp.sum(d_pre.astype(F32), 0, keepdims=True)
+    part = dot(d_pre, w_ref[:, 0, 0].reshape(width, units), ROW_NT)
+
+    @pl.when(pl.program_id(0) == 0)
+    def _():
+        out_ref[...] = part
+
+    @pl.when(pl.program_id(0) > 0)
+    def _():
+        out_ref[...] += part
+
+
+def ffn_backward(d_out, weights, slope):
+    rows, width = d_out.shape
+    owners, blocks, _, part, units = weights.shape
+    whole = pl.BlockSpec((rows, width), lambda t: (0, 0))
+    column = pl.BlockSpec((rows, units), lambda t: (0, t))
+    return pl.pallas_call(
+        ffn_back_kernel,
+        grid=(blocks,),
+        in_specs=[
+            whole,
+            pl.BlockSpec((owners, 1, 2, part, units), lambda t: (0, t, 0, 0, 0)),
+            column,
+        ],
+        out_specs=[whole, column, pl.BlockSpec((1, 1, units), lambda t: (t, 0, 0))],
+        out_shape=[
+            jax.ShapeDtypeStruct((rows, width), F32),
+            jax.ShapeDtypeStruct((rows, blocks * units), BF),
+            jax.ShapeDtypeStruct((blocks, 1, units), F32),
+        ],
+        compiler_params=pltpu.CompilerParams(vmem_limit_bytes=VMEM_LIMIT),
+        cost_estimate=pl.CostEstimate(
+            flops=4 * rows * width * blocks * units, bytes_accessed=2 * weights.size + 6 * rows * blocks * units, transcendentals=0
+        ),
+        name="ffn_backward",
+    )(d_out, weights, slope)
+
+
+def ffn_grad_kernel(xa_ref, xb_ref, da_ref, db_ref, pa_ref, pb_ref, ga_ref, gb_ref, up_ref, down_ref, x_s, d_s):
+    half = xa_ref.shape[0]
+
+    @pl.when(pl.program_id(0) == 0)
+    def _():
+        x_s[...] = jnp.concatenate([xa_ref[...], xb_ref[...]], 0).T
+        d_s[...] = jnp.concatenate([da_ref[...], db_ref[...]], 0).T
+
+    d_pre = jnp.concatenate([pa_ref[...], pb_ref[...]], 0)
+    up_ref[...] = dot(x_s[...], d_pre).astype(BF).reshape(up_ref.shape)
+    active = jnp.concatenate([ga_ref[...], gb_ref[...]], 0)
+    down_ref[...] = dot(d_s[...], active).astype(BF).reshape(down_ref.shape)
+
+
+def ffn_grads(xa, xb, da, db, pa, pb, ga, gb, blocks):
+    rows, width = xa.shape
+    units = pa.shape[1] // blocks
+    whole = pl.BlockSpec((rows, width), lambda t: (0, 0))
+    column = pl.BlockSpec((rows, units), lambda t: (0, t))
+    shape = (2, 2, blocks, width // 4, units)
+    out = pl.BlockSpec((2, 2, 1, width // 4, units), lambda t: (0, 0, t, 0, 0))
+    return pl.pallas_call(
+        ffn_grad_kernel,
+        grid=(blocks,),
+        in_specs=[whole] * 4 + [column] * 4,
+        out_specs=[out, out],
+        out_shape=[jax.ShapeDtypeStruct(shape, BF)] * 2,
+        scratch_shapes=[pltpu.VMEM((width, 2 * rows), BF)] * 2,
+        compiler_params=pltpu.CompilerParams(vmem_limit_bytes=VMEM_LIMIT),
+        cost_estimate=pl.CostEstimate(
+            flops=8 * rows * width * blocks * units, bytes_accessed=8 * rows * width + 8 * rows * blocks * units + 4 * width * blocks * units, transcendentals=0
+        ),
+        name="ffn_grads",
+    )(xa, xb, da, db, pa, pb, ga, gb)
+
+
+def swap(value, axis):
+    return lax.ppermute(value, axis, [(0, 1), (1, 0)])
+
+
+def ordered(bit, mine, other, axis):
+    return jnp.concatenate([jnp.where(bit == 0, mine, other), jnp.where(bit == 0, other, mine)], axis)
+
+
+def chain_gather(value, place, size):
+    up = [(i, i + 1) for i in range(size - 1)]
+    down = [(i + 1, i) for i in range(size - 1)]
+    below, above = [value], [value]
+    for _ in range(size - 1):
+        below.append(lax.ppermute(below[-1], "t", up))
+        above.append(lax.ppermute(above[-1], "t", down))
+    row = jnp.stack(below[:0:-1] + [value] + above[1:])
+    return lax.dynamic_slice_in_dim(row, size - 1 - place, size, 0)
+
+
+def chain_scatter(value, place, size):
+    up = [(i, i + 1) for i in range(size - 1)]
+    down = [(i + 1, i) for i in range(size - 1)]
+    blank = jnp.zeros_like(value[0])
+    row = jnp.concatenate([jnp.stack([blank] * (size - 1)), value, jnp.stack([blank] * (size - 1))])
+    at = lambda away: lax.dynamic_index_in_dim(row, size - 1 + place + away, 0, keepdims=False)
+    rising, falling = None, None
+    for away in range(size - 1, 0, -1):
+        lift, drop = at(away), at(-away)
+        if rising is not None:
+            lift = (lift.astype(F32) + rising.astype(F32)).astype(BF)
+            drop = (drop.astype(F32) + falling.astype(F32)).astype(BF)
+        rising = lax.ppermute(lift, "t", up)
+        falling = lax.ppermute(drop, "t", down)
+    return at(0).astype(F32) + rising.astype(F32) + falling.astype(F32)
+
+
+def halve(value, bit, axis, name):
+    mine = lax.dynamic_index_in_dim(value, bit, axis, keepdims=False)
+    other = lax.dynamic_index_in_dim(value, 1 - bit, axis, keepdims=False)
+    return (mine.astype(F32) + swap(other, name).astype(F32)).astype(BF)
+
+
+def moments(value):
+    mean = jnp.mean(value, -1, keepdims=True)
+    centred = value - mean
+    scale = lax.rsqrt(jnp.mean(centred * centred, -1, keepdims=True) + EPS)
+    return centred, scale
+
+
+def norm_back(d_value, centred, scale, gain):
+    unit = centred * scale
+    d_unit = d_value * gain
+    grad_in = scale * (d_unit - jnp.mean(d_unit, -1, keepdims=True) - unit * jnp.mean(d_unit * unit, -1, keepdims=True))
+    return grad_in, jnp.sum(d_value * unit, 0), jnp.sum(d_value, 0)
+
+
+def clip_local(clips, w_qkv, w_out, w_up, w_down, norm_gain, shifts, bias_qv, up_bias, teacher):
+    y, x, c, t = (lax.axis_index(name) for name in ("y", "x", "c", "t"))
+    every = ("y", "x", "c", "t")
+    steps = 4
+    width = clips.shape[2]
+    odd = t % 2
+
+    first_way, second_way = [], []
+    for column in range(4):
+        for core in range(2):
+            for place in range(4):
+                source = (column * 2 + core) * 4 + place
+                to = (column * 2 + place // 2) * 4 + 2 * core
+                first_way.append((source, to + place % 2))
+                second_way.append((source, to + 1 - place % 2))
+    back = lambda way: [(b, a) for a, b in way]
+
+    def to_chip(value):
+        pick = lambda i: lax.dynamic_index_in_dim(value, i, 0, keepdims=False)
+        return jnp.concatenate([lax.ppermute(pick(odd), every, first_way), lax.ppermute(pick(1 - odd), every, second_way)])
+
+    def from_chip(value):
+        near = lax.ppermute(value[: value.shape[0] // 2], every, back(first_way))
+        far = lax.ppermute(value[value.shape[0] // 2 :], every, back(second_way))
+        return jnp.stack([jnp.where(odd == 0, near, far), jnp.where(odd == 0, far, near)])
+
+    vectors = jnp.concatenate([norm_gain, shifts, jnp.zeros((2, norm_gain.shape[1]), BF)])
+    for bit, name in ((c, "c"), (x, "x"), (y, "y")):
+        vectors = ordered(bit, vectors, swap(vectors, name), 1)
+    vectors = vectors.astype(F32)
+    gains, shift_all = vectors[0:2], vectors[2:6]
+
+    inputs = to_chip(clips)
+
+    dims = w_qkv.shape[1]
+    cols = w_out.shape[0] // 2
+    attn = jnp.concatenate([jnp.swapaxes(w_qkv, 1, 2), w_out[None]]).reshape(4, 2, cols, dims)
+    mine = lax.dynamic_index_in_dim(attn, c, 1, keepdims=False)
+    other = lax.dynamic_index_in_dim(attn, 1 - c, 1, keepdims=False)
+    mine_attn = mine.reshape(4 * cols, dims)
+    other_attn = other.reshape(4 * cols, dims)
+    units = w_up.shape[1] // 2
+    ff = jnp.stack([w_up, w_down.T]).reshape(2, dims, 2, units)
+    mine_ff = lax.dynamic_index_in_dim(ff, c, 2, keepdims=False)
+    other_ff = swap(lax.dynamic_index_in_dim(ff, 1 - c, 2, keepdims=False), "c")
+    ff_piece = ordered(c, mine_ff, other_ff, 1)
+    attn_piece = ordered(c, mine_attn, swap(other_attn, "c"), 1)
+    small = jnp.concatenate([bias_qv.reshape(-1), up_bias, jnp.zeros((2 * dims - bias_qv.size - up_bias.size,), BF)])[None]
+    small_other = swap(small, "c")
+    attn_piece = jnp.concatenate([attn_piece, ordered(c, small, small_other, 0), jnp.zeros((14, 2 * dims), BF)])
+    attn_rows = chain_gather(attn_piece, t, steps)
+    split = 2 * cols
+    part_a, part_b = attn_rows[:, :split], attn_rows[:, split:]
+    part_a = ordered(y, part_a, swap(part_a, "y"), 2)
+    part_b = ordered(x, part_b, swap(part_b, "x"), 2)
+    other_a = swap(part_a, "x")
+    other_b = swap(part_b, "y")
+    piece = 2 * dims
+    part_a = jnp.concatenate(
+        [ordered(x, part_a[..., i * piece : (i + 1) * piece], other_a[..., i * piece : (i + 1) * piece], 2) for i in range(2)], 2
+    )
+    part_b = ordered(y, part_b, other_b, 2)
+    arrange = lambda value: jnp.swapaxes(value.reshape(steps, 2, cols, width), 0, 1).reshape(2, steps * cols, width)
+    w_qk = arrange(part_a)
+    w_vo = arrange(part_b[:, : 2 * cols])
+    w_in = jnp.concatenate([w_qk, w_vo[:1]]).reshape(3 * steps * cols, width)
+    w_back = w_vo[1]
+    biases = part_b[:, 2 * cols : 2 * cols + 2].reshape(steps, 2, 4, piece).astype(F32)
+    biases = lax.dynamic_slice_in_dim(jnp.transpose(biases, (0, 2, 1, 3)).reshape(steps, 8, piece), 4 * c, 4, 1)
+    lane = bias_qv.shape[1]
+    bias_pair = jnp.transpose(biases[..., : 2 * lane].reshape(steps, 4, 2, lane), (2, 0, 1, 3)).reshape(2, steps * cols)
+    up_shift = biases[..., 2 * lane : 2 * lane + up_bias.size].reshape(steps, 1, units)
+
+    ff_all = lax.all_gather(ff_piece, ("y", "x", "t"), axis=0, tiled=False).reshape(4, steps, 2, 2 * dims, units)
+
+    inputs = inputs.astype(F32)
+    centred_one, scale_one = moments(inputs)
+    first = (centred_one * scale_one * gains[0] + shift_all[0]).astype(BF)
+    whole_first = jnp.concatenate([first, swap(first, "c")])
+    half = first.shape[0]
+    seq = 2 * half
+    bias_in = jnp.concatenate([bias_pair[0], jnp.zeros_like(bias_pair[0]), bias_pair[1]])
+    qkv = (dot(w_in, whole_first, ROW_NT) + bias_in[:, None]).astype(BF)
+    heads = steps * cols // HEAD_DIM
+    query, keys, values = qkv.reshape(3, heads, HEAD_DIM, seq)
+    mixed, mixed_wide, lse = attend(query, keys, values, 1664)
+    flat = mixed.reshape(heads * HEAD_DIM, seq)
+    attn_other = dot(flat[:, half:], w_back, ROW_TN)
+    attn_mine = dot(flat[:, :half], w_back, ROW_TN)
+    hidden = inputs + (attn_mine + swap(attn_other, "c")) + shift_all[2]
+
+    centred_two, scale_two = moments(hidden)
+    second = (centred_two * scale_two * gains[1] + shift_all[1]).astype(BF)
+    second_other = swap(second, "c")
+    out_mine, act_mine, slope_mine = ffn_forward(second, ff_all, up_shift)
+    out_other, act_other, slope_other = ffn_forward(second_other, ff_all, up_shift)
+    output = hidden + (out_mine + swap(out_other, "c")) + shift_all[3]
+    d_out = output - to_chip(teacher).astype(F32)
+    result = from_chip(output.astype(BF))
+    d_ffn = d_out.astype(BF)
+    d_ffn_other = swap(d_ffn, "c")
+    d_second, d_pre, sum_mine = ffn_backward(d_ffn, ff_all, slope_mine)
+    d_second_other, d_pre_other, sum_other = ffn_backward(d_ffn_other, ff_all, slope_other)
+    up_sum = (sum_mine + sum_other).reshape(steps, units)
+    d_second = d_second + swap(d_second_other, "c")
+    grad_up, grad_down = ffn_grads(second, second_other, d_ffn, d_ffn_other, d_pre, d_pre_other, act_mine, act_other, steps)
+    grad_up = halve(halve(grad_up, x, 1, "x"), y, 0, "y")
+    grad_down = halve(halve(grad_down, y, 0, "y"), x, 0, "x")
+    grad_ff = chain_scatter(jnp.stack([grad_up, grad_down], 1), t, steps).reshape(2, 2, dims, units)
+    mine = lax.dynamic_index_in_dim(grad_ff, c, 1, keepdims=False)
+    other = swap(lax.dynamic_index_in_dim(grad_ff, 1 - c, 1, keepdims=False), "c")
+    grad_ff = ordered(c, mine, other, 2)
+
+    d_norm, grad_gain_two, grad_shift_two = norm_back(d_second, centred_two, scale_two, gains[1])
+    d_hidden = d_out + d_norm
+    d_attn = d_hidden.astype(BF)
+    d_attn = jnp.concatenate([d_attn, swap(d_attn, "c")])
+
+    d_mixed = dot(w_back, d_attn, ROW_NT).astype(BF)
+    grad_out = dot(flat, d_attn)
+    d_heads = d_mixed.reshape(heads, HEAD_DIM, seq)
+    delta = jnp.sum(d_heads.astype(F32) * mixed_wide, 1, keepdims=True)
+    d_qkv = attend_backward(query, keys, values, d_heads, lse, delta, 256)
+    d_flat = d_qkv.reshape(3 * heads * HEAD_DIM, seq)
+    d_first_other = dot(d_flat[:, half:], w_in, ROW_TN)
+    d_first = dot(d_flat[:, :half], w_in, ROW_TN) + swap(d_first_other, "c")
+    grad_in = dot(d_flat, whole_first)
+    bias_sums = jnp.sum(d_qkv.astype(F32), 3).reshape(3, steps * cols)
+    d_norm, grad_gain_one, grad_shift_one = norm_back(d_first, centred_one, scale_one, gains[0])
+    d_inputs = from_chip((d_hidden + d_norm).astype(BF))
+
+    grad_attn = jnp.concatenate([grad_in, grad_out]).astype(BF).reshape(4, steps, cols, 2, 2, piece)
+    grad_a = halve(halve(grad_attn[:2], x, 4, "x"), y, 3, "y")
+    grad_b = halve(halve(grad_attn[2:], y, 3, "y"), x, 3, "x")
+    grad_attn = jnp.swapaxes(jnp.concatenate([grad_a, grad_b]), 0, 1)
+    grad_attn = chain_scatter(grad_attn, t, steps).reshape(4, cols, 2, dims)
+    mine = lax.dynamic_index_in_dim(grad_attn, c, 2, keepdims=False)
+    other = swap(lax.dynamic_index_in_dim(grad_attn, 1 - c, 2, keepdims=False), "c")
+    grad_attn = ordered(c, mine, other, 1)
+
+    normed = jnp.stack([grad_gain_one, grad_gain_two, grad_shift_one, grad_shift_two, jnp.sum(d_hidden, 0), jnp.sum(d_out, 0)])
+    rows = jnp.swapaxes(normed.reshape(6, 32, width // 32), 0, 1).reshape(32, 6 * (width // 32))
+    pair = jnp.transpose(jnp.stack([bias_sums[0], bias_sums[2]]).reshape(2, steps, 4, lane), (2, 1, 0, 3))
+    ups = jnp.transpose(up_sum.reshape(steps, 4, up_bias.size), (1, 0, 2))
+    mine = jnp.concatenate([pair.reshape(16, 2 * lane), ups.reshape(16, up_bias.size)], 1)
+    here = jnp.where((jnp.arange(2) == c)[:, None, None], mine[None], 0.0).reshape(32, mine.shape[1])
+    sums = lax.psum_scatter(jnp.concatenate([rows, here], 1), every, scatter_dimension=0, tiled=True)[0]
+    thin = width // 32
+    vector_sums = sums[: 6 * thin].reshape(6, thin)
+    return (
+        result,
+        d_inputs,
+        jnp.swapaxes(grad_attn[:3], 1, 2),
+        grad_attn[3],
+        grad_ff[0],
+        grad_ff[1].T,
+        vector_sums[:2],
+        vector_sums[2:],
+        sums[6 * thin : 6 * thin + 2 * lane].reshape(2, lane),
+        sums[6 * thin + 2 * lane :],
+    )
+
+
+def clip_per_chip(mesh):
+    fine = Mesh(mesh.devices.reshape(2, 2, 2, 4), ("y", "x", "c", "t"))
+    dp = ("y", "x", "c")
+    in_specs = (
+        P(dp, "t", None),
+        P(None, dp, "t"),
+        P("t", dp),
+        P(dp, "t"),
+        P("t", dp),
+        P(None, dp),
+        P(None, dp),
+        P(None, ("t",) + dp),
+        P(("t",) + dp),
+        P(dp, "t", None),
+    )
+    out_specs = in_specs[:1] * 2 + in_specs[1:5] + (
+        P(None, dp + ("t",)),
+        P(None, dp + ("t",)),
+        P(None, ("t",) + dp),
+        P(("t",) + dp),
+    )
+    return jax.shard_map(clip_local, mesh=fine, in_specs=in_specs, out_specs=out_specs, check_vma=False)
+
+
 def solution(mesh):
+    if dict(mesh.shape) == {"dp": 8, "tensor": 4}:
+        return clip_per_chip(mesh)
     in_specs = (
         P("dp", "tensor", None),
         P(None, "dp", "tensor"),

time: 2430 us -> 749 us (0.31)
  waiting for transfers between devices: 1760 us -> 207 us
  matrix products: 371 us -> 41.6 us
  Pallas kernels: 0 us -> 165 us
  starting transfers between devices: 0.92 us -> 124 us
  other arithmetic: 179 us -> 69.7 us
  local copies, waits for them, and re-layouts: 42.5 us -> 69.8 us
    reduce_scatter x8 -> x0, waiting for transfers between devices: 1020 us -> none  [the longest x1 214 us: local(): lax.psum_scatter(jnp.einsum('scf,df->scd', piece, wu, preferred_element_t...]
    all_gather x7 -> x1, waiting for transfers between devices: 476 us -> 0.01 us  [clip_local(): lax.all_gather(ff_piece, ('y', 'x', 't'), axis=0, tiled=False)]
    dot_general x26 -> x8, matrix products: 371 us -> 41.6 us  [dot(): return lax.dot_general(left, right, dims, preferred_element_type=F32)]
    unnamed x21 -> x1, waiting for transfers between devices: 263 us -> 0.02 us
    ppermute x0 -> x54, waiting for transfers between devices: none -> 207 us  [the longest x28 129 us: swap(): return lax.ppermute(value, axis, [(0, 1), (1, 0)])]
    pallas_call x0 -> x7, Pallas kernels: none -> 165 us  [the longest x1 56.6 us: attend_backward(): pl.pallas_call(functools.partial(attend_back_kernel, seq, padded, step),...]
    ppermute x0 -> x54, starting transfers between devices: none -> 124 us  [the longest x6 39.1 us: chain_scatter(): rising = lax.ppermute(lift, 't', up)]
    convert_element_type x10 -> x17, other arithmetic: 112 us -> 27.5 us  [the longest x6 8.07 us: halve(): return (mine.astype(F32) + swap(other, name).astype(F32)).astype(BF)]
  transfers between devices with their start and end apart: 18 -> 55, of which waited for: 15 -> 18; matrix products, arithmetic and copies ran while one was open for 5% -> 22% of each run, Pallas kernels for 0% -> 15%
where the time goes in v1:
time: 749 us; the launch traced here: 741 us
  waiting for transfers between devices  207 us (28%)
  Pallas kernels  165 us (22%)
  starting transfers between devices  124 us (17%)
  local copies, waits for them, and re-layouts  69.8 us (9%)
  other arithmetic  69.7 us (9%)
  blocking collectives  47.8 us (6%)
  matrix products  41.6 us (6%)
  between operations  16 us (2%)
    ppermute x28, waiting for transfers between devices, swap(): return lax.ppermute(value, axis, [(0, 1), (1, 0)])  129 us
    ppermute x3, waiting for transfers between devices, chain_gather(): above.append(lax.ppermute(above[-1], 't', down))  60.9 us
    pallas_call x1, Pallas kernels, attend_backward(): pl.pallas_call(functools.partial(attend_back_kernel, seq, padded, step),...  56.6 us
    unnamed x1, blocking collectives  47.8 us
    dot_general x8, matrix products, dot(): return lax.dot_general(left, right, dims, preferred_element_type=F32)  41.6 us
    ppermute x6, starting transfers between devices, chain_scatter(): rising = lax.ppermute(lift, 't', up)  39.1 us
    pallas_call x1, Pallas kernels, attend(): pl.pallas_call(functools.partial(attend_kernel, seq, padded, step), grid=...  29.4 us
    pallas_call x2, Pallas kernels, ffn_forward(): pl.pallas_call(ffn_kernel, grid=(blocks,), in_specs=[whole, pl.BlockSpec(...  28.9 us
  transfers between devices with their start and end apart: 55, of which 18 were waited for; matrix products, arithmetic and copies ran while one was open for 22% of the time, Pallas kernels for 15%

profile of v1, /device:TPU:0, one launch (start us, length us, event | category | flops | bytes accessed | tf_op | source)
XLA Modules:
  0.0 740.9 jit_solution(14553999671406517284)
XLA Ops:
  29.2 5.0 collective-permute-start.5
  39.2 5.3 collective-permute-start.6
  46.3 39.9 %collective-permute-done.8 = bf16[528,256]{1,0:T(8,128)(2,1)} collective-permute-done((bf16[528,256]{1,0:T(8,128)(2,1)}, bf16[528,256]{1,0:T(8,128)(2,1)}, u32[]{:S(2)}, u32[]{:S(2)}) %collective-permute-start.8) | collective-permute-done | bytes 270368 | tf_op jit(solution)/shard_map/ppermute | solution.py:460
  91.7 21.0 %collective-permute-done.9 = bf16[528,256]{1,0:T(8,128)(2,1)S(1)} collective-permute-done((bf16[528,256]{1,0:T(8,128)(2,1)}, bf16[528,256]{1,0:T(8,128)(2,1)S(1)}, u32[]{:S(2)}, u32[]{:S(2)}) %collective-permute-start.9) | collective-permute-done | bytes 270368 | tf_op jit(solution)/shard_map/ppermute | solution.py:460
  115.0 12.7 %collective-permute-done.10 = bf16[4,256,256]{2,1,0:T(8,128)(2,1)S(1)} collective-permute-done((bf16[4,256,256]{2,1,0:T(8,128)(2,1)S(1)}, bf16[4,256,256]{2,1,0:T(8,128)(2,1)S(1)}, u32[]{:S(2)}, u32[]{:S(2)}) %collective-permute-start.10) | collective-permute-done | bytes 524320 | tf_op jit(solution)/shard_map/ppermute | solution.py:447
  132.4 32.5 %collective-permute-done.11 = bf16[4,256,512]{2,1,0:T(8,128)(2,1)S(1)} collective-permute-done((bf16[4,256,512]{2,1,0:T(8,128)(2,1)S(1)}, bf16[4,256,512]{2,1,0:T(8,128)(2,1)S(1)}, u32[]{:S(2)}, u32[]{:S(2)}) %collective-permute-start.11) | collective-permute-done | bytes 1048608 | tf_op jit(solution)/shard_map/ppermute | solution.py:447
  171.9 8.7 %add_convert_fusion = bf16[1536,1568]{0,1:T(8,128)(2,1)S(1)} fusion(bf16[1536,1024]{1,0:T(8,128)(2,1)S(1)} %bitcast.236, f32[1536]{0:T(1024)S(1)} %pad_maximum_fusion.23, bf16[784,1024]{1,0:T(8,128)(2,1)} %collective-permute-done.17, bf16[784,1024]{1,0:T(8,128)(2,1)} %fusion.9), kind=kOutput, calls=%fused_computation.1 | convolution fusion | flops 4943740928 | bytes 11180032 | tf_op jit(solution)/shard_map/dot_general | solution.py:190
  192.3 29.4 %attend.1 = (bf16[8,64,1568]{2,1,0:T(8,128)(2,1)}, f32[8,64,1568]{2,1,0:T(8,128)}, f32[8,1,1568]{2,1,0:T(1,128)}) custom-call(bf16[8,64,1568]{2,1,0:T(8,128)(2,1)} %bitcast.242, bf16[8,64,1568]{2,1,0:T(8,128)(2,1)} %bitcast.244, bf16[8,64,1568]{2,1,0:T(8,128)(2,1)} %bitcast.246), custom_call_target="tpu_custom_call" | custom-call | flops 20141047808 | bytes 9633792 | tf_op jit(solution)/shard_map/attend/pallas_call | solution.py:240
  224.3 5.7 collective-permute-done.18
  238.8 14.4 %ffn.3 = (f32[784,1024]{1,0:T(8,128)}, bf16[784,2048]{1,0:T(8,128)(2,1)}, f32[784,2048]{1,0:T(8,128)}) custom-call(bf16[784,1024]{1,0:T(8,128)(2,1)} %collective-permute-done.20.x_ref.xb_ref, bf16[4,4,2,256,512]{4,3,2,1,0:T(8,128)(2,1)} %bitcast.273, f32[4,1,512]{2,1,0:T(1,128)} %bitcast.271), custom_call_target="tpu_custom_call" | custom-call | flops 6576668672 | bytes 24444928 | tf_op jit(solution)/shard_map/ffn/pallas_call | solution.py:343
  254.1 6.1 collective-permute-start.25
  260.2 14.6 %ffn.2 = (f32[784,1024]{1,0:T(8,128)}, bf16[784,2048]{1,0:T(8,128)(2,1)}, f32[784,2048]{1,0:T(8,128)}) custom-call(bf16[784,1024]{1,0:T(8,128)(2,1)} %add_convert_fusion.1.x_ref.xa_ref, bf16[4,4,2,256,512]{4,3,2,1,0:T(8,128)(2,1)} %bitcast.274, f32[4,1,512]{2,1,0:T(1,128)} %bitcast.272), custom_call_target="tpu_custom_call" | custom-call | flops 6576668672 | bytes 24444928 | tf_op jit(solution)/shard_map/ffn/pallas_call | solution.py:343
  285.2 8.3 %collective-permute-start.26 = (bf16[784,1024]{1,0:T(8,128)(2,1)}, bf16[784,1024]{1,0:T(8,128)(2,1)}, u32[]{:S(2)}, u32[]{:S(2)}) collective-permute-start(bf16[784,1024]{1,0:T(8,128)(2,1)} %fusion.63.d_ref.da_ref), channel_id=1, source_target_pairs={{0,4},{4,0},{1,5},{5,1},{2,6},{6,2},{3,7},{7,3},{8,12},{12,8},{9,1... | collective-permute-start | bytes 4816904 | tf_op jit(solution)/shard_map/ppermute | solution.py:447
  293.6 13.3 %ffn_backward.2 = (f32[784,1024]{1,0:T(8,128)}, bf16[784,2048]{1,0:T(8,128)(2,1)}, f32[4,1,512]{2,1,0:T(1,128)}) custom-call(bf16[784,1024]{1,0:T(8,128)(2,1)} %fusion.63.d_ref.da_ref, bf16[4,4,2,256,512]{4,3,2,1,0:T(8,128)(2,1)} %bitcast.275, f32[784,2048]{1,0:T(8,128)} %get-tuple-element.30.slope_ref), custom_call_target="tpu_custom_call" | custom-call | flops 6576668672 | bytes 18022400 | tf_op jit(solution)/shard_map/ffn_backward/pallas_call | solution.py:388
  306.9 13.3 %ffn_backward.3 = (f32[784,1024]{1,0:T(8,128)}, bf16[784,2048]{1,0:T(8,128)(2,1)}, f32[4,1,512]{2,1,0:T(1,128)}) custom-call(bf16[784,1024]{1,0:T(8,128)(2,1)} %collective-permute-done.26.d_ref.db_ref, bf16[4,4,2,256,512]{4,3,2,1,0:T(8,128)(2,1)} %bitcast.276, f32[784,2048]{1,0:T(8,128)} %get-tuple-element.32.slope_ref), custom_call_target="tpu_custom_call" | custom-call | flops 6576668672 | bytes 18022400 | tf_op jit(solution)/shard_map/ffn_backward/pallas_call | solution.py:388
  320.1 23.6 %ffn_grads.1 = (bf16[2,2,4,256,512]{4,3,2,1,0:T(8,128)(2,1)}, bf16[2,2,4,256,512]{4,3,2,1,0:T(8,128)(2,1)}) custom-call(bf16[784,1024]{1,0:T(8,128)(2,1)} %add_convert_fusion.1.x_ref.xa_ref, bf16[784,1024]{1,0:T(8,128)(2,1)} %collective-permute-done.20.x_ref.xb_ref, bf16[784,1024]{1,0:T(8,128)(2,1)} %fusion.63.d_ref.da_ref, ...), custom_call_target="tpu_custom_call" | custom-call | flops 13153337344 | bytes 27656192 | tf_op jit(solution)/shard_map/ffn_grads/pallas_call | solution.py:431
  353.1 41.5 %collective-permute-done.43 = bf16[2,4,256,512]{3,2,1,0:T(8,128)(2,1)} collective-permute-done((bf16[2,4,256,512]{3,2,1,0:T(8,128)(2,1)}, bf16[2,4,256,512]{3,2,1,0:T(8,128)(2,1)}, u32[]{:S(2)}, u32[]{:S(2)}) %collective-permute-start.43) | collective-permute-done | bytes 2097184 | tf_op jit(solution)/shard_map/ppermute | solution.py:447
  406.5 18.5 %collective-permute-done.44 = bf16[4,256,512]{2,1,0:T(8,128)(2,1)} collective-permute-done((bf16[4,256,512]{2,1,0:T(8,128)(2,1)}, bf16[4,256,512]{2,1,0:T(8,128)(2,1)}, u32[]{:S(2)}, u32[]{:S(2)}) %collective-permute-start.44) | collective-permute-done | bytes 1048608 | tf_op jit(solution)/shard_map/ppermute | solution.py:447
  439.4 11.0 %collective-permute-start.47 = (bf16[2,256,512]{2,1,0:T(8,128)(2,1)}, bf16[2,256,512]{2,1,0:T(8,128)(2,1)S(1)}, u32[]{:S(2)}, u32[]{:S(2)}) collective-permute-start(bf16[2,256,512]{2,1,0:T(8,128)(2,1)} %get-tuple-element.103), channel_id=1, source_target_pairs={{0,1},{1,2},{2,3},{4,5},{5,6},{6,7},{8,9},{9,10},{10,11},{12,13},{... | collective-permute-start | bytes 1572872 | tf_op jit(solution)/shard_map/ppermute | solution.py:477
  455.6 7.8 %collective-permute-start.22 = (bf16[392,1024]{1,0:T(8,128)(2,1)}, bf16[392,1024]{1,0:T(8,128)(2,1)}, u32[]{:S(2)}, u32[]{:S(2)}) collective-permute-start(bf16[392,1024]{1,0:T(8,128)(2,1)} %get-tuple-element.129), channel_id=1, source_target_pairs={{0,0},{1,1},{4,2},{5,3},{2,4},{3,5},{6,6},{7,7},{8,8},{9,9},{12,10... | collective-permute-start | bytes 2408456 | tf_op jit(solution)/shard_map/ppermute | solution.py:524
  469.4 7.3 collective-permute-start.48
  485.7 56.6 %attend_backward.1 = bf16[3,8,64,1568]{3,2,1,0:T(8,128)(2,1)} custom-call(bf16[8,64,1568]{2,1,0:T(8,128)(2,1)} %bitcast.243, bf16[8,64,1568]{2,1,0:T(8,128)(2,1)} %bitcast.245, bf16[8,64,1568]{2,1,0:T(8,128)(2,1)} %bitcast.247, bf16[8,64,1568]{2,1,0:T(8,128)(2,1)} %bitcast.227, f32[8,1,1568]{2,1,0:T(1,128)} %get-tuple-element.34.lse_ref, ...), custom_call_target="tpu_custom_call" | custom-call | flops 50352619520 | bytes 11239424 | tf_op jit(solution)/shard_map/attend_backward/pallas_call | solution.py:293
  546.5 7.5 %convolution_convert_fusion = bf16[1536,1024]{1,0:T(8,128)(2,1)S(1)} fusion(bf16[1536,1568]{1,0:T(8,128)(2,1)S(1)} %bitcast.229, bf16[784,1024]{1,0:T(8,128)(2,1)} %collective-permute-done.17, bf16[784,1024]{1,0:T(8,128)(2,1)} %fusion.9), kind=kOutput, calls=%fused_computation.15 | convolution fusion | flops 4940496896 | bytes 11173888 | tf_op jit(solution)/shard_map/dot_general | solution.py:190
  559.9 5.6 constant_dynamic-slice_fusion.7
  581.4 4.6 collective-permute-start.49
  591.6 8.5 %collective-permute-done.34 = bf16[2,4,128,2,256]{4,2,1,0,3:T(8,128)(2,1)S(1)} collective-permute-done((bf16[2,4,128,2,256]{4,2,1,0,3:T(8,128)(2,1)S(1)}, bf16[2,4,128,2,256]{4,2,1,0,3:T(8,128)(2,1)S(1)}, u32[]{:S(2)}, u32[]{:S(2)}) %collective-permute-start.34) | collective-permute-done | bytes 1048608 | tf_op jit(solution)/shard_map/ppermute | solution.py:447
  613.5 6.7 collective-permute-start.36
  637.8 5.0 collective-permute-start.38
  648.6 5.0 collective-permute-done.41
  655.6 7.8 %fusion.15 = (f32[1024]{0:T(1024)S(1)}, f32[784]{0:T(1024)S(1)}, f32[784]{0:T(1024)S(1)}, f32[1024]{0:T(1024)S(1)}, f32[784,1024]{1,0:T(8,128)S(1)}) fusion(f32[784]{0:T(1024)S(1)} %copy-done.39, f32[784]{0:T(1024)S(1)} %copy-done.35, bf16[392,1024]{1,0:T(8,128)(2,1)S(1)} %copy-done.9, bf16[392,1024]{1,0:T(8,128)(2,1)S(1)} %copy-done.6, ...), kind=kOutput, calls=%fused_computation.24 | convolution fusion | flops 2477486592 | bytes 13951232 | tf_op jit(solution)/shard_map/dot_general | solution.py:190
  666.5 7.8 %collective-permute-start.30 = (bf16[392,1024]{1,0:T(8,128)(2,1)}, bf16[392,1024]{1,0:T(8,128)(2,1)}, u32[]{:S(2)}, u32[]{:S(2)}) collective-permute-start(bf16[392,1024]{1,0:T(8,128)(2,1)} %get-tuple-element.125), channel_id=1, source_target_pairs={{0,0},{1,1},{4,2},{5,3},{2,4},{3,5},{6,6},{7,7},{8,8},{9,9},{12,10... | collective-permute-start | bytes 2408456 | tf_op jit(solution)/shard_map/ppermute | solution.py:524
  680.4 47.8 %all-reduce = f32[32,384]{1,0:T(8,128)S(1)} all-reduce(f32[32,384]{1,0:T(8,128)S(1)} %pad_maximum_fusion.19), channel_id=3, replica_groups=mesh['y'=2,'x'=2,'c'=2,'t'=4] {'y','x','c','t'}, use_global_device_ids=true, to_apply=%region_16.17.clone | all-reduce | flops 12288 | bytes 98304
  (358 shorter events, 222.2 us)
Async XLA Ops:
  7.2 231.6 %all-gather.3.cloned.1.call-start = ((), (), s32[]{:S(2)}) async-start(), calls=%async_computation | async-start | bytes 8912896 | tf_op jit(solution)/shard_map/all_gather | solution.py:575
  15.6 28.8 %collective-permute-start.19 = (bf16[2,128,512]{2,1,0:T(8,128)(2,1)}, bf16[2,128,512]{2,1,0:T(8,128)(2,1)}, u32[]{:S(2)}, u32[]{:S(2)}) collective-permute-start(bf16[2,128,512]{2,1,0:T(8,128)(2,1)} %fusion.56), channel_id=1, source_target_pairs={{0,4},{4,0},{1,5},{5,1},{2,6},{6,2},{3,7},{7,3},{8,12},{12,8},{9,1... | collective-permute-start | bytes 786440 | tf_op jit(solution)/shard_map/ppermute | solution.py:447
  35.2 79.3 %collective-permute-start = (bf16[392,1024]{1,0:T(8,128)(2,1)}, bf16[392,1024]{1,0:T(8,128)(2,1)S(1)}, u32[]{:S(2)}, u32[]{:S(2)}) collective-permute-start(bf16[392,1024]{1,0:T(8,128)(2,1)} %get-tuple-element.131), channel_id=1, source_target_pairs={{0,0},{1,1},{2,4},{3,5},{4,2},{5,3},{6,6},{7,7},{8,8},{9,9},{10,12... | collective-permute-start | bytes 2408456 | tf_op jit(solution)/shard_map/ppermute | solution.py:521
  37.0 77.5 %collective-permute-start.1 = (bf16[392,1024]{1,0:T(8,128)(2,1)S(1)}, bf16[392,1024]{1,0:T(8,128)(2,1)S(1)}, u32[]{:S(2)}, u32[]{:S(2)}) collective-permute-start(bf16[392,1024]{1,0:T(8,128)(2,1)S(1)} %get-tuple-element.132), channel_id=1, source_target_pairs={{0,1},{1,0},{2,5},{3,4},{4,3},{5,2},{6,7},{7,6},{8,9},{9,8},{10,13... | collective-permute-start | bytes 2408456 | tf_op jit(solution)/shard_map/ppermute | solution.py:521
  37.9 48.4 %collective-permute-start.8 = (bf16[528,256]{1,0:T(8,128)(2,1)}, bf16[528,256]{1,0:T(8,128)(2,1)}, u32[]{:S(2)}, u32[]{:S(2)}) collective-permute-start(bf16[528,256]{1,0:T(8,128)(2,1)} %collective-permute-done.7), channel_id=1, source_target_pairs={{1,0},{2,1},{3,2},{5,4},{6,5},{7,6},{9,8},{10,9},{11,10},{13,12},{... | collective-permute-start | bytes 811016 | tf_op jit(solution)/shard_map/ppermute | solution.py:460
  39.2 48.4 %collective-permute-start.6 = (bf16[528,256]{1,0:T(8,128)(2,1)}, bf16[528,256]{1,0:T(8,128)(2,1)}, u32[]{:S(2)}, u32[]{:S(2)}) collective-permute-start(bf16[528,256]{1,0:T(8,128)(2,1)} %collective-permute-done.5), channel_id=1, source_target_pairs={{0,1},{1,2},{2,3},{4,5},{5,6},{6,7},{8,9},{9,10},{10,11},{12,13},{... | collective-permute-start | bytes 811016 | tf_op jit(solution)/shard_map/ppermute | solution.py:459
  86.2 26.4 %collective-permute-start.9 = (bf16[528,256]{1,0:T(8,128)(2,1)}, bf16[528,256]{1,0:T(8,128)(2,1)S(1)}, u32[]{:S(2)}, u32[]{:S(2)}) collective-permute-start(bf16[528,256]{1,0:T(8,128)(2,1)} %collective-permute-done.8), channel_id=1, source_target_pairs={{1,0},{2,1},{3,2},{5,4},{6,5},{7,6},{9,8},{10,9},{11,10},{13,12},{... | collective-permute-start | bytes 811016 | tf_op jit(solution)/shard_map/ppermute | solution.py:460
  127.8 37.0 %collective-permute-start.11 = (bf16[4,256,512]{2,1,0:T(8,128)(2,1)S(1)}, bf16[4,256,512]{2,1,0:T(8,128)(2,1)S(1)}, u32[]{:S(2)}, u32[]{:S(2)}) collective-permute-start(bf16[4,256,512]{2,1,0:T(8,128)(2,1)S(1)} %pad_maximum_fusion.15), channel_id=1, source_target_pairs={{0,8},{8,0},{1,9},{9,1},{2,10},{10,2},{3,11},{11,3},{4,12},{12,4},... | collective-permute-start | bytes 3145736 | tf_op jit(solution)/shard_map/ppermute | solution.py:447
  129.3 39.4 %collective-permute-start.13 = (bf16[4,272,512]{2,1,0:T(8,128)(2,1)S(1)}, bf16[4,272,512]{2,1,0:T(8,128)(2,1)S(1)}, u32[]{:S(2)}, u32[]{:S(2)}) collective-permute-start(bf16[4,272,512]{2,1,0:T(8,128)(2,1)S(1)} %pad_maximum_fusion.14), channel_id=1, source_target_pairs={{0,16},{16,0},{1,17},{17,1},{2,18},{18,2},{3,19},{19,3},{4,20},{20... | collective-permute-start | bytes 3342344 | tf_op jit(solution)/shard_map/ppermute | solution.py:447
  132.4 39.5 %collective-permute-start.17 = (bf16[784,1024]{1,0:T(8,128)(2,1)}, bf16[784,1024]{1,0:T(8,128)(2,1)}, u32[]{:S(2)}, u32[]{:S(2)}) collective-permute-start(bf16[784,1024]{1,0:T(8,128)(2,1)} %fusion.9), channel_id=1, source_target_pairs={{0,4},{4,0},{1,5},{5,1},{2,6},{6,2},{3,7},{7,3},{8,12},{12,8},{9,1... | collective-permute-start | bytes 4816904 | tf_op jit(solution)/shard_map/ppermute | solution.py:447
  253.2 25.4 %collective-permute-start.21 = (f32[784,1024]{1,0:T(8,128)}, f32[784,1024]{1,0:T(8,128)}, u32[]{:S(2)}, u32[]{:S(2)}) collective-permute-start(f32[784,1024]{1,0:T(8,128)} %get-tuple-element.29), channel_id=1, source_target_pairs={{0,4},{4,0},{1,5},{5,1},{2,6},{6,2},{3,7},{7,3},{8,12},{12,8},{9,1... | collective-permute-start | bytes 9633800 | tf_op jit(solution)/shard_map/ppermute | solution.py:447
  254.1 24.4 %collective-permute-start.25 = (bf16[392,1024]{1,0:T(8,128)(2,1)S(1)}, bf16[392,1024]{1,0:T(8,128)(2,1)S(1)}, u32[]{:S(2)}, u32[]{:S(2)}) collective-permute-start(bf16[392,1024]{1,0:T(8,128)(2,1)S(1)} %get-tuple-element.134), channel_id=1, source_target_pairs={{0,1},{1,0},{2,5},{3,4},{4,3},{5,2},{6,7},{7,6},{8,9},{9,8},{10,13... | collective-permute-start | bytes 2408456 | tf_op jit(solution)/shard_map/ppermute | solution.py:521
  285.2 21.6 %collective-permute-start.26 = (bf16[784,1024]{1,0:T(8,128)(2,1)}, bf16[784,1024]{1,0:T(8,128)(2,1)}, u32[]{:S(2)}, u32[]{:S(2)}) collective-permute-start(bf16[784,1024]{1,0:T(8,128)(2,1)} %fusion.63.d_ref.da_ref), channel_id=1, source_target_pairs={{0,4},{4,0},{1,5},{5,1},{2,6},{6,2},{3,7},{7,3},{8,12},{12,8},{9,1... | collective-permute-start | bytes 4816904 | tf_op jit(solution)/shard_map/ppermute | solution.py:447
  346.7 47.9 %collective-permute-start.43 = (bf16[2,4,256,512]{3,2,1,0:T(8,128)(2,1)}, bf16[2,4,256,512]{3,2,1,0:T(8,128)(2,1)}, u32[]{:S(2)}, u32[]{:S(2)}) collective-permute-start(bf16[2,4,256,512]{3,2,1,0:T(8,128)(2,1)} %dynamic-slice_bitcast_fusion.1), channel_id=1, source_target_pairs={{0,8},{8,0},{1,9},{9,1},{2,10},{10,2},{3,11},{11,3},{4,12},{12,4},... | collective-permute-start | bytes 6291464 | tf_op jit(solution)/shard_map/ppermute | solution.py:447
  348.0 78.5 %collective-permute-start.27 = (f32[784,1024]{1,0:T(8,128)}, f32[784,1024]{1,0:T(8,128)}, u32[]{:S(2)}, u32[]{:S(2)}) collective-permute-start(f32[784,1024]{1,0:T(8,128)} %get-tuple-element.33), channel_id=1, source_target_pairs={{0,4},{4,0},{1,5},{5,1},{2,6},{6,2},{3,7},{7,3},{8,12},{12,8},{9,1... | collective-permute-start | bytes 9633800 | tf_op jit(solution)/shard_map/ppermute | solution.py:447
  351.1 51.3 %collective-permute-start.45 = (bf16[2,4,256,512]{3,2,1,0:T(8,128)(2,1)}, bf16[2,4,256,512]{3,2,1,0:T(8,128)(2,1)}, u32[]{:S(2)}, u32[]{:S(2)}) collective-permute-start(bf16[2,4,256,512]{3,2,1,0:T(8,128)(2,1)} %dynamic-slice_bitcast_fusion), channel_id=1, source_target_pairs={{0,16},{16,0},{1,17},{17,1},{2,18},{18,2},{3,19},{19,3},{4,20},{20... | collective-permute-start | bytes 6291464 | tf_op jit(solution)/shard_map/ppermute | solution.py:447
  399.8 25.1 %collective-permute-start.44 = (bf16[4,256,512]{2,1,0:T(8,128)(2,1)}, bf16[4,256,512]{2,1,0:T(8,128)(2,1)}, u32[]{:S(2)}, u32[]{:S(2)}) collective-permute-start(bf16[4,256,512]{2,1,0:T(8,128)(2,1)} %dynamic-slice_bitcast_fusion.3), channel_id=1, source_target_pairs={{0,16},{16,0},{1,17},{17,1},{2,18},{18,2},{3,19},{19,3},{4,20},{20... | collective-permute-start | bytes 3145736 | tf_op jit(solution)/shard_map/ppermute | solution.py:447
  405.5 29.5 %collective-permute-start.46 = (bf16[4,256,512]{2,1,0:T(8,128)(2,1)S(1)}, bf16[4,256,512]{2,1,0:T(8,128)(2,1)S(1)}, u32[]{:S(2)}, u32[]{:S(2)}) collective-permute-start(bf16[4,256,512]{2,1,0:T(8,128)(2,1)S(1)} %dynamic-slice_bitcast_fusion.2), channel_id=1, source_target_pairs={{0,8},{8,0},{1,9},{9,1},{2,10},{10,2},{3,11},{11,3},{4,12},{12,4},... | collective-permute-start | bytes 3145736 | tf_op jit(solution)/shard_map/ppermute | solution.py:447
  435.1 41.6 %collective-permute-start.28 = (bf16[784,1024]{1,0:T(8,128)(2,1)}, bf16[784,1024]{1,0:T(8,128)(2,1)}, u32[]{:S(2)}, u32[]{:S(2)}) collective-permute-start(bf16[784,1024]{1,0:T(8,128)(2,1)} %convert_element_type.269), channel_id=1, source_target_pairs={{0,4},{4,0},{1,5},{5,1},{2,6},{6,2},{3,7},{7,3},{8,12},{12,8},{9,1... | collective-permute-start | bytes 4816904 | tf_op jit(solution)/shard_map/ppermute | solution.py:447
  439.4 28.1 %collective-permute-start.47 = (bf16[2,256,512]{2,1,0:T(8,128)(2,1)}, bf16[2,256,512]{2,1,0:T(8,128)(2,1)S(1)}, u32[]{:S(2)}, u32[]{:S(2)}) collective-permute-start(bf16[2,256,512]{2,1,0:T(8,128)(2,1)} %get-tuple-element.103), channel_id=1, source_target_pairs={{0,1},{1,2},{2,3},{4,5},{5,6},{6,7},{8,9},{9,10},{10,11},{12,13},{... | collective-permute-start | bytes 1572872 | tf_op jit(solution)/shard_map/ppermute | solution.py:477
  452.8 113.9 %collective-permute-start.50 = (bf16[2,256,512]{2,1,0:T(8,128)(2,1)}, bf16[2,256,512]{2,1,0:T(8,128)(2,1)}, u32[]{:S(2)}, u32[]{:S(2)}) collective-permute-start(bf16[2,256,512]{2,1,0:T(8,128)(2,1)} %get-tuple-element.104), channel_id=1, source_target_pairs={{1,0},{2,1},{3,2},{5,4},{6,5},{7,6},{9,8},{10,9},{11,10},{13,12},{... | collective-permute-start | bytes 1572872 | tf_op jit(solution)/shard_map/ppermute | solution.py:478
  455.6 123.0 %collective-permute-start.22 = (bf16[392,1024]{1,0:T(8,128)(2,1)}, bf16[392,1024]{1,0:T(8,128)(2,1)}, u32[]{:S(2)}, u32[]{:S(2)}) collective-permute-start(bf16[392,1024]{1,0:T(8,128)(2,1)} %get-tuple-element.129), channel_id=1, source_target_pairs={{0,0},{1,1},{4,2},{5,3},{2,4},{3,5},{6,6},{7,7},{8,8},{9,9},{12,10... | collective-permute-start | bytes 2408456 | tf_op jit(solution)/shard_map/ppermute | solution.py:524
  463.4 115.2 %collective-permute-start.23 = (bf16[392,1024]{1,0:T(8,128)(2,1)}, bf16[392,1024]{1,0:T(8,128)(2,1)}, u32[]{:S(2)}, u32[]{:S(2)}) collective-permute-start(bf16[392,1024]{1,0:T(8,128)(2,1)} %get-tuple-element.130), channel_id=1, source_target_pairs={{1,0},{0,1},{5,2},{4,3},{3,4},{2,5},{7,6},{6,7},{9,8},{8,9},{13,10... | collective-permute-start | bytes 2408456 | tf_op jit(solution)/shard_map/ppermute | solution.py:525
  469.4 97.3 %collective-permute-start.48 = (bf16[2,256,512]{2,1,0:T(8,128)(2,1)}, bf16[2,256,512]{2,1,0:T(8,128)(2,1)}, u32[]{:S(2)}, u32[]{:S(2)}) collective-permute-start(bf16[2,256,512]{2,1,0:T(8,128)(2,1)} %fusion.37), channel_id=1, source_target_pairs={{0,1},{1,2},{2,3},{4,5},{5,6},{6,7},{8,9},{9,10},{10,11},{12,13},{... | collective-permute-start | bytes 1572872 | tf_op jit(solution)/shard_map/ppermute | solution.py:477
  565.7 23.5 %collective-permute-start.32 = (bf16[2,4,128,2,256]{4,2,1,0,3:T(8,128)(2,1)S(1)}, bf16[2,4,128,2,256]{4,2,1,0,3:T(8,128)(2,1)}, u32[]{:S(2)}, u32[]{:S(2)}) collective-permute-start(bf16[2,4,128,2,256]{4,2,1,0,3:T(8,128)(2,1)S(1)} %bitcast.248), channel_id=1, source_target_pairs={{0,8},{8,0},{1,9},{9,1},{2,10},{10,2},{3,11},{11,3},{4,12},{12,4},... | collective-permute-start | bytes 3145736 | tf_op jit(solution)/shard_map/ppermute | solution.py:447
  576.8 23.2 %collective-permute-start.34 = (bf16[2,4,128,2,256]{4,2,1,0,3:T(8,128)(2,1)S(1)}, bf16[2,4,128,2,256]{4,2,1,0,3:T(8,128)(2,1)S(1)}, u32[]{:S(2)}, u32[]{:S(2)}) collective-permute-start(bf16[2,4,128,2,256]{4,2,1,0,3:T(8,128)(2,1)S(1)} %bitcast.249), channel_id=1, source_target_pairs={{0,16},{16,0},{1,17},{17,1},{2,18},{18,2},{3,19},{19,3},{4,20},{20... | collective-permute-start | bytes 3145736 | tf_op jit(solution)/shard_map/ppermute | solution.py:447
  581.4 48.1 %collective-permute-start.49 = (bf16[2,256,512]{2,1,0:T(8,128)(2,1)S(1)}, bf16[2,256,512]{2,1,0:T(8,128)(2,1)S(1)}, u32[]{:S(2)}, u32[]{:S(2)}) collective-permute-start(bf16[2,256,512]{2,1,0:T(8,128)(2,1)S(1)} %copy-done.33), channel_id=1, source_target_pairs={{0,1},{1,2},{2,3},{4,5},{5,6},{6,7},{8,9},{9,10},{10,11},{12,13},{... | collective-permute-start | bytes 1572872 | tf_op jit(solution)/shard_map/ppermute | solution.py:477
  587.6 41.9 %collective-permute-start.52 = (bf16[2,256,512]{2,1,0:T(8,128)(2,1)S(1)}, bf16[2,256,512]{2,1,0:T(8,128)(2,1)S(1)}, u32[]{:S(2)}, u32[]{:S(2)}) collective-permute-start(bf16[2,256,512]{2,1,0:T(8,128)(2,1)S(1)} %fusion.36), channel_id=1, source_target_pairs={{1,0},{2,1},{3,2},{5,4},{6,5},{7,6},{9,8},{10,9},{11,10},{13,12},{... | collective-permute-start | bytes 1572872 | tf_op jit(solution)/shard_map/ppermute | solution.py:478
  606.2 49.3 %collective-permute-start.29 = (f32[784,1024]{1,0:T(8,128)}, f32[784,1024]{1,0:T(8,128)}, u32[]{:S(2)}, u32[]{:S(2)}) collective-permute-start(f32[784,1024]{1,0:T(8,128)} %fusion.18), channel_id=1, source_target_pairs={{0,4},{4,0},{1,5},{5,1},{2,6},{6,2},{3,7},{7,3},{8,12},{12,8},{9,1... | collective-permute-start | bytes 9633800 | tf_op jit(solution)/shard_map/ppermute | solution.py:447
  655.4 22.8 %collective-permute-start.42 = (f32[4,128,128]{2,1,0:T(8,128)S(1)}, f32[4,128,128]{2,1,0:T(8,128)S(1)}, u32[]{:S(2)}, u32[]{:S(2)}) collective-permute-start(f32[4,128,128]{2,1,0:T(8,128)S(1)} %bitcast.253), channel_id=1, source_target_pairs={{0,4},{4,0},{1,5},{5,1},{2,6},{6,2},{3,7},{7,3},{8,12},{12,8},{9,1... | collective-permute-start | bytes 786440 | tf_op jit(solution)/shard_map/ppermute | solution.py:447
  666.5 64.3 %collective-permute-start.30 = (bf16[392,1024]{1,0:T(8,128)(2,1)}, bf16[392,1024]{1,0:T(8,128)(2,1)}, u32[]{:S(2)}, u32[]{:S(2)}) collective-permute-start(bf16[392,1024]{1,0:T(8,128)(2,1)} %get-tuple-element.125), channel_id=1, source_target_pairs={{0,0},{1,1},{4,2},{5,3},{2,4},{3,5},{6,6},{7,7},{8,8},{9,9},{12,10... | collective-permute-start | bytes 2408456 | tf_op jit(solution)/shard_map/ppermute | solution.py:524
  674.4 56.5 %collective-permute-start.31 = (bf16[392,1024]{1,0:T(8,128)(2,1)}, bf16[392,1024]{1,0:T(8,128)(2,1)}, u32[]{:S(2)}, u32[]{:S(2)}) collective-permute-start(bf16[392,1024]{1,0:T(8,128)(2,1)} %get-tuple-element.126), channel_id=1, source_target_pairs={{1,0},{0,1},{5,2},{4,3},{3,4},{2,5},{7,6},{6,7},{9,8},{8,9},{13,10... | collective-permute-start | bytes 2408456 | tf_op jit(solution)/shard_map/ppermute | solution.py:525
  (69 other events, 892.1 us)
Sparse Core Ops, SparseCore 0:
  46.4 146.8 all-gather.2

commit v2 on v0

--- a/solution.py
+++ b/solution.py
@@ -1,7 +1,11 @@
+import functools
+
 import jax
 import jax.numpy as jnp
 from jax import lax
-from jax.sharding import PartitionSpec as P
+from jax.experimental import pallas as pl
+from jax.experimental.pallas import tpu as pltpu
+from jax.sharding import Mesh, PartitionSpec as P
 
 HEAD_DIM = 64
 
@@ -173,7 +177,817 @@
     )
 
 
+BF = jnp.bfloat16
+F32 = jnp.float32
+LOG2E = 1.4426950408889634
+VMEM_LIMIT = 56 * 2**20
+ROW_NN = (((1,), (0,)), ((), ()))
+ROW_NT = (((1,), (1,)), ((), ()))
+PAIR = 2
+
+
+def dot(left, right, dims=ROW_NN):
+    return lax.dot_general(left, right, dims, preferred_element_type=F32)
+
+
+def call(body, grid, in_specs, out_specs, out_shape, args, scratch=(), name=None):
+    return pl.pallas_call(
+        body,
+        grid=grid,
+        in_specs=in_specs,
+        out_specs=out_specs,
+        out_shape=out_shape,
+        scratch_shapes=list(scratch),
+        compiler_params=pltpu.CompilerParams(vmem_limit_bytes=VMEM_LIMIT),
+        cost_estimate=pl.CostEstimate(flops=1000, bytes_accessed=1000, transcendentals=0),
+        name=name,
+    )(*args)
+
+
+def shaped(shape, dtype=BF):
+    return jax.ShapeDtypeStruct(shape, dtype)
+
+
+def three_parts(value):
+    high = value.astype(BF)
+    rest = value - high.astype(F32)
+    middle = rest.astype(BF)
+    return high, middle, (rest - middle.astype(F32)).astype(BF)
+
+
+def query_blocks(seq, step):
+    blocks = []
+    start = 0
+    while start < seq:
+        used = min(step, seq - start)
+        blocks.append((start, -(-used // 128) * 128, used))
+        start += used
+    return blocks
+
+
+def pad_columns(value, width):
+    extra = width - value.shape[1]
+    if extra == 0:
+        return value
+    return jnp.concatenate([value, jnp.zeros((value.shape[0], extra), value.dtype)], 1)
+
+
+def place_block(place_ref, step):
+    return lax.rem(place_ref[0] + step, 4)
+
+
+def row_blocks(ref, place, start, stop):
+    return jnp.concatenate([ref[owner, place, start:stop] for owner in range(ref.shape[0])], 1)
+
+
+def key_blocks(ref, place, which):
+    return jnp.concatenate([ref[owner, place, which] for owner in range(ref.shape[0])], 1)
+
+
+def project_kernel(place_ref, xa_ref, xb_ref, qk_ref, v_ref, b_ref, out_ref, t_ref, x_s):
+    half = xa_ref.shape[0]
+    group = pl.program_id(0)
+
+    @pl.when(group == 0)
+    def _():
+        x_s[0:half] = xa_ref[...]
+        x_s[half:] = xb_ref[...]
+        t_ref[...] = x_s[...].T
+
+    cols = v_ref.shape[2]
+    places = [place_block(place_ref, PAIR * group + p) for p in range(PAIR)]
+    for i in range(3):
+        pick = (lambda place: row_blocks(v_ref, place, 0, cols)) if i == 2 else (lambda place: key_blocks(qk_ref, place, i))
+        weights = jnp.concatenate([pick(place) for place in places], 0)
+        value = dot(weights, x_s[...], ROW_NT) + b_ref[0, i]
+        out_ref[0, i] = value.astype(BF).reshape(out_ref.shape[2:])
+
+
+SCALAR = pl.BlockSpec(memory_space=pltpu.SMEM)
+
+
+def project(place, xa, xb, w_qk, w_vo, bias):
+    half, width = xa.shape
+    owners, places, _, cols, part = w_qk.shape
+    groups = places // PAIR
+    heads = PAIR * cols // HEAD_DIM
+    whole = pl.BlockSpec((half, width), lambda g: (0, 0))
+    return call(
+        project_kernel,
+        (groups,),
+        [
+            SCALAR,
+            whole,
+            whole,
+            pl.BlockSpec((owners, places, 2, cols, part), lambda g: (0, 0, 0, 0, 0)),
+            pl.BlockSpec((owners, places, cols, part), lambda g: (0, 0, 0, 0)),
+            pl.BlockSpec((1, 3, PAIR * cols, 1), lambda g: (g, 0, 0, 0)),
+        ],
+        [
+            pl.BlockSpec((1, 3, heads, HEAD_DIM, 2 * half), lambda g: (g, 0, 0, 0, 0)),
+            pl.BlockSpec((width, 2 * half), lambda g: (0, 0)),
+        ],
+        [shaped((groups, 3, heads, HEAD_DIM, 2 * half)), shaped((width, 2 * half))],
+        (place, xa, xb, w_qk, w_vo, bias),
+        [pltpu.VMEM((2 * half, width), BF)],
+        name="project",
+    )
+
+
+def attend_kernel(seq, padded, step, q_ref, k_ref, v_ref, o_ref, row_ref, wide_ref, lse_ref, key_s, query_s, value_s, hold_s):
+    key = k_ref[0, 0, 0]
+    key_s[...] = jnp.concatenate([key, key, key, jnp.zeros((HEAD_DIM, seq), BF)], 0).T
+    parts = three_parts(pad_columns(q_ref[0, 0, 0].astype(F32) * (LOG2E * HEAD_DIM**-0.5), padded))
+    query_s[...] = jnp.concatenate([*parts, jnp.zeros((HEAD_DIM, padded), BF)], 0)
+    value_s[0:HEAD_DIM] = v_ref[0, 0, 0]
+    value_s[HEAD_DIM : HEAD_DIM + 16] = jnp.ones((16, seq), BF)
+    for start, width, used in query_blocks(seq, step):
+        scores = dot(key_s[...], query_s[:, start : start + width])
+        top = jnp.max(scores, 0, keepdims=True)
+        prob = jnp.exp2(scores - top).astype(BF)
+        mixed = dot(value_s[...], prob)
+        total = mixed[HEAD_DIM : HEAD_DIM + 1]
+        result = (mixed[0:HEAD_DIM] * (1.0 / total))[:, :used]
+        wide_ref[0, :, start : start + used] = result
+        o_ref[0, :, start : start + used] = result.astype(BF)
+        lse_ref[0, :, start : start + used] = (top + jnp.log2(total))[:, :used]
+    odd = pl.program_id(0) % 2
+    hold_s[pl.ds(pl.multiple_of(odd * HEAD_DIM, HEAD_DIM), HEAD_DIM)] = o_ref[0]
+
+    @pl.when(odd == 1)
+    def _():
+        row_ref[...] = hold_s[...].T
+
+
+def attend(qkv, group, step):
+    _, _, heads, _, seq = qkv.shape
+    padded = -(-seq // 128) * 128
+    part = lambda i: pl.BlockSpec((1, 1, 1, HEAD_DIM, seq), lambda h: (group, i, h, 0, 0))
+    spec = lambda rows: pl.BlockSpec((1, rows, seq), lambda h: (h, 0, 0))
+    return call(
+        functools.partial(attend_kernel, seq, padded, step),
+        (heads,),
+        [part(0), part(1), part(2)],
+        [spec(HEAD_DIM), pl.BlockSpec((seq, 2 * HEAD_DIM), lambda h: (0, h // 2)), spec(HEAD_DIM), spec(1)],
+        [
+            shaped((heads, HEAD_DIM, seq)),
+            shaped((seq, heads * HEAD_DIM)),
+            shaped((heads, HEAD_DIM, seq), F32),
+            shaped((heads, 1, seq), F32),
+        ],
+        (qkv, qkv, qkv),
+        [
+            pltpu.VMEM((seq, 4 * HEAD_DIM), BF),
+            pltpu.VMEM((4 * HEAD_DIM, padded), BF),
+            pltpu.VMEM((HEAD_DIM + 16, seq), BF),
+            pltpu.VMEM((2 * HEAD_DIM, seq), BF),
+        ],
+        name="attend",
+    )
+
+
+def attend_back_kernel(
+    seq, padded, step, q_ref, k_ref, v_ref, d_ref, lse_ref, delta_ref, out_ref, sum_ref, key_s, query_s, value_s, dmix_s, hold_s
+):
+    key = k_ref[0, 0, 0]
+    ones = jnp.ones((16, seq), BF)
+    key_s[...] = jnp.concatenate([key, key, key, ones, jnp.zeros((48, seq), BF)], 0).T
+    value_s[...] = jnp.concatenate([v_ref[0, 0, 0], ones, jnp.zeros((48, seq), BF)], 0).T
+    query = pad_columns(q_ref[0, 0, 0], padded).astype(F32)
+    blank = jnp.zeros((13, padded), BF)
+    tail = jnp.zeros((48, padded), BF)
+    lse = jnp.concatenate([*three_parts(pad_columns(-lse_ref[0], padded)), blank], 0)
+    delta = jnp.concatenate([*three_parts(pad_columns(-delta_ref[0], padded)), blank], 0)
+    query_s[...] = jnp.concatenate([*three_parts(query * (LOG2E * HEAD_DIM**-0.5)), lse, tail], 0)
+    dmix_s[...] = jnp.concatenate([pad_columns(d_ref[0], padded), delta, tail], 0)
+    scaled = (query * HEAD_DIM**-0.5).astype(BF)
+    odd = pl.program_id(0) % 2
+    here = pl.ds(pl.multiple_of(odd * HEAD_DIM, HEAD_DIM), HEAD_DIM)
+    d_keys = jnp.zeros((HEAD_DIM, seq), F32)
+    d_values = jnp.zeros((HEAD_DIM, seq), F32)
+    for start, width, used in query_blocks(seq, step):
+        prob = jnp.exp2(dot(key_s[...], query_s[:, start : start + width]))
+        d_scores = (prob * dot(value_s[...], dmix_s[:, start : start + width])).astype(BF)
+        d_values = d_values + dot(dmix_s[0:HEAD_DIM, start : start + width], prob.astype(BF), ROW_NT)
+        d_keys = d_keys + dot(scaled[:, start : start + width], d_scores, ROW_NT)
+        d_query = dot(key, d_scores) * HEAD_DIM**-0.5
+        hold_s[0, here, start : start + used] = d_query[:, :used].astype(BF)
+    hold_s[1, here] = d_keys.astype(BF)
+    hold_s[2, here] = d_values.astype(BF)
+
+    @pl.when(odd == 1)
+    def _():
+        for i in range(3):
+            turned = hold_s[i].T
+            out_ref[i] = turned
+            sum_ref[i] = jnp.sum(turned.astype(F32), 0, keepdims=True)
+
+
+def attend_backward(qkv, d_mixed, lse, delta, group, first, count, step):
+    _, _, inner, _, seq = qkv.shape
+    padded = -(-seq // 128) * 128
+    part = lambda i: pl.BlockSpec((1, 1, 1, HEAD_DIM, seq), lambda h: (group, i, first + h, 0, 0))
+    spec = lambda rows: pl.BlockSpec((1, rows, seq), lambda h: (group * inner + first + h, 0, 0))
+    return call(
+        functools.partial(attend_back_kernel, seq, padded, step),
+        (count,),
+        [part(0), part(1), part(2), spec(HEAD_DIM), pl.BlockSpec((1, 1, seq), lambda h: (first + h, 0, 0)), spec(1)],
+        [
+            pl.BlockSpec((3, seq, 2 * HEAD_DIM), lambda h: (0, 0, h // 2)),
+            pl.BlockSpec((3, 1, 2 * HEAD_DIM), lambda h: (0, 0, h // 2)),
+        ],
+        [shaped((3, seq, count * HEAD_DIM)), shaped((3, 1, count * HEAD_DIM), F32)],
+        (qkv, qkv, qkv, d_mixed, lse, delta),
+        [
+            pltpu.VMEM((seq, 4 * HEAD_DIM), BF),
+            pltpu.VMEM((4 * HEAD_DIM, padded), BF),
+            pltpu.VMEM((seq, 2 * HEAD_DIM), BF),
+            pltpu.VMEM((2 * HEAD_DIM, padded), BF),
+            pltpu.VMEM((3, 2 * HEAD_DIM, seq), BF),
+        ],
+        name="attend_backward",
+    )
+
+
+def mix_kernel(place_ref, oa_ref, ob_ref, w_ref, out_ref):
+    places, cols = w_ref.shape[1:3]
+    weights = [row_blocks(w_ref, place_block(place_ref, j), 0, cols) for j in range(places)]
+    out_ref[...] = dot(jnp.concatenate([oa_ref[...], ob_ref[...]], 1), jnp.concatenate(weights, 0))
+
+
+def mix(place, rows, weights, which):
+    seq, wide = rows[0].shape
+    owners, places, _, part = weights.shape
+    cols = PAIR * wide // places
+    half = seq // 2
+    return call(
+        mix_kernel,
+        (2,),
+        [
+            SCALAR,
+            pl.BlockSpec((half, wide), lambda n: (which, 0)),
+            pl.BlockSpec((half, wide), lambda n: (which, 0)),
+            pl.BlockSpec((owners // 2, places, cols, part), lambda n: (n, 0, 1, 0)),
+        ],
+        pl.BlockSpec((half, owners * part // 2), lambda n: (0, n)),
+        shaped((half, owners * part), F32),
+        (place, *rows, weights),
+        name="mix",
+    )
+
+
+def mix_back_kernel(place_ref, da_ref, db_ref, w_ref, oa_ref, ob_ref, wa_ref, wb_ref, d_ref, delta_ref, *refs):
+    *grad_refs, d_s = refs
+    half, width = da_ref.shape
+    cols = w_ref.shape[2]
+    heads = oa_ref.shape[0]
+    group = pl.program_id(0)
+
+    @pl.when(group == 0)
+    def _():
+        d_s[0:half] = da_ref[...]
+        d_s[half:] = db_ref[...]
+
+    places = [place_block(place_ref, PAIR * group + p) for p in range(PAIR)]
+    weights = jnp.concatenate([row_blocks(w_ref, place, 0, cols) for place in places], 0)
+    d_heads = dot(weights, d_s[...], ROW_NT).astype(BF).reshape(oa_ref.shape)
+    d_ref[...] = d_heads
+    for which, o_ref, wide_ref in ((0, oa_ref, wa_ref), (1, ob_ref, wb_ref)):
+
+        @pl.when(group == which)
+        def _():
+            delta_ref[...] = jnp.sum(d_heads.astype(F32) * wide_ref[...], 1, keepdims=True)
+            grad = dot(o_ref[...].reshape(heads * HEAD_DIM, 2 * half), d_s[...]).astype(BF).T
+            for p in range(PAIR):
+                grad_refs[p][:, :, 0] = grad[:, p * cols : (p + 1) * cols].reshape(2, 2, width // 4, cols)
+
+
+def mix_back(place, da, db, weights, mixed, wide):
+    half, width = da.shape
+    owners, places, _, part = weights.shape
+    heads, _, seq = mixed[0].shape
+    groups = places // PAIR
+    cols = heads * HEAD_DIM // PAIR
+    whole = pl.BlockSpec((half, width), lambda g: (0, 0))
+    fixed = pl.BlockSpec((heads, HEAD_DIM, seq), lambda g: (0, 0, 0))
+    spec = lambda rows: pl.BlockSpec((heads, rows, seq), lambda g: (g, 0, 0))
+    grad = pl.BlockSpec((2, 2, 1, width // 4, cols), lambda g: (0, 0, g, 0, 0))
+    return call(
+        mix_back_kernel,
+        (groups,),
+        [SCALAR, whole, whole, pl.BlockSpec((owners, places, cols, part), lambda g: (0, 0, 1, 0))] + [fixed] * 4,
+        [spec(HEAD_DIM), spec(1), grad, grad],
+        [shaped((groups * heads, HEAD_DIM, seq)), shaped((groups * heads, 1, seq), F32)]
+        + [shaped((2, 2, groups, width // 4, cols))] * PAIR,
+        (place, da, db, weights, *mixed, *wide),
+        [pltpu.VMEM((seq, width), BF)],
+        name="mix_back",
+    )
+
+
+def project_grad_kernel(t_ref, da_ref, db_ref, *grad_refs):
+    width = t_ref.shape[0]
+    cols = da_ref.shape[2]
+    grad = dot(t_ref[...], jnp.concatenate([da_ref[0], db_ref[0]], 1)).astype(BF)
+    for p, grad_ref in enumerate(grad_refs):
+        grad_ref[:, :, 0] = grad[:, p * cols : (p + 1) * cols].reshape(2, 2, width // 4, cols)
+
+
+def project_grads(turned, da, db):
+    width, seq = turned.shape
+    cols = da.shape[2]
+    piece = pl.BlockSpec((1, seq, cols), lambda i: (i, 0, 0))
+    grad = pl.BlockSpec((2, 2, 1, width // 4, cols), lambda i: (0, 0, i, 0, 0))
+    return call(
+        project_grad_kernel,
+        (3,),
+        [pl.BlockSpec((width, seq), lambda i: (0, 0)), piece, piece],
+        [grad, grad],
+        [shaped((2, 2, 3, width // 4, cols))] * 2,
+        (turned, da, db),
+        name="project_grads",
+    )
+
+
+def project_back_kernel(place_ref, a_ref, b_ref, c_ref, d_ref, qk_ref, v_ref, out_ref):
+    total = None
+    for first, refs in ((0, (a_ref, b_ref)), (PAIR, (c_ref, d_ref))):
+        places = [place_block(place_ref, first + p) for p in range(PAIR)]
+        left = [ref[i] for i in range(3) for ref in refs]
+        right = [qk_ref[0, place, i] for i in range(2) for place in places] + [v_ref[0, place] for place in places]
+        part = dot(jnp.concatenate(left, 1), jnp.concatenate(right, 0))
+        total = part if total is None else total + part
+    out_ref[...] = total
+
+
+def project_back(place, pieces, w_qk, w_vo, which):
+    seq = pieces[0].shape[1]
+    owners, places, _, cols, part = w_qk.shape
+    half = seq // 2
+    return call(
+        project_back_kernel,
+        (owners,),
+        [SCALAR]
+        + [pl.BlockSpec((3, half, cols), lambda n: (0, which, 0)) for piece in pieces]
+        + [
+            pl.BlockSpec((1, places, 2, cols, part), lambda n: (n, 0, 0, 0, 0)),
+            pl.BlockSpec((1, places, cols, part), lambda n: (n, 0, 0, 0)),
+        ],
+        pl.BlockSpec((half, part), lambda n: (0, n)),
+        shaped((half, owners * part), F32),
+        (place, *pieces, w_qk, w_vo),
+        name="project_back",
+    )
+
+
+def gelu_pair(value):
+    cdf = 0.5 * (1.0 + lax.erf(value * 0.7071067811865476))
+    return value * cdf, cdf + value * (jnp.exp(-0.5 * value * value) * 0.3989422804014327)
+
+
+def all_blocks(ref):
+    return jnp.concatenate([ref[0, t] for t in range(ref.shape[1])], 1)
+
+
+def ffn_kernel(x_ref, first_ref, last_ref, b_ref, out_ref, g_ref, slope_ref, hold_s):
+    blocks = hold_s.shape[0]
+    step = pl.program_id(0)
+
+    @pl.when(step < blocks)
+    def _():
+        pre = dot(x_ref[...], first_ref[...].reshape(x_ref.shape[1], -1)) + b_ref[0]
+        active, slope = gelu_pair(pre)
+        active = active.astype(BF)
+        hold_s[step] = active
+        g_ref[...] = active
+        slope_ref[...] = slope.astype(BF)
+
+    @pl.when(step >= blocks)
+    def _():
+        left = jnp.concatenate([hold_s[t] for t in range(blocks)], 1)
+        out_ref[...] = dot(left, all_blocks(last_ref), ROW_NT)
+
+
+def ffn_specs(rows, weights):
+    owners, blocks, part, units = weights.shape
+    early = lambda s: jnp.minimum(s, blocks - 1)
+    late = lambda s: jnp.maximum(s - blocks, 0)
+    return (
+        pl.BlockSpec((rows, owners * part), lambda s: (0, 0)),
+        pl.BlockSpec((owners, 1, part, units), lambda s: (0, early(s), 0, 0)),
+        pl.BlockSpec((1, blocks, part, units), lambda s: (late(s), 0, 0, 0)),
+        pl.BlockSpec((rows, units), lambda s: (0, early(s))),
+        pl.BlockSpec((1, 1, units), lambda s: (early(s), 0, 0)),
+        pl.BlockSpec((rows, part), lambda s: (0, late(s))),
+    )
+
+
+def ffn_forward(x, up, down, bias):
+    rows, width = x.shape
+    owners, blocks, _, units = up.shape
+    whole, early, late, column, thin, out = ffn_specs(rows, up)
+    return call(
+        ffn_kernel,
+        (blocks + owners,),
+        [whole, early, late, thin],
+        [out, column, column],
+        [shaped((rows, width), F32), shaped((rows, blocks * units)), shaped((rows, blocks * units))],
+        (x, up, down, bias),
+        [pltpu.VMEM((blocks, rows, units), BF)],
+        name="ffn",
+    )
+
+
+def ffn_back_kernel(d_ref, first_ref, last_ref, slope_ref, out_ref, dpre_ref, sum_ref, hold_s):
+    blocks = hold_s.shape[0]
+    step = pl.program_id(0)
+
+    @pl.when(step < blocks)
+    def _():
+        d_pre = (dot(d_ref[...], first_ref[...].reshape(d_ref.shape[1], -1)) * slope_ref[...].astype(F32)).astype(BF)
+        hold_s[step] = d_pre
+        dpre_ref[...] = d_pre
+        sum_ref[0] = jnp.sum(d_pre.astype(F32), 0, keepdims=True)
+
+    @pl.when(step >= blocks)
+    def _():
+        left = jnp.concatenate([hold_s[t] for t in range(blocks)], 1)
+        out_ref[...] = dot(left, all_blocks(last_ref), ROW_NT)
+
+
+def ffn_backward(d_out, up, down, slope):
+    rows, width = d_out.shape
+    owners, blocks, _, units = up.shape
+    whole, early, late, column, thin, out = ffn_specs(rows, up)
+    return call(
+        ffn_back_kernel,
+        (blocks + owners,),
+        [whole, early, late, column],
+        [out, column, thin],
+        [shaped((rows, width), F32), shaped((rows, blocks * units)), shaped((blocks, 1, units), F32)],
+        (d_out, down, up, slope),
+        [pltpu.VMEM((blocks, rows, units), BF)],
+        name="ffn_backward",
+    )
+
+
+def ffn_grad_kernel(xa_ref, xb_ref, ca_ref, cb_ref, first_ref, last_ref, x_s):
+    half = xa_ref.shape[0]
+
+    @pl.when(pl.program_id(0) == 0)
+    def _():
+        x_s[...] = jnp.concatenate([xa_ref[...], xb_ref[...]], 0).T
+
+    column = jnp.concatenate([ca_ref[...], cb_ref[...]], 0)
+    grad = dot(x_s[...], column).astype(BF).reshape(first_ref.shape)
+
+    @pl.when(pl.program_id(0) < PAIR)
+    def _():
+        first_ref[...] = grad
+
+    @pl.when(pl.program_id(0) >= PAIR)
+    def _():
+        last_ref[...] = grad
+
+
+def ffn_grad(xa, xb, ca, cb, blocks):
+    rows, width = xa.shape
+    units = ca.shape[1] // blocks
+    whole = pl.BlockSpec((rows, width), lambda t: (0, 0))
+    column = pl.BlockSpec((rows, units), lambda t: (0, t))
+    return call(
+        ffn_grad_kernel,
+        (blocks,),
+        [whole, whole, column, column],
+        [
+            pl.BlockSpec((2, 2, 1, width // 4, units), lambda t: (0, 0, jnp.minimum(t, PAIR - 1), 0, 0)),
+            pl.BlockSpec((2, 2, 1, width // 4, units), lambda t: (0, 0, jnp.maximum(t - PAIR, 0), 0, 0)),
+        ],
+        [shaped((2, 2, PAIR, width // 4, units))] * 2,
+        (xa, xb, ca, cb),
+        [pltpu.VMEM((width, 2 * rows), BF)],
+        name="ffn_grad",
+    )
+
+
+def swap(value, axis):
+    return lax.ppermute(value, axis, [(0, 1), (1, 0)])
+
+
+def after(value, *others):
+    return lax.optimization_barrier((value, *others))[0]
+
+
+def together(*values):
+    return lax.optimization_barrier(values)
+
+
+def ordered(bit, mine, other, axis):
+    return jnp.concatenate([jnp.where(bit == 0, mine, other), jnp.where(bit == 0, other, mine)], axis)
+
+
+def chosen(value, bit, axis):
+    return lax.dynamic_index_in_dim(value, bit, axis, keepdims=False)
+
+
+def added(mine, other):
+    return (mine.astype(F32) + other.astype(F32)).astype(BF)
+
+
+def moments(value):
+    mean = jnp.mean(value, -1, keepdims=True)
+    centred = value - mean
+    scale = lax.rsqrt(jnp.mean(centred * centred, -1, keepdims=True) + EPS)
+    return centred, scale
+
+
+def norm_back(d_value, centred, scale, gain):
+    unit = centred * scale
+    d_unit = d_value * gain
+    grad_in = scale * (d_unit - jnp.mean(d_unit, -1, keepdims=True) - unit * jnp.mean(d_unit * unit, -1, keepdims=True))
+    return grad_in, jnp.sum(d_value * unit, 0), jnp.sum(d_value, 0)
+
+
+def clip_local(clips, w_qkv, w_out, w_up, w_down, norm_gain, shifts, bias_qv, up_bias, teacher):
+    y, x, c, t = (lax.axis_index(name) for name in ("y", "x", "c", "t"))
+    every = ("y", "x", "c", "t")
+    steps = 4
+    width = clips.shape[2]
+    odd = t % 2
+
+    first_way, second_way = [], []
+    for column in range(4):
+        for core in range(2):
+            for place in range(4):
+                source = (column * 2 + core) * 4 + place
+                to = (column * 2 + place // 2) * 4 + 2 * core
+                first_way.append((source, to + place % 2))
+                second_way.append((source, to + 1 - place % 2))
+    first_way = [(a, b) for a, b in first_way if a != b]
+    back = lambda way: [(b, a) for a, b in way]
+    stays = t // 2 == c
+
+    def to_chip(value):
+        return lax.ppermute(chosen(value, odd, 0), every, first_way), lax.ppermute(chosen(value, 1 - odd, 0), every, second_way)
+
+    def from_chip(value):
+        half = value.shape[0] // 2
+        return lax.ppermute(value[:half], every, back(first_way)), lax.ppermute(value[half:], every, back(second_way))
+
+    rings = [[(i, (i + away) % steps) for i in range(steps)] for away in range(steps)]
+
+    def ring_gather(value):
+        return tuple(lax.ppermute(value, "t", rings[-j % steps]) for j in range(1, steps))
+
+    def ring_scatter(blocks):
+        return tuple(lax.ppermute(blocks[j], "t", rings[j]) for j in range(1, steps))
+
+    def placed(value, axis):
+        return lax.dynamic_slice_in_dim(jnp.concatenate([value, value], axis), steps - t, steps, axis)
+
+    def relative(value, axis):
+        return lax.dynamic_slice_in_dim(jnp.concatenate([value, value], axis), t, steps, axis)
+
+    def on_chip(value, near, far):
+        return jnp.concatenate([jnp.where(stays, chosen(value, odd, 0), near), far])
+
+    def as_clips(value, near, far):
+        near = jnp.where(stays, value[: value.shape[0] // 2], near)
+        return jnp.stack([jnp.where(odd == 0, near, far), jnp.where(odd == 0, far, near)])
+
+    def piece_of(values, *places):
+        parts = []
+        for value in values:
+            for bit, axis in places:
+                value = chosen(value, bit, axis)
+            parts.append(value)
+        return parts[0] if len(parts) == 1 else jnp.concatenate(parts, parts[0].ndim - 3)
+
+    def scatter_start(one, two):
+        return swap(piece_of(one, (1 - x, 1)), "x"), swap(piece_of(two, (1 - y, 0)), "y")
+
+    def sums_of(one, two, parts, row, column):
+        first = piece_of(one, (x, 1), (row, 0)).astype(F32) + chosen(parts[0], row, 0).astype(F32)
+        return first, piece_of(two, (y, 0), (column, 0)).astype(F32) + chosen(parts[1], column, 0).astype(F32)
+
+    def scatter_middle(one, two, parts):
+        first, second = sums_of(one, two, parts, 1 - y, 1 - x)
+        return swap(first.astype(BF), "y"), swap(second.astype(BF), "x")
+
+    def scatter_end(one, two, parts, ends):
+        first, second = sums_of(one, two, parts, y, x)
+        return (first + ends[0].astype(F32)).astype(BF), (second + ends[1].astype(F32)).astype(BF)
+
+    dims = w_qkv.shape[1]
+    cols = w_out.shape[0] // 2
+    lane = bias_qv.shape[1]
+    units = w_up.shape[1] // 2
+    attn = jnp.concatenate([jnp.swapaxes(w_qkv, 1, 2), w_out[None]]).reshape(4, 2, cols, dims)
+    small = jnp.concatenate([bias_qv.reshape(-1), up_bias, jnp.zeros((16 * dims - bias_qv.size - up_bias.size,), BF)])
+    small = small.reshape(16, dims)
+    mine, other = chosen(attn, c, 1).reshape(4 * cols, dims), chosen(attn, 1 - c, 1).reshape(4 * cols, dims)
+    other = swap(jnp.concatenate([other, small]), "c")
+    attn_piece = ordered(c, jnp.concatenate([mine, small]), other, 1)
+    qk_piece, vo_piece = attn_piece[: 2 * cols], attn_piece[2 * cols :]
+    ff = jnp.stack([w_up, w_down.T]).reshape(2, dims, 2, units)
+    ff_piece = ordered(c, chosen(ff, c, 2), swap(chosen(ff, 1 - c, 2), "c"), 1)
+
+    vectors = jnp.concatenate([norm_gain, shifts, jnp.zeros((2, norm_gain.shape[1]), BF)])
+    for bit, name in ((c, "c"), (x, "x"), (y, "y")):
+        vectors = ordered(bit, vectors, swap(vectors, name), 1)
+    vectors = vectors.astype(F32)
+    gains, shift_all = vectors[0:2], vectors[2:6]
+
+    near, far = to_chip(clips)
+    whole = ("y", "x", "t")
+    w_vo = lax.all_gather(vo_piece, whole, axis=0, tiled=False).reshape(4, steps, 2 * cols + 16, 2 * dims)
+    qk_rows = together(*ring_gather(qk_piece))
+    qk_rows = placed(jnp.stack([qk_piece, *qk_rows]), 0)
+    qk_a, qk_b = qk_rows[:, :cols], qk_rows[:, cols:]
+    swapped, near = together((swap(qk_a, "y"), swap(qk_b, "x")), near)
+    qk_a, qk_b = ordered(y, qk_a[None], swapped[0][None], 0), ordered(x, qk_b[None], swapped[1][None], 0)
+    swapped, far = together((swap(qk_a, "x"), swap(qk_b, "y")), far)
+    qk_a = ordered(x, qk_a[:, None], swapped[0][:, None], 1).reshape(4, steps, cols, 2 * dims)
+    qk_b = ordered(y, qk_b[None], swapped[1][None], 0).reshape(4, steps, cols, 2 * dims)
+    w_qk = jnp.stack([qk_a, qk_b], 2)
+    up_piece, down_piece = ff_piece
+    up_piece, far = together(up_piece, far)
+    up_rows = ring_gather(up_piece)
+    down_piece, w_vo = together(down_piece, w_vo)
+    down_all = lax.all_gather(down_piece, whole, axis=0, tiled=False).reshape(4, steps, 2 * dims, units)
+    place = t.reshape(1)
+
+    rows = w_vo[:, :, 2 * cols :].reshape(4, steps, 16, 2, dims)
+    rows = jnp.transpose(rows, (1, 0, 3, 2, 4)).reshape(steps, 8, 16 * dims).astype(F32)
+    rows = lax.dynamic_slice_in_dim(rows, 4 * c, 4, 1)
+    bias_pair = jnp.transpose(rows[..., : 2 * lane].reshape(steps, 4, 2, lane), (2, 0, 1, 3)).reshape(2, steps, cols)
+    bias_pair = relative(bias_pair, 1).reshape(2, 2, 2 * cols)
+    up_shift = rows[..., 2 * lane : 2 * lane + up_bias.size].reshape(steps, 1, units)
+
+    inputs = on_chip(clips, near, far).astype(F32)
+    centred_one, scale_one = moments(inputs)
+    first = (centred_one * scale_one * gains[0] + shift_all[0]).astype(BF)
+    first_other = swap(first, "c")
+    bias_in = jnp.stack([bias_pair[0], jnp.zeros_like(bias_pair[0]), bias_pair[1]], 1)
+    qkv, turned = project(place, first, first_other, w_qk, w_vo, bias_in[..., None])
+    mixed_a, rows_a, wide_a, lse_a = attend(qkv, 0, 1664)
+    up_rows, rows_a = together(up_rows, rows_a)
+    up_rows = placed(jnp.stack([up_piece, *up_rows]), 0)
+    up_a, up_b = up_rows[:PAIR], up_rows[PAIR:]
+    swapped = swap(up_a, "y"), swap(up_b, "x")
+    mixed_b, rows_b, wide_b, lse_b = attend(after(qkv, rows_a), 1, 1664)
+    swapped, rows_b = together(swapped, rows_b)
+    up_a, up_b = ordered(y, up_a[None], swapped[0][None], 0), ordered(x, up_b[None], swapped[1][None], 0)
+    swapped = swap(up_a, "x"), swap(up_b, "y")
+    rows = (rows_a, rows_b)
+    attn_other = mix(place, rows, w_vo, 1)
+    down_all, attn_other = together(down_all, attn_other)
+    attn_mine = mix(place, (after(rows_a, attn_other), rows_b), w_vo, 0)
+    hidden = inputs + (attn_mine + swap(attn_other, "c")) + shift_all[2]
+
+    centred_two, scale_two = moments(hidden)
+    second = (centred_two * scale_two * gains[1] + shift_all[1]).astype(BF)
+    second_other = swap(second, "c")
+    swapped, second = together(swapped, second)
+    up_a = ordered(x, up_a[:, None], swapped[0][:, None], 1).reshape(4, PAIR, 2 * dims, units)
+    up_b = ordered(y, up_b[None], swapped[1][None], 0).reshape(4, PAIR, 2 * dims, units)
+    up_all = jnp.concatenate([up_a, up_b], 1)
+    near, far = to_chip(after(teacher, second))
+    out_mine, act_mine, slope_mine = ffn_forward(second, up_all, down_all, up_shift)
+    out_mine, near = together(out_mine, near)
+    out_other, act_other, slope_other = ffn_forward(after(second_other, near), up_all, down_all, up_shift)
+    out_other, far = together(out_other, far)
+    output = hidden + (out_mine + swap(out_other, "c")) + shift_all[3]
+    d_out = output - on_chip(teacher, near, far).astype(F32)
+    d_ffn = d_out.astype(BF)
+    d_ffn_other = swap(d_ffn, "c")
+    d_second, d_pre, sum_mine = ffn_backward(d_ffn, up_all, down_all, slope_mine)
+    d_ffn_other, d_pre = together(d_ffn_other, d_pre)
+    d_second_other, d_pre_other, sum_other = ffn_backward(d_ffn_other, up_all, down_all, slope_other)
+    d_second_swapped = swap(d_second_other, "c")
+    up_sum = (sum_mine + sum_other).reshape(steps, units)
+
+    grad_down = ffn_grad(after(d_ffn, d_pre_other), d_ffn_other, act_mine, act_other, steps)
+    grad_down = [grad_down[0]], [grad_down[1]]
+    down = scatter_start(*grad_down)
+    result, grad_down = together(output.astype(BF), grad_down)
+    out_near, out_far = from_chip(result)
+    d_second_swapped, grad_down = together(d_second_swapped, grad_down)
+    d_second = d_second + d_second_swapped
+    d_norm, grad_gain_two, grad_shift_two = norm_back(d_second, centred_two, scale_two, gains[1])
+    d_hidden = d_out + d_norm
+    d_attn = d_hidden.astype(BF)
+    d_attn_other = swap(d_attn, "c")
+    grad_up = ffn_grad(after(second, d_attn), second_other, d_pre, d_pre_other, steps)
+    grad_up = [grad_up[0]], [grad_up[1]]
+    up = scatter_start(*grad_up)
+    d_attn_other, grad_up = together(d_attn_other, grad_up)
+
+    d_heads, delta, *grad_o = mix_back(place, d_attn, d_attn_other, w_vo, (mixed_a, mixed_b), (wide_a, wide_b))
+    down, delta = together(down, delta)
+    down_ends = scatter_middle(*grad_down, down)
+    back_a, sum_a = attend_backward(qkv, d_heads, lse_b, delta, 1, 0, 2, 256)
+    up, out_near, back_a = together(up, out_near, back_a)
+    up_ends = scatter_middle(*grad_up, up)
+    back_b, sum_b = attend_backward(qkv, after(d_heads, back_a), lse_b, delta, 1, 2, 2, 256)
+    up_ends, down_ends, out_far, back_b = together(up_ends, down_ends, out_far, back_b)
+    ups, downs = scatter_end(*grad_up, up, up_ends), scatter_end(*grad_down, down, down_ends)
+    grad_ff = jnp.concatenate([jnp.stack(pair, 1) for pair in zip(ups, downs)]).reshape(steps * 4 * dims, units)
+    ff_total = lax.psum_scatter(grad_ff, "t", scatter_dimension=0, tiled=True)
+    grad_one = [[grad, grad_o[p]] for p, grad in enumerate(project_grads(turned, back_a, back_b))]
+    one = scatter_start(*grad_one)
+    delta, grad_ff, grad_one = together(delta, grad_ff, grad_one)
+    back_c, sum_c = attend_backward(qkv, after(d_heads, back_b), lse_a, delta, 0, 2, 2, 256)
+    one, back_c = together(one, back_c)
+    one_ends = scatter_middle(*grad_one, one)
+    back_d, sum_d = attend_backward(qkv, after(d_heads, back_c), lse_a, delta, 0, 0, 2, 256)
+    one_ends, back_d = together(one_ends, back_d)
+    grad_two = project_grads(turned, back_d, back_c)
+    grad_two = [grad_two[0]], [grad_two[1]]
+    two = scatter_start(*grad_two)
+    pieces = (back_d, back_c, back_a, back_b)
+    d_first_other = project_back(place, pieces, w_qk, after(w_vo, grad_two), 1)
+    d_first_swapped = swap(d_first_other, "c")
+    one = scatter_end(*grad_one, one, one_ends)
+    early = [lax.ppermute(jnp.concatenate([one[p][:3], one[p][4:]]), "t", rings[PAIR + p]) for p in range(PAIR)]
+    two, d_first_other = together(two, d_first_other)
+    two_ends = scatter_middle(*grad_two, two)
+    d_first = project_back(place, pieces, w_qk, after(w_vo, d_first_other), 0)
+    ff_total, early, d_first = together(ff_total, early, d_first)
+    d_first_swapped, d_first = together(d_first_swapped, d_first)
+    d_first = d_first + d_first_swapped
+    d_norm, grad_gain_one, grad_shift_one = norm_back(d_first, centred_one, scale_one, gains[0])
+    d_inputs = (d_hidden + d_norm).astype(BF)
+    grad_near, grad_far = from_chip(d_inputs)
+    two_ends, d_inputs = together(two_ends, d_inputs)
+    two = scatter_end(*grad_two, two, two_ends)
+    late = lax.ppermute(jnp.concatenate([two[1], one[1][3:4]]), "t", rings[1])
+    late, grad_near, out_near, out_far = together(late, grad_near, out_near, out_far)
+
+    grad_ff = ff_total.astype(F32).reshape(2, 2, dims, units)
+    grad_ff = ordered(c, chosen(grad_ff, c, 1), swap(chosen(grad_ff, 1 - c, 1), "c"), 2)
+    grad_attn = jnp.concatenate([two[0], one[0][3:4]]).astype(F32)
+    grad_attn = sum((part.astype(F32) for part in (*early, late)), grad_attn).reshape(4, 2, dims, cols)
+    grad_attn = ordered(c, chosen(grad_attn, c, 1), swap(chosen(grad_attn, 1 - c, 1), "c"), 2)
+
+    normed = jnp.stack([grad_gain_one, grad_gain_two, grad_shift_one, grad_shift_two, jnp.sum(d_hidden, 0), jnp.sum(d_out, 0)])
+    thin = width // 32
+    rows = jnp.swapaxes(normed.reshape(6, 32, thin), 0, 1).reshape(32, 6 * thin)
+    sums = jnp.concatenate([sum_d, sum_c, sum_a, sum_b], 2)
+    pair = placed(jnp.stack([sums[0], sums[2]]).reshape(2, steps, 4, lane), 1)
+    pair = jnp.transpose(pair, (2, 1, 0, 3))
+    ups = jnp.transpose(up_sum.reshape(steps, 4, up_bias.size), (1, 0, 2))
+    mine = jnp.concatenate([pair.reshape(16, 2 * lane), ups.reshape(16, up_bias.size)], 1)
+    here = jnp.where((jnp.arange(2) == c)[:, None, None], mine[None], 0.0).reshape(32, mine.shape[1])
+    sums = after(jnp.concatenate([rows, here], 1), grad_near)
+    for bit, name in ((y, "y"), (x, "x"), (c, "c")):
+        sums = sums.reshape(2, sums.shape[0] // 2, sums.shape[1])
+        sums = chosen(sums, bit, 0) + swap(chosen(sums, 1 - bit, 0), name)
+    total = chosen(sums, t, 0)
+    for away in range(1, steps):
+        total = total + lax.ppermute(chosen(sums, (t + away) % steps, 0), "t", rings[away])
+    vector_sums = total[: 6 * thin].reshape(6, thin)
+    return (
+        as_clips(result, out_near, out_far),
+        as_clips(d_inputs, grad_near, grad_far),
+        grad_attn[:3],
+        grad_attn[3].T,
+        grad_ff[0],
+        grad_ff[1].T,
+        vector_sums[:2],
+        vector_sums[2:],
+        total[6 * thin : 6 * thin + 2 * lane].reshape(2, lane),
+        total[6 * thin + 2 * lane :],
+    )
+
+
+def clip_per_chip(mesh):
+    fine = Mesh(mesh.devices.reshape(2, 2, 2, 4), ("y", "x", "c", "t"))
+    dp = ("y", "x", "c")
+    in_specs = (
+        P(dp, "t", None),
+        P(None, dp, "t"),
+        P("t", dp),
+        P(dp, "t"),
+        P("t", dp),
+        P(None, dp),
+        P(None, dp),
+        P(None, ("t",) + dp),
+        P(("t",) + dp),
+        P(dp, "t", None),
+    )
+    out_specs = in_specs[:1] * 2 + in_specs[1:5] + (
+        P(None, dp + ("t",)),
+        P(None, dp + ("t",)),
+        P(None, ("t",) + dp),
+        P(("t",) + dp),
+    )
+    return jax.shard_map(clip_local, mesh=fine, in_specs=in_specs, out_specs=out_specs, check_vma=False)
+
+
 def solution(mesh):
+    if dict(mesh.shape) == {"dp": 8, "tensor": 4}:
+        return clip_per_chip(mesh)
     in_specs = (
         P("dp", "tensor", None),
         P(None, "dp", "tensor"),

time: 2430 us -> 610 us (0.25)
  waiting for transfers between devices: 1760 us -> 109 us
  matrix products: 371 us -> 0 us
  Pallas kernels: 0 us -> 241 us
  other arithmetic: 179 us -> 83.8 us
  starting transfers between devices: 0.92 us -> 89.7 us
  blocking collectives: 60.2 us -> 0 us
    reduce_scatter x8 -> x1, waiting for transfers between devices: 1020 us -> 0.01 us  [clip_local(): ff_total = lax.psum_scatter(grad_ff, 't', scatter_dimension=0, tiled=True)]
    all_gather x7 -> x2, waiting for transfers between devices: 476 us -> 9.81 us  [the longest x1 7.52 us: clip_local(): lax.all_gather(down_piece, whole, axis=0, tiled=False)]
    dot_general x26 -> x0, matrix products: 371 us -> none  [the longest x2 54.3 us: attend_back(): jnp.einsum('qhe,khe->hqk', d_mixed, values, preferred_element_type=jnp.fl...]
    unnamed x21 -> x3, waiting for transfers between devices: 263 us -> 0.05 us
    pallas_call x0 -> x20, Pallas kernels: none -> 241 us  [call(): pl.pallas_call(body, grid=grid, in_specs=in_specs, out_specs=out_specs, o...]
    ppermute x0 -> x62, waiting for transfers between devices: none -> 99 us  [the longest x6 51.2 us: ring_gather(): lax.ppermute(value, 't', rings[-j % steps])]
    ppermute x0 -> x62, starting transfers between devices: none -> 89.6 us  [the longest x42 58.2 us: swap(): return lax.ppermute(value, axis, [(0, 1), (1, 0)])]
    convert_element_type x10 -> x19, other arithmetic: 112 us -> 24.6 us  [the longest x8 11.3 us: scatter_middle(): return (swap(first.astype(BF), 'y'), swap(second.astype(BF), 'x'))]
  transfers between devices with their start and end apart: 18 -> 65, of which waited for: 15 -> 17; matrix products, arithmetic and copies ran while one was open for 5% -> 18% of each run, Pallas kernels for 0% -> 37%
where the time goes in v2:
time: 610 us; the launch traced here: 602 us
  Pallas kernels  241 us (40%)
  waiting for transfers between devices  109 us (18%)
  starting transfers between devices  89.7 us (15%)
  other arithmetic  83.8 us (14%)
  local copies, waits for them, and re-layouts  62.8 us (10%)
  between operations  15.6 us (3%)
    pallas_call x20, Pallas kernels, call(): pl.pallas_call(body, grid=grid, in_specs=in_specs, out_specs=out_specs, o...  241 us
    ppermute x42, starting transfers between devices, swap(): return lax.ppermute(value, axis, [(0, 1), (1, 0)])  58.2 us
    ppermute x6, waiting for transfers between devices, ring_gather(): lax.ppermute(value, 't', rings[-j % steps])  51.2 us
    ppermute x42, waiting for transfers between devices, swap(): return lax.ppermute(value, axis, [(0, 1), (1, 0)])  42 us
    squeeze x20, local copies, waits for them, and re-layouts, chosen(): return lax.dynamic_index_in_dim(value, bit, axis, keepdims=False)  20.1 us
    unnamed x148, local copies, waits for them, and re-layouts  13.7 us
  transfers between devices with their start and end apart: 65, of which 17 were waited for; matrix products, arithmetic and copies ran while one was open for 18% of the time, Pallas kernels for 37%

profile of v2, /device:TPU:0, one launch (start us, length us, event | category | flops | bytes accessed | tf_op | source)
XLA Modules:
  0.0 601.9 jit_solution(13956043219794792828)
XLA Ops:
  30.4 15.4 %collective-permute-done.1 = bf16[256,256]{1,0:T(8,128)(2,1)S(1)} collective-permute-done((bf16[256,256]{1,0:T(8,128)(2,1)S(1)}, bf16[256,256]{1,0:T(8,128)(2,1)S(1)}, u32[]{:S(2)}, u32[]{:S(2)}) %collective-permute-start.1) | collective-permute-done | bytes 131104 | tf_op jit(solution)/shard_map/ppermute | solution.py:740
  49.5 35.8 %collective-permute-done.2 = bf16[256,256]{1,0:T(8,128)(2,1)S(1)} collective-permute-done((bf16[256,256]{1,0:T(8,128)(2,1)S(1)}, bf16[256,256]{1,0:T(8,128)(2,1)S(1)}, u32[]{:S(2)}, u32[]{:S(2)}) %collective-permute-start.2) | collective-permute-done | bytes 131104 | tf_op jit(solution)/shard_map/ppermute | solution.py:740
  106.9 9.8 %collective-permute-done.9 = bf16[2,4,128,256]{3,2,1,0:T(8,128)(2,1)S(1)} collective-permute-done((bf16[2,4,128,256]{3,2,1,0:T(8,128)(2,1)S(1)}, bf16[2,4,128,256]{3,2,1,0:T(8,128)(2,1)S(1)}, u32[]{:S(2)}, u32[]{:S(2)}) %collective-permute-start.9) | collective-permute-done | bytes 524320 | tf_op jit(solution)/shard_map/ppermute | solution.py:674
  129.5 11.9 %project.1 = (bf16[2,3,4,64,1568]{4,3,2,1,0:T(8,128)(2,1)}, bf16[1024,1568]{1,0:T(8,128)(2,1)}) custom-call(s32[1]{0:T(128)} %bitcast.20.place_ref, bf16[784,1024]{1,0:T(8,128)(2,1)} %copy-done.14, bf16[784,1024]{1,0:T(8,128)(2,1)} %collective-permute-done.17.xb_ref, bf16[4,4,2,128,256]{4,3,2,1,0:T(8,128)(2,1)} %pad_maximum_fusion.1.qk_ref, ...), custom_call_target="tpu_custom_call" | custom-call | flops 1000 | bytes 1000 | tf_op jit(solution)/shard_map/project/pallas_call | solution.py:194
  141.4 16.4 %attend.2 = (bf16[4,64,1568]{2,1,0:T(8,128)(2,1)}, bf16[1568,256]{1,0:T(8,128)(2,1)}, f32[4,64,1568]{2,1,0:T(8,128)}, f32[4,1,1568]{2,1,0:T(1,128)}) custom-call(bf16[2,3,4,64,1568]{4,3,2,1,0:T(8,128)(2,1)} %get-tuple-element.161.q_ref.k_ref.v_ref, bf16[2,3,4,64,1568]{4,3,2,1,0:T(8,128)(2,1)} %get-tuple-element.161.q_ref.k_ref.v_ref, ...), custom_call_target="tpu_custom_call" | custom-call | flops 1000 | bytes 1000 | tf_op jit(solution)/shard_map/attend/pallas_call | solution.py:194
  160.0 16.2 %attend.3 = (bf16[4,64,1568]{2,1,0:T(8,128)(2,1)}, bf16[1568,256]{1,0:T(8,128)(2,1)}, f32[4,64,1568]{2,1,0:T(8,128)}, f32[4,1,1568]{2,1,0:T(1,128)}) custom-call(bf16[2,3,4,64,1568]{4,3,2,1,0:T(8,128)(2,1)} %get-tuple-element.161.q_ref.k_ref.v_ref, bf16[2,3,4,64,1568]{4,3,2,1,0:T(8,128)(2,1)} %get-tuple-element.161.q_ref.k_ref.v_ref, ...), custom_call_target="tpu_custom_call" | custom-call | flops 1000 | bytes 1000 | tf_op jit(solution)/shard_map/attend/pallas_call | solution.py:194
  176.3 6.7 %collective-permute-done.18 = bf16[2,256,512]{2,1,0:T(8,128)(2,1)S(1)} collective-permute-done((bf16[2,256,512]{2,1,0:T(8,128)(2,1)S(1)}, bf16[2,256,512]{2,1,0:T(8,128)(2,1)S(1)}, u32[]{:S(2)}, u32[]{:S(2)}) %collective-permute-start.18) | collective-permute-done | bytes 524320 | tf_op jit(solution)/shard_map/ppermute | solution.py:674
  182.9 3.7 mix.2
  186.6 7.5 %all-gather.7.cloned.1.call-done = bf16[4096,512]{1,0:T(8,128)(2,1)} async-done(((bf16[256,512]{1,0:T(8,128)(2,1)}), bf16[4096,512]{1,0:T(8,128)(2,1)}) %all-gather.7.cloned.1.call-update) | async-done | bytes 4194320 | tf_op jit(solution)/shard_map/all_gather | solution.py:817
  198.6 4.2 mix.3
  211.8 9.5 %collective-permute-done.22 = bf16[2,2,256,512]{3,2,1,0:T(8,128)(2,1)} collective-permute-done((bf16[2,2,256,512]{3,2,1,0:T(8,128)(2,1)}, bf16[2,2,256,512]{3,2,1,0:T(8,128)(2,1)}, u32[]{:S(2)}, u32[]{:S(2)}) %collective-permute-start.22) | collective-permute-done | bytes 1048608 | tf_op jit(solution)/shard_map/ppermute | solution.py:674
  235.9 15.1 %ffn.2 = (f32[784,1024]{1,0:T(8,128)}, bf16[784,2048]{1,0:T(8,128)(2,1)}, bf16[784,2048]{1,0:T(8,128)(2,1)}) custom-call(bf16[784,1024]{1,0:T(8,128)(2,1)} %add_convert_fusion.x_ref.xa_ref, bf16[4,4,256,512]{3,2,1,0:T(8,128)(2,1)} %pad_maximum_fusion.first_ref.last_ref, bf16[4,4,256,512]{3,2,1,0:T(8,128)(2,1)} %bitcast.311, f32[4,1,512]{2,1,0:T(1,128)} %bitcast.331), custom_call_target="tpu_custom_call" | custom-call | flops 1000 | bytes 1000 | tf_op jit(solution)/shard_map/ffn/pallas_call | solution.py:194
  251.1 15.3 %ffn.3 = (f32[784,1024]{1,0:T(8,128)}, bf16[784,2048]{1,0:T(8,128)(2,1)}, bf16[784,2048]{1,0:T(8,128)(2,1)}) custom-call(bf16[784,1024]{1,0:T(8,128)(2,1)} %collective-permute-done.24.x_ref.xb_ref, bf16[4,4,256,512]{3,2,1,0:T(8,128)(2,1)} %pad_maximum_fusion.first_ref.last_ref, bf16[4,4,256,512]{3,2,1,0:T(8,128)(2,1)} %bitcast.312, f32[4,1,512]{2,1,0:T(1,128)} %bitcast.332), custom_call_target="tpu_custom_call" | custom-call | flops 1000 | bytes 1000 | tf_op jit(solution)/shard_map/ffn/pallas_call | solution.py:194
  267.2 6.6 %collective-permute-start.26 = (f32[784,1024]{1,0:T(8,128)}, f32[784,1024]{1,0:T(8,128)S(1)}, u32[]{:S(2)}, u32[]{:S(2)}) collective-permute-start(f32[784,1024]{1,0:T(8,128)} %get-tuple-element.178), channel_id=1, source_target_pairs={{0,4},{4,0},{1,5},{5,1},{2,6},{6,2},{3,7},{7,3},{8,12},{12,8},{9,1... | collective-permute-start | bytes 9633800 | tf_op jit(solution)/shard_map/ppermute | solution.py:674
  274.0 5.5 collective-permute-done.26
  285.9 13.6 %ffn_backward.2 = (f32[784,1024]{1,0:T(8,128)}, bf16[784,2048]{1,0:T(8,128)(2,1)}, f32[4,1,512]{2,1,0:T(1,128)}) custom-call(bf16[784,1024]{1,0:T(8,128)(2,1)} %get-tuple-element.185.d_ref.xa_ref, bf16[4,4,256,512]{3,2,1,0:T(8,128)(2,1)} %bitcast.313, bf16[4,4,256,512]{3,2,1,0:T(8,128)(2,1)} %pad_maximum_fusion.first_ref.last_ref, ...), custom_call_target="tpu_custom_call" | custom-call | flops 1000 | bytes 1000 | tf_op jit(solution)/shard_map/ffn_backward/pallas_call | solution.py:194
  299.5 13.7 %ffn_backward.3 = (f32[784,1024]{1,0:T(8,128)}, bf16[784,2048]{1,0:T(8,128)(2,1)}, f32[4,1,512]{2,1,0:T(1,128)}) custom-call(bf16[784,1024]{1,0:T(8,128)(2,1)} %collective-permute-done.27.d_ref.xb_ref, bf16[4,4,256,512]{3,2,1,0:T(8,128)(2,1)} %bitcast.314, bf16[4,4,256,512]{3,2,1,0:T(8,128)(2,1)} %pad_maximum_fusion.first_ref.last_ref, ...), custom_call_target="tpu_custom_call" | custom-call | flops 1000 | bytes 1000 | tf_op jit(solution)/shard_map/ffn_backward/pallas_call | solution.py:194
  313.3 13.6 %ffn_grad.2 = (bf16[2,2,2,256,512]{4,3,2,1,0:T(8,128)(2,1)}, bf16[2,2,2,256,512]{4,3,2,1,0:T(8,128)(2,1)}) custom-call(bf16[784,1024]{1,0:T(8,128)(2,1)} %get-tuple-element.185.d_ref.xa_ref, bf16[784,1024]{1,0:T(8,128)(2,1)} %collective-permute-done.27.d_ref.xb_ref, bf16[784,2048]{1,0:T(8,128)(2,1)} %get-tuple-element.186.ca_ref, ...), custom_call_target="tpu_custom_call" | custom-call | flops 1000 | bytes 1000 | tf_op jit(solution)/shard_map/ffn_grad/pallas_call | solution.py:194
  327.0 4.5 multiply_reduce_fusion
  342.9 13.5 %ffn_grad.3 = (bf16[2,2,2,256,512]{4,3,2,1,0:T(8,128)(2,1)}, bf16[2,2,2,256,512]{4,3,2,1,0:T(8,128)(2,1)}) custom-call(bf16[784,1024]{1,0:T(8,128)(2,1)} %add_convert_fusion.x_ref.xa_ref, bf16[784,1024]{1,0:T(8,128)(2,1)} %collective-permute-done.24.x_ref.xb_ref, bf16[784,2048]{1,0:T(8,128)(2,1)} %get-tuple-element.198.ca_ref, ...), custom_call_target="tpu_custom_call" | custom-call | flops 1000 | bytes 1000 | tf_op jit(solution)/shard_map/ffn_grad/pallas_call | solution.py:194
  364.9 10.2 %mix_back.1 = (bf16[8,64,1568]{2,1,0:T(8,128)(2,1)}, f32[8,1,1568]{2,1,0:T(1,128)}, bf16[2,2,2,256,128]{4,3,2,1,0:T(8,128)(2,1)}, bf16[2,2,2,256,128]{4,3,2,1,0:T(8,128)(2,1)}) custom-call(s32[1]{0:T(128)} %bitcast.20.place_ref, bf16[784,1024]{1,0:T(8,128)(2,1)} %copy-done.15, bf16[784,1024]{1,0:T(8,128)(2,1)} %collective-permute-done.31.db_ref, ...), custom_call_target="tpu_custom_call" | custom-call | flops 1000 | bytes 1000 | tf_op jit(solution)/shard_map/mix_back/pallas_call | solution.py:194
  375.2 16.5 %attend_backward.4 = (bf16[3,1568,128]{2,1,0:T(8,128)(2,1)}, f32[3,1,128]{2,1,0:T(1,128)}) custom-call(bf16[2,3,4,64,1568]{4,3,2,1,0:T(8,128)(2,1)} %get-tuple-element.161.q_ref.k_ref.v_ref, bf16[2,3,4,64,1568]{4,3,2,1,0:T(8,128)(2,1)} %get-tuple-element.161.q_ref.k_ref.v_ref, bf16[2,3,4,64,1568]{4,3,2,1,0:T(8,128)(2,1)} %get-tuple-element.161.q_ref.k_ref.v_ref, ...), custom_call_target="tpu_custom_call" | custom-call | flops 1000 | bytes 1000 | tf_op jit(solution)/shard_map/attend_backward/pallas_call | solution.py:194
  403.5 16.5 %attend_backward.5 = (bf16[3,1568,128]{2,1,0:T(8,128)(2,1)}, f32[3,1,128]{2,1,0:T(1,128)}) custom-call(bf16[2,3,4,64,1568]{4,3,2,1,0:T(8,128)(2,1)} %get-tuple-element.161.q_ref.k_ref.v_ref, bf16[2,3,4,64,1568]{4,3,2,1,0:T(8,128)(2,1)} %get-tuple-element.161.q_ref.k_ref.v_ref, bf16[2,3,4,64,1568]{4,3,2,1,0:T(8,128)(2,1)} %get-tuple-element.161.q_ref.k_ref.v_ref, ...), custom_call_target="tpu_custom_call" | custom-call | flops 1000 | bytes 1000 | tf_op jit(solution)/shard_map/attend_backward/pallas_call | solution.py:194
  428.3 6.6 %project_grads.2 = (bf16[2,2,3,256,128]{4,3,2,1,0:T(8,128)(2,1)}, bf16[2,2,3,256,128]{4,3,2,1,0:T(8,128)(2,1)}) custom-call(bf16[1024,1568]{1,0:T(8,128)(2,1)} %get-tuple-element.191.t_ref, bf16[3,1568,128]{2,1,0:T(8,128)(2,1)} %get-tuple-element.219.da_ref.c_ref, bf16[3,1568,128]{2,1,0:T(8,128)(2,1)} %get-tuple-element.226.db_ref.d_ref), custom_call_target="tpu_custom_call" | custom-call | flops 1000 | bytes 1000 | tf_op jit(solution)/shard_map/project_grads/pallas_call | solution.py:194
  443.4 16.9 %attend_backward.6 = (bf16[3,1568,128]{2,1,0:T(8,128)(2,1)}, f32[3,1,128]{2,1,0:T(1,128)}) custom-call(bf16[2,3,4,64,1568]{4,3,2,1,0:T(8,128)(2,1)} %get-tuple-element.161.q_ref.k_ref.v_ref, bf16[2,3,4,64,1568]{4,3,2,1,0:T(8,128)(2,1)} %get-tuple-element.161.q_ref.k_ref.v_ref, bf16[2,3,4,64,1568]{4,3,2,1,0:T(8,128)(2,1)} %get-tuple-element.161.q_ref.k_ref.v_ref, ...), custom_call_target="tpu_custom_call" | custom-call | flops 1000 | bytes 1000 | tf_op jit(solution)/shard_map/attend_backward/pallas_call | solution.py:194
  464.2 16.4 %attend_backward.7 = (bf16[3,1568,128]{2,1,0:T(8,128)(2,1)}, f32[3,1,128]{2,1,0:T(1,128)}) custom-call(bf16[2,3,4,64,1568]{4,3,2,1,0:T(8,128)(2,1)} %get-tuple-element.161.q_ref.k_ref.v_ref, bf16[2,3,4,64,1568]{4,3,2,1,0:T(8,128)(2,1)} %get-tuple-element.161.q_ref.k_ref.v_ref, bf16[2,3,4,64,1568]{4,3,2,1,0:T(8,128)(2,1)} %get-tuple-element.161.q_ref.k_ref.v_ref, ...), custom_call_target="tpu_custom_call" | custom-call | flops 1000 | bytes 1000 | tf_op jit(solution)/shard_map/attend_backward/pallas_call | solution.py:194
  480.7 6.9 %project_grads.3 = (bf16[2,2,3,256,128]{4,3,2,1,0:T(8,128)(2,1)}, bf16[2,2,3,256,128]{4,3,2,1,0:T(8,128)(2,1)}) custom-call(bf16[1024,1568]{1,0:T(8,128)(2,1)} %get-tuple-element.191.t_ref, bf16[3,1568,128]{2,1,0:T(8,128)(2,1)} %get-tuple-element.244.da_ref.a_ref, bf16[3,1568,128]{2,1,0:T(8,128)(2,1)} %get-tuple-element.241.db_ref.b_ref), custom_call_target="tpu_custom_call" | custom-call | flops 1000 | bytes 1000 | tf_op jit(solution)/shard_map/project_grads/pallas_call | solution.py:194
  487.6 6.8 %project_back.2 = f32[784,1024]{1,0:T(8,128)} custom-call(s32[1]{0:T(128)} %bitcast.20.place_ref, bf16[3,1568,128]{2,1,0:T(8,128)(2,1)} %get-tuple-element.244.da_ref.a_ref, bf16[3,1568,128]{2,1,0:T(8,128)(2,1)} %get-tuple-element.241.db_ref.b_ref, bf16[3,1568,128]{2,1,0:T(8,128)(2,1)} %get-tuple-element.219.da_ref.c_ref, ...), custom_call_target="tpu_custom_call" | custom-call | flops 1000 | bytes 1000 | tf_op jit(solution)/shard_map/project_back/pallas_call | solution.py:194
  500.5 4.8 collective-permute-start.50
  509.8 7.1 %project_back.3 = f32[784,1024]{1,0:T(8,128)} custom-call(s32[1]{0:T(128)} %bitcast.20.place_ref, bf16[3,1568,128]{2,1,0:T(8,128)(2,1)} %get-tuple-element.244.da_ref.a_ref, bf16[3,1568,128]{2,1,0:T(8,128)(2,1)} %get-tuple-element.241.db_ref.b_ref, bf16[3,1568,128]{2,1,0:T(8,128)(2,1)} %get-tuple-element.219.da_ref.c_ref, ...), custom_call_target="tpu_custom_call" | custom-call | flops 1000 | bytes 1000 | tf_op jit(solution)/shard_map/project_back/pallas_call | solution.py:194
  523.4 4.9 fusion.13
  559.3 11.7 %collective-permute-start.54 = (f32[4,128,128]{1,2,0:T(8,128)}, f32[4,128,128]{1,2,0:T(8,128)}, u32[]{:S(2)}, u32[]{:S(2)}) collective-permute-start(f32[4,128,128]{1,2,0:T(8,128)} %bitcast.327), channel_id=1, source_target_pairs={{0,4},{4,0},{1,5},{5,1},{2,6},{6,2},{3,7},{7,3},{8,12},{12,8},{9,1... | collective-permute-start | bytes 786440 | tf_op jit(solution)/shard_map/ppermute | solution.py:674
  (455 shorter events, 222.5 us)
Async XLA Ops:
  7.2 82.4 %all-gather.5.cloned.1.call-start = ((), (), s32[]{:S(2)}) async-start(), calls=%async_computation.2 | async-start | bytes 2367488 | tf_op jit(solution)/shard_map/all_gather | solution.py:803
  14.0 180.2 %all-gather.7.cloned.1.call-start = ((), (), s32[]{:S(2)}) async-start(), calls=%async_computation.3 | async-start | bytes 4456448 | tf_op jit(solution)/shard_map/all_gather | solution.py:817
  15.1 88.8 %collective-permute-start.6 = (bf16[392,1024]{1,0:T(8,128)(2,1)S(1)}, bf16[392,1024]{1,0:T(8,128)(2,1)}, u32[]{:S(2)}, u32[]{:S(2)}) collective-permute-start(bf16[392,1024]{1,0:T(8,128)(2,1)S(1)} %get-tuple-element.345), channel_id=1, source_target_pairs={{2,4},{3,5},{4,2},{5,3},{10,12},{11,13},{12,10},{13,11},{18,20},{1... | collective-permute-start | bytes 2408456 | tf_op jit(solution)/shard_map/ppermute | solution.py:731
  16.6 90.2 %collective-permute-start.10 = (bf16[392,1024]{1,0:T(8,128)(2,1)}, bf16[392,1024]{1,0:T(8,128)(2,1)S(1)}, u32[]{:S(2)}, u32[]{:S(2)}) collective-permute-start(bf16[392,1024]{1,0:T(8,128)(2,1)} %get-tuple-element.344), channel_id=1, source_target_pairs={{0,1},{1,0},{2,5},{3,4},{4,3},{5,2},{6,7},{7,6},{8,9},{9,8},{10,13... | collective-permute-start | bytes 2408456 | tf_op jit(solution)/shard_map/ppermute | solution.py:731
  28.4 56.9 %collective-permute-start.2 = (bf16[256,256]{1,0:T(8,128)(2,1)S(1)}, bf16[256,256]{1,0:T(8,128)(2,1)S(1)}, u32[]{:S(2)}, u32[]{:S(2)}) collective-permute-start(bf16[256,256]{1,0:T(8,128)(2,1)S(1)} %get-tuple-element.325), channel_id=1, source_target_pairs={{0,2},{1,3},{2,0},{3,1},{4,6},{5,7},{6,4},{7,5},{8,10},{9,11},{10,... | collective-permute-start | bytes 393224 | tf_op jit(solution)/shard_map/ppermute | solution.py:740
  28.4 56.9 %collective-permute-start.3 = (bf16[256,256]{1,0:T(8,128)(2,1)S(1)}, bf16[256,256]{1,0:T(8,128)(2,1)S(1)}, u32[]{:S(2)}, u32[]{:S(2)}) collective-permute-start(bf16[256,256]{1,0:T(8,128)(2,1)S(1)} %get-tuple-element.325), channel_id=1, source_target_pairs={{0,1},{1,2},{2,3},{3,0},{4,5},{5,6},{6,7},{7,4},{8,9},{9,10},{10,1... | collective-permute-start | bytes 393224 | tf_op jit(solution)/shard_map/ppermute | solution.py:740
  45.9 52.1 %collective-permute-start.15 = (bf16[8,256]{1,0:T(8,128)(2,1)S(1)}, bf16[8,256]{1,0:T(8,128)(2,1)S(1)}, u32[]{:S(2)}, u32[]{:S(2)}) collective-permute-start(bf16[8,256]{1,0:T(8,128)(2,1)S(1)} %pad_maximum_fusion.29), channel_id=1, source_target_pairs={{0,8},{8,0},{1,9},{9,1},{2,10},{10,2},{3,11},{11,3},{4,12},{12,4},... | collective-permute-start | bytes 12296 | tf_op jit(solution)/shard_map/ppermute | solution.py:674
  89.6 433.8 %reduce-scatter.2.cloned.1.call-start = ((), (), s32[]{:S(2)}) async-start(), calls=%async_computation.1 | async-start | bytes 2621440 | tf_op jit(solution)/shard_map/reduce_scatter | solution.py:896
  116.7 41.0 %collective-permute-start.11 = (bf16[256,512]{1,0:T(8,128)(2,1)S(1)}, bf16[256,512]{1,0:T(8,128)(2,1)S(1)}, u32[]{:S(2)}, u32[]{:S(2)}) collective-permute-start(bf16[256,512]{1,0:T(8,128)(2,1)S(1)} %get-tuple-element.150), channel_id=1, source_target_pairs={{0,3},{1,0},{2,1},{3,2},{4,7},{5,4},{6,5},{7,6},{8,11},{9,8},{10,9... | collective-permute-start | bytes 786440 | tf_op jit(solution)/shard_map/ppermute | solution.py:740
  120.4 37.4 %collective-permute-start.12 = (bf16[256,512]{1,0:T(8,128)(2,1)S(1)}, bf16[256,512]{1,0:T(8,128)(2,1)S(1)}, u32[]{:S(2)}, u32[]{:S(2)}) collective-permute-start(bf16[256,512]{1,0:T(8,128)(2,1)S(1)} %get-tuple-element.150), channel_id=1, source_target_pairs={{0,2},{1,3},{2,0},{3,1},{4,6},{5,7},{6,4},{7,5},{8,10},{9,11},{10,... | collective-permute-start | bytes 786440 | tf_op jit(solution)/shard_map/ppermute | solution.py:740
  120.7 37.1 %collective-permute-start.13 = (bf16[256,512]{1,0:T(8,128)(2,1)S(1)}, bf16[256,512]{1,0:T(8,128)(2,1)S(1)}, u32[]{:S(2)}, u32[]{:S(2)}) collective-permute-start(bf16[256,512]{1,0:T(8,128)(2,1)S(1)} %get-tuple-element.150), channel_id=1, source_target_pairs={{0,1},{1,2},{2,3},{3,0},{4,5},{5,6},{6,7},{7,4},{8,9},{9,10},{10,1... | collective-permute-start | bytes 786440 | tf_op jit(solution)/shard_map/ppermute | solution.py:740
  158.1 24.8 %collective-permute-start.18 = (bf16[2,256,512]{2,1,0:T(8,128)(2,1)S(1)}, bf16[2,256,512]{2,1,0:T(8,128)(2,1)S(1)}, u32[]{:S(2)}, u32[]{:S(2)}) collective-permute-start(bf16[2,256,512]{2,1,0:T(8,128)(2,1)S(1)} %get-tuple-element.337), channel_id=1, source_target_pairs={{0,16},{16,0},{1,17},{17,1},{2,18},{18,2},{3,19},{19,3},{4,20},{20... | collective-permute-start | bytes 1572872 | tf_op jit(solution)/shard_map/ppermute | solution.py:674
  159.3 23.6 %collective-permute-start.19 = (bf16[2,256,512]{2,1,0:T(8,128)(2,1)S(1)}, bf16[2,256,512]{2,1,0:T(8,128)(2,1)S(1)}, u32[]{:S(2)}, u32[]{:S(2)}) collective-permute-start(bf16[2,256,512]{2,1,0:T(8,128)(2,1)S(1)} %get-tuple-element.336), channel_id=1, source_target_pairs={{0,8},{8,0},{1,9},{9,1},{2,10},{10,2},{3,11},{11,3},{4,12},{12,4},... | collective-permute-start | bytes 1572872 | tf_op jit(solution)/shard_map/ppermute | solution.py:674
  195.4 25.9 %collective-permute-start.22 = (bf16[2,2,256,512]{3,2,1,0:T(8,128)(2,1)}, bf16[2,2,256,512]{3,2,1,0:T(8,128)(2,1)}, u32[]{:S(2)}, u32[]{:S(2)}) collective-permute-start(bf16[2,2,256,512]{3,2,1,0:T(8,128)(2,1)} %pad_maximum_fusion.10), channel_id=1, source_target_pairs={{0,16},{16,0},{1,17},{17,1},{2,18},{18,2},{3,19},{19,3},{4,20},{20... | collective-permute-start | bytes 3145736 | tf_op jit(solution)/shard_map/ppermute | solution.py:674
  198.2 25.6 %collective-permute-start.21 = (bf16[2,2,256,512]{3,2,1,0:T(8,128)(2,1)}, bf16[2,2,256,512]{3,2,1,0:T(8,128)(2,1)}, u32[]{:S(2)}, u32[]{:S(2)}) collective-permute-start(bf16[2,2,256,512]{3,2,1,0:T(8,128)(2,1)} %pad_maximum_fusion.9), channel_id=1, source_target_pairs={{0,8},{8,0},{1,9},{9,1},{2,10},{10,2},{3,11},{11,3},{4,12},{12,4},... | collective-permute-start | bytes 3145736 | tf_op jit(solution)/shard_map/ppermute | solution.py:674
  210.3 40.8 %collective-permute-start.24 = (bf16[784,1024]{1,0:T(8,128)(2,1)}, bf16[784,1024]{1,0:T(8,128)(2,1)}, u32[]{:S(2)}, u32[]{:S(2)}) collective-permute-start(bf16[784,1024]{1,0:T(8,128)(2,1)} %add_convert_fusion.x_ref.xa_ref), channel_id=1, source_target_pairs={{0,4},{4,0},{1,5},{5,1},{2,6},{6,2},{3,7},{7,3},{8,12},{12,8},{9,1... | collective-permute-start | bytes 4816904 | tf_op jit(solution)/shard_map/ppermute | solution.py:674
  226.4 24.6 %collective-permute-start.23 = (bf16[392,1024]{1,0:T(8,128)(2,1)}, bf16[392,1024]{1,0:T(8,128)(2,1)}, u32[]{:S(2)}, u32[]{:S(2)}) collective-permute-start(bf16[392,1024]{1,0:T(8,128)(2,1)} %get-tuple-element.343), channel_id=1, source_target_pairs={{2,4},{3,5},{4,2},{5,3},{10,12},{11,13},{12,10},{13,11},{18,20},{1... | collective-permute-start | bytes 2408456 | tf_op jit(solution)/shard_map/ppermute | solution.py:731
  228.0 38.3 %collective-permute-start.25 = (bf16[392,1024]{1,0:T(8,128)(2,1)}, bf16[392,1024]{1,0:T(8,128)(2,1)S(1)}, u32[]{:S(2)}, u32[]{:S(2)}) collective-permute-start(bf16[392,1024]{1,0:T(8,128)(2,1)} %get-tuple-element.342), channel_id=1, source_target_pairs={{0,1},{1,0},{2,5},{3,4},{4,3},{5,2},{6,7},{7,6},{8,9},{9,8},{10,13... | collective-permute-start | bytes 2408456 | tf_op jit(solution)/shard_map/ppermute | solution.py:731
  335.5 28.7 %collective-permute-start.31 = (bf16[784,1024]{1,0:T(8,128)(2,1)S(1)}, bf16[784,1024]{1,0:T(8,128)(2,1)}, u32[]{:S(2)}, u32[]{:S(2)}) collective-permute-start(bf16[784,1024]{1,0:T(8,128)(2,1)S(1)} %convert_element_type.315.da_ref), channel_id=1, source_target_pairs={{0,4},{4,0},{1,5},{5,1},{2,6},{6,2},{3,7},{7,3},{8,12},{12,8},{9,1... | collective-permute-start | bytes 4816904 | tf_op jit(solution)/shard_map/ppermute | solution.py:674
  338.4 36.7 %collective-permute-start.29 = (bf16[2,2,256,512]{3,2,1,0:T(8,128)(2,1)}, bf16[2,2,256,512]{3,2,1,0:T(8,128)(2,1)}, u32[]{:S(2)}, u32[]{:S(2)}) collective-permute-start(bf16[2,2,256,512]{3,2,1,0:T(8,128)(2,1)} %dynamic-slice_bitcast_fusion.2), channel_id=1, source_target_pairs={{0,16},{16,0},{1,17},{17,1},{2,18},{18,2},{3,19},{19,3},{4,20},{20... | collective-permute-start | bytes 3145736 | tf_op jit(solution)/shard_map/ppermute | solution.py:674
  341.4 33.8 %collective-permute-start.28 = (bf16[2,2,256,512]{3,2,1,0:T(8,128)(2,1)}, bf16[2,2,256,512]{3,2,1,0:T(8,128)(2,1)}, u32[]{:S(2)}, u32[]{:S(2)}) collective-permute-start(bf16[2,2,256,512]{3,2,1,0:T(8,128)(2,1)} %dynamic-slice_bitcast_fusion.3), channel_id=1, source_target_pairs={{0,8},{8,0},{1,9},{9,1},{2,10},{10,2},{3,11},{11,3},{4,12},{12,4},... | collective-permute-start | bytes 3145736 | tf_op jit(solution)/shard_map/ppermute | solution.py:674
  358.8 32.9 %collective-permute-start.32 = (bf16[2,2,256,512]{3,2,1,0:T(8,128)(2,1)}, bf16[2,2,256,512]{3,2,1,0:T(8,128)(2,1)}, u32[]{:S(2)}, u32[]{:S(2)}) collective-permute-start(bf16[2,2,256,512]{3,2,1,0:T(8,128)(2,1)} %dynamic-slice_bitcast_fusion.1), channel_id=1, source_target_pairs={{0,8},{8,0},{1,9},{9,1},{2,10},{10,2},{3,11},{11,3},{4,12},{12,4},... | collective-permute-start | bytes 3145736 | tf_op jit(solution)/shard_map/ppermute | solution.py:674
  361.6 30.1 %collective-permute-start.33 = (bf16[2,2,256,512]{3,2,1,0:T(8,128)(2,1)}, bf16[2,2,256,512]{3,2,1,0:T(8,128)(2,1)}, u32[]{:S(2)}, u32[]{:S(2)}) collective-permute-start(bf16[2,2,256,512]{3,2,1,0:T(8,128)(2,1)} %dynamic-slice_bitcast_fusion), channel_id=1, source_target_pairs={{0,16},{16,0},{1,17},{17,1},{2,18},{18,2},{3,19},{19,3},{4,20},{20... | collective-permute-start | bytes 3145736 | tf_op jit(solution)/shard_map/ppermute | solution.py:674
  364.2 27.5 %collective-permute-start.34 = (bf16[392,1024]{1,0:T(8,128)(2,1)}, bf16[392,1024]{1,0:T(8,128)(2,1)S(1)}, u32[]{:S(2)}, u32[]{:S(2)}) collective-permute-start(bf16[392,1024]{1,0:T(8,128)(2,1)} %get-tuple-element.341), channel_id=1, source_target_pairs={{4,2},{5,3},{2,4},{3,5},{12,10},{13,11},{10,12},{11,13},{20,18},{2... | collective-permute-start | bytes 2408456 | tf_op jit(solution)/shard_map/ppermute | solution.py:735
  375.1 46.9 %collective-permute-start.39 = (bf16[392,1024]{1,0:T(8,128)(2,1)}, bf16[392,1024]{1,0:T(8,128)(2,1)S(1)}, u32[]{:S(2)}, u32[]{:S(2)}) collective-permute-start(bf16[392,1024]{1,0:T(8,128)(2,1)} %get-tuple-element.340), channel_id=1, source_target_pairs={{1,0},{0,1},{5,2},{4,3},{3,4},{2,5},{7,6},{6,7},{9,8},{8,9},{13,10... | collective-permute-start | bytes 2408456 | tf_op jit(solution)/shard_map/ppermute | solution.py:735
  393.2 28.9 %collective-permute-start.38 = (bf16[2,256,512]{2,1,0:T(8,128)(2,1)S(1)}, bf16[2,256,512]{2,1,0:T(8,128)(2,1)}, u32[]{:S(2)}, u32[]{:S(2)}) collective-permute-start(bf16[2,256,512]{2,1,0:T(8,128)(2,1)S(1)} %fusion.22), channel_id=1, source_target_pairs={{0,8},{8,0},{1,9},{9,1},{2,10},{10,2},{3,11},{11,3},{4,12},{12,4},... | collective-permute-start | bytes 1572872 | tf_op jit(solution)/shard_map/ppermute | solution.py:674
  395.7 26.3 %collective-permute-start.37 = (bf16[2,256,512]{2,1,0:T(8,128)(2,1)}, bf16[2,256,512]{2,1,0:T(8,128)(2,1)}, u32[]{:S(2)}, u32[]{:S(2)}) collective-permute-start(bf16[2,256,512]{2,1,0:T(8,128)(2,1)} %fusion.23), channel_id=1, source_target_pairs={{0,16},{16,0},{1,17},{17,1},{2,18},{18,2},{3,19},{19,3},{4,20},{20... | collective-permute-start | bytes 1572872 | tf_op jit(solution)/shard_map/ppermute | solution.py:674
  436.9 24.2 %collective-permute-start.41 = (bf16[2,5,256,128]{3,2,1,0:T(8,128)(2,1)}, bf16[2,5,256,128]{3,2,1,0:T(8,128)(2,1)}, u32[]{:S(2)}, u32[]{:S(2)}) collective-permute-start(bf16[2,5,256,128]{3,2,1,0:T(8,128)(2,1)} %pad_maximum_fusion.12), channel_id=1, source_target_pairs={{0,16},{16,0},{1,17},{17,1},{2,18},{18,2},{3,19},{19,3},{4,20},{20... | collective-permute-start | bytes 1966088 | tf_op jit(solution)/shard_map/ppermute | solution.py:674
  494.4 29.0 %collective-permute-start.48 = (f32[784,1024]{1,0:T(8,128)}, f32[784,1024]{1,0:T(8,128)}, u32[]{:S(2)}, u32[]{:S(2)}) collective-permute-start(f32[784,1024]{1,0:T(8,128)} %project_back.2), channel_id=1, source_target_pairs={{0,4},{4,0},{1,5},{5,1},{2,6},{6,2},{3,7},{7,3},{8,12},{12,8},{9,1... | collective-permute-start | bytes 9633800 | tf_op jit(solution)/shard_map/ppermute | solution.py:674
  531.4 22.7 %collective-permute-start.52 = (bf16[392,1024]{1,0:T(8,128)(2,1)}, bf16[392,1024]{1,0:T(8,128)(2,1)S(1)}, u32[]{:S(2)}, u32[]{:S(2)}) collective-permute-start(bf16[392,1024]{1,0:T(8,128)(2,1)} %get-tuple-element.339), channel_id=1, source_target_pairs={{4,2},{5,3},{2,4},{3,5},{12,10},{13,11},{10,12},{11,13},{20,18},{2... | collective-permute-start | bytes 2408456 | tf_op jit(solution)/shard_map/ppermute | solution.py:735
  544.5 33.0 %collective-permute-start.53 = (bf16[392,1024]{1,0:T(8,128)(2,1)}, bf16[392,1024]{1,0:T(8,128)(2,1)}, u32[]{:S(2)}, u32[]{:S(2)}) collective-permute-start(bf16[392,1024]{1,0:T(8,128)(2,1)} %get-tuple-element.338), channel_id=1, source_target_pairs={{1,0},{0,1},{5,2},{4,3},{3,4},{2,5},{7,6},{6,7},{9,8},{8,9},{13,10... | collective-permute-start | bytes 2408456 | tf_op jit(solution)/shard_map/ppermute | solution.py:735
  559.3 33.1 %collective-permute-start.54 = (f32[4,128,128]{1,2,0:T(8,128)}, f32[4,128,128]{1,2,0:T(8,128)}, u32[]{:S(2)}, u32[]{:S(2)}) collective-permute-start(f32[4,128,128]{1,2,0:T(8,128)} %bitcast.327), channel_id=1, source_target_pairs={{0,4},{4,0},{1,5},{5,1},{2,6},{6,2},{3,7},{7,3},{8,12},{12,8},{9,1... | collective-permute-start | bytes 786440 | tf_op jit(solution)/shard_map/ppermute | solution.py:674
  (98 other events, 1021.9 us)
Sparse Core Ops, SparseCore 0:
  14.1 75.4 all-gather.4
  92.9 101.2 all-gather.6
  442.9 45.1 reduce-scatter.1

commit v3 on v2

--- a/solution.py
+++ b/solution.py
@@ -190,14 +190,13 @@
     return lax.dot_general(left, right, dims, preferred_element_type=F32)
 
 
-def call(body, grid, in_specs, out_specs, out_shape, args, scratch=(), name=None):
+def call(body, grid, in_specs, out_specs, out_shape, args, scratch=(), name=None, prefetch=0):
     return pl.pallas_call(
         body,
-        grid=grid,
-        in_specs=in_specs,
-        out_specs=out_specs,
+        grid_spec=pltpu.PrefetchScalarGridSpec(
+            num_scalar_prefetch=prefetch, grid=grid, in_specs=in_specs, out_specs=out_specs, scratch_shapes=list(scratch)
+        ),
         out_shape=out_shape,
-        scratch_shapes=list(scratch),
         compiler_params=pltpu.CompilerParams(vmem_limit_bytes=VMEM_LIMIT),
         cost_estimate=pl.CostEstimate(flops=1000, bytes_accessed=1000, transcendentals=0),
         name=name,
@@ -232,19 +231,19 @@
     return jnp.concatenate([value, jnp.zeros((value.shape[0], extra), value.dtype)], 1)
 
 
-def place_block(place_ref, step):
-    return lax.rem(place_ref[0] + step, 4)
-
-
 def row_blocks(ref, place, start, stop):
     return jnp.concatenate([ref[owner, place, start:stop] for owner in range(ref.shape[0])], 1)
 
 
+def turned_owner(owner):
+    return owner % 2 * 2 + owner // 2
+
+
 def key_blocks(ref, place, which):
-    return jnp.concatenate([ref[owner, place, which] for owner in range(ref.shape[0])], 1)
-
-
-def project_kernel(place_ref, xa_ref, xb_ref, qk_ref, v_ref, b_ref, out_ref, t_ref, x_s):
+    return jnp.concatenate([ref[turned_owner(owner), place, which] for owner in range(ref.shape[0])], 1)
+
+
+def project_kernel(xa_ref, xb_ref, qk_ref, v_ref, b_ref, out_ref, t_ref, x_s):
     half = xa_ref.shape[0]
     group = pl.program_id(0)
 
@@ -255,7 +254,7 @@
         t_ref[...] = x_s[...].T
 
     cols = v_ref.shape[2]
-    places = [place_block(place_ref, PAIR * group + p) for p in range(PAIR)]
+    places = [PAIR * group + p for p in range(PAIR)]
     for i in range(3):
         pick = (lambda place: row_blocks(v_ref, place, 0, cols)) if i == 2 else (lambda place: key_blocks(qk_ref, place, i))
         weights = jnp.concatenate([pick(place) for place in places], 0)
@@ -263,10 +262,7 @@
         out_ref[0, i] = value.astype(BF).reshape(out_ref.shape[2:])
 
 
-SCALAR = pl.BlockSpec(memory_space=pltpu.SMEM)
-
-
-def project(place, xa, xb, w_qk, w_vo, bias):
+def project(xa, xb, w_qk, w_vo, bias):
     half, width = xa.shape
     owners, places, _, cols, part = w_qk.shape
     groups = places // PAIR
@@ -276,7 +272,6 @@
         project_kernel,
         (groups,),
         [
-            SCALAR,
             whole,
             whole,
             pl.BlockSpec((owners, places, 2, cols, part), lambda g: (0, 0, 0, 0, 0)),
@@ -288,7 +283,7 @@
             pl.BlockSpec((width, 2 * half), lambda g: (0, 0)),
         ],
         [shaped((groups, 3, heads, HEAD_DIM, 2 * half)), shaped((width, 2 * half))],
-        (place, xa, xb, w_qk, w_vo, bias),
+        (xa, xb, w_qk, w_vo, bias),
         [pltpu.VMEM((2 * half, width), BF)],
         name="project",
     )
@@ -409,13 +404,13 @@
     )
 
 
-def mix_kernel(place_ref, oa_ref, ob_ref, w_ref, out_ref):
+def mix_kernel(oa_ref, ob_ref, w_ref, out_ref):
     places, cols = w_ref.shape[1:3]
-    weights = [row_blocks(w_ref, place_block(place_ref, j), 0, cols) for j in range(places)]
+    weights = [row_blocks(w_ref, j, 0, cols) for j in range(places)]
     out_ref[...] = dot(jnp.concatenate([oa_ref[...], ob_ref[...]], 1), jnp.concatenate(weights, 0))
 
 
-def mix(place, rows, weights, which):
+def mix(rows, weights, which):
     seq, wide = rows[0].shape
     owners, places, _, part = weights.shape
     cols = PAIR * wide // places
@@ -424,19 +419,18 @@
         mix_kernel,
         (2,),
         [
-            SCALAR,
             pl.BlockSpec((half, wide), lambda n: (which, 0)),
             pl.BlockSpec((half, wide), lambda n: (which, 0)),
             pl.BlockSpec((owners // 2, places, cols, part), lambda n: (n, 0, 1, 0)),
         ],
         pl.BlockSpec((half, owners * part // 2), lambda n: (0, n)),
         shaped((half, owners * part), F32),
-        (place, *rows, weights),
+        (*rows, weights),
         name="mix",
     )
 
 
-def mix_back_kernel(place_ref, da_ref, db_ref, w_ref, oa_ref, ob_ref, wa_ref, wb_ref, d_ref, delta_ref, *refs):
+def mix_back_kernel(bits_ref, da_ref, db_ref, w_ref, oa_ref, ob_ref, wa_ref, wb_ref, d_ref, delta_ref, *refs):
     *grad_refs, d_s = refs
     half, width = da_ref.shape
     cols = w_ref.shape[2]
@@ -448,7 +442,7 @@
         d_s[0:half] = da_ref[...]
         d_s[half:] = db_ref[...]
 
-    places = [place_block(place_ref, PAIR * group + p) for p in range(PAIR)]
+    places = [PAIR * group + p for p in range(PAIR)]
     weights = jnp.concatenate([row_blocks(w_ref, place, 0, cols) for place in places], 0)
     d_heads = dot(weights, d_s[...], ROW_NT).astype(BF).reshape(oa_ref.shape)
     d_ref[...] = d_heads
@@ -459,60 +453,64 @@
             delta_ref[...] = jnp.sum(d_heads.astype(F32) * wide_ref[...], 1, keepdims=True)
             grad = dot(o_ref[...].reshape(heads * HEAD_DIM, 2 * half), d_s[...]).astype(BF).T
             for p in range(PAIR):
-                grad_refs[p][:, :, 0] = grad[:, p * cols : (p + 1) * cols].reshape(2, 2, width // 4, cols)
-
-
-def mix_back(place, da, db, weights, mixed, wide):
+                part = grad[:, p * cols : (p + 1) * cols]
+                put_halves(bits_ref, part, p, grad_refs[2 * p], grad_refs[2 * p + 1], (slice(None), 0))
+
+
+def mix_back(bits, da, db, weights, mixed, wide):
     half, width = da.shape
     owners, places, _, part = weights.shape
     heads, _, seq = mixed[0].shape
     groups = places // PAIR
     cols = heads * HEAD_DIM // PAIR
-    whole = pl.BlockSpec((half, width), lambda g: (0, 0))
-    fixed = pl.BlockSpec((heads, HEAD_DIM, seq), lambda g: (0, 0, 0))
-    spec = lambda rows: pl.BlockSpec((heads, rows, seq), lambda g: (g, 0, 0))
-    grad = pl.BlockSpec((2, 2, 1, width // 4, cols), lambda g: (0, 0, g, 0, 0))
-    return call(
+    whole = pl.BlockSpec((half, width), lambda g, bits: (0, 0))
+    fixed = pl.BlockSpec((heads, HEAD_DIM, seq), lambda g, bits: (0, 0, 0))
+    spec = lambda rows: pl.BlockSpec((heads, rows, seq), lambda g, bits: (g, 0, 0))
+    grad = pl.BlockSpec((2, 1, width // 4, cols), lambda g, bits: (0, g, 0, 0))
+    d_heads, delta, keep_a, send_a, keep_b, send_b = call(
         mix_back_kernel,
         (groups,),
-        [SCALAR, whole, whole, pl.BlockSpec((owners, places, cols, part), lambda g: (0, 0, 1, 0))] + [fixed] * 4,
-        [spec(HEAD_DIM), spec(1), grad, grad],
+        [whole, whole, pl.BlockSpec((owners, places, cols, part), lambda g, bits: (0, 0, 1, 0))] + [fixed] * 4,
+        [spec(HEAD_DIM), spec(1)] + [grad] * 4,
         [shaped((groups * heads, HEAD_DIM, seq)), shaped((groups * heads, 1, seq), F32)]
-        + [shaped((2, 2, groups, width // 4, cols))] * PAIR,
-        (place, da, db, weights, *mixed, *wide),
+        + [shaped((2, groups, width // 4, cols))] * 4,
+        (bits, da, db, weights, *mixed, *wide),
         [pltpu.VMEM((seq, width), BF)],
         name="mix_back",
-    )
-
-
-def project_grad_kernel(t_ref, da_ref, db_ref, *grad_refs):
-    width = t_ref.shape[0]
+        prefetch=1,
+    )
+    return d_heads, delta, (keep_a, keep_b), (send_a, send_b)
+
+
+def project_grad_kernel(bits_ref, t_ref, da_ref, db_ref, *refs):
     cols = da_ref.shape[2]
     grad = dot(t_ref[...], jnp.concatenate([da_ref[0], db_ref[0]], 1)).astype(BF)
-    for p, grad_ref in enumerate(grad_refs):
-        grad_ref[:, :, 0] = grad[:, p * cols : (p + 1) * cols].reshape(2, 2, width // 4, cols)
-
-
-def project_grads(turned, da, db):
+    for p in range(PAIR):
+        put_halves(bits_ref, grad[:, p * cols : (p + 1) * cols], p, refs[2 * p], refs[2 * p + 1], (slice(None), 0))
+
+
+def project_grads(bits, turned, da, db):
     width, seq = turned.shape
     cols = da.shape[2]
-    piece = pl.BlockSpec((1, seq, cols), lambda i: (i, 0, 0))
-    grad = pl.BlockSpec((2, 2, 1, width // 4, cols), lambda i: (0, 0, i, 0, 0))
-    return call(
+    piece = pl.BlockSpec((1, seq, cols), lambda i, bits: (i, 0, 0))
+    grad = pl.BlockSpec((2, 1, width // 4, cols), lambda i, bits: (0, i, 0, 0))
+    keep_a, send_a, keep_b, send_b = call(
         project_grad_kernel,
         (3,),
-        [pl.BlockSpec((width, seq), lambda i: (0, 0)), piece, piece],
-        [grad, grad],
-        [shaped((2, 2, 3, width // 4, cols))] * 2,
-        (turned, da, db),
+        [pl.BlockSpec((width, seq), lambda i, bits: (0, 0)), piece, piece],
+        [grad] * 4,
+        [shaped((2, 3, width // 4, cols))] * 4,
+        (bits, turned, da, db),
         name="project_grads",
-    )
-
-
-def project_back_kernel(place_ref, a_ref, b_ref, c_ref, d_ref, qk_ref, v_ref, out_ref):
+        prefetch=1,
+    )
+    return (keep_a, keep_b), (send_a, send_b)
+
+
+def project_back_kernel(a_ref, b_ref, c_ref, d_ref, qk_ref, v_ref, out_ref):
     total = None
     for first, refs in ((0, (a_ref, b_ref)), (PAIR, (c_ref, d_ref))):
-        places = [place_block(place_ref, first + p) for p in range(PAIR)]
+        places = [first + p for p in range(PAIR)]
         left = [ref[i] for i in range(3) for ref in refs]
         right = [qk_ref[0, place, i] for i in range(2) for place in places] + [v_ref[0, place] for place in places]
         part = dot(jnp.concatenate(left, 1), jnp.concatenate(right, 0))
@@ -520,22 +518,21 @@
     out_ref[...] = total
 
 
-def project_back(place, pieces, w_qk, w_vo, which):
+def project_back(pieces, w_qk, w_vo, which):
     seq = pieces[0].shape[1]
     owners, places, _, cols, part = w_qk.shape
     half = seq // 2
     return call(
         project_back_kernel,
         (owners,),
-        [SCALAR]
-        + [pl.BlockSpec((3, half, cols), lambda n: (0, which, 0)) for piece in pieces]
+        [pl.BlockSpec((3, half, cols), lambda n: (0, which, 0)) for piece in pieces]
         + [
-            pl.BlockSpec((1, places, 2, cols, part), lambda n: (n, 0, 0, 0, 0)),
+            pl.BlockSpec((1, places, 2, cols, part), lambda n: (turned_owner(n), 0, 0, 0, 0)),
             pl.BlockSpec((1, places, cols, part), lambda n: (n, 0, 0, 0)),
         ],
         pl.BlockSpec((half, part), lambda n: (0, n)),
         shaped((half, owners * part), F32),
-        (place, *pieces, w_qk, w_vo),
+        (*pieces, w_qk, w_vo),
         name="project_back",
     )
 
@@ -549,13 +546,26 @@
     return jnp.concatenate([ref[0, t] for t in range(ref.shape[1])], 1)
 
 
-def ffn_kernel(x_ref, first_ref, last_ref, b_ref, out_ref, g_ref, slope_ref, hold_s):
+def relative_block(block, place, blocks):
+    return lax.rem(block + blocks - place, blocks)
+
+
+def either(first_ref, last_ref, index, pick):
+    half = first_ref.shape[1]
+    one = pick(first_ref, jnp.minimum(index, half - 1))
+    return jnp.where(index < half, one, pick(last_ref, jnp.maximum(index - half, 0)))
+
+
+def ffn_kernel(place_ref, x_ref, one_ref, two_ref, last_ref, b_ref, out_ref, g_ref, slope_ref, hold_s):
     blocks = hold_s.shape[0]
     step = pl.program_id(0)
 
     @pl.when(step < blocks)
     def _():
-        pre = dot(x_ref[...], first_ref[...].reshape(x_ref.shape[1], -1)) + b_ref[0]
+        ones = jnp.concatenate([one_ref[turned_owner(owner), 0] for owner in range(one_ref.shape[0])], 0)
+        twos = two_ref[...].reshape(ones.shape)
+        weights = jnp.where(relative_block(step, place_ref[0], blocks) < blocks // 2, ones, twos)
+        pre = dot(x_ref[...], weights) + b_ref[0]
         active, slope = gelu_pair(pre)
         active = active.astype(BF)
         hold_s[step] = active
@@ -568,37 +578,46 @@
         out_ref[...] = dot(left, all_blocks(last_ref), ROW_NT)
 
 
-def ffn_specs(rows, weights):
-    owners, blocks, part, units = weights.shape
+def ffn_specs(rows, down):
+    owners, blocks, part, units = down.shape
     early = lambda s: jnp.minimum(s, blocks - 1)
     late = lambda s: jnp.maximum(s - blocks, 0)
     return (
-        pl.BlockSpec((rows, owners * part), lambda s: (0, 0)),
-        pl.BlockSpec((owners, 1, part, units), lambda s: (0, early(s), 0, 0)),
-        pl.BlockSpec((1, blocks, part, units), lambda s: (late(s), 0, 0, 0)),
-        pl.BlockSpec((rows, units), lambda s: (0, early(s))),
-        pl.BlockSpec((1, 1, units), lambda s: (early(s), 0, 0)),
-        pl.BlockSpec((rows, part), lambda s: (0, late(s))),
-    )
-
-
-def ffn_forward(x, up, down, bias):
+        blocks,
+        early,
+        late,
+        pl.BlockSpec((rows, owners * part), lambda s, place: (0, 0)),
+        pl.BlockSpec((rows, units), lambda s, place: (0, early(s))),
+        pl.BlockSpec((1, 1, units), lambda s, place: (early(s), 0, 0)),
+        pl.BlockSpec((rows, part), lambda s, place: (0, late(s))),
+    )
+
+
+def ffn_forward(place, x, up, down, bias):
     rows, width = x.shape
-    owners, blocks, _, units = up.shape
-    whole, early, late, column, thin, out = ffn_specs(rows, up)
+    owners, blocks, part, units = down.shape
+    blocks, early, late, whole, column, thin, out = ffn_specs(rows, down)
+    index = lambda s, place: relative_block(early(s), place[0], blocks)
     return call(
         ffn_kernel,
         (blocks + owners,),
-        [whole, early, late, thin],
+        [
+            whole,
+            pl.BlockSpec((owners, 1, part, units), lambda s, place: (0, jnp.minimum(index(s, place), PAIR - 1), 0, 0)),
+            pl.BlockSpec((owners, 1, part, units), lambda s, place: (0, jnp.maximum(index(s, place) - PAIR, 0), 0, 0)),
+            pl.BlockSpec((1, blocks, part, units), lambda s, place: (late(s), 0, 0, 0)),
+            thin,
+        ],
         [out, column, column],
         [shaped((rows, width), F32), shaped((rows, blocks * units)), shaped((rows, blocks * units))],
-        (x, up, down, bias),
+        (place, x, *up, down, bias),
         [pltpu.VMEM((blocks, rows, units), BF)],
         name="ffn",
-    )
-
-
-def ffn_back_kernel(d_ref, first_ref, last_ref, slope_ref, out_ref, dpre_ref, sum_ref, hold_s):
+        prefetch=1,
+    )
+
+
+def ffn_back_kernel(place_ref, d_ref, first_ref, one_ref, two_ref, slope_ref, out_ref, dpre_ref, sum_ref, hold_s):
     blocks = hold_s.shape[0]
     step = pl.program_id(0)
 
@@ -612,62 +631,80 @@
     @pl.when(step >= blocks)
     def _():
         left = jnp.concatenate([hold_s[t] for t in range(blocks)], 1)
-        out_ref[...] = dot(left, all_blocks(last_ref), ROW_NT)
-
-
-def ffn_backward(d_out, up, down, slope):
+        order = [relative_block(t, place_ref[0], blocks) for t in range(blocks)]
+        weights = [either(one_ref, two_ref, index, lambda ref, i: ref[0, i]) for index in order]
+        out_ref[...] = dot(left, jnp.concatenate(weights, 1), ROW_NT)
+
+
+def ffn_backward(place, d_out, up, down, slope):
     rows, width = d_out.shape
-    owners, blocks, _, units = up.shape
-    whole, early, late, column, thin, out = ffn_specs(rows, up)
+    owners, blocks, part, units = down.shape
+    blocks, early, late, whole, column, thin, out = ffn_specs(rows, down)
     return call(
         ffn_back_kernel,
         (blocks + owners,),
-        [whole, early, late, column],
+        [
+            whole,
+            pl.BlockSpec((owners, 1, part, units), lambda s, place: (0, early(s), 0, 0)),
+            pl.BlockSpec((1, PAIR, part, units), lambda s, place: (turned_owner(late(s)), 0, 0, 0)),
+            pl.BlockSpec((1, PAIR, part, units), lambda s, place: (late(s), 0, 0, 0)),
+            column,
+        ],
         [out, column, thin],
         [shaped((rows, width), F32), shaped((rows, blocks * units)), shaped((blocks, 1, units), F32)],
-        (d_out, down, up, slope),
+        (place, d_out, down, *up, slope),
         [pltpu.VMEM((blocks, rows, units), BF)],
         name="ffn_backward",
-    )
-
-
-def ffn_grad_kernel(xa_ref, xb_ref, ca_ref, cb_ref, first_ref, last_ref, x_s):
-    half = xa_ref.shape[0]
-
-    @pl.when(pl.program_id(0) == 0)
+        prefetch=1,
+    )
+
+
+def put_halves(bits_ref, grad, which, keep_ref, send_ref, at):
+    grad = grad.reshape((2, 2, grad.shape[0] // 4) + grad.shape[1:])
+    pair = (grad[:, 0], grad[:, 1]) if which == 0 else (grad[0], grad[1])
+    low = bits_ref[which] == 0
+    keep_ref[at] = jnp.where(low, pair[0], pair[1])
+    send_ref[at] = jnp.where(low, pair[1], pair[0])
+
+
+def ffn_grad_kernel(bits_ref, xa_ref, xb_ref, ca_ref, cb_ref, keep_a, send_a, keep_b, send_b, x_s):
+    step = pl.program_id(0)
+
+    @pl.when(step == 0)
     def _():
         x_s[...] = jnp.concatenate([xa_ref[...], xb_ref[...]], 0).T
 
     column = jnp.concatenate([ca_ref[...], cb_ref[...]], 0)
-    grad = dot(x_s[...], column).astype(BF).reshape(first_ref.shape)
-
-    @pl.when(pl.program_id(0) < PAIR)
+    grad = dot(x_s[...], column).astype(BF)
+
+    @pl.when(step < PAIR)
     def _():
-        first_ref[...] = grad
-
-    @pl.when(pl.program_id(0) >= PAIR)
+        put_halves(bits_ref, grad, 0, keep_a, send_a, (slice(None), 0))
+
+    @pl.when(step >= PAIR)
     def _():
-        last_ref[...] = grad
-
-
-def ffn_grad(xa, xb, ca, cb, blocks):
+        put_halves(bits_ref, grad, 1, keep_b, send_b, (slice(None), 0))
+
+
+def ffn_grad(bits, xa, xb, ca, cb, blocks):
     rows, width = xa.shape
     units = ca.shape[1] // blocks
-    whole = pl.BlockSpec((rows, width), lambda t: (0, 0))
-    column = pl.BlockSpec((rows, units), lambda t: (0, t))
-    return call(
+    whole = pl.BlockSpec((rows, width), lambda t, bits: (0, 0))
+    column = pl.BlockSpec((rows, units), lambda t, bits: (0, t))
+    first = pl.BlockSpec((2, 1, width // 4, units), lambda t, bits: (0, jnp.minimum(t, PAIR - 1), 0, 0))
+    last = pl.BlockSpec((2, 1, width // 4, units), lambda t, bits: (0, jnp.maximum(t - PAIR, 0), 0, 0))
+    keep_a, send_a, keep_b, send_b = call(
         ffn_grad_kernel,
         (blocks,),
         [whole, whole, column, column],
-        [
-            pl.BlockSpec((2, 2, 1, width // 4, units), lambda t: (0, 0, jnp.minimum(t, PAIR - 1), 0, 0)),
-            pl.BlockSpec((2, 2, 1, width // 4, units), lambda t: (0, 0, jnp.maximum(t - PAIR, 0), 0, 0)),
-        ],
-        [shaped((2, 2, PAIR, width // 4, units))] * 2,
-        (xa, xb, ca, cb),
+        [first, first, last, last],
+        [shaped((2, PAIR, width // 4, units))] * 4,
+        (bits, xa, xb, ca, cb),
         [pltpu.VMEM((width, 2 * rows), BF)],
         name="ffn_grad",
-    )
+        prefetch=1,
+    )
+    return (keep_a, keep_b), (send_a, send_b)
 
 
 def swap(value, axis):
@@ -727,8 +764,11 @@
     back = lambda way: [(b, a) for a, b in way]
     stays = t // 2 == c
 
+    def sent(pair):
+        return lax.ppermute(pair[0], every, first_way), lax.ppermute(pair[1], every, second_way)
+
     def to_chip(value):
-        return lax.ppermute(chosen(value, odd, 0), every, first_way), lax.ppermute(chosen(value, 1 - odd, 0), every, second_way)
+        return sent((chosen(value, odd, 0), chosen(value, 1 - odd, 0)))
 
     def from_chip(value):
         half = value.shape[0] // 2
@@ -745,9 +785,6 @@
     def placed(value, axis):
         return lax.dynamic_slice_in_dim(jnp.concatenate([value, value], axis), steps - t, steps, axis)
 
-    def relative(value, axis):
-        return lax.dynamic_slice_in_dim(jnp.concatenate([value, value], axis), t, steps, axis)
-
     def on_chip(value, near, far):
         return jnp.concatenate([jnp.where(stays, chosen(value, odd, 0), near), far])
 
@@ -755,27 +792,20 @@
         near = jnp.where(stays, value[: value.shape[0] // 2], near)
         return jnp.stack([jnp.where(odd == 0, near, far), jnp.where(odd == 0, far, near)])
 
-    def piece_of(values, *places):
-        parts = []
-        for value in values:
-            for bit, axis in places:
-                value = chosen(value, bit, axis)
-            parts.append(value)
-        return parts[0] if len(parts) == 1 else jnp.concatenate(parts, parts[0].ndim - 3)
-
-    def scatter_start(one, two):
-        return swap(piece_of(one, (1 - x, 1)), "x"), swap(piece_of(two, (1 - y, 0)), "y")
-
-    def sums_of(one, two, parts, row, column):
-        first = piece_of(one, (x, 1), (row, 0)).astype(F32) + chosen(parts[0], row, 0).astype(F32)
-        return first, piece_of(two, (y, 0), (column, 0)).astype(F32) + chosen(parts[1], column, 0).astype(F32)
-
-    def scatter_middle(one, two, parts):
-        first, second = sums_of(one, two, parts, 1 - y, 1 - x)
+    def scatter_start(sends):
+        return swap(sends[0], "x"), swap(sends[1], "y")
+
+    def sums_of(keeps, parts, row, column):
+        pick = lambda values, bit: jnp.concatenate([chosen(value, bit, 0) for value in values])
+        first = pick(keeps[0], row).astype(F32) + chosen(parts[0], row, 0).astype(F32)
+        return first, pick(keeps[1], column).astype(F32) + chosen(parts[1], column, 0).astype(F32)
+
+    def scatter_middle(keeps, parts):
+        first, second = sums_of(keeps, parts, 1 - y, 1 - x)
         return swap(first.astype(BF), "y"), swap(second.astype(BF), "x")
 
-    def scatter_end(one, two, parts, ends):
-        first, second = sums_of(one, two, parts, y, x)
+    def scatter_end(keeps, parts, ends):
+        first, second = sums_of(keeps, parts, y, x)
         return (first + ends[0].astype(F32)).astype(BF), (second + ends[1].astype(F32)).astype(BF)
 
     dims = w_qkv.shape[1]
@@ -783,93 +813,89 @@
     lane = bias_qv.shape[1]
     units = w_up.shape[1] // 2
     attn = jnp.concatenate([jnp.swapaxes(w_qkv, 1, 2), w_out[None]]).reshape(4, 2, cols, dims)
-    small = jnp.concatenate([bias_qv.reshape(-1), up_bias, jnp.zeros((16 * dims - bias_qv.size - up_bias.size,), BF)])
-    small = small.reshape(16, dims)
     mine, other = chosen(attn, c, 1).reshape(4 * cols, dims), chosen(attn, 1 - c, 1).reshape(4 * cols, dims)
-    other = swap(jnp.concatenate([other, small]), "c")
-    attn_piece = ordered(c, jnp.concatenate([mine, small]), other, 1)
-    qk_piece, vo_piece = attn_piece[: 2 * cols], attn_piece[2 * cols :]
+    attn_piece = ordered(c, mine, swap(other, "c"), 1)
     ff = jnp.stack([w_up, w_down.T]).reshape(2, dims, 2, units)
     ff_piece = ordered(c, chosen(ff, c, 2), swap(chosen(ff, 1 - c, 2), "c"), 1)
 
-    vectors = jnp.concatenate([norm_gain, shifts, jnp.zeros((2, norm_gain.shape[1]), BF)])
+    pad = lambda value: jnp.pad(value, (0, dims - value.shape[0]))[None]
+    tails = jnp.concatenate([pad(bias_qv[0]), pad(bias_qv[1]), pad(up_bias), jnp.zeros((7, dims), BF)])
+    vectors = jnp.concatenate([norm_gain, shifts, tails])
     for bit, name in ((c, "c"), (x, "x"), (y, "y")):
         vectors = ordered(bit, vectors, swap(vectors, name), 1)
-    vectors = vectors.astype(F32)
-    gains, shift_all = vectors[0:2], vectors[2:6]
-
-    near, far = to_chip(clips)
+    gains, shift_all = vectors[0:2].astype(F32), vectors[2:6].astype(F32)
+    tails = vectors[6:16]
+    tails = jnp.stack([part[:3] for part in (tails, *ring_gather(tails))]).astype(F32)
+    tails = lax.dynamic_slice_in_dim(tails, 4 * dims * c, 4 * dims, 2)
+    pair = tails[:, :2].reshape(steps, 2, 4, dims)[..., :lane]
+    bias_pair = jnp.swapaxes(pair, 0, 1).reshape(2, 2, 2 * cols)
+    bias_in = jnp.stack([bias_pair[0], jnp.zeros_like(bias_pair[0]), bias_pair[1]], 1)[..., None]
+    up_shift = placed(tails[:, 2:3], 0)
+
     whole = ("y", "x", "t")
-    w_vo = lax.all_gather(vo_piece, whole, axis=0, tiled=False).reshape(4, steps, 2 * cols + 16, 2 * dims)
-    qk_rows = together(*ring_gather(qk_piece))
-    qk_rows = placed(jnp.stack([qk_piece, *qk_rows]), 0)
-    qk_a, qk_b = qk_rows[:, :cols], qk_rows[:, cols:]
-    swapped, near = together((swap(qk_a, "y"), swap(qk_b, "x")), near)
-    qk_a, qk_b = ordered(y, qk_a[None], swapped[0][None], 0), ordered(x, qk_b[None], swapped[1][None], 0)
-    swapped, far = together((swap(qk_a, "x"), swap(qk_b, "y")), far)
-    qk_a = ordered(x, qk_a[:, None], swapped[0][:, None], 1).reshape(4, steps, cols, 2 * dims)
-    qk_b = ordered(y, qk_b[None], swapped[1][None], 0).reshape(4, steps, cols, 2 * dims)
-    w_qk = jnp.stack([qk_a, qk_b], 2)
+    attn_rows = together(*ring_gather(attn_piece))
+    near, far = to_chip(after(clips, attn_rows))
+    attn_rows = (attn_piece, *attn_rows)
+    qk_rows = jnp.stack([part[: 2 * cols] for part in attn_rows])
+    vo_rows = jnp.stack([part[2 * cols :] for part in attn_rows])
+    targets = chosen(teacher, odd, 0), chosen(teacher, 1 - odd, 0)
+    swapped, near, targets, bias_in, up_shift = together(
+        (swap(qk_rows, "y"), swap(vo_rows, "x")), near, targets, bias_in, up_shift
+    )
+    w_qk, w_vo = ordered(y, qk_rows[None], swapped[0][None], 0), ordered(x, vo_rows[None], swapped[1][None], 0)
+    swapped, far = together((swap(w_qk, "x"), swap(w_vo, "y")), far)
+    w_qk = ordered(x, w_qk[None], swapped[0][None], 0).reshape(4, steps, 2, cols, 2 * dims)
+    w_vo = ordered(y, w_vo[None], swapped[1][None], 0).reshape(4, steps, 2 * cols, 2 * dims)
     up_piece, down_piece = ff_piece
-    up_piece, far = together(up_piece, far)
+    up_piece, down_piece, far = together(up_piece, down_piece, far)
     up_rows = ring_gather(up_piece)
-    down_piece, w_vo = together(down_piece, w_vo)
     down_all = lax.all_gather(down_piece, whole, axis=0, tiled=False).reshape(4, steps, 2 * dims, units)
     place = t.reshape(1)
-
-    rows = w_vo[:, :, 2 * cols :].reshape(4, steps, 16, 2, dims)
-    rows = jnp.transpose(rows, (1, 0, 3, 2, 4)).reshape(steps, 8, 16 * dims).astype(F32)
-    rows = lax.dynamic_slice_in_dim(rows, 4 * c, 4, 1)
-    bias_pair = jnp.transpose(rows[..., : 2 * lane].reshape(steps, 4, 2, lane), (2, 0, 1, 3)).reshape(2, steps, cols)
-    bias_pair = relative(bias_pair, 1).reshape(2, 2, 2 * cols)
-    up_shift = rows[..., 2 * lane : 2 * lane + up_bias.size].reshape(steps, 1, units)
 
     inputs = on_chip(clips, near, far).astype(F32)
     centred_one, scale_one = moments(inputs)
     first = (centred_one * scale_one * gains[0] + shift_all[0]).astype(BF)
     first_other = swap(first, "c")
-    bias_in = jnp.stack([bias_pair[0], jnp.zeros_like(bias_pair[0]), bias_pair[1]], 1)
-    qkv, turned = project(place, first, first_other, w_qk, w_vo, bias_in[..., None])
+    qkv, turned = project(first, first_other, w_qk, w_vo, bias_in)
     mixed_a, rows_a, wide_a, lse_a = attend(qkv, 0, 1664)
     up_rows, rows_a = together(up_rows, rows_a)
-    up_rows = placed(jnp.stack([up_piece, *up_rows]), 0)
-    up_a, up_b = up_rows[:PAIR], up_rows[PAIR:]
+    up_a, up_b = jnp.stack([up_piece, up_rows[0]]), jnp.stack(up_rows[1:])
     swapped = swap(up_a, "y"), swap(up_b, "x")
     mixed_b, rows_b, wide_b, lse_b = attend(after(qkv, rows_a), 1, 1664)
     swapped, rows_b = together(swapped, rows_b)
     up_a, up_b = ordered(y, up_a[None], swapped[0][None], 0), ordered(x, up_b[None], swapped[1][None], 0)
     swapped = swap(up_a, "x"), swap(up_b, "y")
     rows = (rows_a, rows_b)
-    attn_other = mix(place, rows, w_vo, 1)
-    down_all, attn_other = together(down_all, attn_other)
-    attn_mine = mix(place, (after(rows_a, attn_other), rows_b), w_vo, 0)
+    attn_other = mix(rows, w_vo, 1)
+    attn_mine = mix((after(rows_a, attn_other), rows_b), w_vo, 0)
     hidden = inputs + (attn_mine + swap(attn_other, "c")) + shift_all[2]
 
     centred_two, scale_two = moments(hidden)
     second = (centred_two * scale_two * gains[1] + shift_all[1]).astype(BF)
     second_other = swap(second, "c")
     swapped, second = together(swapped, second)
-    up_a = ordered(x, up_a[:, None], swapped[0][:, None], 1).reshape(4, PAIR, 2 * dims, units)
+    up_a = ordered(x, up_a[None], swapped[0][None], 0).reshape(4, PAIR, 2 * dims, units)
     up_b = ordered(y, up_b[None], swapped[1][None], 0).reshape(4, PAIR, 2 * dims, units)
-    up_all = jnp.concatenate([up_a, up_b], 1)
-    near, far = to_chip(after(teacher, second))
-    out_mine, act_mine, slope_mine = ffn_forward(second, up_all, down_all, up_shift)
+    up_all = up_a, up_b
+    targets, second, down_all = together(targets, second, down_all)
+    near, far = sent(targets)
+    out_mine, act_mine, slope_mine = ffn_forward(place, second, up_all, down_all, up_shift)
     out_mine, near = together(out_mine, near)
-    out_other, act_other, slope_other = ffn_forward(after(second_other, near), up_all, down_all, up_shift)
+    out_other, act_other, slope_other = ffn_forward(place, after(second_other, near), up_all, down_all, up_shift)
     out_other, far = together(out_other, far)
     output = hidden + (out_mine + swap(out_other, "c")) + shift_all[3]
     d_out = output - on_chip(teacher, near, far).astype(F32)
     d_ffn = d_out.astype(BF)
     d_ffn_other = swap(d_ffn, "c")
-    d_second, d_pre, sum_mine = ffn_backward(d_ffn, up_all, down_all, slope_mine)
+    d_second, d_pre, sum_mine = ffn_backward(place, d_ffn, up_all, down_all, slope_mine)
     d_ffn_other, d_pre = together(d_ffn_other, d_pre)
-    d_second_other, d_pre_other, sum_other = ffn_backward(d_ffn_other, up_all, down_all, slope_other)
+    d_second_other, d_pre_other, sum_other = ffn_backward(place, d_ffn_other, up_all, down_all, slope_other)
     d_second_swapped = swap(d_second_other, "c")
     up_sum = (sum_mine + sum_other).reshape(steps, units)
 
-    grad_down = ffn_grad(after(d_ffn, d_pre_other), d_ffn_other, act_mine, act_other, steps)
-    grad_down = [grad_down[0]], [grad_down[1]]
-    down = scatter_start(*grad_down)
+    bits = jnp.stack([x, y])
+    grad_down, sends = ffn_grad(bits, after(d_ffn, d_pre_other), d_ffn_other, act_mine, act_other, steps)
+    down = scatter_start(sends)
     result, grad_down = together(output.astype(BF), grad_down)
     out_near, out_far = from_chip(result)
     d_second_swapped, grad_down = together(d_second_swapped, grad_down)
@@ -878,51 +904,52 @@
     d_hidden = d_out + d_norm
     d_attn = d_hidden.astype(BF)
     d_attn_other = swap(d_attn, "c")
-    grad_up = ffn_grad(after(second, d_attn), second_other, d_pre, d_pre_other, steps)
-    grad_up = [grad_up[0]], [grad_up[1]]
-    up = scatter_start(*grad_up)
+    grad_up, sends = ffn_grad(bits, after(second, d_attn), second_other, d_pre, d_pre_other, steps)
+    up = scatter_start(sends)
     d_attn_other, grad_up = together(d_attn_other, grad_up)
 
-    d_heads, delta, *grad_o = mix_back(place, d_attn, d_attn_other, w_vo, (mixed_a, mixed_b), (wide_a, wide_b))
+    d_heads, delta, grad_o, sends_o = mix_back(bits, d_attn, d_attn_other, w_vo, (mixed_a, mixed_b), (wide_a, wide_b))
     down, delta = together(down, delta)
-    down_ends = scatter_middle(*grad_down, down)
+    grad_down, grad_up = [[keep] for keep in grad_down], [[keep] for keep in grad_up]
+    down_ends = scatter_middle(grad_down, down)
     back_a, sum_a = attend_backward(qkv, d_heads, lse_b, delta, 1, 0, 2, 256)
     up, out_near, back_a = together(up, out_near, back_a)
-    up_ends = scatter_middle(*grad_up, up)
+    up_ends = scatter_middle(grad_up, up)
     back_b, sum_b = attend_backward(qkv, after(d_heads, back_a), lse_b, delta, 1, 2, 2, 256)
     up_ends, down_ends, out_far, back_b = together(up_ends, down_ends, out_far, back_b)
-    ups, downs = scatter_end(*grad_up, up, up_ends), scatter_end(*grad_down, down, down_ends)
+    ups, downs = scatter_end(grad_up, up, up_ends), scatter_end(grad_down, down, down_ends)
     grad_ff = jnp.concatenate([jnp.stack(pair, 1) for pair in zip(ups, downs)]).reshape(steps * 4 * dims, units)
     ff_total = lax.psum_scatter(grad_ff, "t", scatter_dimension=0, tiled=True)
-    grad_one = [[grad, grad_o[p]] for p, grad in enumerate(project_grads(turned, back_a, back_b))]
-    one = scatter_start(*grad_one)
+    grad_one, sends = project_grads(bits, turned, back_a, back_b)
+    one = scatter_start([jnp.concatenate(pair, 1) for pair in zip(sends, sends_o)])
+    grad_one = list(zip(grad_one, grad_o))
     delta, grad_ff, grad_one = together(delta, grad_ff, grad_one)
     back_c, sum_c = attend_backward(qkv, after(d_heads, back_b), lse_a, delta, 0, 2, 2, 256)
     one, back_c = together(one, back_c)
-    one_ends = scatter_middle(*grad_one, one)
+    one_ends = scatter_middle(grad_one, one)
     back_d, sum_d = attend_backward(qkv, after(d_heads, back_c), lse_a, delta, 0, 0, 2, 256)
     one_ends, back_d = together(one_ends, back_d)
-    grad_two = project_grads(turned, back_d, back_c)
-    grad_two = [grad_two[0]], [grad_two[1]]
-    two = scatter_start(*grad_two)
+    grad_two, sends = project_grads(bits, turned, back_d, back_c)
+    two = scatter_start(sends)
     pieces = (back_d, back_c, back_a, back_b)
-    d_first_other = project_back(place, pieces, w_qk, after(w_vo, grad_two), 1)
+    d_first_other = project_back(pieces, w_qk, after(w_vo, grad_two), 1)
     d_first_swapped = swap(d_first_other, "c")
-    one = scatter_end(*grad_one, one, one_ends)
+    one = scatter_end(grad_one, one, one_ends)
     early = [lax.ppermute(jnp.concatenate([one[p][:3], one[p][4:]]), "t", rings[PAIR + p]) for p in range(PAIR)]
     two, d_first_other = together(two, d_first_other)
-    two_ends = scatter_middle(*grad_two, two)
-    d_first = project_back(place, pieces, w_qk, after(w_vo, d_first_other), 0)
+    two_ends = scatter_middle([[keep] for keep in grad_two], two)
+    d_first = project_back(pieces, w_qk, after(w_vo, d_first_other), 0)
     ff_total, early, d_first = together(ff_total, early, d_first)
     d_first_swapped, d_first = together(d_first_swapped, d_first)
     d_first = d_first + d_first_swapped
     d_norm, grad_gain_one, grad_shift_one = norm_back(d_first, centred_one, scale_one, gains[0])
     d_inputs = (d_hidden + d_norm).astype(BF)
     grad_near, grad_far = from_chip(d_inputs)
-    two_ends, d_inputs = together(two_ends, d_inputs)
-    two = scatter_end(*grad_two, two, two_ends)
+    small = (sum_a, sum_b, sum_c, sum_d, up_sum, grad_gain_one, grad_shift_one)
+    two_ends, small, grad_near, out_near, out_far = together(two_ends, small, grad_near, out_near, out_far)
+    sum_a, sum_b, sum_c, sum_d, up_sum, grad_gain_one, grad_shift_one = small
+    two = scatter_end([[keep] for keep in grad_two], two, two_ends)
     late = lax.ppermute(jnp.concatenate([two[1], one[1][3:4]]), "t", rings[1])
-    late, grad_near, out_near, out_far = together(late, grad_near, out_near, out_far)
 
     grad_ff = ff_total.astype(F32).reshape(2, 2, dims, units)
     grad_ff = ordered(c, chosen(grad_ff, c, 1), swap(chosen(grad_ff, 1 - c, 1), "c"), 2)
@@ -930,23 +957,21 @@
     grad_attn = sum((part.astype(F32) for part in (*early, late)), grad_attn).reshape(4, 2, dims, cols)
     grad_attn = ordered(c, chosen(grad_attn, c, 1), swap(chosen(grad_attn, 1 - c, 1), "c"), 2)
 
+    heads_sum = jnp.concatenate([sum_d, sum_c, sum_a, sum_b], 2).reshape(3, steps, 4, lane)
+    heads_sum = placed(jnp.stack([heads_sum[0], heads_sum[2]]), 1)
+    heads_sum = jnp.pad(heads_sum, ((0, 0), (0, 0), (0, 0), (0, dims - lane))).reshape(2 * steps, 4 * dims)
+    own = jnp.concatenate([heads_sum, up_sum])
+    own = jnp.concatenate([jnp.where(c == 0, own, 0.0), jnp.where(c == 1, own, 0.0)], 1)
     normed = jnp.stack([grad_gain_one, grad_gain_two, grad_shift_one, grad_shift_two, jnp.sum(d_hidden, 0), jnp.sum(d_out, 0)])
+    sums = jnp.concatenate([normed, jnp.zeros((2, width), F32), own])
+    for bit, name in ((y, "y"), (x, "x"), (c, "c")):
+        half = sums.shape[1] // 2
+        part = lambda which: lax.dynamic_slice_in_dim(sums, which * half, half, 1)
+        sums = part(bit) + swap(part(1 - bit), name)
+    sums = sum((lax.ppermute(sums, "t", rings[away]) for away in range(1, steps)), sums)
     thin = width // 32
-    rows = jnp.swapaxes(normed.reshape(6, 32, thin), 0, 1).reshape(32, 6 * thin)
-    sums = jnp.concatenate([sum_d, sum_c, sum_a, sum_b], 2)
-    pair = placed(jnp.stack([sums[0], sums[2]]).reshape(2, steps, 4, lane), 1)
-    pair = jnp.transpose(pair, (2, 1, 0, 3))
-    ups = jnp.transpose(up_sum.reshape(steps, 4, up_bias.size), (1, 0, 2))
-    mine = jnp.concatenate([pair.reshape(16, 2 * lane), ups.reshape(16, up_bias.size)], 1)
-    here = jnp.where((jnp.arange(2) == c)[:, None, None], mine[None], 0.0).reshape(32, mine.shape[1])
-    sums = after(jnp.concatenate([rows, here], 1), grad_near)
-    for bit, name in ((y, "y"), (x, "x"), (c, "c")):
-        sums = sums.reshape(2, sums.shape[0] // 2, sums.shape[1])
-        sums = chosen(sums, bit, 0) + swap(chosen(sums, 1 - bit, 0), name)
-    total = chosen(sums, t, 0)
-    for away in range(1, steps):
-        total = total + lax.ppermute(chosen(sums, (t + away) % steps, 0), "t", rings[away])
-    vector_sums = total[: 6 * thin].reshape(6, thin)
+    vector_sums = lax.dynamic_slice_in_dim(sums[:6], thin * t, thin, 1)
+    place_sums = lax.dynamic_index_in_dim(sums[8:].reshape(3, steps, dims), t, 1, keepdims=False)
     return (
         as_clips(result, out_near, out_far),
         as_clips(d_inputs, grad_near, grad_far),
@@ -956,8 +981,8 @@
         grad_ff[1].T,
         vector_sums[:2],
         vector_sums[2:],
-        total[6 * thin : 6 * thin + 2 * lane].reshape(2, lane),
-        total[6 * thin + 2 * lane :],
+        place_sums[:2, :lane],
+        place_sums[2],
     )
 
 

time: 610 us -> 581 us (0.952)
  local copies, waits for them, and re-layouts: 62.8 us -> 29.5 us
  waiting for transfers between devices: 109 us -> 130 us
  starting transfers between devices: 89.7 us -> 72.2 us
    ppermute x6 -> x9, waiting for transfers between devices: 51.2 us -> 21.6 us  [ring_gather(): lax.ppermute(value, 't', rings[-j % steps])]
    ppermute x2, waiting for transfers between devices: 2.56 us -> 24.3 us  [from_chip(): lax.ppermute(value[half:], every, back(second_way))]
    ppermute x7, waiting for transfers between devices: 0.02 us -> 19.6 us  [the longest x2 19.4 us: sent(): lax.ppermute(pair[1], every, second_way)]
    ppermute x42, starting transfers between devices: 58.2 us -> 41.6 us  [swap(): return lax.ppermute(value, axis, [(0, 1), (1, 0)])]
    squeeze x20 -> x7, local copies, waits for them, and re-layouts: 20.1 us -> 5.01 us  [chosen(): return lax.dynamic_index_in_dim(value, bit, axis, keepdims=False)]
    ppermute x42, waiting for transfers between devices: 42 us -> 53.1 us  [swap(): return lax.ppermute(value, axis, [(0, 1), (1, 0)])]
    ppermute x2, waiting for transfers between devices: 0.03 us -> 8.98 us  [clip_local(): lax.ppermute(jnp.concatenate([one[p][:3], one[p][4:]]), 't', rings[PAIR +...]
    unnamed x148 -> x132, local copies, waits for them, and re-layouts: 13.7 us -> 8.61 us
  transfers between devices with their start and end apart: 65 -> 67, of which waited for: 17 -> 22; matrix products, arithmetic and copies ran while one was open for 18% -> 14% of each run, Pallas kernels for 37% -> 39%
where the time goes in v3:
time: 581 us; the launch traced here: 574 us
  Pallas kernels  244 us (42%)
  waiting for transfers between devices  130 us (22%)
  other arithmetic  82 us (14%)
  starting transfers between devices  72.2 us (12%)
  local copies, waits for them, and re-layouts  29.5 us (5%)
  between operations  15.9 us (3%)
    pallas_call x20, Pallas kernels, call(): pl.pallas_call(body, grid_spec=pltpu.PrefetchScalarGridSpec(num_scalar_pr...  244 us
    ppermute x42, waiting for transfers between devices, swap(): return lax.ppermute(value, axis, [(0, 1), (1, 0)])  53.1 us
    ppermute x42, starting transfers between devices, swap(): return lax.ppermute(value, axis, [(0, 1), (1, 0)])  41.6 us
    ppermute x2, waiting for transfers between devices, from_chip(): lax.ppermute(value[half:], every, back(second_way))  24.3 us
    ppermute x9, waiting for transfers between devices, ring_gather(): lax.ppermute(value, 't', rings[-j % steps])  21.6 us
    ppermute x2, waiting for transfers between devices, sent(): lax.ppermute(pair[1], every, second_way)  19.4 us
  transfers between devices with their start and end apart: 67, of which 22 were waited for; matrix products, arithmetic and copies ran while one was open for 14% of the time, Pallas kernels for 39%

profile of v3, /device:TPU:0, one launch (start us, length us, event | category | flops | bytes accessed | tf_op | source)
XLA Modules:
  0.0 573.9 jit_solution(43994627712242519)
XLA Ops:
  37.0 6.1 %collective-permute-done.1 = bf16[512,256]{1,0:T(8,128)(2,1)S(1)} collective-permute-done((bf16[512,256]{1,0:T(8,128)(2,1)S(1)}, bf16[512,256]{1,0:T(8,128)(2,1)S(1)}, u32[]{:S(2)}, u32[]{:S(2)}) %collective-permute-start.1) | collective-permute-done | bytes 262176 | tf_op jit(solution)/shard_map/ppermute | solution.py:780
  43.1 13.0 %collective-permute-done.2 = bf16[512,256]{1,0:T(8,128)(2,1)S(1)} collective-permute-done((bf16[512,256]{1,0:T(8,128)(2,1)S(1)}, bf16[512,256]{1,0:T(8,128)(2,1)S(1)}, u32[]{:S(2)}, u32[]{:S(2)}) %collective-permute-start.2) | collective-permute-done | bytes 262176 | tf_op jit(solution)/shard_map/ppermute | solution.py:780
  63.7 9.1 %collective-permute-done.5 = bf16[4,256,256]{2,1,0:T(8,128)(2,1)} collective-permute-done((bf16[4,256,256]{2,1,0:T(8,128)(2,1)}, bf16[4,256,256]{2,1,0:T(8,128)(2,1)}, u32[]{:S(2)}, u32[]{:S(2)}) %collective-permute-start.5) | collective-permute-done | bytes 524320 | tf_op jit(solution)/shard_map/ppermute | solution.py:711
  81.1 19.4 %collective-permute-done.16 = bf16[392,1024]{1,0:T(8,128)(2,1)S(1)} collective-permute-done((bf16[392,1024]{1,0:T(8,128)(2,1)S(1)}, bf16[392,1024]{1,0:T(8,128)(2,1)S(1)}, u32[]{:S(2)}, u32[]{:S(2)}) %collective-permute-start.16) | collective-permute-done | bytes 802848 | tf_op jit(solution)/shard_map/ppermute | solution.py:768
  116.1 11.8 %project.1 = (bf16[2,3,4,64,1568]{4,3,2,1,0:T(8,128)(2,1)}, bf16[1024,1568]{1,0:T(8,128)(2,1)}) custom-call(bf16[784,1024]{1,0:T(8,128)(2,1)} %copy-done.15, bf16[784,1024]{1,0:T(8,128)(2,1)} %collective-permute-done.20.xb_ref, bf16[4,4,2,128,256]{4,3,2,1,0:T(8,128)(2,1)} %bitcast.272, bf16[4,4,256,256]{3,2,1,0:T(8,128)(2,1)} %bitcast.254, ...), custom_call_target="tpu_custom_call" | custom-call | flops 1000 | bytes 1000 | tf_op jit(solution)/shard_map/project/pallas_call | solution.py:194
  127.8 16.2 %attend.2 = (bf16[4,64,1568]{2,1,0:T(8,128)(2,1)}, bf16[1568,256]{1,0:T(8,128)(2,1)}, f32[4,64,1568]{2,1,0:T(8,128)}, f32[4,1,1568]{2,1,0:T(1,128)}) custom-call(bf16[2,3,4,64,1568]{4,3,2,1,0:T(8,128)(2,1)} %get-tuple-element.180.q_ref.k_ref.v_ref, bf16[2,3,4,64,1568]{4,3,2,1,0:T(8,128)(2,1)} %get-tuple-element.180.q_ref.k_ref.v_ref, ...), custom_call_target="tpu_custom_call" | custom-call | flops 1000 | bytes 1000 | tf_op jit(solution)/shard_map/attend/pallas_call | solution.py:194
  146.1 16.2 %attend.3 = (bf16[4,64,1568]{2,1,0:T(8,128)(2,1)}, bf16[1568,256]{1,0:T(8,128)(2,1)}, f32[4,64,1568]{2,1,0:T(8,128)}, f32[4,1,1568]{2,1,0:T(1,128)}) custom-call(bf16[2,3,4,64,1568]{4,3,2,1,0:T(8,128)(2,1)} %get-tuple-element.180.q_ref.k_ref.v_ref, bf16[2,3,4,64,1568]{4,3,2,1,0:T(8,128)(2,1)} %get-tuple-element.180.q_ref.k_ref.v_ref, ...), custom_call_target="tpu_custom_call" | custom-call | flops 1000 | bytes 1000 | tf_op jit(solution)/shard_map/attend/pallas_call | solution.py:194
  162.9 3.7 mix.2
  171.4 4.1 mix.3
  183.0 24.6 %collective-permute-done.25 = bf16[2,2,256,512]{3,2,1,0:T(8,128)(2,1)} collective-permute-done((bf16[2,2,256,512]{3,2,1,0:T(8,128)(2,1)}, bf16[2,2,256,512]{3,2,1,0:T(8,128)(2,1)}, u32[]{:S(2)}, u32[]{:S(2)}) %collective-permute-start.25) | collective-permute-done | bytes 1048608 | tf_op jit(solution)/shard_map/ppermute | solution.py:711
  218.4 15.4 %ffn.2 = (f32[784,1024]{1,0:T(8,128)}, bf16[784,2048]{1,0:T(8,128)(2,1)}, bf16[784,2048]{1,0:T(8,128)(2,1)}) custom-call(s32[1]{0:T(128)} %bitcast.51.place_ref, bf16[784,1024]{1,0:T(8,128)(2,1)} %add_convert_fusion.x_ref.xa_ref, bf16[4,2,256,512]{3,2,1,0:T(8,128)(2,1)} %bitcast.268, bf16[4,2,256,512]{3,2,1,0:T(8,128)(2,1)} %bitcast.264, ...), custom_call_target="tpu_custom_call" | custom-call | flops 1000 | bytes 1000 | tf_op jit(solution)/shard_map/ffn/pallas_call | solution.py:194
  233.9 15.6 %ffn.3 = (f32[784,1024]{1,0:T(8,128)}, bf16[784,2048]{1,0:T(8,128)(2,1)}, bf16[784,2048]{1,0:T(8,128)(2,1)}) custom-call(s32[1]{0:T(128)} %bitcast.51.place_ref, bf16[784,1024]{1,0:T(8,128)(2,1)} %collective-permute-done.27.x_ref.xb_ref, bf16[4,2,256,512]{3,2,1,0:T(8,128)(2,1)} %bitcast.269, bf16[4,2,256,512]{3,2,1,0:T(8,128)(2,1)} %bitcast.265, ...), custom_call_target="tpu_custom_call" | custom-call | flops 1000 | bytes 1000 | tf_op jit(solution)/shard_map/ffn/pallas_call | solution.py:194
  250.4 7.4 %collective-permute-start.29 = (f32[784,1024]{1,0:T(8,128)}, f32[784,1024]{1,0:T(8,128)S(1)}, u32[]{:S(2)}, u32[]{:S(2)}) collective-permute-start(f32[784,1024]{1,0:T(8,128)} %get-tuple-element.202), channel_id=1, source_target_pairs={{0,4},{4,0},{1,5},{5,1},{2,6},{6,2},{3,7},{7,3},{8,12},{12,8},{9,1... | collective-permute-start | bytes 9633800 | tf_op jit(solution)/shard_map/ppermute | solution.py:711
  257.9 5.5 collective-permute-done.29
  269.8 13.7 %ffn_backward.2 = (f32[784,1024]{1,0:T(8,128)}, bf16[784,2048]{1,0:T(8,128)(2,1)}, f32[4,1,512]{2,1,0:T(1,128)}) custom-call(s32[1]{0:T(128)} %bitcast.51.place_ref, bf16[784,1024]{1,0:T(8,128)(2,1)} %get-tuple-element.209.d_ref.xa_ref, bf16[4,4,256,512]{3,2,1,0:T(8,128)(2,1)} %bitcast.262, bf16[4,2,256,512]{3,2,1,0:T(8,128)(2,1)} %bitcast.270, ...), custom_call_target="tpu_custom_call" | custom-call | flops 1000 | bytes 1000 | tf_op jit(solution)/shard_map/ffn_backward/pallas_call | solution.py:194
  283.5 13.7 %ffn_backward.3 = (f32[784,1024]{1,0:T(8,128)}, bf16[784,2048]{1,0:T(8,128)(2,1)}, f32[4,1,512]{2,1,0:T(1,128)}) custom-call(s32[1]{0:T(128)} %bitcast.51.place_ref, bf16[784,1024]{1,0:T(8,128)(2,1)} %collective-permute-done.30.d_ref.xb_ref, bf16[4,4,256,512]{3,2,1,0:T(8,128)(2,1)} %bitcast.263, bf16[4,2,256,512]{3,2,1,0:T(8,128)(2,1)} %bitcast.271, ...), custom_call_target="tpu_custom_call" | custom-call | flops 1000 | bytes 1000 | tf_op jit(solution)/shard_map/ffn_backward/pallas_call | solution.py:194
  297.9 14.4 %ffn_grad.2 = (bf16[2,2,256,512]{3,2,1,0:T(8,128)(2,1)}, bf16[2,2,256,512]{3,2,1,0:T(8,128)(2,1)}, bf16[2,2,256,512]{3,2,1,0:T(8,128)(2,1)}, bf16[2,2,256,512]{3,2,1,0:T(8,128)(2,1)}) custom-call(s32[2]{0:T(128)} %pad_add_fusion.bits_ref, bf16[784,1024]{1,0:T(8,128)(2,1)} %get-tuple-element.209.d_ref.xa_ref, ...), custom_call_target="tpu_custom_call" | custom-call | flops 1000 | bytes 1000 | tf_op jit(solution)/shard_map/ffn_grad/pallas_call | solution.py:194
  312.3 4.5 multiply_reduce_fusion
  323.3 14.4 %ffn_grad.3 = (bf16[2,2,256,512]{3,2,1,0:T(8,128)(2,1)}, bf16[2,2,256,512]{3,2,1,0:T(8,128)(2,1)}, bf16[2,2,256,512]{3,2,1,0:T(8,128)(2,1)}, bf16[2,2,256,512]{3,2,1,0:T(8,128)(2,1)}) custom-call(s32[2]{0:T(128)} %pad_add_fusion.bits_ref, bf16[784,1024]{1,0:T(8,128)(2,1)} %add_convert_fusion.x_ref.xa_ref, ...), custom_call_target="tpu_custom_call" | custom-call | flops 1000 | bytes 1000 | tf_op jit(solution)/shard_map/ffn_grad/pallas_call | solution.py:194
  342.7 10.8 %mix_back.1 = (bf16[8,64,1568]{2,1,0:T(8,128)(2,1)}, f32[8,1,1568]{2,1,0:T(1,128)}, bf16[2,2,256,128]{3,2,1,0:T(8,128)(2,1)}, bf16[2,2,256,128]{3,2,1,0:T(8,128)...) custom-call(s32[2]{0:T(128)} %pad_add_fusion.bits_ref, bf16[784,1024]{1,0:T(8,128)(2,1)} %copy-done.14, ...), custom_call_target="tpu_custom_call" | custom-call | flops 1000 | bytes 1000 | tf_op jit(solution)/shard_map/mix_back/pallas_call | solution.py:194
  353.7 16.5 %attend_backward.4 = (bf16[3,1568,128]{2,1,0:T(8,128)(2,1)}, f32[3,1,128]{2,1,0:T(1,128)}) custom-call(bf16[2,3,4,64,1568]{4,3,2,1,0:T(8,128)(2,1)} %get-tuple-element.180.q_ref.k_ref.v_ref, bf16[2,3,4,64,1568]{4,3,2,1,0:T(8,128)(2,1)} %get-tuple-element.180.q_ref.k_ref.v_ref, bf16[2,3,4,64,1568]{4,3,2,1,0:T(8,128)(2,1)} %get-tuple-element.180.q_ref.k_ref.v_ref, ...), custom_call_target="tpu_custom_call" | custom-call | flops 1000 | bytes 1000 | tf_op jit(solution)/shard_map/attend_backward/pallas_call | solution.py:194
  383.0 16.9 %attend_backward.5 = (bf16[3,1568,128]{2,1,0:T(8,128)(2,1)}, f32[3,1,128]{2,1,0:T(1,128)}) custom-call(bf16[2,3,4,64,1568]{4,3,2,1,0:T(8,128)(2,1)} %get-tuple-element.180.q_ref.k_ref.v_ref, bf16[2,3,4,64,1568]{4,3,2,1,0:T(8,128)(2,1)} %get-tuple-element.180.q_ref.k_ref.v_ref, bf16[2,3,4,64,1568]{4,3,2,1,0:T(8,128)(2,1)} %get-tuple-element.180.q_ref.k_ref.v_ref, ...), custom_call_target="tpu_custom_call" | custom-call | flops 1000 | bytes 1000 | tf_op jit(solution)/shard_map/attend_backward/pallas_call | solution.py:194
  406.2 7.4 %project_grads.2 = (bf16[2,3,256,128]{3,2,1,0:T(8,128)(2,1)}, bf16[2,3,256,128]{3,2,1,0:T(8,128)(2,1)}, bf16[2,3,256,128]{3,2,1,0:T(8,128)(2,1)}, bf16[2,3,256,128]{3,2,1,0:T(8,128)(2,1)}) custom-call(s32[2]{0:T(128)} %pad_add_fusion.bits_ref, bf16[1024,1568]{1,0:T(8,128)(2,1)} %get-tuple-element.215.t_ref, ...), custom_call_target="tpu_custom_call" | custom-call | flops 1000 | bytes 1000 | tf_op jit(solution)/shard_map/project_grads/pallas_call | solution.py:194
  420.6 16.4 %attend_backward.6 = (bf16[3,1568,128]{2,1,0:T(8,128)(2,1)}, f32[3,1,128]{2,1,0:T(1,128)}) custom-call(bf16[2,3,4,64,1568]{4,3,2,1,0:T(8,128)(2,1)} %get-tuple-element.180.q_ref.k_ref.v_ref, bf16[2,3,4,64,1568]{4,3,2,1,0:T(8,128)(2,1)} %get-tuple-element.180.q_ref.k_ref.v_ref, bf16[2,3,4,64,1568]{4,3,2,1,0:T(8,128)(2,1)} %get-tuple-element.180.q_ref.k_ref.v_ref, ...), custom_call_target="tpu_custom_call" | custom-call | flops 1000 | bytes 1000 | tf_op jit(solution)/shard_map/attend_backward/pallas_call | solution.py:194
  440.1 16.4 %attend_backward.7 = (bf16[3,1568,128]{2,1,0:T(8,128)(2,1)}, f32[3,1,128]{2,1,0:T(1,128)}) custom-call(bf16[2,3,4,64,1568]{4,3,2,1,0:T(8,128)(2,1)} %get-tuple-element.180.q_ref.k_ref.v_ref, bf16[2,3,4,64,1568]{4,3,2,1,0:T(8,128)(2,1)} %get-tuple-element.180.q_ref.k_ref.v_ref, bf16[2,3,4,64,1568]{4,3,2,1,0:T(8,128)(2,1)} %get-tuple-element.180.q_ref.k_ref.v_ref, ...), custom_call_target="tpu_custom_call" | custom-call | flops 1000 | bytes 1000 | tf_op jit(solution)/shard_map/attend_backward/pallas_call | solution.py:194
  456.5 7.3 %project_grads.3 = (bf16[2,3,256,128]{3,2,1,0:T(8,128)(2,1)}, bf16[2,3,256,128]{3,2,1,0:T(8,128)(2,1)}, bf16[2,3,256,128]{3,2,1,0:T(8,128)(2,1)}, bf16[2,3,256,128]{3,2,1,0:T(8,128)(2,1)}) custom-call(s32[2]{0:T(128)} %pad_add_fusion.bits_ref, bf16[1024,1568]{1,0:T(8,128)(2,1)} %get-tuple-element.215.t_ref, ...), custom_call_target="tpu_custom_call" | custom-call | flops 1000 | bytes 1000 | tf_op jit(solution)/shard_map/project_grads/pallas_call | solution.py:194
  463.8 6.7 %project_back.2 = f32[784,1024]{1,0:T(8,128)} custom-call(bf16[3,1568,128]{2,1,0:T(8,128)(2,1)} %get-tuple-element.276.da_ref.a_ref, bf16[3,1568,128]{2,1,0:T(8,128)(2,1)} %get-tuple-element.273.db_ref.b_ref, bf16[3,1568,128]{2,1,0:T(8,128)(2,1)} %get-tuple-element.247.da_ref.c_ref, bf16[3,1568,128]{2,1,0:T(8,128)(2,1)} %get-tuple-element.254.db_ref.d_ref, ...), custom_call_target="tpu_custom_call" | custom-call | flops 1000 | bytes 1000 | tf_op jit(solution)/shard_map/project_back/pallas_call | solution.py:194
  476.6 6.7 %project_back.3 = f32[784,1024]{1,0:T(8,128)} custom-call(bf16[3,1568,128]{2,1,0:T(8,128)(2,1)} %get-tuple-element.276.da_ref.a_ref, bf16[3,1568,128]{2,1,0:T(8,128)(2,1)} %get-tuple-element.273.db_ref.b_ref, bf16[3,1568,128]{2,1,0:T(8,128)(2,1)} %get-tuple-element.247.da_ref.c_ref, bf16[3,1568,128]{2,1,0:T(8,128)(2,1)} %get-tuple-element.254.db_ref.d_ref, ...), custom_call_target="tpu_custom_call" | custom-call | flops 1000 | bytes 1000 | tf_op jit(solution)/shard_map/project_back/pallas_call | solution.py:194
  485.4 9.0 %collective-permute-done.52 = bf16[4,256,128]{2,1,0:T(8,128)(2,1)} collective-permute-done((bf16[4,256,128]{2,1,0:T(8,128)(2,1)S(1)}, bf16[4,256,128]{2,1,0:T(8,128)(2,1)}, u32[]{:S(2)}, u32[]{:S(2)}) %collective-permute-start.52) | collective-permute-done | bytes 262176 | tf_op jit(solution)/shard_map/ppermute | solution.py:938
  494.4 4.3 fusion.9
  522.0 24.3 %collective-permute-done.55 = bf16[392,1024]{1,0:T(8,128)(2,1)} collective-permute-done((bf16[392,1024]{1,0:T(8,128)(2,1)}, bf16[392,1024]{1,0:T(8,128)(2,1)}, u32[]{:S(2)}, u32[]{:S(2)}) %collective-permute-start.55) | collective-permute-done | bytes 802848 | tf_op jit(solution)/shard_map/ppermute | solution.py:775
  553.0 3.8 collective-permute-start.62
  (424 shorter events, 182.7 us)
Async XLA Ops:
  7.2 202.8 %all-gather.3.cloned.1.call-start = ((), (), s32[]{:S(2)}) async-start(), calls=%async_computation.2 | async-start | bytes 4456448 | tf_op jit(solution)/shard_map/all_gather | solution.py:852
  12.6 20.4 %collective-permute-start = (bf16[512,128]{1,0:T(8,128)(2,1)S(1)}, bf16[512,128]{1,0:T(8,128)(2,1)S(1)}, u32[]{:S(2)}, u32[]{:S(2)}) collective-permute-start(bf16[512,128]{1,0:T(8,128)(2,1)S(1)} %bitcast.289), channel_id=1, source_target_pairs={{0,4},{4,0},{1,5},{5,1},{2,6},{6,2},{3,7},{7,3},{8,12},{12,8},{9,1... | collective-permute-start | bytes 393224 | tf_op jit(solution)/shard_map/ppermute | solution.py:711
  18.8 61.4 %collective-permute-start.13 = (bf16[2,128,512]{2,1,0:T(8,128)(2,1)}, bf16[2,128,512]{2,1,0:T(8,128)(2,1)S(1)}, u32[]{:S(2)}, u32[]{:S(2)}) collective-permute-start(bf16[2,128,512]{2,1,0:T(8,128)(2,1)} %fusion.43), channel_id=1, source_target_pairs={{0,4},{4,0},{1,5},{5,1},{2,6},{6,2},{3,7},{7,3},{8,12},{12,8},{9,1... | collective-permute-start | bytes 786440 | tf_op jit(solution)/shard_map/ppermute | solution.py:711
  77.0 23.5 %collective-permute-start.15 = (bf16[2,4,256,256]{3,2,1,0:T(8,128)(2,1)S(1)}, bf16[2,4,256,256]{3,2,1,0:T(8,128)(2,1)}, u32[]{:S(2)}, u32[]{:S(2)}) collective-permute-start(bf16[2,4,256,256]{3,2,1,0:T(8,128)(2,1)S(1)} %pad_maximum_fusion.8), channel_id=1, source_target_pairs={{0,16},{16,0},{1,17},{17,1},{2,18},{18,2},{3,19},{19,3},{4,20},{20... | collective-permute-start | bytes 3145736 | tf_op jit(solution)/shard_map/ppermute | solution.py:711
  79.0 23.1 %collective-permute-start.14 = (bf16[2,4,256,256]{3,2,1,0:T(8,128)(2,1)S(1)}, bf16[2,4,256,256]{3,2,1,0:T(8,128)(2,1)}, u32[]{:S(2)}, u32[]{:S(2)}) collective-permute-start(bf16[2,4,256,256]{3,2,1,0:T(8,128)(2,1)S(1)} %pad_maximum_fusion.7), channel_id=1, source_target_pairs={{0,8},{8,0},{1,9},{9,1},{2,10},{10,2},{3,11},{11,3},{4,12},{12,4},... | collective-permute-start | bytes 3145736 | tf_op jit(solution)/shard_map/ppermute | solution.py:711
  79.7 20.8 %collective-permute-start.16 = (bf16[392,1024]{1,0:T(8,128)(2,1)S(1)}, bf16[392,1024]{1,0:T(8,128)(2,1)S(1)}, u32[]{:S(2)}, u32[]{:S(2)}) collective-permute-start(bf16[392,1024]{1,0:T(8,128)(2,1)S(1)} %copy-done.42), channel_id=1, source_target_pairs={{0,1},{1,0},{2,5},{3,4},{4,3},{5,2},{6,7},{7,6},{8,9},{9,8},{10,13... | collective-permute-start | bytes 2408456 | tf_op jit(solution)/shard_map/ppermute | solution.py:768
  103.0 391.4 %reduce-scatter.2.cloned.1.call-start = ((), (), s32[]{:S(2)}) async-start(), calls=%async_computation.1 | async-start | bytes 2621440 | tf_op jit(solution)/shard_map/reduce_scatter | solution.py:922
  107.9 36.1 %collective-permute-start.17 = (bf16[256,512]{1,0:T(8,128)(2,1)S(1)}, bf16[256,512]{1,0:T(8,128)(2,1)S(1)}, u32[]{:S(2)}, u32[]{:S(2)}) collective-permute-start(bf16[256,512]{1,0:T(8,128)(2,1)S(1)} %get-tuple-element.170), channel_id=1, source_target_pairs={{0,3},{1,0},{2,1},{3,2},{4,7},{5,4},{6,5},{7,6},{8,11},{9,8},{10,9... | collective-permute-start | bytes 786440 | tf_op jit(solution)/shard_map/ppermute | solution.py:780
  107.9 36.2 %collective-permute-start.18 = (bf16[256,512]{1,0:T(8,128)(2,1)S(1)}, bf16[256,512]{1,0:T(8,128)(2,1)S(1)}, u32[]{:S(2)}, u32[]{:S(2)}) collective-permute-start(bf16[256,512]{1,0:T(8,128)(2,1)S(1)} %get-tuple-element.170), channel_id=1, source_target_pairs={{0,2},{1,3},{2,0},{3,1},{4,6},{5,7},{6,4},{7,5},{8,10},{9,11},{10,... | collective-permute-start | bytes 786440 | tf_op jit(solution)/shard_map/ppermute | solution.py:780
  109.9 34.2 %collective-permute-start.19 = (bf16[256,512]{1,0:T(8,128)(2,1)S(1)}, bf16[256,512]{1,0:T(8,128)(2,1)S(1)}, u32[]{:S(2)}, u32[]{:S(2)}) collective-permute-start(bf16[256,512]{1,0:T(8,128)(2,1)S(1)} %get-tuple-element.170), channel_id=1, source_target_pairs={{0,1},{1,2},{2,3},{3,0},{4,5},{5,6},{6,7},{7,4},{8,9},{9,10},{10,1... | collective-permute-start | bytes 786440 | tf_op jit(solution)/shard_map/ppermute | solution.py:780
  167.9 39.6 %collective-permute-start.25 = (bf16[2,2,256,512]{3,2,1,0:T(8,128)(2,1)}, bf16[2,2,256,512]{3,2,1,0:T(8,128)(2,1)}, u32[]{:S(2)}, u32[]{:S(2)}) collective-permute-start(bf16[2,2,256,512]{3,2,1,0:T(8,128)(2,1)} %pad_maximum_fusion.10), channel_id=1, source_target_pairs={{0,16},{16,0},{1,17},{17,1},{2,18},{18,2},{3,19},{19,3},{4,20},{20... | collective-permute-start | bytes 3145736 | tf_op jit(solution)/shard_map/ppermute | solution.py:711
  170.8 36.8 %collective-permute-start.24 = (bf16[2,2,256,512]{3,2,1,0:T(8,128)(2,1)}, bf16[2,2,256,512]{3,2,1,0:T(8,128)(2,1)}, u32[]{:S(2)}, u32[]{:S(2)}) collective-permute-start(bf16[2,2,256,512]{3,2,1,0:T(8,128)(2,1)} %pad_maximum_fusion.9), channel_id=1, source_target_pairs={{0,8},{8,0},{1,9},{9,1},{2,10},{10,2},{3,11},{11,3},{4,12},{12,4},... | collective-permute-start | bytes 3145736 | tf_op jit(solution)/shard_map/ppermute | solution.py:711
  182.9 51.0 %collective-permute-start.27 = (bf16[784,1024]{1,0:T(8,128)(2,1)}, bf16[784,1024]{1,0:T(8,128)(2,1)}, u32[]{:S(2)}, u32[]{:S(2)}) collective-permute-start(bf16[784,1024]{1,0:T(8,128)(2,1)} %add_convert_fusion.x_ref.xa_ref), channel_id=1, source_target_pairs={{0,4},{4,0},{1,5},{5,1},{2,6},{6,2},{3,7},{7,3},{8,12},{12,8},{9,1... | collective-permute-start | bytes 4816904 | tf_op jit(solution)/shard_map/ppermute | solution.py:711
  210.0 23.9 %collective-permute-start.26 = (bf16[392,1024]{1,0:T(8,128)(2,1)}, bf16[392,1024]{1,0:T(8,128)(2,1)S(1)}, u32[]{:S(2)}, u32[]{:S(2)}) collective-permute-start(bf16[392,1024]{1,0:T(8,128)(2,1)} %get-tuple-element.196), channel_id=1, source_target_pairs={{2,4},{3,5},{4,2},{5,3},{10,12},{11,13},{12,10},{13,11},{18,20},{1... | collective-permute-start | bytes 2408456 | tf_op jit(solution)/shard_map/ppermute | solution.py:768
  210.8 38.7 %collective-permute-start.28 = (bf16[392,1024]{1,0:T(8,128)(2,1)}, bf16[392,1024]{1,0:T(8,128)(2,1)S(1)}, u32[]{:S(2)}, u32[]{:S(2)}) collective-permute-start(bf16[392,1024]{1,0:T(8,128)(2,1)} %get-tuple-element.201), channel_id=1, source_target_pairs={{0,1},{1,0},{2,5},{3,4},{4,3},{5,2},{6,7},{7,6},{8,9},{9,8},{10,13... | collective-permute-start | bytes 2408456 | tf_op jit(solution)/shard_map/ppermute | solution.py:768
  320.8 20.2 %collective-permute-start.34 = (bf16[784,1024]{1,0:T(8,128)(2,1)S(1)}, bf16[784,1024]{1,0:T(8,128)(2,1)S(1)}, u32[]{:S(2)}, u32[]{:S(2)}) collective-permute-start(bf16[784,1024]{1,0:T(8,128)(2,1)S(1)} %convert_element_type.282.da_ref), channel_id=1, source_target_pairs={{0,4},{4,0},{1,5},{5,1},{2,6},{6,2},{3,7},{7,3},{8,12},{12,8},{9,1... | collective-permute-start | bytes 4816904 | tf_op jit(solution)/shard_map/ppermute | solution.py:711
  321.3 32.3 %collective-permute-start.31 = (bf16[2,2,256,512]{3,2,1,0:T(8,128)(2,1)}, bf16[2,2,256,512]{3,2,1,0:T(8,128)(2,1)}, u32[]{:S(2)}, u32[]{:S(2)}) collective-permute-start(bf16[2,2,256,512]{3,2,1,0:T(8,128)(2,1)} %get-tuple-element.216), channel_id=1, source_target_pairs={{0,8},{8,0},{1,9},{9,1},{2,10},{10,2},{3,11},{11,3},{4,12},{12,4},... | collective-permute-start | bytes 3145736 | tf_op jit(solution)/shard_map/ppermute | solution.py:711
  323.3 30.4 %collective-permute-start.32 = (bf16[2,2,256,512]{3,2,1,0:T(8,128)(2,1)}, bf16[2,2,256,512]{3,2,1,0:T(8,128)(2,1)}, u32[]{:S(2)}, u32[]{:S(2)}) collective-permute-start(bf16[2,2,256,512]{3,2,1,0:T(8,128)(2,1)} %get-tuple-element.217), channel_id=1, source_target_pairs={{0,16},{16,0},{1,17},{17,1},{2,18},{18,2},{3,19},{19,3},{4,20},{20... | collective-permute-start | bytes 3145736 | tf_op jit(solution)/shard_map/ppermute | solution.py:711
  337.7 32.4 %collective-permute-start.35 = (bf16[2,2,256,512]{3,2,1,0:T(8,128)(2,1)}, bf16[2,2,256,512]{3,2,1,0:T(8,128)(2,1)}, u32[]{:S(2)}, u32[]{:S(2)}) collective-permute-start(bf16[2,2,256,512]{3,2,1,0:T(8,128)(2,1)} %get-tuple-element.235), channel_id=1, source_target_pairs={{0,8},{8,0},{1,9},{9,1},{2,10},{10,2},{3,11},{11,3},{4,12},{12,4},... | collective-permute-start | bytes 3145736 | tf_op jit(solution)/shard_map/ppermute | solution.py:711
  337.8 33.2 %collective-permute-start.36 = (bf16[2,2,256,512]{3,2,1,0:T(8,128)(2,1)}, bf16[2,2,256,512]{3,2,1,0:T(8,128)(2,1)}, u32[]{:S(2)}, u32[]{:S(2)}) collective-permute-start(bf16[2,2,256,512]{3,2,1,0:T(8,128)(2,1)} %get-tuple-element.236), channel_id=1, source_target_pairs={{0,16},{16,0},{1,17},{17,1},{2,18},{18,2},{3,19},{19,3},{4,20},{20... | collective-permute-start | bytes 3145736 | tf_op jit(solution)/shard_map/ppermute | solution.py:711
  341.1 29.1 %collective-permute-start.37 = (bf16[392,1024]{1,0:T(8,128)(2,1)}, bf16[392,1024]{1,0:T(8,128)(2,1)}, u32[]{:S(2)}, u32[]{:S(2)}) collective-permute-start(bf16[392,1024]{1,0:T(8,128)(2,1)} %get-tuple-element.367), channel_id=1, source_target_pairs={{4,2},{5,3},{2,4},{3,5},{12,10},{13,11},{10,12},{11,13},{20,18},{2... | collective-permute-start | bytes 2408456 | tf_op jit(solution)/shard_map/ppermute | solution.py:775
  353.6 46.3 %collective-permute-start.42 = (bf16[392,1024]{1,0:T(8,128)(2,1)}, bf16[392,1024]{1,0:T(8,128)(2,1)S(1)}, u32[]{:S(2)}, u32[]{:S(2)}) collective-permute-start(bf16[392,1024]{1,0:T(8,128)(2,1)} %get-tuple-element.366), channel_id=1, source_target_pairs={{1,0},{0,1},{5,2},{4,3},{3,4},{2,5},{7,6},{6,7},{9,8},{8,9},{13,10... | collective-permute-start | bytes 2408456 | tf_op jit(solution)/shard_map/ppermute | solution.py:775
  373.0 26.9 %collective-permute-start.41 = (bf16[2,256,512]{2,1,0:T(8,128)(2,1)}, bf16[2,256,512]{2,1,0:T(8,128)(2,1)}, u32[]{:S(2)}, u32[]{:S(2)}) collective-permute-start(bf16[2,256,512]{2,1,0:T(8,128)(2,1)} %fusion.29), channel_id=1, source_target_pairs={{0,8},{8,0},{1,9},{9,1},{2,10},{10,2},{3,11},{11,3},{4,12},{12,4},... | collective-permute-start | bytes 1572872 | tf_op jit(solution)/shard_map/ppermute | solution.py:711
  376.2 23.7 %collective-permute-start.40 = (bf16[2,256,512]{2,1,0:T(8,128)(2,1)}, bf16[2,256,512]{2,1,0:T(8,128)(2,1)}, u32[]{:S(2)}, u32[]{:S(2)}) collective-permute-start(bf16[2,256,512]{2,1,0:T(8,128)(2,1)} %fusion.28), channel_id=1, source_target_pairs={{0,16},{16,0},{1,17},{17,1},{2,18},{18,2},{3,19},{19,3},{4,20},{20... | collective-permute-start | bytes 1572872 | tf_op jit(solution)/shard_map/ppermute | solution.py:711
  378.4 21.6 %collective-permute-start.39 = (bf16[2,256,512]{2,1,0:T(8,128)(2,1)}, bf16[2,256,512]{2,1,0:T(8,128)(2,1)}, u32[]{:S(2)}, u32[]{:S(2)}) collective-permute-start(bf16[2,256,512]{2,1,0:T(8,128)(2,1)} %fusion.27), channel_id=1, source_target_pairs={{0,8},{8,0},{1,9},{9,1},{2,10},{10,2},{3,11},{11,3},{4,12},{12,4},... | collective-permute-start | bytes 1572872 | tf_op jit(solution)/shard_map/ppermute | solution.py:711
  415.5 21.6 %collective-permute-start.44 = (bf16[2,5,256,128]{3,2,1,0:T(8,128)(2,1)}, bf16[2,5,256,128]{3,2,1,0:T(8,128)(2,1)S(1)}, u32[]{:S(2)}, u32[]{:S(2)}) collective-permute-start(bf16[2,5,256,128]{3,2,1,0:T(8,128)(2,1)} %pad_maximum_fusion.12), channel_id=1, source_target_pairs={{0,16},{16,0},{1,17},{17,1},{2,18},{18,2},{3,19},{19,3},{4,20},{20... | collective-permute-start | bytes 1966088 | tf_op jit(solution)/shard_map/ppermute | solution.py:711
  470.6 23.8 %collective-permute-start.51 = (f32[784,1024]{1,0:T(8,128)}, f32[784,1024]{1,0:T(8,128)}, u32[]{:S(2)}, u32[]{:S(2)}) collective-permute-start(f32[784,1024]{1,0:T(8,128)} %project_back.2), channel_id=1, source_target_pairs={{0,4},{4,0},{1,5},{5,1},{2,6},{6,2},{3,7},{7,3},{8,12},{12,8},{9,1... | collective-permute-start | bytes 9633800 | tf_op jit(solution)/shard_map/ppermute | solution.py:711
  483.3 22.8 %collective-permute-start.47 = (bf16[2,3,256,128]{3,2,1,0:T(8,128)(2,1)}, bf16[2,3,256,128]{3,2,1,0:T(8,128)(2,1)}, u32[]{:S(2)}, u32[]{:S(2)}) collective-permute-start(bf16[2,3,256,128]{3,2,1,0:T(8,128)(2,1)} %get-tuple-element.278), channel_id=1, source_target_pairs={{0,8},{8,0},{1,9},{9,1},{2,10},{10,2},{3,11},{11,3},{4,12},{12,4},... | collective-permute-start | bytes 1179656 | tf_op jit(solution)/shard_map/ppermute | solution.py:711
  484.6 21.6 %collective-permute-start.48 = (bf16[2,3,256,128]{3,2,1,0:T(8,128)(2,1)}, bf16[2,3,256,128]{3,2,1,0:T(8,128)(2,1)}, u32[]{:S(2)}, u32[]{:S(2)}) collective-permute-start(bf16[2,3,256,128]{3,2,1,0:T(8,128)(2,1)} %get-tuple-element.279), channel_id=1, source_target_pairs={{0,16},{16,0},{1,17},{17,1},{2,18},{18,2},{3,19},{19,3},{4,20},{20... | collective-permute-start | bytes 1179656 | tf_op jit(solution)/shard_map/ppermute | solution.py:711
  511.1 35.2 %collective-permute-start.55 = (bf16[392,1024]{1,0:T(8,128)(2,1)}, bf16[392,1024]{1,0:T(8,128)(2,1)}, u32[]{:S(2)}, u32[]{:S(2)}) collective-permute-start(bf16[392,1024]{1,0:T(8,128)(2,1)} %get-tuple-element.364), channel_id=1, source_target_pairs={{1,0},{0,1},{5,2},{4,3},{3,4},{2,5},{7,6},{6,7},{9,8},{8,9},{13,10... | collective-permute-start | bytes 2408456 | tf_op jit(solution)/shard_map/ppermute | solution.py:775
  519.0 28.6 %collective-permute-start.59 = (f32[20,512]{1,0:T(8,128)S(1)}, f32[20,512]{1,0:T(8,128)S(1)}, u32[]{:S(2)}, u32[]{:S(2)}) collective-permute-start(f32[20,512]{1,0:T(8,128)S(1)} %constant_dynamic-slice_fusion.5), channel_id=1, source_target_pairs={{0,16},{16,0},{1,17},{17,1},{2,18},{18,2},{3,19},{19,3},{4,20},{20... | collective-permute-start | bytes 122888 | tf_op jit(solution)/shard_map/ppermute | solution.py:711
  520.6 40.8 %collective-permute-start.56 = (bf16[4,256,128]{2,1,0:T(8,128)(2,1)S(1)}, bf16[4,256,128]{2,1,0:T(8,128)(2,1)S(1)}, u32[]{:S(2)}, u32[]{:S(2)}) collective-permute-start(bf16[4,256,128]{2,1,0:T(8,128)(2,1)S(1)} %pad_maximum_fusion.22), channel_id=1, source_target_pairs={{0,1},{1,2},{2,3},{3,0},{4,5},{5,6},{6,7},{7,4},{8,9},{9,10},{10,1... | collective-permute-start | bytes 786440 | tf_op jit(solution)/shard_map/ppermute | solution.py:952
  (97 other events, 968.2 us)
Sparse Core Ops, SparseCore 0:
  103.1 106.8 all-gather.2
  420.6 45.7 reduce-scatter.1

commit v4 on v3

--- a/solution.py
+++ b/solution.py
@@ -407,10 +407,11 @@
 def mix_kernel(oa_ref, ob_ref, w_ref, out_ref):
     places, cols = w_ref.shape[1:3]
     weights = [row_blocks(w_ref, j, 0, cols) for j in range(places)]
-    out_ref[...] = dot(jnp.concatenate([oa_ref[...], ob_ref[...]], 1), jnp.concatenate(weights, 0))
-
-
-def mix(rows, weights, which):
+    mixed = dot(jnp.concatenate([oa_ref[...], ob_ref[...]], 1), jnp.concatenate(weights, 0))
+    out_ref[...] = mixed.astype(out_ref.dtype)
+
+
+def mix(rows, weights, which, dtype):
     seq, wide = rows[0].shape
     owners, places, _, part = weights.shape
     cols = PAIR * wide // places
@@ -424,7 +425,7 @@
             pl.BlockSpec((owners // 2, places, cols, part), lambda n: (n, 0, 1, 0)),
         ],
         pl.BlockSpec((half, owners * part // 2), lambda n: (0, n)),
-        shaped((half, owners * part), F32),
+        shaped((half, owners * part), dtype),
         (*rows, weights),
         name="mix",
     )
@@ -575,7 +576,7 @@
     @pl.when(step >= blocks)
     def _():
         left = jnp.concatenate([hold_s[t] for t in range(blocks)], 1)
-        out_ref[...] = dot(left, all_blocks(last_ref), ROW_NT)
+        out_ref[...] = dot(left, all_blocks(last_ref), ROW_NT).astype(out_ref.dtype)
 
 
 def ffn_specs(rows, down):
@@ -593,7 +594,7 @@
     )
 
 
-def ffn_forward(place, x, up, down, bias):
+def ffn_forward(place, x, up, down, bias, dtype):
     rows, width = x.shape
     owners, blocks, part, units = down.shape
     blocks, early, late, whole, column, thin, out = ffn_specs(rows, down)
@@ -609,7 +610,7 @@
             thin,
         ],
         [out, column, column],
-        [shaped((rows, width), F32), shaped((rows, blocks * units)), shaped((rows, blocks * units))],
+        [shaped((rows, width), dtype), shaped((rows, blocks * units)), shaped((rows, blocks * units))],
         (place, x, *up, down, bias),
         [pltpu.VMEM((blocks, rows, units), BF)],
         name="ffn",
@@ -633,10 +634,10 @@
         left = jnp.concatenate([hold_s[t] for t in range(blocks)], 1)
         order = [relative_block(t, place_ref[0], blocks) for t in range(blocks)]
         weights = [either(one_ref, two_ref, index, lambda ref, i: ref[0, i]) for index in order]
-        out_ref[...] = dot(left, jnp.concatenate(weights, 1), ROW_NT)
-
-
-def ffn_backward(place, d_out, up, down, slope):
+        out_ref[...] = dot(left, jnp.concatenate(weights, 1), ROW_NT).astype(out_ref.dtype)
+
+
+def ffn_backward(place, d_out, up, down, slope, dtype):
     rows, width = d_out.shape
     owners, blocks, part, units = down.shape
     blocks, early, late, whole, column, thin, out = ffn_specs(rows, down)
@@ -651,7 +652,7 @@
             column,
         ],
         [out, column, thin],
-        [shaped((rows, width), F32), shaped((rows, blocks * units)), shaped((blocks, 1, units), F32)],
+        [shaped((rows, width), dtype), shaped((rows, blocks * units)), shaped((blocks, 1, units), F32)],
         (place, d_out, down, *up, slope),
         [pltpu.VMEM((blocks, rows, units), BF)],
         name="ffn_backward",
@@ -707,6 +708,122 @@
     return (keep_a, keep_b), (send_a, send_b)
 
 
+def add_kernel(bits_ref, *refs):
+    count = len(refs) // 3
+    for i in range(count):
+        refs[2 * count + i][0] = (refs[2 * i][0].astype(F32) + refs[2 * i + 1][0].astype(F32)).astype(BF)
+
+
+def add_middle(bits, keeps, parts):
+    args, in_specs = [], []
+    for i, (keep, part) in enumerate(zip(keeps, parts)):
+        args += [keep, part]
+        block = (1,) + keep.shape[1:]
+        in_specs += [pl.BlockSpec(block, lambda s, bits, i=i: (1 - bits[1 - i % 2], 0, 0, 0))] * 2
+    shapes = [(1,) + keep.shape[1:] for keep in keeps]
+    outs = call(
+        add_kernel,
+        (1,),
+        in_specs,
+        [pl.BlockSpec(shape, lambda s, bits: (0, 0, 0, 0)) for shape in shapes],
+        [shaped(shape) for shape in shapes],
+        (bits, *args),
+        name="add_middle",
+        prefetch=1,
+    )
+    return [out[0] for out in outs]
+
+
+def add_end_kernel(bits_ref, *refs):
+    out_ref = refs[-1]
+    for i in range(len(refs) // 3):
+        keep, part, end = refs[3 * i : 3 * i + 3]
+        total = keep[0].astype(F32) + part[0].astype(F32) + end[...].astype(F32)
+        half = total.shape[0]
+        at = i % 2 * half
+        out_ref[at : at + half, i // 2] = total.astype(BF)
+
+
+def add_end(bits, keeps, parts, ends):
+    args, in_specs = [], []
+    for i, (keep, part, end) in enumerate(zip(keeps, parts, ends)):
+        args += [keep, part, end]
+        block = (1,) + keep.shape[1:]
+        in_specs += [pl.BlockSpec(block, lambda s, bits, i=i: (bits[1 - i % 2], 0, 0, 0))] * 2
+        in_specs.append(pl.BlockSpec(end.shape, lambda s, bits: (0, 0, 0)))
+    _, blocks, rows, units = keeps[0].shape
+    shape = (2 * blocks, len(keeps) // 2, rows, units)
+    return call(
+        add_end_kernel,
+        (1,),
+        in_specs,
+        pl.BlockSpec(shape, lambda s, bits: (0, 0, 0, 0)),
+        shaped(shape),
+        (bits, *args),
+        name="add_end",
+        prefetch=1,
+    )
+
+
+def norm_back_block(da_ref, db_ref, x_ref, rest_ref, gain_ref, sum_ref):
+    d_value = da_ref[...] + db_ref[...].astype(F32)
+    value = x_ref[...].astype(F32)
+    centred = value - jnp.mean(value, -1, keepdims=True)
+    scale = lax.rsqrt(jnp.mean(centred * centred, -1, keepdims=True) + EPS)
+    unit = centred * scale
+    d_unit = d_value * gain_ref[...]
+    inner = jnp.mean(d_unit * unit, -1, keepdims=True)
+    rest = rest_ref[...]
+    result = rest + scale * (d_unit - jnp.mean(d_unit, -1, keepdims=True) - unit * inner)
+    parts = [d_value * unit, d_value, result, rest]
+    sums = jnp.concatenate([jnp.sum(part, 0, keepdims=True) for part in parts] + [jnp.zeros((4, value.shape[1]), F32)], 0)
+
+    @pl.when(pl.program_id(0) == 0)
+    def _():
+        sum_ref[...] = sums
+
+    @pl.when(pl.program_id(0) > 0)
+    def _():
+        sum_ref[...] += sums
+
+    return result
+
+
+def norm_back_kernel(da_ref, db_ref, x_ref, rest_ref, gain_ref, out_ref, low_ref, sum_ref):
+    result = norm_back_block(da_ref, db_ref, x_ref, rest_ref, gain_ref, sum_ref)
+    out_ref[...] = result
+    low_ref[...] = result.astype(BF)
+
+
+def norm_back_halves_kernel(da_ref, db_ref, x_ref, rest_ref, gain_ref, near_ref, far_ref, sum_ref):
+    result = norm_back_block(da_ref, db_ref, x_ref, rest_ref, gain_ref, sum_ref).astype(BF)
+
+    @pl.when(pl.program_id(0) == 0)
+    def _():
+        near_ref[...] = result
+
+    @pl.when(pl.program_id(0) == 1)
+    def _():
+        far_ref[...] = result
+
+
+def norm_backward(da, db, x, rest, gain, halves):
+    rows, width = da.shape
+    steps = 2 if halves else 1
+    row = pl.BlockSpec((rows // steps, width), lambda i: (i, 0))
+    whole = lambda count: pl.BlockSpec((count, width), lambda i: (0, 0))
+    return call(
+        norm_back_halves_kernel if halves else norm_back_kernel,
+        (steps,),
+        [row] * 4 + [whole(1)],
+        [whole(rows // 2)] * 2 + [whole(8)] if halves else [row, row, whole(8)],
+        ([shaped((rows // 2, width))] * 2 if halves else [shaped((rows, width), F32), shaped((rows, width))])
+        + [shaped((8, width), F32)],
+        (da, db, x, rest, gain[None]),
+        name="norm_backward",
+    )
+
+
 def swap(value, axis):
     return lax.ppermute(value, axis, [(0, 1), (1, 0)])
 
@@ -736,13 +853,6 @@
     centred = value - mean
     scale = lax.rsqrt(jnp.mean(centred * centred, -1, keepdims=True) + EPS)
     return centred, scale
-
-
-def norm_back(d_value, centred, scale, gain):
-    unit = centred * scale
-    d_unit = d_value * gain
-    grad_in = scale * (d_unit - jnp.mean(d_unit, -1, keepdims=True) - unit * jnp.mean(d_unit * unit, -1, keepdims=True))
-    return grad_in, jnp.sum(d_value * unit, 0), jnp.sum(d_value, 0)
 
 
 def clip_local(clips, w_qkv, w_out, w_up, w_down, norm_gain, shifts, bias_qv, up_bias, teacher):
@@ -770,9 +880,12 @@
     def to_chip(value):
         return sent((chosen(value, odd, 0), chosen(value, 1 - odd, 0)))
 
+    def sent_back(near, far):
+        return lax.ppermute(near, every, back(first_way)), lax.ppermute(far, every, back(second_way))
+
     def from_chip(value):
         half = value.shape[0] // 2
-        return lax.ppermute(value[:half], every, back(first_way)), lax.ppermute(value[half:], every, back(second_way))
+        return sent_back(value[:half], value[half:])
 
     rings = [[(i, (i + away) % steps) for i in range(steps)] for away in range(steps)]
 
@@ -788,8 +901,8 @@
     def on_chip(value, near, far):
         return jnp.concatenate([jnp.where(stays, chosen(value, odd, 0), near), far])
 
-    def as_clips(value, near, far):
-        near = jnp.where(stays, value[: value.shape[0] // 2], near)
+    def as_clips(mine, near, far):
+        near = jnp.where(stays, mine, near)
         return jnp.stack([jnp.where(odd == 0, near, far), jnp.where(odd == 0, far, near)])
 
     def scatter_start(sends):
@@ -856,6 +969,7 @@
     centred_one, scale_one = moments(inputs)
     first = (centred_one * scale_one * gains[0] + shift_all[0]).astype(BF)
     first_other = swap(first, "c")
+    half = first.shape[0] // 2
     qkv, turned = project(first, first_other, w_qk, w_vo, bias_in)
     mixed_a, rows_a, wide_a, lse_a = attend(qkv, 0, 1664)
     up_rows, rows_a = together(up_rows, rows_a)
@@ -866,9 +980,9 @@
     up_a, up_b = ordered(y, up_a[None], swapped[0][None], 0), ordered(x, up_b[None], swapped[1][None], 0)
     swapped = swap(up_a, "x"), swap(up_b, "y")
     rows = (rows_a, rows_b)
-    attn_other = mix(rows, w_vo, 1)
-    attn_mine = mix((after(rows_a, attn_other), rows_b), w_vo, 0)
-    hidden = inputs + (attn_mine + swap(attn_other, "c")) + shift_all[2]
+    attn_other = mix(rows, w_vo, 1, BF)
+    attn_mine = mix((after(rows_a, attn_other), rows_b), w_vo, 0, F32)
+    hidden = inputs + (attn_mine + swap(attn_other, "c").astype(F32)) + shift_all[2]
 
     centred_two, scale_two = moments(hidden)
     second = (centred_two * scale_two * gains[1] + shift_all[1]).astype(BF)
@@ -879,17 +993,17 @@
     up_all = up_a, up_b
     targets, second, down_all = together(targets, second, down_all)
     near, far = sent(targets)
-    out_mine, act_mine, slope_mine = ffn_forward(place, second, up_all, down_all, up_shift)
+    out_mine, act_mine, slope_mine = ffn_forward(place, second, up_all, down_all, up_shift, F32)
     out_mine, near = together(out_mine, near)
-    out_other, act_other, slope_other = ffn_forward(place, after(second_other, near), up_all, down_all, up_shift)
+    out_other, act_other, slope_other = ffn_forward(place, after(second_other, near), up_all, down_all, up_shift, BF)
     out_other, far = together(out_other, far)
-    output = hidden + (out_mine + swap(out_other, "c")) + shift_all[3]
+    output = hidden + (out_mine + swap(out_other, "c").astype(F32)) + shift_all[3]
     d_out = output - on_chip(teacher, near, far).astype(F32)
     d_ffn = d_out.astype(BF)
     d_ffn_other = swap(d_ffn, "c")
-    d_second, d_pre, sum_mine = ffn_backward(place, d_ffn, up_all, down_all, slope_mine)
+    d_second, d_pre, sum_mine = ffn_backward(place, d_ffn, up_all, down_all, slope_mine, F32)
     d_ffn_other, d_pre = together(d_ffn_other, d_pre)
-    d_second_other, d_pre_other, sum_other = ffn_backward(place, d_ffn_other, up_all, down_all, slope_other)
+    d_second_other, d_pre_other, sum_other = ffn_backward(place, d_ffn_other, up_all, down_all, slope_other, BF)
     d_second_swapped = swap(d_second_other, "c")
     up_sum = (sum_mine + sum_other).reshape(steps, units)
 
@@ -899,26 +1013,21 @@
     result, grad_down = together(output.astype(BF), grad_down)
     out_near, out_far = from_chip(result)
     d_second_swapped, grad_down = together(d_second_swapped, grad_down)
-    d_second = d_second + d_second_swapped
-    d_norm, grad_gain_two, grad_shift_two = norm_back(d_second, centred_two, scale_two, gains[1])
-    d_hidden = d_out + d_norm
-    d_attn = d_hidden.astype(BF)
+    d_hidden, d_attn, sums_two = norm_backward(d_second, d_second_swapped, hidden, d_out, gains[1], False)
     d_attn_other = swap(d_attn, "c")
     grad_up, sends = ffn_grad(bits, after(second, d_attn), second_other, d_pre, d_pre_other, steps)
     up = scatter_start(sends)
     d_attn_other, grad_up = together(d_attn_other, grad_up)
 
     d_heads, delta, grad_o, sends_o = mix_back(bits, d_attn, d_attn_other, w_vo, (mixed_a, mixed_b), (wide_a, wide_b))
-    down, delta = together(down, delta)
-    grad_down, grad_up = [[keep] for keep in grad_down], [[keep] for keep in grad_up]
-    down_ends = scatter_middle(grad_down, down)
+    keeps = (*grad_up, *grad_down)
     back_a, sum_a = attend_backward(qkv, d_heads, lse_b, delta, 1, 0, 2, 256)
-    up, out_near, back_a = together(up, out_near, back_a)
-    up_ends = scatter_middle(grad_up, up)
+    up, down, out_near, back_a = together(up, down, out_near, back_a)
+    ends = add_middle(bits, keeps, (*up, *down))
+    ends = [swap(part, name) for part, name in zip(ends, ("y", "x", "y", "x"))]
     back_b, sum_b = attend_backward(qkv, after(d_heads, back_a), lse_b, delta, 1, 2, 2, 256)
-    up_ends, down_ends, out_far, back_b = together(up_ends, down_ends, out_far, back_b)
-    ups, downs = scatter_end(grad_up, up, up_ends), scatter_end(grad_down, down, down_ends)
-    grad_ff = jnp.concatenate([jnp.stack(pair, 1) for pair in zip(ups, downs)]).reshape(steps * 4 * dims, units)
+    ends, out_far, back_b = together(ends, out_far, back_b)
+    grad_ff = add_end(bits, keeps, (*up, *down), ends).reshape(steps * 4 * dims, units)
     ff_total = lax.psum_scatter(grad_ff, "t", scatter_dimension=0, tiled=True)
     grad_one, sends = project_grads(bits, turned, back_a, back_b)
     one = scatter_start([jnp.concatenate(pair, 1) for pair in zip(sends, sends_o)])
@@ -939,15 +1048,15 @@
     two, d_first_other = together(two, d_first_other)
     two_ends = scatter_middle([[keep] for keep in grad_two], two)
     d_first = project_back(pieces, w_qk, after(w_vo, d_first_other), 0)
-    ff_total, early, d_first = together(ff_total, early, d_first)
+    ff_total, d_first = together(ff_total, d_first)
     d_first_swapped, d_first = together(d_first_swapped, d_first)
-    d_first = d_first + d_first_swapped
-    d_norm, grad_gain_one, grad_shift_one = norm_back(d_first, centred_one, scale_one, gains[0])
-    d_inputs = (d_hidden + d_norm).astype(BF)
-    grad_near, grad_far = from_chip(d_inputs)
-    small = (sum_a, sum_b, sum_c, sum_d, up_sum, grad_gain_one, grad_shift_one)
-    two_ends, small, grad_near, out_near, out_far = together(two_ends, small, grad_near, out_near, out_far)
-    sum_a, sum_b, sum_c, sum_d, up_sum, grad_gain_one, grad_shift_one = small
+    *d_inputs, sums_one = norm_backward(d_first, d_first_swapped, inputs, d_hidden, gains[0], True)
+    early, sums_one = together(early, sums_one)
+    grad_near, grad_far = sent_back(*d_inputs)
+    small = (sum_a, sum_b, sum_c, sum_d, up_sum, sums_one)
+    small, d_inputs = together(small, d_inputs)
+    two_ends, grad_near, out_near, out_far = together(two_ends, grad_near, out_near, out_far)
+    sum_a, sum_b, sum_c, sum_d, up_sum, sums_one = small
     two = scatter_end([[keep] for keep in grad_two], two, two_ends)
     late = lax.ppermute(jnp.concatenate([two[1], one[1][3:4]]), "t", rings[1])
 
@@ -962,19 +1071,20 @@
     heads_sum = jnp.pad(heads_sum, ((0, 0), (0, 0), (0, 0), (0, dims - lane))).reshape(2 * steps, 4 * dims)
     own = jnp.concatenate([heads_sum, up_sum])
     own = jnp.concatenate([jnp.where(c == 0, own, 0.0), jnp.where(c == 1, own, 0.0)], 1)
-    normed = jnp.stack([grad_gain_one, grad_gain_two, grad_shift_one, grad_shift_two, jnp.sum(d_hidden, 0), jnp.sum(d_out, 0)])
-    sums = jnp.concatenate([normed, jnp.zeros((2, width), F32), own])
+    normed = [sums_one[0:1], sums_two[0:1], sums_one[1:2], sums_two[1:4]]
+    sums = jnp.concatenate(normed + [jnp.zeros((2, width), F32), own])
     for bit, name in ((y, "y"), (x, "x"), (c, "c")):
         half = sums.shape[1] // 2
         part = lambda which: lax.dynamic_slice_in_dim(sums, which * half, half, 1)
         sums = part(bit) + swap(part(1 - bit), name)
+    sums, grad_near = together(sums, grad_near)
     sums = sum((lax.ppermute(sums, "t", rings[away]) for away in range(1, steps)), sums)
     thin = width // 32
     vector_sums = lax.dynamic_slice_in_dim(sums[:6], thin * t, thin, 1)
     place_sums = lax.dynamic_index_in_dim(sums[8:].reshape(3, steps, dims), t, 1, keepdims=False)
     return (
-        as_clips(result, out_near, out_far),
-        as_clips(d_inputs, grad_near, grad_far),
+        as_clips(result[: result.shape[0] // 2], out_near, out_far),
+        as_clips(d_inputs[0], grad_near, grad_far),
         grad_attn[:3],
         grad_attn[3].T,
         grad_ff[0],

time: 581 us -> 558 us (0.960)
  waiting for transfers between devices: 130 us -> 77.3 us
  starting transfers between devices: 72.2 us -> 105 us
  other arithmetic: 82 us -> 52.5 us
  Pallas kernels: 244 us -> 270 us
    pallas_call x20 -> x24, Pallas kernels: 244 us -> 270 us  [call(): pl.pallas_call(body, grid_spec=pltpu.PrefetchScalarGridSpec(num_scalar_pr...]
    ppermute x4, waiting for transfers between devices: 24.3 us -> 0.01 us  [the longest x2 0.01 us: sent_back(): lax.ppermute(far, every, back(second_way))]
    ppermute x42, starting transfers between devices: 41.6 us -> 58.5 us  [swap(): return lax.ppermute(value, axis, [(0, 1), (1, 0)])]
    ppermute x2, waiting for transfers between devices: 19.4 us -> 3.81 us  [sent(): lax.ppermute(pair[1], every, second_way)]
    reduce_sum x4 -> x0, other arithmetic: 14.4 us -> none  [the longest x1 4.54 us: norm_back(): return (grad_in, jnp.sum(d_value * unit, 0), jnp.sum(d_value, 0))]
    ppermute x3, starting transfers between devices: 6.86 us -> 18.7 us  [clip_local(): lax.ppermute(sums, 't', rings[away])]
    convert_element_type x8 -> x4, other arithmetic: 11.4 us -> 2.57 us  [scatter_middle(): return (swap(first.astype(BF), 'y'), swap(second.astype(BF), 'x'))]
    ppermute x2, waiting for transfers between devices: 8.98 us -> 0.46 us  [clip_local(): lax.ppermute(jnp.concatenate([one[p][:3], one[p][4:]]), 't', rings[PAIR +...]
  transfers between devices with their start and end apart: 67 -> 67, of which waited for: 22 -> 20; matrix products, arithmetic and copies ran while one was open for 14% -> 10% of each run, Pallas kernels for 39% -> 44%
where the time goes in v4:
time: 558 us; the launch traced here: 550 us
  Pallas kernels  270 us (48%)
  starting transfers between devices  105 us (19%)
  waiting for transfers between devices  77.3 us (14%)
  other arithmetic  52.5 us (9%)
  local copies, waits for them, and re-layouts  29.3 us (5%)
  between operations  15.7 us (3%)
    pallas_call x24, Pallas kernels, call(): pl.pallas_call(body, grid_spec=pltpu.PrefetchScalarGridSpec(num_scalar_pr...  270 us
    ppermute x42, starting transfers between devices, swap(): return lax.ppermute(value, axis, [(0, 1), (1, 0)])  58.5 us
    ppermute x42, waiting for transfers between devices, swap(): return lax.ppermute(value, axis, [(0, 1), (1, 0)])  46.8 us
    ppermute x9, waiting for transfers between devices, ring_gather(): lax.ppermute(value, 't', rings[-j % steps])  21.6 us
    ppermute x3, starting transfers between devices, clip_local(): lax.ppermute(sums, 't', rings[away])  18.7 us
    ppermute x9, starting transfers between devices, ring_gather(): lax.ppermute(value, 't', rings[-j % steps])  13.5 us
  transfers between devices with their start and end apart: 67, of which 20 were waited for; matrix products, arithmetic and copies ran while one was open for 10% of the time, Pallas kernels for 44%

profile of v4, /device:TPU:0, one launch (start us, length us, event | category | flops | bytes accessed | tf_op | source)
XLA Modules:
  0.0 549.9 jit_solution(13645158787541972071)
XLA Ops:
  33.3 6.1 %collective-permute-done.1 = bf16[512,256]{1,0:T(8,128)(2,1)S(1)} collective-permute-done((bf16[512,256]{1,0:T(8,128)(2,1)S(1)}, bf16[512,256]{1,0:T(8,128)(2,1)S(1)}, u32[]{:S(2)}, u32[]{:S(2)}) %collective-permute-start.1) | collective-permute-done | bytes 262176 | tf_op jit(solution)/shard_map/ppermute | solution.py:893
  39.4 13.0 %collective-permute-done.2 = bf16[512,256]{1,0:T(8,128)(2,1)S(1)} collective-permute-done((bf16[512,256]{1,0:T(8,128)(2,1)S(1)}, bf16[512,256]{1,0:T(8,128)(2,1)S(1)}, u32[]{:S(2)}, u32[]{:S(2)}) %collective-permute-start.2) | collective-permute-done | bytes 262176 | tf_op jit(solution)/shard_map/ppermute | solution.py:893
  59.4 7.7 %collective-permute-done.5 = bf16[4,256,256]{2,1,0:T(8,128)(2,1)} collective-permute-done((bf16[4,256,256]{2,1,0:T(8,128)(2,1)}, bf16[4,256,256]{2,1,0:T(8,128)(2,1)}, u32[]{:S(2)}, u32[]{:S(2)}) %collective-permute-start.5) | collective-permute-done | bytes 524320 | tf_op jit(solution)/shard_map/ppermute | solution.py:828
  86.6 4.6 collective-permute-start.13
  100.4 5.1 collective-permute-start.20
  116.6 11.7 %project.1 = (bf16[2,3,4,64,1568]{4,3,2,1,0:T(8,128)(2,1)}, bf16[1024,1568]{1,0:T(8,128)(2,1)}) custom-call(bf16[784,1024]{1,0:T(8,128)(2,1)} %copy-done.11, bf16[784,1024]{1,0:T(8,128)(2,1)} %collective-permute-done.20.xb_ref, bf16[4,4,2,128,256]{4,3,2,1,0:T(8,128)(2,1)} %bitcast.234, bf16[4,4,256,256]{3,2,1,0:T(8,128)(2,1)} %bitcast.216, ...), custom_call_target="tpu_custom_call" | custom-call | flops 1000 | bytes 1000 | tf_op jit(solution)/shard_map/project/pallas_call | solution.py:194
  128.4 16.3 %attend.2 = (bf16[4,64,1568]{2,1,0:T(8,128)(2,1)}, bf16[1568,256]{1,0:T(8,128)(2,1)}, f32[4,64,1568]{2,1,0:T(8,128)}, f32[4,1,1568]{2,1,0:T(1,128)}) custom-call(bf16[2,3,4,64,1568]{4,3,2,1,0:T(8,128)(2,1)} %get-tuple-element.192.q_ref.k_ref.v_ref, bf16[2,3,4,64,1568]{4,3,2,1,0:T(8,128)(2,1)} %get-tuple-element.192.q_ref.k_ref.v_ref, ...), custom_call_target="tpu_custom_call" | custom-call | flops 1000 | bytes 1000 | tf_op jit(solution)/shard_map/attend/pallas_call | solution.py:194
  147.1 16.3 %attend.3 = (bf16[4,64,1568]{2,1,0:T(8,128)(2,1)}, bf16[1568,256]{1,0:T(8,128)(2,1)}, f32[4,64,1568]{2,1,0:T(8,128)}, f32[4,1,1568]{2,1,0:T(1,128)}) custom-call(bf16[2,3,4,64,1568]{4,3,2,1,0:T(8,128)(2,1)} %get-tuple-element.192.q_ref.k_ref.v_ref, bf16[2,3,4,64,1568]{4,3,2,1,0:T(8,128)(2,1)} %get-tuple-element.192.q_ref.k_ref.v_ref, ...), custom_call_target="tpu_custom_call" | custom-call | flops 1000 | bytes 1000 | tf_op jit(solution)/shard_map/attend/pallas_call | solution.py:194
  179.7 23.5 %collective-permute-done.25 = bf16[2,2,256,512]{3,2,1,0:T(8,128)(2,1)} collective-permute-done((bf16[2,2,256,512]{3,2,1,0:T(8,128)(2,1)S(1)}, bf16[2,2,256,512]{3,2,1,0:T(8,128)(2,1)}, u32[]{:S(2)}, u32[]{:S(2)}) %collective-permute-start.25) | collective-permute-done | bytes 1048608 | tf_op jit(solution)/shard_map/ppermute | solution.py:828
  211.7 15.4 %ffn.2 = (f32[784,1024]{1,0:T(8,128)}, bf16[784,2048]{1,0:T(8,128)(2,1)}, bf16[784,2048]{1,0:T(8,128)(2,1)}) custom-call(s32[1]{0:T(128)} %bitcast.51.place_ref, bf16[784,1024]{1,0:T(8,128)(2,1)} %add_convert_fusion.x_ref.xa_ref, bf16[4,2,256,512]{3,2,1,0:T(8,128)(2,1)} %bitcast.230, bf16[4,2,256,512]{3,2,1,0:T(8,128)(2,1)} %bitcast.226, ...), custom_call_target="tpu_custom_call" | custom-call | flops 1000 | bytes 1000 | tf_op jit(solution)/shard_map/ffn/pallas_call | solution.py:194
  227.2 15.1 %ffn.3 = (bf16[784,1024]{1,0:T(8,128)(2,1)}, bf16[784,2048]{1,0:T(8,128)(2,1)}, bf16[784,2048]{1,0:T(8,128)(2,1)}) custom-call(s32[1]{0:T(128)} %bitcast.51.place_ref, bf16[784,1024]{1,0:T(8,128)(2,1)} %collective-permute-done.27.x_ref.xb_ref, bf16[4,2,256,512]{3,2,1,0:T(8,128)(2,1)} %bitcast.231, bf16[4,2,256,512]{3,2,1,0:T(8,128)(2,1)} %bitcast.227, ...), custom_call_target="tpu_custom_call" | custom-call | flops 1000 | bytes 1000 | tf_op jit(solution)/shard_map/ffn/pallas_call | solution.py:194
  242.3 8.1 %collective-permute-start.29 = (bf16[784,1024]{1,0:T(8,128)(2,1)}, bf16[784,1024]{1,0:T(8,128)(2,1)S(1)}, u32[]{:S(2)}, u32[]{:S(2)}) collective-permute-start(bf16[784,1024]{1,0:T(8,128)(2,1)} %get-tuple-element.214), channel_id=1, source_target_pairs={{0,4},{4,0},{1,5},{5,1},{2,6},{6,2},{3,7},{7,3},{8,12},{12,8},{9,1... | collective-permute-start | bytes 4816904 | tf_op jit(solution)/shard_map/ppermute | solution.py:828
  253.7 5.1 fusion.44
  260.0 13.7 %ffn_backward.2 = (f32[784,1024]{1,0:T(8,128)}, bf16[784,2048]{1,0:T(8,128)(2,1)}, f32[4,1,512]{2,1,0:T(1,128)}) custom-call(s32[1]{0:T(128)} %bitcast.51.place_ref, bf16[784,1024]{1,0:T(8,128)(2,1)} %copy-done.7, bf16[4,4,256,512]{3,2,1,0:T(8,128)(2,1)} %bitcast.224, bf16[4,2,256,512]{3,2,1,0:T(8,128)(2,1)} %bitcast.232, ...), custom_call_target="tpu_custom_call" | custom-call | flops 1000 | bytes 1000 | tf_op jit(solution)/shard_map/ffn_backward/pallas_call | solution.py:194
  274.9 13.3 %ffn_backward.3 = (bf16[784,1024]{1,0:T(8,128)(2,1)}, bf16[784,2048]{1,0:T(8,128)(2,1)}, f32[4,1,512]{2,1,0:T(1,128)}) custom-call(s32[1]{0:T(128)} %bitcast.51.place_ref, bf16[784,1024]{1,0:T(8,128)(2,1)} %copy-done.10, bf16[4,4,256,512]{3,2,1,0:T(8,128)(2,1)} %bitcast.225, bf16[4,2,256,512]{3,2,1,0:T(8,128)(2,1)} %bitcast.233, ...), custom_call_target="tpu_custom_call" | custom-call | flops 1000 | bytes 1000 | tf_op jit(solution)/shard_map/ffn_backward/pallas_call | solution.py:194
  289.2 14.4 %ffn_grad.2 = (bf16[2,2,256,512]{3,2,1,0:T(8,128)(2,1)}, bf16[2,2,256,512]{3,2,1,0:T(8,128)(2,1)}, bf16[2,2,256,512]{3,2,1,0:T(8,128)(2,1)}, bf16[2,2,256,512]{3,2,1,0:T(8,128)(2,1)}) custom-call(s32[2]{0:T(128)} %pad_add_fusion.bits_ref, bf16[784,1024]{1,0:T(8,128)(2,1)} %copy-done.7, bf16[784,1024]{1,0:T(8,128)(2,1)} %copy-done.10, ...), custom_call_target="tpu_custom_call" | custom-call | flops 1000 | bytes 1000 | tf_op jit(solution)/shard_map/ffn_grad/pallas_call | solution.py:194
  304.7 9.2 %norm_backward.2 = (f32[784,1024]{1,0:T(8,128)}, bf16[784,1024]{1,0:T(8,128)(2,1)}, f32[8,1024]{1,0:T(8,128)}) custom-call(f32[784,1024]{1,0:T(8,128)} %get-tuple-element.228.da_ref, bf16[784,1024]{1,0:T(8,128)(2,1)} %copy-done.29, f32[784,1024]{1,0:T(8,128)} %copy-done, f32[784,1024]{1,0:T(8,128)} %get-tuple-element.359.rest_ref, f32[1,1024]{1,0:T(1,128)} %copy-done.54), custom_call_target="tpu_custom_call" | custom-call | flops 1000 | bytes 1000 | tf_op jit(solution)/shard_map/norm_backward/pallas_call | solution.py:194
  317.0 14.2 %ffn_grad.3 = (bf16[2,2,256,512]{3,2,1,0:T(8,128)(2,1)}, bf16[2,2,256,512]{3,2,1,0:T(8,128)(2,1)}, bf16[2,2,256,512]{3,2,1,0:T(8,128)(2,1)}, bf16[2,2,256,512]{3,2,1,0:T(8,128)(2,1)}) custom-call(s32[2]{0:T(128)} %pad_add_fusion.bits_ref, bf16[784,1024]{1,0:T(8,128)(2,1)} %add_convert_fusion.x_ref.xa_ref, ...), custom_call_target="tpu_custom_call" | custom-call | flops 1000 | bytes 1000 | tf_op jit(solution)/shard_map/ffn_grad/pallas_call | solution.py:194
  334.9 10.9 %mix_back.1 = (bf16[8,64,1568]{2,1,0:T(8,128)(2,1)}, f32[8,1,1568]{2,1,0:T(1,128)}, bf16[2,2,256,128]{3,2,1,0:T(8,128)(2,1)}, bf16[2,2,256,128]{3,2,1,0:T(8,128)...) custom-call(s32[2]{0:T(128)} %pad_add_fusion.bits_ref, ...), custom_call_target="tpu_custom_call" | custom-call | flops 1000 | bytes 1000 | tf_op jit(solution)/shard_map/mix_back/pallas_call | solution.py:194
  345.8 16.7 %attend_backward.4 = (bf16[3,1568,128]{2,1,0:T(8,128)(2,1)}, f32[3,1,128]{2,1,0:T(1,128)}) custom-call(bf16[2,3,4,64,1568]{4,3,2,1,0:T(8,128)(2,1)} %get-tuple-element.192.q_ref.k_ref.v_ref, bf16[2,3,4,64,1568]{4,3,2,1,0:T(8,128)(2,1)} %get-tuple-element.192.q_ref.k_ref.v_ref, bf16[2,3,4,64,1568]{4,3,2,1,0:T(8,128)(2,1)} %get-tuple-element.192.q_ref.k_ref.v_ref, ...), custom_call_target="tpu_custom_call" | custom-call | flops 1000 | bytes 1000 | tf_op jit(solution)/shard_map/attend_backward/pallas_call | solution.py:194
  365.7 4.3 add_middle.1
  374.0 16.3 %attend_backward.5 = (bf16[3,1568,128]{2,1,0:T(8,128)(2,1)}, f32[3,1,128]{2,1,0:T(1,128)}) custom-call(bf16[2,3,4,64,1568]{4,3,2,1,0:T(8,128)(2,1)} %get-tuple-element.192.q_ref.k_ref.v_ref, bf16[2,3,4,64,1568]{4,3,2,1,0:T(8,128)(2,1)} %get-tuple-element.192.q_ref.k_ref.v_ref, bf16[2,3,4,64,1568]{4,3,2,1,0:T(8,128)(2,1)} %get-tuple-element.192.q_ref.k_ref.v_ref, ...), custom_call_target="tpu_custom_call" | custom-call | flops 1000 | bytes 1000 | tf_op jit(solution)/shard_map/attend_backward/pallas_call | solution.py:194
  392.8 7.4 %project_grads.2 = (bf16[2,3,256,128]{3,2,1,0:T(8,128)(2,1)}, bf16[2,3,256,128]{3,2,1,0:T(8,128)(2,1)}, bf16[2,3,256,128]{3,2,1,0:T(8,128)(2,1)}, bf16[2,3,256,128]{3,2,1,0:T(8,128)(2,1)}) custom-call(s32[2]{0:T(128)} %pad_add_fusion.bits_ref, bf16[1024,1568]{1,0:T(8,128)(2,1)} %get-tuple-element.227.t_ref, ...), custom_call_target="tpu_custom_call" | custom-call | flops 1000 | bytes 1000 | tf_op jit(solution)/shard_map/project_grads/pallas_call | solution.py:194
  404.5 5.6 %add_end.1 = bf16[4,2,256,512]{3,2,1,0:T(8,128)(2,1)} custom-call(s32[2]{0:T(128)} %pad_add_fusion.bits_ref, bf16[2,2,256,512]{3,2,1,0:T(8,128)(2,1)} %get-tuple-element.244.refs_0_, bf16[2,2,256,512]{3,2,1,0:T(8,128)(2,1)} %copy-done.24, bf16[2,256,512]{2,1,0:T(8,128)(2,1)} %copy-done.40, bf16[2,2,256,512]{3,2,1,0:T(8,128)(2,1)} %get-tuple-element.253.refs_2_.refs_3_, ...), custom_call_target="tpu_custom_call" | custom-call | flops 1000 | bytes 1000 | tf_op jit(solution)/shard_map/add_end/pallas_call | solution.py:194
  410.3 16.5 %attend_backward.6 = (bf16[3,1568,128]{2,1,0:T(8,128)(2,1)}, f32[3,1,128]{2,1,0:T(1,128)}) custom-call(bf16[2,3,4,64,1568]{4,3,2,1,0:T(8,128)(2,1)} %get-tuple-element.192.q_ref.k_ref.v_ref, bf16[2,3,4,64,1568]{4,3,2,1,0:T(8,128)(2,1)} %get-tuple-element.192.q_ref.k_ref.v_ref, bf16[2,3,4,64,1568]{4,3,2,1,0:T(8,128)(2,1)} %get-tuple-element.192.q_ref.k_ref.v_ref, ...), custom_call_target="tpu_custom_call" | custom-call | flops 1000 | bytes 1000 | tf_op jit(solution)/shard_map/attend_backward/pallas_call | solution.py:194
  429.5 16.4 %attend_backward.7 = (bf16[3,1568,128]{2,1,0:T(8,128)(2,1)}, f32[3,1,128]{2,1,0:T(1,128)}) custom-call(bf16[2,3,4,64,1568]{4,3,2,1,0:T(8,128)(2,1)} %get-tuple-element.192.q_ref.k_ref.v_ref, bf16[2,3,4,64,1568]{4,3,2,1,0:T(8,128)(2,1)} %get-tuple-element.192.q_ref.k_ref.v_ref, bf16[2,3,4,64,1568]{4,3,2,1,0:T(8,128)(2,1)} %get-tuple-element.192.q_ref.k_ref.v_ref, ...), custom_call_target="tpu_custom_call" | custom-call | flops 1000 | bytes 1000 | tf_op jit(solution)/shard_map/attend_backward/pallas_call | solution.py:194
  445.9 7.3 %project_grads.3 = (bf16[2,3,256,128]{3,2,1,0:T(8,128)(2,1)}, bf16[2,3,256,128]{3,2,1,0:T(8,128)(2,1)}, bf16[2,3,256,128]{3,2,1,0:T(8,128)(2,1)}, bf16[2,3,256,128]{3,2,1,0:T(8,128)(2,1)}) custom-call(s32[2]{0:T(128)} %pad_add_fusion.bits_ref, bf16[1024,1568]{1,0:T(8,128)(2,1)} %get-tuple-element.227.t_ref, ...), custom_call_target="tpu_custom_call" | custom-call | flops 1000 | bytes 1000 | tf_op jit(solution)/shard_map/project_grads/pallas_call | solution.py:194
  453.2 6.8 %project_back.2 = f32[784,1024]{1,0:T(8,128)} custom-call(bf16[3,1568,128]{2,1,0:T(8,128)(2,1)} %get-tuple-element.292.da_ref.a_ref, bf16[3,1568,128]{2,1,0:T(8,128)(2,1)} %get-tuple-element.289.db_ref.b_ref, bf16[3,1568,128]{2,1,0:T(8,128)(2,1)} %get-tuple-element.263.da_ref.c_ref, bf16[3,1568,128]{2,1,0:T(8,128)(2,1)} %get-tuple-element.270.db_ref.d_ref, ...), custom_call_target="tpu_custom_call" | custom-call | flops 1000 | bytes 1000 | tf_op jit(solution)/shard_map/project_back/pallas_call | solution.py:194
  469.9 6.8 %project_back.3.da_ref = f32[784,1024]{1,0:T(8,128)} custom-call(bf16[3,1568,128]{2,1,0:T(8,128)(2,1)} %get-tuple-element.292.da_ref.a_ref, bf16[3,1568,128]{2,1,0:T(8,128)(2,1)} %get-tuple-element.289.db_ref.b_ref, bf16[3,1568,128]{2,1,0:T(8,128)(2,1)} %get-tuple-element.263.da_ref.c_ref, bf16[3,1568,128]{2,1,0:T(8,128)(2,1)} %get-tuple-element.270.db_ref.d_ref, ...), custom_call_target="tpu_custom_call" | custom-call | flops 1000 | bytes 1000 | tf_op jit(solution)/shard_map/project_back/pallas_call | solution.py:194
  477.5 7.3 %norm_backward.3 = (bf16[392,1024]{1,0:T(8,128)(2,1)}, bf16[392,1024]{1,0:T(8,128)(2,1)}, f32[8,1024]{1,0:T(8,128)}) custom-call(f32[784,1024]{1,0:T(8,128)} %project_back.3.da_ref, f32[784,1024]{1,0:T(8,128)} %collective-permute-done.51.db_ref, f32[784,1024]{1,0:T(8,128)} %fusion.43.x_ref, f32[784,1024]{1,0:T(8,128)} %get-tuple-element.303.rest_ref, ...), custom_call_target="tpu_custom_call" | custom-call | flops 1000 | bytes 1000 | tf_op jit(solution)/shard_map/norm_backward/pallas_call | solution.py:194
  507.4 17.0 %collective-permute-start.63 = (f32[20,128]{1,0:T(8,128)S(1)}, f32[20,128]{1,0:T(8,128)S(1)}, u32[]{:S(2)}, u32[]{:S(2)}) collective-permute-start(f32[20,128]{1,0:T(8,128)S(1)} %fusion.35), channel_id=1, source_target_pairs={{0,2},{1,3},{2,0},{3,1},{4,6},{5,7},{6,4},{7,5},{8,10},{9,11},{10,... | collective-permute-start | bytes 30728 | tf_op jit(solution)/shard_map/ppermute | solution.py:1081
  532.7 4.5 collective-permute-done.63
  (413 shorter events, 177.3 us)
Async XLA Ops:
  7.2 196.1 %all-gather.3.cloned.1.call-start = ((), (), s32[]{:S(2)}) async-start(), calls=%async_computation.2 | async-start | bytes 4456448 | tf_op jit(solution)/shard_map/all_gather | solution.py:965
  32.6 19.8 %collective-permute-start.2 = (bf16[512,256]{1,0:T(8,128)(2,1)S(1)}, bf16[512,256]{1,0:T(8,128)(2,1)S(1)}, u32[]{:S(2)}, u32[]{:S(2)}) collective-permute-start(bf16[512,256]{1,0:T(8,128)(2,1)S(1)} %pad_maximum_fusion.18), channel_id=1, source_target_pairs={{0,2},{1,3},{2,0},{3,1},{4,6},{5,7},{6,4},{7,5},{8,10},{9,11},{10,... | collective-permute-start | bytes 786440 | tf_op jit(solution)/shard_map/ppermute | solution.py:893
  32.6 19.8 %collective-permute-start.3 = (bf16[512,256]{1,0:T(8,128)(2,1)S(1)}, bf16[512,256]{1,0:T(8,128)(2,1)S(1)}, u32[]{:S(2)}, u32[]{:S(2)}) collective-permute-start(bf16[512,256]{1,0:T(8,128)(2,1)S(1)} %pad_maximum_fusion.18), channel_id=1, source_target_pairs={{0,1},{1,2},{2,3},{3,0},{4,5},{5,6},{6,7},{7,4},{8,9},{9,10},{10,1... | collective-permute-start | bytes 786440 | tf_op jit(solution)/shard_map/ppermute | solution.py:893
  72.9 25.6 %collective-permute-start.15 = (bf16[2,4,256,256]{3,2,1,0:T(8,128)(2,1)}, bf16[2,4,256,256]{3,2,1,0:T(8,128)(2,1)}, u32[]{:S(2)}, u32[]{:S(2)}) collective-permute-start(bf16[2,4,256,256]{3,2,1,0:T(8,128)(2,1)} %pad_maximum_fusion.8), channel_id=1, source_target_pairs={{0,16},{16,0},{1,17},{17,1},{2,18},{18,2},{3,19},{19,3},{4,20},{20... | collective-permute-start | bytes 3145736 | tf_op jit(solution)/shard_map/ppermute | solution.py:828
  76.3 22.2 %collective-permute-start.14 = (bf16[2,4,256,256]{3,2,1,0:T(8,128)(2,1)}, bf16[2,4,256,256]{3,2,1,0:T(8,128)(2,1)}, u32[]{:S(2)}, u32[]{:S(2)}) collective-permute-start(bf16[2,4,256,256]{3,2,1,0:T(8,128)(2,1)} %pad_maximum_fusion.7), channel_id=1, source_target_pairs={{0,8},{8,0},{1,9},{9,1},{2,10},{10,2},{3,11},{11,3},{4,12},{12,4},... | collective-permute-start | bytes 3145736 | tf_op jit(solution)/shard_map/ppermute | solution.py:828
  76.8 21.7 %collective-permute-start.16 = (bf16[392,1024]{1,0:T(8,128)(2,1)}, bf16[392,1024]{1,0:T(8,128)(2,1)S(1)}, u32[]{:S(2)}, u32[]{:S(2)}) collective-permute-start(bf16[392,1024]{1,0:T(8,128)(2,1)} %get-tuple-element.377), channel_id=1, source_target_pairs={{0,1},{1,0},{2,5},{3,4},{4,3},{5,2},{6,7},{7,6},{8,9},{9,8},{10,13... | collective-permute-start | bytes 2408456 | tf_op jit(solution)/shard_map/ppermute | solution.py:878
  98.5 378.1 %reduce-scatter.2.cloned.1.call-start = ((), (), s32[]{:S(2)}) async-start(), calls=%async_computation.1 | async-start | bytes 2621440 | tf_op jit(solution)/shard_map/reduce_scatter | solution.py:1031
  106.7 38.0 %collective-permute-start.17 = (bf16[256,512]{1,0:T(8,128)(2,1)}, bf16[256,512]{1,0:T(8,128)(2,1)S(1)}, u32[]{:S(2)}, u32[]{:S(2)}) collective-permute-start(bf16[256,512]{1,0:T(8,128)(2,1)} %get-tuple-element.182), channel_id=1, source_target_pairs={{0,3},{1,0},{2,1},{3,2},{4,7},{5,4},{6,5},{7,6},{8,11},{9,8},{10,9... | collective-permute-start | bytes 786440 | tf_op jit(solution)/shard_map/ppermute | solution.py:893
  106.9 37.9 %collective-permute-start.18 = (bf16[256,512]{1,0:T(8,128)(2,1)}, bf16[256,512]{1,0:T(8,128)(2,1)S(1)}, u32[]{:S(2)}, u32[]{:S(2)}) collective-permute-start(bf16[256,512]{1,0:T(8,128)(2,1)} %get-tuple-element.182), channel_id=1, source_target_pairs={{0,2},{1,3},{2,0},{3,1},{4,6},{5,7},{6,4},{7,5},{8,10},{9,11},{10,... | collective-permute-start | bytes 786440 | tf_op jit(solution)/shard_map/ppermute | solution.py:893
  110.5 34.2 %collective-permute-start.19 = (bf16[256,512]{1,0:T(8,128)(2,1)}, bf16[256,512]{1,0:T(8,128)(2,1)S(1)}, u32[]{:S(2)}, u32[]{:S(2)}) collective-permute-start(bf16[256,512]{1,0:T(8,128)(2,1)} %get-tuple-element.182), channel_id=1, source_target_pairs={{0,1},{1,2},{2,3},{3,0},{4,5},{5,6},{6,7},{7,4},{8,9},{9,10},{10,1... | collective-permute-start | bytes 786440 | tf_op jit(solution)/shard_map/ppermute | solution.py:893
  167.2 36.1 %collective-permute-start.25 = (bf16[2,2,256,512]{3,2,1,0:T(8,128)(2,1)S(1)}, bf16[2,2,256,512]{3,2,1,0:T(8,128)(2,1)}, u32[]{:S(2)}, u32[]{:S(2)}) collective-permute-start(bf16[2,2,256,512]{3,2,1,0:T(8,128)(2,1)S(1)} %pad_maximum_fusion.10), channel_id=1, source_target_pairs={{0,16},{16,0},{1,17},{17,1},{2,18},{18,2},{3,19},{19,3},{4,20},{20... | collective-permute-start | bytes 3145736 | tf_op jit(solution)/shard_map/ppermute | solution.py:828
  169.0 34.2 %collective-permute-start.24 = (bf16[2,2,256,512]{3,2,1,0:T(8,128)(2,1)}, bf16[2,2,256,512]{3,2,1,0:T(8,128)(2,1)}, u32[]{:S(2)}, u32[]{:S(2)}) collective-permute-start(bf16[2,2,256,512]{3,2,1,0:T(8,128)(2,1)} %pad_maximum_fusion.9), channel_id=1, source_target_pairs={{0,8},{8,0},{1,9},{9,1},{2,10},{10,2},{3,11},{11,3},{4,12},{12,4},... | collective-permute-start | bytes 3145736 | tf_op jit(solution)/shard_map/ppermute | solution.py:828
  179.5 47.6 %collective-permute-start.27 = (bf16[784,1024]{1,0:T(8,128)(2,1)}, bf16[784,1024]{1,0:T(8,128)(2,1)}, u32[]{:S(2)}, u32[]{:S(2)}) collective-permute-start(bf16[784,1024]{1,0:T(8,128)(2,1)} %add_convert_fusion.x_ref.xa_ref), channel_id=1, source_target_pairs={{0,4},{4,0},{1,5},{5,1},{2,6},{6,2},{3,7},{7,3},{8,12},{12,8},{9,1... | collective-permute-start | bytes 4816904 | tf_op jit(solution)/shard_map/ppermute | solution.py:828
  203.3 23.8 %collective-permute-start.26 = (bf16[392,1024]{1,0:T(8,128)(2,1)}, bf16[392,1024]{1,0:T(8,128)(2,1)S(1)}, u32[]{:S(2)}, u32[]{:S(2)}) collective-permute-start(bf16[392,1024]{1,0:T(8,128)(2,1)} %get-tuple-element.208), channel_id=1, source_target_pairs={{2,4},{3,5},{4,2},{5,3},{10,12},{11,13},{12,10},{13,11},{18,20},{1... | collective-permute-start | bytes 2408456 | tf_op jit(solution)/shard_map/ppermute | solution.py:878
  204.1 38.2 %collective-permute-start.28 = (bf16[392,1024]{1,0:T(8,128)(2,1)}, bf16[392,1024]{1,0:T(8,128)(2,1)S(1)}, u32[]{:S(2)}, u32[]{:S(2)}) collective-permute-start(bf16[392,1024]{1,0:T(8,128)(2,1)} %get-tuple-element.213), channel_id=1, source_target_pairs={{0,1},{1,0},{2,5},{3,4},{4,3},{5,2},{6,7},{7,6},{8,9},{9,8},{10,13... | collective-permute-start | bytes 2408456 | tf_op jit(solution)/shard_map/ppermute | solution.py:878
  313.9 20.3 %collective-permute-start.32 = (bf16[784,1024]{1,0:T(8,128)(2,1)}, bf16[784,1024]{1,0:T(8,128)(2,1)}, u32[]{:S(2)}, u32[]{:S(2)}) collective-permute-start(bf16[784,1024]{1,0:T(8,128)(2,1)} %get-tuple-element.233.da_ref), channel_id=1, source_target_pairs={{0,4},{4,0},{1,5},{5,1},{2,6},{6,2},{3,7},{7,3},{8,12},{12,8},{9,1... | collective-permute-start | bytes 4816904 | tf_op jit(solution)/shard_map/ppermute | solution.py:828
  314.9 47.6 %collective-permute-start.35 = (bf16[2,2,256,512]{3,2,1,0:T(8,128)(2,1)}, bf16[2,2,256,512]{3,2,1,0:T(8,128)(2,1)S(1)}, u32[]{:S(2)}, u32[]{:S(2)}) collective-permute-start(bf16[2,2,256,512]{3,2,1,0:T(8,128)(2,1)} %get-tuple-element.247), channel_id=1, source_target_pairs={{0,8},{8,0},{1,9},{9,1},{2,10},{10,2},{3,11},{11,3},{4,12},{12,4},... | collective-permute-start | bytes 3145736 | tf_op jit(solution)/shard_map/ppermute | solution.py:828
  316.5 46.0 %collective-permute-start.36 = (bf16[2,2,256,512]{3,2,1,0:T(8,128)(2,1)}, bf16[2,2,256,512]{3,2,1,0:T(8,128)(2,1)S(1)}, u32[]{:S(2)}, u32[]{:S(2)}) collective-permute-start(bf16[2,2,256,512]{3,2,1,0:T(8,128)(2,1)} %get-tuple-element.248), channel_id=1, source_target_pairs={{0,16},{16,0},{1,17},{17,1},{2,18},{18,2},{3,19},{19,3},{4,20},{20... | collective-permute-start | bytes 3145736 | tf_op jit(solution)/shard_map/ppermute | solution.py:828
  331.3 31.6 %collective-permute-start.33 = (bf16[2,2,256,512]{3,2,1,0:T(8,128)(2,1)}, bf16[2,2,256,512]{3,2,1,0:T(8,128)(2,1)S(1)}, u32[]{:S(2)}, u32[]{:S(2)}) collective-permute-start(bf16[2,2,256,512]{3,2,1,0:T(8,128)(2,1)} %get-tuple-element.245), channel_id=1, source_target_pairs={{0,8},{8,0},{1,9},{9,1},{2,10},{10,2},{3,11},{11,3},{4,12},{12,4},... | collective-permute-start | bytes 3145736 | tf_op jit(solution)/shard_map/ppermute | solution.py:828
  333.5 31.2 %collective-permute-start.34 = (bf16[2,2,256,512]{3,2,1,0:T(8,128)(2,1)}, bf16[2,2,256,512]{3,2,1,0:T(8,128)(2,1)S(1)}, u32[]{:S(2)}, u32[]{:S(2)}) collective-permute-start(bf16[2,2,256,512]{3,2,1,0:T(8,128)(2,1)} %get-tuple-element.246), channel_id=1, source_target_pairs={{0,16},{16,0},{1,17},{17,1},{2,18},{18,2},{3,19},{19,3},{4,20},{20... | collective-permute-start | bytes 3145736 | tf_op jit(solution)/shard_map/ppermute | solution.py:828
  334.2 56.1 %collective-permute-start.42 = (bf16[392,1024]{1,0:T(8,128)(2,1)S(1)}, bf16[392,1024]{1,0:T(8,128)(2,1)S(1)}, u32[]{:S(2)}, u32[]{:S(2)}) collective-permute-start(bf16[392,1024]{1,0:T(8,128)(2,1)S(1)} %get-tuple-element.375), channel_id=1, source_target_pairs={{1,0},{0,1},{5,2},{4,3},{3,4},{2,5},{7,6},{6,7},{9,8},{8,9},{13,10... | collective-permute-start | bytes 2408456 | tf_op jit(solution)/shard_map/ppermute | solution.py:884
  370.0 20.4 %collective-permute-start.38 = (bf16[2,256,512]{2,1,0:T(8,128)(2,1)}, bf16[2,256,512]{2,1,0:T(8,128)(2,1)S(1)}, u32[]{:S(2)}, u32[]{:S(2)}) collective-permute-start(bf16[2,256,512]{2,1,0:T(8,128)(2,1)} %bitcast.266), channel_id=1, source_target_pairs={{0,16},{16,0},{1,17},{17,1},{2,18},{18,2},{3,19},{19,3},{4,20},{20... | collective-permute-start | bytes 1572872 | tf_op jit(solution)/shard_map/ppermute | solution.py:828
  370.5 19.9 %collective-permute-start.39 = (bf16[2,256,512]{2,1,0:T(8,128)(2,1)}, bf16[2,256,512]{2,1,0:T(8,128)(2,1)S(1)}, u32[]{:S(2)}, u32[]{:S(2)}) collective-permute-start(bf16[2,256,512]{2,1,0:T(8,128)(2,1)} %bitcast.265), channel_id=1, source_target_pairs={{0,8},{8,0},{1,9},{9,1},{2,10},{10,2},{3,11},{11,3},{4,12},{12,4},... | collective-permute-start | bytes 1572872 | tf_op jit(solution)/shard_map/ppermute | solution.py:828
  371.8 20.3 %collective-permute-start.40 = (bf16[2,256,512]{2,1,0:T(8,128)(2,1)}, bf16[2,256,512]{2,1,0:T(8,128)(2,1)S(1)}, u32[]{:S(2)}, u32[]{:S(2)}) collective-permute-start(bf16[2,256,512]{2,1,0:T(8,128)(2,1)} %bitcast.264), channel_id=1, source_target_pairs={{0,16},{16,0},{1,17},{17,1},{2,18},{18,2},{3,19},{19,3},{4,20},{20... | collective-permute-start | bytes 1572872 | tf_op jit(solution)/shard_map/ppermute | solution.py:828
  372.5 20.3 %collective-permute-start.41 = (bf16[2,256,512]{2,1,0:T(8,128)(2,1)}, bf16[2,256,512]{2,1,0:T(8,128)(2,1)S(1)}, u32[]{:S(2)}, u32[]{:S(2)}) collective-permute-start(bf16[2,256,512]{2,1,0:T(8,128)(2,1)} %bitcast.263), channel_id=1, source_target_pairs={{0,8},{8,0},{1,9},{9,1},{2,10},{10,2},{3,11},{11,3},{4,12},{12,4},... | collective-permute-start | bytes 1572872 | tf_op jit(solution)/shard_map/ppermute | solution.py:828
  401.3 25.6 %collective-permute-start.44 = (bf16[2,5,256,128]{3,2,1,0:T(8,128)(2,1)S(1)}, bf16[2,5,256,128]{3,2,1,0:T(8,128)(2,1)S(1)}, u32[]{:S(2)}, u32[]{:S(2)}) collective-permute-start(bf16[2,5,256,128]{3,2,1,0:T(8,128)(2,1)S(1)} %pad_maximum_fusion.12), channel_id=1, source_target_pairs={{0,16},{16,0},{1,17},{17,1},{2,18},{18,2},{3,19},{19,3},{4,20},{20... | collective-permute-start | bytes 1966088 | tf_op jit(solution)/shard_map/ppermute | solution.py:828
  404.1 22.8 %collective-permute-start.43 = (bf16[2,5,256,128]{3,2,1,0:T(8,128)(2,1)S(1)}, bf16[2,5,256,128]{3,2,1,0:T(8,128)(2,1)S(1)}, u32[]{:S(2)}, u32[]{:S(2)}) collective-permute-start(bf16[2,5,256,128]{3,2,1,0:T(8,128)(2,1)S(1)} %pad_maximum_fusion.11), channel_id=1, source_target_pairs={{0,8},{8,0},{1,9},{9,1},{2,10},{10,2},{3,11},{11,3},{4,12},{12,4},... | collective-permute-start | bytes 1966088 | tf_op jit(solution)/shard_map/ppermute | solution.py:828
  427.0 18.9 %collective-permute-start.46 = (bf16[5,256,128]{2,1,0:T(8,128)(2,1)S(1)}, bf16[5,256,128]{2,1,0:T(8,128)(2,1)S(1)}, u32[]{:S(2)}, u32[]{:S(2)}) collective-permute-start(bf16[5,256,128]{2,1,0:T(8,128)(2,1)S(1)} %fusion.4), channel_id=1, source_target_pairs={{0,8},{8,0},{1,9},{9,1},{2,10},{10,2},{3,11},{11,3},{4,12},{12,4},... | collective-permute-start | bytes 983048 | tf_op jit(solution)/shard_map/ppermute | solution.py:828
  465.0 19.8 %collective-permute-start.54 = (bf16[4,256,128]{2,1,0:T(8,128)(2,1)S(1)}, bf16[4,256,128]{2,1,0:T(8,128)(2,1)}, u32[]{:S(2)}, u32[]{:S(2)}) collective-permute-start(bf16[4,256,128]{2,1,0:T(8,128)(2,1)S(1)} %pad_maximum_fusion.21), channel_id=1, source_target_pairs={{0,3},{1,0},{2,1},{3,2},{4,7},{5,4},{6,5},{7,6},{8,11},{9,8},{10,9... | collective-permute-start | bytes 786440 | tf_op jit(solution)/shard_map/ppermute | solution.py:1047
  499.0 29.8 %collective-permute-start.58 = (bf16[392,1024]{1,0:T(8,128)(2,1)}, bf16[392,1024]{1,0:T(8,128)(2,1)S(1)}, u32[]{:S(2)}, u32[]{:S(2)}) collective-permute-start(bf16[392,1024]{1,0:T(8,128)(2,1)} %get-tuple-element.319), channel_id=1, source_target_pairs={{1,0},{0,1},{5,2},{4,3},{3,4},{2,5},{7,6},{6,7},{9,8},{8,9},{13,10... | collective-permute-start | bytes 2408456 | tf_op jit(solution)/shard_map/ppermute | solution.py:884
  505.8 27.0 %collective-permute-start.62 = (f32[20,128]{1,0:T(8,128)S(1)}, f32[20,128]{1,0:T(8,128)S(1)}, u32[]{:S(2)}, u32[]{:S(2)}) collective-permute-start(f32[20,128]{1,0:T(8,128)S(1)} %fusion.35), channel_id=1, source_target_pairs={{0,1},{1,2},{2,3},{3,0},{4,5},{5,6},{6,7},{7,4},{8,9},{9,10},{10,1... | collective-permute-start | bytes 30728 | tf_op jit(solution)/shard_map/ppermute | solution.py:1081
  507.4 29.8 %collective-permute-start.63 = (f32[20,128]{1,0:T(8,128)S(1)}, f32[20,128]{1,0:T(8,128)S(1)}, u32[]{:S(2)}, u32[]{:S(2)}) collective-permute-start(f32[20,128]{1,0:T(8,128)S(1)} %fusion.35), channel_id=1, source_target_pairs={{0,2},{1,3},{2,0},{3,1},{4,6},{5,7},{6,4},{7,5},{8,10},{9,11},{10,... | collective-permute-start | bytes 30728 | tf_op jit(solution)/shard_map/ppermute | solution.py:1081
  (98 other events, 1037.9 us)
Sparse Core Ops, SparseCore 0:
  98.7 104.4 all-gather.2
  410.3 45.7 reduce-scatter.1

commit v5 on v4

--- a/solution.py
+++ b/solution.py
@@ -190,13 +190,14 @@
     return lax.dot_general(left, right, dims, preferred_element_type=F32)
 
 
-def call(body, grid, in_specs, out_specs, out_shape, args, scratch=(), name=None, prefetch=0):
+def call(body, grid, in_specs, out_specs, out_shape, args, scratch=(), name=None, prefetch=0, aliases=None):
     return pl.pallas_call(
         body,
         grid_spec=pltpu.PrefetchScalarGridSpec(
             num_scalar_prefetch=prefetch, grid=grid, in_specs=in_specs, out_specs=out_specs, scratch_shapes=list(scratch)
         ),
         out_shape=out_shape,
+        input_output_aliases=aliases or {},
         compiler_params=pltpu.CompilerParams(vmem_limit_bytes=VMEM_LIMIT),
         cost_estimate=pl.CostEstimate(flops=1000, bytes_accessed=1000, transcendentals=0),
         name=name,
@@ -239,11 +240,16 @@
     return owner % 2 * 2 + owner // 2
 
 
-def key_blocks(ref, place, which):
-    return jnp.concatenate([ref[turned_owner(owner), place, which] for owner in range(ref.shape[0])], 1)
-
-
-def project_kernel(xa_ref, xb_ref, qk_ref, v_ref, b_ref, out_ref, t_ref, x_s):
+def owners_of(bits_ref, which, mine_ref, other_ref, pick):
+    parts = []
+    for owner in range(4):
+        row, column = owner // 2, owner % 2
+        inner, outer = (row, column) if which == 0 else (column, row)
+        parts.append(jnp.where(bits_ref[which] == outer, pick(mine_ref, inner), pick(other_ref, inner)))
+    return parts
+
+
+def project_kernel(bits_ref, xa_ref, xb_ref, qk_ref, qk_other, v_ref, v_other, b_ref, out_ref, t_ref, x_s):
     half = xa_ref.shape[0]
     group = pl.program_id(0)
 
@@ -254,42 +260,47 @@
         t_ref[...] = x_s[...].T
 
     cols = v_ref.shape[2]
-    places = [PAIR * group + p for p in range(PAIR)]
     for i in range(3):
-        pick = (lambda place: row_blocks(v_ref, place, 0, cols)) if i == 2 else (lambda place: key_blocks(qk_ref, place, i))
-        weights = jnp.concatenate([pick(place) for place in places], 0)
-        value = dot(weights, x_s[...], ROW_NT) + b_ref[0, i]
+        rows = slice(i * cols, (i + 1) * cols)
+        weights = []
+        for p in range(PAIR):
+            if i == 2:
+                parts = owners_of(bits_ref, 1, v_ref, v_other, lambda ref, inner: ref[inner, p])
+            else:
+                parts = owners_of(bits_ref, 0, qk_ref, qk_other, lambda ref, inner: ref[inner, p, rows])
+            weights.append(jnp.concatenate(parts, 1))
+        value = dot(jnp.concatenate(weights, 0), x_s[...], ROW_NT) + b_ref[0, i]
         out_ref[0, i] = value.astype(BF).reshape(out_ref.shape[2:])
 
 
-def project(xa, xb, w_qk, w_vo, bias):
+def project(bits, xa, xb, w_qk, w_vo, bias):
     half, width = xa.shape
-    owners, places, _, cols, part = w_qk.shape
+    _, places, rows, part = w_qk[0].shape
+    cols = rows // 2
     groups = places // PAIR
     heads = PAIR * cols // HEAD_DIM
-    whole = pl.BlockSpec((half, width), lambda g: (0, 0))
+    whole = pl.BlockSpec((half, width), lambda g, bits: (0, 0))
     return call(
         project_kernel,
         (groups,),
+        [whole, whole]
+        + [pl.BlockSpec((2, PAIR, rows, part), lambda g, bits: (0, g, 0, 0))] * 2
+        + [pl.BlockSpec((2, PAIR, cols, part), lambda g, bits: (0, g, 0, 0))] * 2
+        + [pl.BlockSpec((1, 3, PAIR * cols, 1), lambda g, bits: (g, 0, 0, 0))],
         [
-            whole,
-            whole,
-            pl.BlockSpec((owners, places, 2, cols, part), lambda g: (0, 0, 0, 0, 0)),
-            pl.BlockSpec((owners, places, cols, part), lambda g: (0, 0, 0, 0)),
-            pl.BlockSpec((1, 3, PAIR * cols, 1), lambda g: (g, 0, 0, 0)),
-        ],
-        [
-            pl.BlockSpec((1, 3, heads, HEAD_DIM, 2 * half), lambda g: (g, 0, 0, 0, 0)),
-            pl.BlockSpec((width, 2 * half), lambda g: (0, 0)),
+            pl.BlockSpec((1, 3, heads, HEAD_DIM, 2 * half), lambda g, bits: (g, 0, 0, 0, 0)),
+            pl.BlockSpec((width, 2 * half), lambda g, bits: (0, 0)),
         ],
         [shaped((groups, 3, heads, HEAD_DIM, 2 * half)), shaped((width, 2 * half))],
-        (xa, xb, w_qk, w_vo, bias),
+        (bits, xa, xb, *w_qk, *w_vo, bias),
         [pltpu.VMEM((2 * half, width), BF)],
         name="project",
-    )
-
-
-def attend_kernel(seq, padded, step, q_ref, k_ref, v_ref, o_ref, row_ref, wide_ref, lse_ref, key_s, query_s, value_s, hold_s):
+        prefetch=1,
+    )
+
+
+def attend_kernel(seq, padded, step, q_ref, k_ref, v_ref, *refs):
+    o_ref, row_ref, wide_ref, lse_ref, key_s, query_s, value_s, hold_s = refs[-8:]
     key = k_ref[0, 0, 0]
     key_s[...] = jnp.concatenate([key, key, key, jnp.zeros((HEAD_DIM, seq), BF)], 0).T
     parts = three_parts(pad_columns(q_ref[0, 0, 0].astype(F32) * (LOG2E * HEAD_DIM**-0.5), padded))
@@ -314,23 +325,29 @@
         row_ref[...] = hold_s[...].T
 
 
-def attend(qkv, group, step):
-    _, _, heads, _, seq = qkv.shape
+def attend(qkv, group, step, into=()):
+    groups, _, heads, _, seq = qkv.shape
     padded = -(-seq // 128) * 128
     part = lambda i: pl.BlockSpec((1, 1, 1, HEAD_DIM, seq), lambda h: (group, i, h, 0, 0))
-    spec = lambda rows: pl.BlockSpec((1, rows, seq), lambda h: (h, 0, 0))
+    spec = lambda rows: pl.BlockSpec((1, rows, seq), lambda h: (group * heads + h, 0, 0))
+    total = groups * heads
     return call(
         functools.partial(attend_kernel, seq, padded, step),
         (heads,),
-        [part(0), part(1), part(2)],
-        [spec(HEAD_DIM), pl.BlockSpec((seq, 2 * HEAD_DIM), lambda h: (0, h // 2)), spec(HEAD_DIM), spec(1)],
+        [part(0), part(1), part(2)] + [pl.BlockSpec(memory_space=pl.ANY)] * len(into),
         [
-            shaped((heads, HEAD_DIM, seq)),
-            shaped((seq, heads * HEAD_DIM)),
-            shaped((heads, HEAD_DIM, seq), F32),
-            shaped((heads, 1, seq), F32),
+            spec(HEAD_DIM),
+            pl.BlockSpec((seq, 2 * HEAD_DIM), lambda h: (0, group * heads // 2 + h // 2)),
+            spec(HEAD_DIM),
+            spec(1),
         ],
-        (qkv, qkv, qkv),
+        [
+            shaped((total, HEAD_DIM, seq)),
+            shaped((seq, total * HEAD_DIM)),
+            shaped((total, HEAD_DIM, seq), F32),
+            shaped((total, 1, seq), F32),
+        ],
+        (qkv, qkv, qkv, *into),
         [
             pltpu.VMEM((seq, 4 * HEAD_DIM), BF),
             pltpu.VMEM((4 * HEAD_DIM, padded), BF),
@@ -338,6 +355,7 @@
             pltpu.VMEM((2 * HEAD_DIM, seq), BF),
         ],
         name="attend",
+        aliases={3 + i: i for i in range(len(into))},
     )
 
 
@@ -386,7 +404,7 @@
     return call(
         functools.partial(attend_back_kernel, seq, padded, step),
         (count,),
-        [part(0), part(1), part(2), spec(HEAD_DIM), pl.BlockSpec((1, 1, seq), lambda h: (first + h, 0, 0)), spec(1)],
+        [part(0), part(1), part(2), spec(HEAD_DIM), spec(1), spec(1)],
         [
             pl.BlockSpec((3, seq, 2 * HEAD_DIM), lambda h: (0, 0, h // 2)),
             pl.BlockSpec((3, 1, 2 * HEAD_DIM), lambda h: (0, 0, h // 2)),
@@ -404,78 +422,68 @@
     )
 
 
-def mix_kernel(oa_ref, ob_ref, w_ref, out_ref):
+def mix_kernel(o_ref, w_ref, out_ref):
     places, cols = w_ref.shape[1:3]
     weights = [row_blocks(w_ref, j, 0, cols) for j in range(places)]
-    mixed = dot(jnp.concatenate([oa_ref[...], ob_ref[...]], 1), jnp.concatenate(weights, 0))
-    out_ref[...] = mixed.astype(out_ref.dtype)
+    out_ref[...] = dot(o_ref[...], jnp.concatenate(weights, 0)).astype(out_ref.dtype)
 
 
 def mix(rows, weights, which, dtype):
-    seq, wide = rows[0].shape
+    seq, wide = rows.shape
     owners, places, _, part = weights.shape
-    cols = PAIR * wide // places
+    cols = wide // places
     half = seq // 2
     return call(
         mix_kernel,
         (2,),
         [
             pl.BlockSpec((half, wide), lambda n: (which, 0)),
-            pl.BlockSpec((half, wide), lambda n: (which, 0)),
             pl.BlockSpec((owners // 2, places, cols, part), lambda n: (n, 0, 1, 0)),
         ],
         pl.BlockSpec((half, owners * part // 2), lambda n: (0, n)),
         shaped((half, owners * part), dtype),
-        (*rows, weights),
+        (rows, weights),
         name="mix",
     )
 
 
-def mix_back_kernel(bits_ref, da_ref, db_ref, w_ref, oa_ref, ob_ref, wa_ref, wb_ref, d_ref, delta_ref, *refs):
+def mix_back_kernel(bits_ref, da_ref, db_ref, w_ref, o_ref, wide_ref, d_ref, delta_ref, *refs):
     *grad_refs, d_s = refs
     half, width = da_ref.shape
     cols = w_ref.shape[2]
-    heads = oa_ref.shape[0]
-    group = pl.program_id(0)
-
-    @pl.when(group == 0)
+    heads = o_ref.shape[0]
+
+    @pl.when(pl.program_id(0) == 0)
     def _():
         d_s[0:half] = da_ref[...]
         d_s[half:] = db_ref[...]
 
-    places = [PAIR * group + p for p in range(PAIR)]
-    weights = jnp.concatenate([row_blocks(w_ref, place, 0, cols) for place in places], 0)
-    d_heads = dot(weights, d_s[...], ROW_NT).astype(BF).reshape(oa_ref.shape)
+    weights = jnp.concatenate([row_blocks(w_ref, p, 0, cols) for p in range(PAIR)], 0)
+    d_heads = dot(weights, d_s[...], ROW_NT).astype(BF).reshape(o_ref.shape)
     d_ref[...] = d_heads
-    for which, o_ref, wide_ref in ((0, oa_ref, wa_ref), (1, ob_ref, wb_ref)):
-
-        @pl.when(group == which)
-        def _():
-            delta_ref[...] = jnp.sum(d_heads.astype(F32) * wide_ref[...], 1, keepdims=True)
-            grad = dot(o_ref[...].reshape(heads * HEAD_DIM, 2 * half), d_s[...]).astype(BF).T
-            for p in range(PAIR):
-                part = grad[:, p * cols : (p + 1) * cols]
-                put_halves(bits_ref, part, p, grad_refs[2 * p], grad_refs[2 * p + 1], (slice(None), 0))
+    delta_ref[...] = jnp.sum(d_heads.astype(F32) * wide_ref[...], 1, keepdims=True)
+    grad = dot(o_ref[...].reshape(heads * HEAD_DIM, 2 * half), d_s[...]).astype(BF).T
+    for p in range(PAIR):
+        part = grad[:, p * cols : (p + 1) * cols]
+        put_halves(bits_ref, part, p, grad_refs[2 * p], grad_refs[2 * p + 1], (slice(None), 0))
 
 
 def mix_back(bits, da, db, weights, mixed, wide):
     half, width = da.shape
     owners, places, _, part = weights.shape
-    heads, _, seq = mixed[0].shape
+    heads, _, seq = mixed.shape
     groups = places // PAIR
-    cols = heads * HEAD_DIM // PAIR
+    cols = heads * HEAD_DIM // places
     whole = pl.BlockSpec((half, width), lambda g, bits: (0, 0))
-    fixed = pl.BlockSpec((heads, HEAD_DIM, seq), lambda g, bits: (0, 0, 0))
-    spec = lambda rows: pl.BlockSpec((heads, rows, seq), lambda g, bits: (g, 0, 0))
+    spec = lambda rows: pl.BlockSpec((heads // groups, rows, seq), lambda g, bits: (g, 0, 0))
     grad = pl.BlockSpec((2, 1, width // 4, cols), lambda g, bits: (0, g, 0, 0))
     d_heads, delta, keep_a, send_a, keep_b, send_b = call(
         mix_back_kernel,
         (groups,),
-        [whole, whole, pl.BlockSpec((owners, places, cols, part), lambda g, bits: (0, 0, 1, 0))] + [fixed] * 4,
+        [whole, whole, pl.BlockSpec((owners, PAIR, cols, part), lambda g, bits: (0, g, 1, 0)), spec(HEAD_DIM), spec(HEAD_DIM)],
         [spec(HEAD_DIM), spec(1)] + [grad] * 4,
-        [shaped((groups * heads, HEAD_DIM, seq)), shaped((groups * heads, 1, seq), F32)]
-        + [shaped((2, groups, width // 4, cols))] * 4,
-        (bits, da, db, weights, *mixed, *wide),
+        [shaped((heads, HEAD_DIM, seq)), shaped((heads, 1, seq), F32)] + [shaped((2, groups, width // 4, cols))] * 4,
+        (bits, da, db, weights, mixed, wide),
         [pltpu.VMEM((seq, width), BF)],
         name="mix_back",
         prefetch=1,
@@ -711,54 +719,48 @@
 def add_kernel(bits_ref, *refs):
     count = len(refs) // 3
     for i in range(count):
-        refs[2 * count + i][0] = (refs[2 * i][0].astype(F32) + refs[2 * i + 1][0].astype(F32)).astype(BF)
+        refs[2 * count + i][...] = (refs[2 * i][0].astype(F32) + refs[2 * i + 1][0].astype(F32)).astype(BF)
 
 
 def add_middle(bits, keeps, parts):
+    _, blocks, rows, units = keeps[0].shape
     args, in_specs = [], []
-    for i, (keep, part) in enumerate(zip(keeps, parts)):
-        args += [keep, part]
-        block = (1,) + keep.shape[1:]
-        in_specs += [pl.BlockSpec(block, lambda s, bits, i=i: (1 - bits[1 - i % 2], 0, 0, 0))] * 2
-    shapes = [(1,) + keep.shape[1:] for keep in keeps]
-    outs = call(
+    for i, pair in enumerate(zip(keeps, parts)):
+        args += pair
+        in_specs += [pl.BlockSpec((1, 1, rows, units), lambda s, bits, i=i: (1 - bits[1 - i % 2], s, 0, 0))] * 2
+    return call(
         add_kernel,
-        (1,),
+        (blocks,),
         in_specs,
-        [pl.BlockSpec(shape, lambda s, bits: (0, 0, 0, 0)) for shape in shapes],
-        [shaped(shape) for shape in shapes],
+        [pl.BlockSpec((1, rows, units), lambda s, bits: (s, 0, 0))] * len(keeps),
+        [shaped((blocks, rows, units))] * len(keeps),
         (bits, *args),
         name="add_middle",
         prefetch=1,
     )
-    return [out[0] for out in outs]
 
 
 def add_end_kernel(bits_ref, *refs):
-    out_ref = refs[-1]
     for i in range(len(refs) // 3):
         keep, part, end = refs[3 * i : 3 * i + 3]
-        total = keep[0].astype(F32) + part[0].astype(F32) + end[...].astype(F32)
-        half = total.shape[0]
-        at = i % 2 * half
-        out_ref[at : at + half, i // 2] = total.astype(BF)
+        total = keep[0, 0].astype(F32) + part[0, 0].astype(F32) + end[0].astype(F32)
+        refs[-1][i % 2, 0, i // 2] = total.astype(BF)
 
 
 def add_end(bits, keeps, parts, ends):
+    _, blocks, rows, units = keeps[0].shape
     args, in_specs = [], []
-    for i, (keep, part, end) in enumerate(zip(keeps, parts, ends)):
-        args += [keep, part, end]
-        block = (1,) + keep.shape[1:]
-        in_specs += [pl.BlockSpec(block, lambda s, bits, i=i: (bits[1 - i % 2], 0, 0, 0))] * 2
-        in_specs.append(pl.BlockSpec(end.shape, lambda s, bits: (0, 0, 0)))
-    _, blocks, rows, units = keeps[0].shape
-    shape = (2 * blocks, len(keeps) // 2, rows, units)
+    for i, triple in enumerate(zip(keeps, parts, ends)):
+        args += triple
+        in_specs += [pl.BlockSpec((1, 1, rows, units), lambda s, bits, i=i: (bits[1 - i % 2], s, 0, 0))] * 2
+        in_specs.append(pl.BlockSpec((1, rows, units), lambda s, bits: (s, 0, 0)))
+    count = len(keeps) // 2
     return call(
         add_end_kernel,
-        (1,),
+        (blocks,),
         in_specs,
-        pl.BlockSpec(shape, lambda s, bits: (0, 0, 0, 0)),
-        shaped(shape),
+        pl.BlockSpec((2, 1, count, rows, units), lambda s, bits: (0, s, 0, 0, 0)),
+        shaped((2, blocks, count, rows, units)),
         (bits, *args),
         name="add_end",
         prefetch=1,
@@ -957,8 +959,8 @@
     )
     w_qk, w_vo = ordered(y, qk_rows[None], swapped[0][None], 0), ordered(x, vo_rows[None], swapped[1][None], 0)
     swapped, far = together((swap(w_qk, "x"), swap(w_vo, "y")), far)
-    w_qk = ordered(x, w_qk[None], swapped[0][None], 0).reshape(4, steps, 2, cols, 2 * dims)
-    w_vo = ordered(y, w_vo[None], swapped[1][None], 0).reshape(4, steps, 2 * cols, 2 * dims)
+    bits = jnp.stack([x, y])
+    parts_qk, parts_vo = (w_qk, swapped[0]), (w_vo, swapped[1])
     up_piece, down_piece = ff_piece
     up_piece, down_piece, far = together(up_piece, down_piece, far)
     up_rows = ring_gather(up_piece)
@@ -970,18 +972,20 @@
     first = (centred_one * scale_one * gains[0] + shift_all[0]).astype(BF)
     first_other = swap(first, "c")
     half = first.shape[0] // 2
-    qkv, turned = project(first, first_other, w_qk, w_vo, bias_in)
-    mixed_a, rows_a, wide_a, lse_a = attend(qkv, 0, 1664)
-    up_rows, rows_a = together(up_rows, rows_a)
+    qkv, turned = project(bits, first, first_other, parts_qk, parts_vo, bias_in)
+    parts_qk, parts_vo, qkv = together(parts_qk, parts_vo, qkv)
+    w_qk = ordered(x, parts_qk[0][None], parts_qk[1][None], 0).reshape(4, steps, 2, cols, 2 * dims)
+    w_vo = ordered(y, parts_vo[0][None], parts_vo[1][None], 0).reshape(4, steps, 2 * cols, 2 * dims)
+    mixed, rows, wide, lse = attend(qkv, 0, 1664)
+    up_rows, rows = together(up_rows, rows)
     up_a, up_b = jnp.stack([up_piece, up_rows[0]]), jnp.stack(up_rows[1:])
     swapped = swap(up_a, "y"), swap(up_b, "x")
-    mixed_b, rows_b, wide_b, lse_b = attend(after(qkv, rows_a), 1, 1664)
-    swapped, rows_b = together(swapped, rows_b)
+    mixed, rows, wide, lse = attend(qkv, 1, 1664, (mixed, rows, wide, lse))
+    swapped, rows = together(swapped, rows)
     up_a, up_b = ordered(y, up_a[None], swapped[0][None], 0), ordered(x, up_b[None], swapped[1][None], 0)
     swapped = swap(up_a, "x"), swap(up_b, "y")
-    rows = (rows_a, rows_b)
     attn_other = mix(rows, w_vo, 1, BF)
-    attn_mine = mix((after(rows_a, attn_other), rows_b), w_vo, 0, F32)
+    attn_mine = mix(after(rows, attn_other), w_vo, 0, F32)
     hidden = inputs + (attn_mine + swap(attn_other, "c").astype(F32)) + shift_all[2]
 
     centred_two, scale_two = moments(hidden)
@@ -1007,7 +1011,6 @@
     d_second_swapped = swap(d_second_other, "c")
     up_sum = (sum_mine + sum_other).reshape(steps, units)
 
-    bits = jnp.stack([x, y])
     grad_down, sends = ffn_grad(bits, after(d_ffn, d_pre_other), d_ffn_other, act_mine, act_other, steps)
     down = scatter_start(sends)
     result, grad_down = together(output.astype(BF), grad_down)
@@ -1019,13 +1022,13 @@
     up = scatter_start(sends)
     d_attn_other, grad_up = together(d_attn_other, grad_up)
 
-    d_heads, delta, grad_o, sends_o = mix_back(bits, d_attn, d_attn_other, w_vo, (mixed_a, mixed_b), (wide_a, wide_b))
+    d_heads, delta, grad_o, sends_o = mix_back(bits, d_attn, d_attn_other, w_vo, mixed, wide)
     keeps = (*grad_up, *grad_down)
-    back_a, sum_a = attend_backward(qkv, d_heads, lse_b, delta, 1, 0, 2, 256)
+    back_a, sum_a = attend_backward(qkv, d_heads, lse, delta, 1, 0, 2, 256)
     up, down, out_near, back_a = together(up, down, out_near, back_a)
     ends = add_middle(bits, keeps, (*up, *down))
     ends = [swap(part, name) for part, name in zip(ends, ("y", "x", "y", "x"))]
-    back_b, sum_b = attend_backward(qkv, after(d_heads, back_a), lse_b, delta, 1, 2, 2, 256)
+    back_b, sum_b = attend_backward(qkv, after(d_heads, back_a), lse, delta, 1, 2, 2, 256)
     ends, out_far, back_b = together(ends, out_far, back_b)
     grad_ff = add_end(bits, keeps, (*up, *down), ends).reshape(steps * 4 * dims, units)
     ff_total = lax.psum_scatter(grad_ff, "t", scatter_dimension=0, tiled=True)
@@ -1033,10 +1036,10 @@
     one = scatter_start([jnp.concatenate(pair, 1) for pair in zip(sends, sends_o)])
     grad_one = list(zip(grad_one, grad_o))
     delta, grad_ff, grad_one = together(delta, grad_ff, grad_one)
-    back_c, sum_c = attend_backward(qkv, after(d_heads, back_b), lse_a, delta, 0, 2, 2, 256)
+    back_c, sum_c = attend_backward(qkv, after(d_heads, back_b), lse, delta, 0, 2, 2, 256)
     one, back_c = together(one, back_c)
     one_ends = scatter_middle(grad_one, one)
-    back_d, sum_d = attend_backward(qkv, after(d_heads, back_c), lse_a, delta, 0, 0, 2, 256)
+    back_d, sum_d = attend_backward(qkv, after(d_heads, back_c), lse, delta, 0, 0, 2, 256)
     one_ends, back_d = together(one_ends, back_d)
     grad_two, sends = project_grads(bits, turned, back_d, back_c)
     two = scatter_start(sends)

time: 558 us -> 554 us (level)
  waiting for transfers between devices: 77.3 us -> 97.8 us
  starting transfers between devices: 105 us -> 96.9 us
  local copies, waits for them, and re-layouts: 29.3 us -> 22.9 us
  other arithmetic: 52.5 us -> 46.9 us
    ppermute x42, waiting for transfers between devices: 46.8 us -> 61.8 us  [swap(): return lax.ppermute(value, axis, [(0, 1), (1, 0)])]
    ppermute x2, waiting for transfers between devices: 3.81 us -> 9.85 us  [sent(): lax.ppermute(pair[1], every, second_way)]
  transfers between devices with their start and end apart: 67 -> 67, of which waited for: 20 -> 21; matrix products, arithmetic and copies ran while one was open for 10% -> 9% of each run, Pallas kernels for 44% -> 43%
where the time goes in v5:
time: 554 us; the launch traced here: 547 us
  Pallas kernels  267 us (48%)
  waiting for transfers between devices  97.8 us (18%)
  starting transfers between devices  96.9 us (17%)
  other arithmetic  46.9 us (8%)
  local copies, waits for them, and re-layouts  22.9 us (4%)
  between operations  15.8 us (3%)
    pallas_call x24, Pallas kernels, call(): pl.pallas_call(body, grid_spec=pltpu.PrefetchScalarGridSpec(num_scalar_pr...  267 us
    ppermute x42, waiting for transfers between devices, swap(): return lax.ppermute(value, axis, [(0, 1), (1, 0)])  61.8 us
    ppermute x42, starting transfers between devices, swap(): return lax.ppermute(value, axis, [(0, 1), (1, 0)])  54.8 us
    ppermute x9, waiting for transfers between devices, ring_gather(): lax.ppermute(value, 't', rings[-j % steps])  24.4 us
    ppermute x3, starting transfers between devices, clip_local(): lax.ppermute(sums, 't', rings[away])  19.1 us
    ppermute x9, starting transfers between devices, ring_gather(): lax.ppermute(value, 't', rings[-j % steps])  11.3 us
  transfers between devices with their start and end apart: 67, of which 21 were waited for; matrix products, arithmetic and copies ran while one was open for 9% of the time, Pallas kernels for 43%

profile of v5, /device:TPU:0, one launch (start us, length us, event | category | flops | bytes accessed | tf_op | source)
XLA Modules:
  0.0 547.3 jit_solution(13311113163201438050)
XLA Ops:
  33.0 4.5 collective-permute-done.1
  37.5 15.2 %collective-permute-done.2 = bf16[512,256]{1,0:T(8,128)(2,1)S(1)} collective-permute-done((bf16[512,256]{1,0:T(8,128)(2,1)S(1)}, bf16[512,256]{1,0:T(8,128)(2,1)S(1)}, u32[]{:S(2)}, u32[]{:S(2)}) %collective-permute-start.2) | collective-permute-done | bytes 262176 | tf_op jit(solution)/shard_map/ppermute | solution.py:895
  58.8 10.0 %collective-permute-done.4 = bf16[4,256,256]{2,1,0:T(8,128)(2,1)S(1)} collective-permute-done((bf16[4,256,256]{2,1,0:T(8,128)(2,1)}, bf16[4,256,256]{2,1,0:T(8,128)(2,1)S(1)}, u32[]{:S(2)}, u32[]{:S(2)}) %collective-permute-start.4) | collective-permute-done | bytes 524320 | tf_op jit(solution)/shard_map/ppermute | solution.py:830
  78.0 4.0 collective-permute-start.13
  85.2 9.9 %collective-permute-done.16 = bf16[392,1024]{1,0:T(8,128)(2,1)S(1)} collective-permute-done((bf16[392,1024]{1,0:T(8,128)(2,1)}, bf16[392,1024]{1,0:T(8,128)(2,1)S(1)}, u32[]{:S(2)}, u32[]{:S(2)}) %collective-permute-start.16) | collective-permute-done | bytes 802848 | tf_op jit(solution)/shard_map/ppermute | solution.py:880
  106.6 11.9 %project.1 = (bf16[2,3,4,64,1568]{4,3,2,1,0:T(8,128)(2,1)}, bf16[1024,1568]{1,0:T(8,128)(2,1)}) custom-call(s32[2]{0:T(128)} %pad_add_fusion.bits_ref, bf16[784,1024]{1,0:T(8,128)(2,1)} %copy-done.16, bf16[784,1024]{1,0:T(8,128)(2,1)} %collective-permute-done.20.xb_ref, bf16[2,4,256,256]{3,2,1,0:T(8,128)(2,1)} %copy-done.11, ...), custom_call_target="tpu_custom_call" | custom-call | flops 1000 | bytes 1000 | tf_op jit(solution)/shard_map/project/pallas_call | solution.py:194
  118.5 16.2 %attend.2 = (bf16[8,64,1568]{2,1,0:T(8,128)(2,1)}, bf16[1568,512]{1,0:T(8,128)(2,1)}, f32[8,64,1568]{2,1,0:T(8,128)}, f32[8,1,1568]{2,1,0:T(1,128)}) custom-call(bf16[2,3,4,64,1568]{4,3,2,1,0:T(8,128)(2,1)} %get-tuple-element.191.q_ref.k_ref.v_ref, bf16[2,3,4,64,1568]{4,3,2,1,0:T(8,128)(2,1)} %get-tuple-element.191.q_ref.k_ref.v_ref, ...), custom_call_target="tpu_custom_call" | custom-call | flops 1000 | bytes 1000 | tf_op jit(solution)/shard_map/attend/pallas_call | solution.py:194
  136.9 16.3 %attend.3 = (bf16[8,64,1568]{2,1,0:T(8,128)(2,1)}, bf16[1568,512]{1,0:T(8,128)(2,1)}, f32[8,64,1568]{2,1,0:T(8,128)}, f32[8,1,1568]{2,1,0:T(1,128)}) custom-call(bf16[2,3,4,64,1568]{4,3,2,1,0:T(8,128)(2,1)} %get-tuple-element.191.q_ref.k_ref.v_ref, ...), custom_call_target="tpu_custom_call", output_to_operand_aliasing={{0}: (3, {}), {1}: (4, {}), {2}: (5, {}), {3}: (6, {})} | custom-call | flops 1000 | bytes 1000 | tf_op jit(solution)/shard_map/attend/pallas_call | solution.py:194
  159.5 4.2 mix.3
  170.5 31.3 %collective-permute-done.24 = bf16[2,2,256,512]{3,2,1,0:T(8,128)(2,1)} collective-permute-done((bf16[2,2,256,512]{3,2,1,0:T(8,128)(2,1)S(1)}, bf16[2,2,256,512]{3,2,1,0:T(8,128)(2,1)}, u32[]{:S(2)}, u32[]{:S(2)}) %collective-permute-start.24) | collective-permute-done | bytes 1048608 | tf_op jit(solution)/shard_map/ppermute | solution.py:830
  210.4 15.4 %ffn.2 = (f32[784,1024]{1,0:T(8,128)}, bf16[784,2048]{1,0:T(8,128)(2,1)}, bf16[784,2048]{1,0:T(8,128)(2,1)}) custom-call(s32[1]{0:T(128)} %bitcast.51.place_ref, bf16[784,1024]{1,0:T(8,128)(2,1)} %add_convert_fusion.x_ref.xa_ref, bf16[4,2,256,512]{3,2,1,0:T(8,128)(2,1)} %bitcast.223, bf16[4,2,256,512]{3,2,1,0:T(8,128)(2,1)} %bitcast.227, ...), custom_call_target="tpu_custom_call" | custom-call | flops 1000 | bytes 1000 | tf_op jit(solution)/shard_map/ffn/pallas_call | solution.py:194
  225.8 15.1 %ffn.3 = (bf16[784,1024]{1,0:T(8,128)(2,1)}, bf16[784,2048]{1,0:T(8,128)(2,1)}, bf16[784,2048]{1,0:T(8,128)(2,1)}) custom-call(s32[1]{0:T(128)} %bitcast.51.place_ref, bf16[784,1024]{1,0:T(8,128)(2,1)} %collective-permute-done.27.x_ref.xb_ref, bf16[4,2,256,512]{3,2,1,0:T(8,128)(2,1)} %bitcast.224, bf16[4,2,256,512]{3,2,1,0:T(8,128)(2,1)} %bitcast.228, ...), custom_call_target="tpu_custom_call" | custom-call | flops 1000 | bytes 1000 | tf_op jit(solution)/shard_map/ffn/pallas_call | solution.py:194
  241.0 8.0 %collective-permute-start.29 = (bf16[784,1024]{1,0:T(8,128)(2,1)}, bf16[784,1024]{1,0:T(8,128)(2,1)S(1)}, u32[]{:S(2)}, u32[]{:S(2)}) collective-permute-start(bf16[784,1024]{1,0:T(8,128)(2,1)} %get-tuple-element.223), channel_id=1, source_target_pairs={{0,4},{4,0},{1,5},{5,1},{2,6},{6,2},{3,7},{7,3},{8,12},{12,8},{9,1... | collective-permute-start | bytes 4816904 | tf_op jit(solution)/shard_map/ppermute | solution.py:830
  252.2 5.1 fusion.46
  258.5 13.7 %ffn_backward.2 = (f32[784,1024]{1,0:T(8,128)}, bf16[784,2048]{1,0:T(8,128)(2,1)}, f32[4,1,512]{2,1,0:T(1,128)}) custom-call(s32[1]{0:T(128)} %bitcast.51.place_ref, bf16[784,1024]{1,0:T(8,128)(2,1)} %copy-done.7, bf16[4,4,256,512]{3,2,1,0:T(8,128)(2,1)} %bitcast.221, bf16[4,2,256,512]{3,2,1,0:T(8,128)(2,1)} %bitcast.225, ...), custom_call_target="tpu_custom_call" | custom-call | flops 1000 | bytes 1000 | tf_op jit(solution)/shard_map/ffn_backward/pallas_call | solution.py:194
  273.3 13.3 %ffn_backward.3 = (bf16[784,1024]{1,0:T(8,128)(2,1)}, bf16[784,2048]{1,0:T(8,128)(2,1)}, f32[4,1,512]{2,1,0:T(1,128)}) custom-call(s32[1]{0:T(128)} %bitcast.51.place_ref, bf16[784,1024]{1,0:T(8,128)(2,1)} %copy-done.15, bf16[4,4,256,512]{3,2,1,0:T(8,128)(2,1)} %bitcast.222, bf16[4,2,256,512]{3,2,1,0:T(8,128)(2,1)} %bitcast.226, ...), custom_call_target="tpu_custom_call" | custom-call | flops 1000 | bytes 1000 | tf_op jit(solution)/shard_map/ffn_backward/pallas_call | solution.py:194
  287.0 14.4 %ffn_grad.2 = (bf16[2,2,256,512]{3,2,1,0:T(8,128)(2,1)}, bf16[2,2,256,512]{3,2,1,0:T(8,128)(2,1)}, bf16[2,2,256,512]{3,2,1,0:T(8,128)(2,1)}, bf16[2,2,256,512]{3,2,1,0:T(8,128)(2,1)}) custom-call(s32[2]{0:T(128)} %pad_add_fusion.bits_ref, bf16[784,1024]{1,0:T(8,128)(2,1)} %copy-done.7, bf16[784,1024]{1,0:T(8,128)(2,1)} %copy-done.15, ...), custom_call_target="tpu_custom_call" | custom-call | flops 1000 | bytes 1000 | tf_op jit(solution)/shard_map/ffn_grad/pallas_call | solution.py:194
  302.7 9.1 %norm_backward.2 = (f32[784,1024]{1,0:T(8,128)}, bf16[784,1024]{1,0:T(8,128)(2,1)}, f32[8,1024]{1,0:T(8,128)}) custom-call(f32[784,1024]{1,0:T(8,128)} %get-tuple-element.237.da_ref, bf16[784,1024]{1,0:T(8,128)(2,1)} %copy-done.29, f32[784,1024]{1,0:T(8,128)} %copy-done, f32[784,1024]{1,0:T(8,128)} %get-tuple-element.367.rest_ref, f32[1,1024]{1,0:T(1,128)} %copy-done.56), custom_call_target="tpu_custom_call" | custom-call | flops 1000 | bytes 1000 | tf_op jit(solution)/shard_map/norm_backward/pallas_call | solution.py:194
  315.7 14.3 %ffn_grad.3 = (bf16[2,2,256,512]{3,2,1,0:T(8,128)(2,1)}, bf16[2,2,256,512]{3,2,1,0:T(8,128)(2,1)}, bf16[2,2,256,512]{3,2,1,0:T(8,128)(2,1)}, bf16[2,2,256,512]{3,2,1,0:T(8,128)(2,1)}) custom-call(s32[2]{0:T(128)} %pad_add_fusion.bits_ref, bf16[784,1024]{1,0:T(8,128)(2,1)} %add_convert_fusion.x_ref.xa_ref, ...), custom_call_target="tpu_custom_call" | custom-call | flops 1000 | bytes 1000 | tf_op jit(solution)/shard_map/ffn_grad/pallas_call | solution.py:194
  332.9 9.0 %mix_back.1 = (bf16[8,64,1568]{2,1,0:T(8,128)(2,1)}, f32[8,1,1568]{2,1,0:T(1,128)}, bf16[2,2,256,128]{3,2,1,0:T(8,128)(2,1)}, bf16[2,2,256,128]{3,2,1,0:T(8,128)...) custom-call(s32[2]{0:T(128)} %pad_add_fusion.bits_ref, ...), custom_call_target="tpu_custom_call" | custom-call | flops 1000 | bytes 1000 | tf_op jit(solution)/shard_map/mix_back/pallas_call | solution.py:194
  341.9 16.3 %attend_backward.4 = (bf16[3,1568,128]{2,1,0:T(8,128)(2,1)}, f32[3,1,128]{2,1,0:T(1,128)}) custom-call(bf16[2,3,4,64,1568]{4,3,2,1,0:T(8,128)(2,1)} %get-tuple-element.191.q_ref.k_ref.v_ref, bf16[2,3,4,64,1568]{4,3,2,1,0:T(8,128)(2,1)} %get-tuple-element.191.q_ref.k_ref.v_ref, bf16[2,3,4,64,1568]{4,3,2,1,0:T(8,128)(2,1)} %get-tuple-element.191.q_ref.k_ref.v_ref, ...), custom_call_target="tpu_custom_call" | custom-call | flops 1000 | bytes 1000 | tf_op jit(solution)/shard_map/attend_backward/pallas_call | solution.py:194
  363.5 4.0 add_middle.1
  371.6 16.7 %attend_backward.5 = (bf16[3,1568,128]{2,1,0:T(8,128)(2,1)}, f32[3,1,128]{2,1,0:T(1,128)}) custom-call(bf16[2,3,4,64,1568]{4,3,2,1,0:T(8,128)(2,1)} %get-tuple-element.191.q_ref.k_ref.v_ref, bf16[2,3,4,64,1568]{4,3,2,1,0:T(8,128)(2,1)} %get-tuple-element.191.q_ref.k_ref.v_ref, bf16[2,3,4,64,1568]{4,3,2,1,0:T(8,128)(2,1)} %get-tuple-element.191.q_ref.k_ref.v_ref, ...), custom_call_target="tpu_custom_call" | custom-call | flops 1000 | bytes 1000 | tf_op jit(solution)/shard_map/attend_backward/pallas_call | solution.py:194
  394.0 7.4 %project_grads.2 = (bf16[2,3,256,128]{3,2,1,0:T(8,128)(2,1)}, bf16[2,3,256,128]{3,2,1,0:T(8,128)(2,1)}, bf16[2,3,256,128]{3,2,1,0:T(8,128)(2,1)}, bf16[2,3,256,128]{3,2,1,0:T(8,128)(2,1)}) custom-call(s32[2]{0:T(128)} %pad_add_fusion.bits_ref, bf16[1024,1568]{1,0:T(8,128)(2,1)} %get-tuple-element.236.t_ref, ...), custom_call_target="tpu_custom_call" | custom-call | flops 1000 | bytes 1000 | tf_op jit(solution)/shard_map/project_grads/pallas_call | solution.py:194
  406.1 5.0 add_end.1
  411.3 16.5 %attend_backward.6 = (bf16[3,1568,128]{2,1,0:T(8,128)(2,1)}, f32[3,1,128]{2,1,0:T(1,128)}) custom-call(bf16[2,3,4,64,1568]{4,3,2,1,0:T(8,128)(2,1)} %get-tuple-element.191.q_ref.k_ref.v_ref, bf16[2,3,4,64,1568]{4,3,2,1,0:T(8,128)(2,1)} %get-tuple-element.191.q_ref.k_ref.v_ref, bf16[2,3,4,64,1568]{4,3,2,1,0:T(8,128)(2,1)} %get-tuple-element.191.q_ref.k_ref.v_ref, ...), custom_call_target="tpu_custom_call" | custom-call | flops 1000 | bytes 1000 | tf_op jit(solution)/shard_map/attend_backward/pallas_call | solution.py:194
  433.1 16.4 %attend_backward.7 = (bf16[3,1568,128]{2,1,0:T(8,128)(2,1)}, f32[3,1,128]{2,1,0:T(1,128)}) custom-call(bf16[2,3,4,64,1568]{4,3,2,1,0:T(8,128)(2,1)} %get-tuple-element.191.q_ref.k_ref.v_ref, bf16[2,3,4,64,1568]{4,3,2,1,0:T(8,128)(2,1)} %get-tuple-element.191.q_ref.k_ref.v_ref, bf16[2,3,4,64,1568]{4,3,2,1,0:T(8,128)(2,1)} %get-tuple-element.191.q_ref.k_ref.v_ref, ...), custom_call_target="tpu_custom_call" | custom-call | flops 1000 | bytes 1000 | tf_op jit(solution)/shard_map/attend_backward/pallas_call | solution.py:194
  449.6 7.3 %project_grads.3 = (bf16[2,3,256,128]{3,2,1,0:T(8,128)(2,1)}, bf16[2,3,256,128]{3,2,1,0:T(8,128)(2,1)}, bf16[2,3,256,128]{3,2,1,0:T(8,128)(2,1)}, bf16[2,3,256,128]{3,2,1,0:T(8,128)(2,1)}) custom-call(s32[2]{0:T(128)} %pad_add_fusion.bits_ref, bf16[1024,1568]{1,0:T(8,128)(2,1)} %get-tuple-element.236.t_ref, ...), custom_call_target="tpu_custom_call" | custom-call | flops 1000 | bytes 1000 | tf_op jit(solution)/shard_map/project_grads/pallas_call | solution.py:194
  456.8 6.8 %project_back.2 = f32[784,1024]{1,0:T(8,128)} custom-call(bf16[3,1568,128]{2,1,0:T(8,128)(2,1)} %get-tuple-element.298.da_ref.a_ref, bf16[3,1568,128]{2,1,0:T(8,128)(2,1)} %get-tuple-element.295.db_ref.b_ref, bf16[3,1568,128]{2,1,0:T(8,128)(2,1)} %get-tuple-element.270.da_ref.c_ref, bf16[3,1568,128]{2,1,0:T(8,128)(2,1)} %get-tuple-element.277.db_ref.d_ref, ...), custom_call_target="tpu_custom_call" | custom-call | flops 1000 | bytes 1000 | tf_op jit(solution)/shard_map/project_back/pallas_call | solution.py:194
  468.9 6.8 %project_back.3.da_ref = f32[784,1024]{1,0:T(8,128)} custom-call(bf16[3,1568,128]{2,1,0:T(8,128)(2,1)} %get-tuple-element.298.da_ref.a_ref, bf16[3,1568,128]{2,1,0:T(8,128)(2,1)} %get-tuple-element.295.db_ref.b_ref, bf16[3,1568,128]{2,1,0:T(8,128)(2,1)} %get-tuple-element.270.da_ref.c_ref, bf16[3,1568,128]{2,1,0:T(8,128)(2,1)} %get-tuple-element.277.db_ref.d_ref, ...), custom_call_target="tpu_custom_call" | custom-call | flops 1000 | bytes 1000 | tf_op jit(solution)/shard_map/project_back/pallas_call | solution.py:194
  477.3 7.3 %norm_backward.3 = (bf16[392,1024]{1,0:T(8,128)(2,1)}, bf16[392,1024]{1,0:T(8,128)(2,1)}, f32[8,1024]{1,0:T(8,128)}) custom-call(f32[784,1024]{1,0:T(8,128)} %project_back.3.da_ref, f32[784,1024]{1,0:T(8,128)} %collective-permute-done.51.db_ref, f32[784,1024]{1,0:T(8,128)} %fusion.45.x_ref, f32[784,1024]{1,0:T(8,128)} %get-tuple-element.311.rest_ref, ...), custom_call_target="tpu_custom_call" | custom-call | flops 1000 | bytes 1000 | tf_op jit(solution)/shard_map/norm_backward/pallas_call | solution.py:194
  504.9 18.6 %collective-permute-start.64 = (f32[20,128]{1,0:T(8,128)S(1)}, f32[20,128]{1,0:T(8,128)S(1)}, u32[]{:S(2)}, u32[]{:S(2)}) collective-permute-start(f32[20,128]{1,0:T(8,128)S(1)} %fusion.37), channel_id=1, source_target_pairs={{0,3},{1,0},{2,1},{3,2},{4,7},{5,4},{6,5},{7,6},{8,11},{9,8},{10,9... | collective-permute-start | bytes 30728 | tf_op jit(solution)/shard_map/ppermute | solution.py:1084
  (415 shorter events, 161.5 us)
Async XLA Ops:
  7.2 195.2 %all-gather.3.cloned.1.call-start = ((), (), s32[]{:S(2)}) async-start(), calls=%async_computation.2 | async-start | bytes 4456448 | tf_op jit(solution)/shard_map/all_gather | solution.py:967
  30.5 22.2 %collective-permute-start.2 = (bf16[512,256]{1,0:T(8,128)(2,1)S(1)}, bf16[512,256]{1,0:T(8,128)(2,1)S(1)}, u32[]{:S(2)}, u32[]{:S(2)}) collective-permute-start(bf16[512,256]{1,0:T(8,128)(2,1)S(1)} %pad_maximum_fusion.18), channel_id=1, source_target_pairs={{0,2},{1,3},{2,0},{3,1},{4,6},{5,7},{6,4},{7,5},{8,10},{9,11},{10,... | collective-permute-start | bytes 786440 | tf_op jit(solution)/shard_map/ppermute | solution.py:895
  31.0 21.6 %collective-permute-start.3 = (bf16[512,256]{1,0:T(8,128)(2,1)S(1)}, bf16[512,256]{1,0:T(8,128)(2,1)S(1)}, u32[]{:S(2)}, u32[]{:S(2)}) collective-permute-start(bf16[512,256]{1,0:T(8,128)(2,1)S(1)} %pad_maximum_fusion.18), channel_id=1, source_target_pairs={{0,1},{1,2},{2,3},{3,0},{4,5},{5,6},{6,7},{7,4},{8,9},{9,10},{10,1... | collective-permute-start | bytes 786440 | tf_op jit(solution)/shard_map/ppermute | solution.py:895
  69.5 25.5 %collective-permute-start.14 = (bf16[2,4,256,256]{3,2,1,0:T(8,128)(2,1)S(1)}, bf16[2,4,256,256]{3,2,1,0:T(8,128)(2,1)}, u32[]{:S(2)}, u32[]{:S(2)}) collective-permute-start(bf16[2,4,256,256]{3,2,1,0:T(8,128)(2,1)S(1)} %pad_maximum_fusion.7.qk_ref), channel_id=1, source_target_pairs={{0,8},{8,0},{1,9},{9,1},{2,10},{10,2},{3,11},{11,3},{4,12},{12,4},... | collective-permute-start | bytes 3145736 | tf_op jit(solution)/shard_map/ppermute | solution.py:830
  71.3 23.7 %collective-permute-start.15 = (bf16[2,4,256,256]{3,2,1,0:T(8,128)(2,1)S(1)}, bf16[2,4,256,256]{3,2,1,0:T(8,128)(2,1)}, u32[]{:S(2)}, u32[]{:S(2)}) collective-permute-start(bf16[2,4,256,256]{3,2,1,0:T(8,128)(2,1)S(1)} %pad_maximum_fusion.8.v_ref), channel_id=1, source_target_pairs={{0,16},{16,0},{1,17},{17,1},{2,18},{18,2},{3,19},{19,3},{4,20},{20... | collective-permute-start | bytes 3145736 | tf_op jit(solution)/shard_map/ppermute | solution.py:830
  74.1 21.0 %collective-permute-start.16 = (bf16[392,1024]{1,0:T(8,128)(2,1)}, bf16[392,1024]{1,0:T(8,128)(2,1)S(1)}, u32[]{:S(2)}, u32[]{:S(2)}) collective-permute-start(bf16[392,1024]{1,0:T(8,128)(2,1)} %get-tuple-element.385), channel_id=1, source_target_pairs={{0,1},{1,0},{2,5},{3,4},{4,3},{5,2},{6,7},{7,6},{8,9},{9,8},{10,13... | collective-permute-start | bytes 2408456 | tf_op jit(solution)/shard_map/ppermute | solution.py:880
  95.1 382.1 %reduce-scatter.2.cloned.1.call-start = ((), (), s32[]{:S(2)}) async-start(), calls=%async_computation.1 | async-start | bytes 2621440 | tf_op jit(solution)/shard_map/reduce_scatter | solution.py:1034
  101.3 33.4 %collective-permute-start.17 = (bf16[256,512]{1,0:T(8,128)(2,1)S(1)}, bf16[256,512]{1,0:T(8,128)(2,1)S(1)}, u32[]{:S(2)}, u32[]{:S(2)}) collective-permute-start(bf16[256,512]{1,0:T(8,128)(2,1)S(1)} %get-tuple-element.186), channel_id=1, source_target_pairs={{0,3},{1,0},{2,1},{3,2},{4,7},{5,4},{6,5},{7,6},{8,11},{9,8},{10,9... | collective-permute-start | bytes 786440 | tf_op jit(solution)/shard_map/ppermute | solution.py:895
  101.4 33.3 %collective-permute-start.18 = (bf16[256,512]{1,0:T(8,128)(2,1)S(1)}, bf16[256,512]{1,0:T(8,128)(2,1)S(1)}, u32[]{:S(2)}, u32[]{:S(2)}) collective-permute-start(bf16[256,512]{1,0:T(8,128)(2,1)S(1)} %get-tuple-element.186), channel_id=1, source_target_pairs={{0,2},{1,3},{2,0},{3,1},{4,6},{5,7},{6,4},{7,5},{8,10},{9,11},{10,... | collective-permute-start | bytes 786440 | tf_op jit(solution)/shard_map/ppermute | solution.py:895
  104.4 30.4 %collective-permute-start.19 = (bf16[256,512]{1,0:T(8,128)(2,1)S(1)}, bf16[256,512]{1,0:T(8,128)(2,1)S(1)}, u32[]{:S(2)}, u32[]{:S(2)}) collective-permute-start(bf16[256,512]{1,0:T(8,128)(2,1)S(1)} %get-tuple-element.186), channel_id=1, source_target_pairs={{0,1},{1,2},{2,3},{3,0},{4,5},{5,6},{6,7},{7,4},{8,9},{9,10},{10,1... | collective-permute-start | bytes 786440 | tf_op jit(solution)/shard_map/ppermute | solution.py:895
  134.8 21.3 %collective-permute-start.21 = (bf16[2,256,512]{2,1,0:T(8,128)(2,1)S(1)}, bf16[2,256,512]{2,1,0:T(8,128)(2,1)S(1)}, u32[]{:S(2)}, u32[]{:S(2)}) collective-permute-start(bf16[2,256,512]{2,1,0:T(8,128)(2,1)S(1)} %pad_maximum_fusion.16), channel_id=1, source_target_pairs={{0,16},{16,0},{1,17},{17,1},{2,18},{18,2},{3,19},{19,3},{4,20},{20... | collective-permute-start | bytes 1572872 | tf_op jit(solution)/shard_map/ppermute | solution.py:830
  136.3 19.8 %collective-permute-start.22 = (bf16[2,256,512]{2,1,0:T(8,128)(2,1)S(1)}, bf16[2,256,512]{2,1,0:T(8,128)(2,1)S(1)}, u32[]{:S(2)}, u32[]{:S(2)}) collective-permute-start(bf16[2,256,512]{2,1,0:T(8,128)(2,1)S(1)} %pad_maximum_fusion.17), channel_id=1, source_target_pairs={{0,8},{8,0},{1,9},{9,1},{2,10},{10,2},{3,11},{11,3},{4,12},{12,4},... | collective-permute-start | bytes 1572872 | tf_op jit(solution)/shard_map/ppermute | solution.py:830
  163.9 37.8 %collective-permute-start.24 = (bf16[2,2,256,512]{3,2,1,0:T(8,128)(2,1)S(1)}, bf16[2,2,256,512]{3,2,1,0:T(8,128)(2,1)}, u32[]{:S(2)}, u32[]{:S(2)}) collective-permute-start(bf16[2,2,256,512]{3,2,1,0:T(8,128)(2,1)S(1)} %pad_maximum_fusion.9), channel_id=1, source_target_pairs={{0,8},{8,0},{1,9},{9,1},{2,10},{10,2},{3,11},{11,3},{4,12},{12,4},... | collective-permute-start | bytes 3145736 | tf_op jit(solution)/shard_map/ppermute | solution.py:830
  165.7 36.1 %collective-permute-start.25 = (bf16[2,2,256,512]{3,2,1,0:T(8,128)(2,1)S(1)}, bf16[2,2,256,512]{3,2,1,0:T(8,128)(2,1)}, u32[]{:S(2)}, u32[]{:S(2)}) collective-permute-start(bf16[2,2,256,512]{3,2,1,0:T(8,128)(2,1)S(1)} %pad_maximum_fusion.10), channel_id=1, source_target_pairs={{0,16},{16,0},{1,17},{17,1},{2,18},{18,2},{3,19},{19,3},{4,20},{20... | collective-permute-start | bytes 3145736 | tf_op jit(solution)/shard_map/ppermute | solution.py:830
  169.7 56.1 %collective-permute-start.27 = (bf16[784,1024]{1,0:T(8,128)(2,1)}, bf16[784,1024]{1,0:T(8,128)(2,1)}, u32[]{:S(2)}, u32[]{:S(2)}) collective-permute-start(bf16[784,1024]{1,0:T(8,128)(2,1)} %add_convert_fusion.x_ref.xa_ref), channel_id=1, source_target_pairs={{0,4},{4,0},{1,5},{5,1},{2,6},{6,2},{3,7},{7,3},{8,12},{12,8},{9,1... | collective-permute-start | bytes 4816904 | tf_op jit(solution)/shard_map/ppermute | solution.py:830
  202.4 23.4 %collective-permute-start.26 = (bf16[392,1024]{1,0:T(8,128)(2,1)}, bf16[392,1024]{1,0:T(8,128)(2,1)S(1)}, u32[]{:S(2)}, u32[]{:S(2)}) collective-permute-start(bf16[392,1024]{1,0:T(8,128)(2,1)} %get-tuple-element.217), channel_id=1, source_target_pairs={{2,4},{3,5},{4,2},{5,3},{10,12},{11,13},{12,10},{13,11},{18,20},{1... | collective-permute-start | bytes 2408456 | tf_op jit(solution)/shard_map/ppermute | solution.py:880
  203.3 37.7 %collective-permute-start.28 = (bf16[392,1024]{1,0:T(8,128)(2,1)}, bf16[392,1024]{1,0:T(8,128)(2,1)S(1)}, u32[]{:S(2)}, u32[]{:S(2)}) collective-permute-start(bf16[392,1024]{1,0:T(8,128)(2,1)} %get-tuple-element.222), channel_id=1, source_target_pairs={{0,1},{1,0},{2,5},{3,4},{4,3},{5,2},{6,7},{7,6},{8,9},{9,8},{10,13... | collective-permute-start | bytes 2408456 | tf_op jit(solution)/shard_map/ppermute | solution.py:880
  311.9 20.7 %collective-permute-start.32 = (bf16[784,1024]{1,0:T(8,128)(2,1)}, bf16[784,1024]{1,0:T(8,128)(2,1)}, u32[]{:S(2)}, u32[]{:S(2)}) collective-permute-start(bf16[784,1024]{1,0:T(8,128)(2,1)} %get-tuple-element.242.da_ref), channel_id=1, source_target_pairs={{0,4},{4,0},{1,5},{5,1},{2,6},{6,2},{3,7},{7,3},{8,12},{12,8},{9,1... | collective-permute-start | bytes 4816904 | tf_op jit(solution)/shard_map/ppermute | solution.py:830
  312.1 19.6 %collective-permute-start.37 = (bf16[392,1024]{1,0:T(8,128)(2,1)S(1)}, bf16[392,1024]{1,0:T(8,128)(2,1)S(1)}, u32[]{:S(2)}, u32[]{:S(2)}) collective-permute-start(bf16[392,1024]{1,0:T(8,128)(2,1)S(1)} %get-tuple-element.384), channel_id=1, source_target_pairs={{4,2},{5,3},{2,4},{3,5},{12,10},{13,11},{10,12},{11,13},{20,18},{2... | collective-permute-start | bytes 2408456 | tf_op jit(solution)/shard_map/ppermute | solution.py:886
  312.8 45.4 %collective-permute-start.35 = (bf16[2,2,256,512]{3,2,1,0:T(8,128)(2,1)}, bf16[2,2,256,512]{3,2,1,0:T(8,128)(2,1)S(1)}, u32[]{:S(2)}, u32[]{:S(2)}) collective-permute-start(bf16[2,2,256,512]{3,2,1,0:T(8,128)(2,1)} %get-tuple-element.254), channel_id=1, source_target_pairs={{0,8},{8,0},{1,9},{9,1},{2,10},{10,2},{3,11},{11,3},{4,12},{12,4},... | collective-permute-start | bytes 3145736 | tf_op jit(solution)/shard_map/ppermute | solution.py:830
  314.3 44.0 %collective-permute-start.36 = (bf16[2,2,256,512]{3,2,1,0:T(8,128)(2,1)}, bf16[2,2,256,512]{3,2,1,0:T(8,128)(2,1)S(1)}, u32[]{:S(2)}, u32[]{:S(2)}) collective-permute-start(bf16[2,2,256,512]{3,2,1,0:T(8,128)(2,1)} %get-tuple-element.255), channel_id=1, source_target_pairs={{0,16},{16,0},{1,17},{17,1},{2,18},{18,2},{3,19},{19,3},{4,20},{20... | collective-permute-start | bytes 3145736 | tf_op jit(solution)/shard_map/ppermute | solution.py:830
  329.9 30.9 %collective-permute-start.33 = (bf16[2,2,256,512]{3,2,1,0:T(8,128)(2,1)}, bf16[2,2,256,512]{3,2,1,0:T(8,128)(2,1)S(1)}, u32[]{:S(2)}, u32[]{:S(2)}) collective-permute-start(bf16[2,2,256,512]{3,2,1,0:T(8,128)(2,1)} %get-tuple-element.252), channel_id=1, source_target_pairs={{0,8},{8,0},{1,9},{9,1},{2,10},{10,2},{3,11},{11,3},{4,12},{12,4},... | collective-permute-start | bytes 3145736 | tf_op jit(solution)/shard_map/ppermute | solution.py:830
  332.6 29.9 %collective-permute-start.34 = (bf16[2,2,256,512]{3,2,1,0:T(8,128)(2,1)}, bf16[2,2,256,512]{3,2,1,0:T(8,128)(2,1)S(1)}, u32[]{:S(2)}, u32[]{:S(2)}) collective-permute-start(bf16[2,2,256,512]{3,2,1,0:T(8,128)(2,1)} %get-tuple-element.253), channel_id=1, source_target_pairs={{0,16},{16,0},{1,17},{17,1},{2,18},{18,2},{3,19},{19,3},{4,20},{20... | collective-permute-start | bytes 3145736 | tf_op jit(solution)/shard_map/ppermute | solution.py:830
  332.6 55.7 %collective-permute-start.42 = (bf16[392,1024]{1,0:T(8,128)(2,1)S(1)}, bf16[392,1024]{1,0:T(8,128)(2,1)S(1)}, u32[]{:S(2)}, u32[]{:S(2)}) collective-permute-start(bf16[392,1024]{1,0:T(8,128)(2,1)S(1)} %get-tuple-element.383), channel_id=1, source_target_pairs={{1,0},{0,1},{5,2},{4,3},{3,4},{2,5},{7,6},{6,7},{9,8},{8,9},{13,10... | collective-permute-start | bytes 2408456 | tf_op jit(solution)/shard_map/ppermute | solution.py:886
  367.5 20.8 %collective-permute-start.38 = (bf16[2,256,512]{2,1,0:T(8,128)(2,1)}, bf16[2,256,512]{2,1,0:T(8,128)(2,1)S(1)}, u32[]{:S(2)}, u32[]{:S(2)}) collective-permute-start(bf16[2,256,512]{2,1,0:T(8,128)(2,1)} %get-tuple-element.266), channel_id=1, source_target_pairs={{0,16},{16,0},{1,17},{17,1},{2,18},{18,2},{3,19},{19,3},{4,20},{20... | collective-permute-start | bytes 1572872 | tf_op jit(solution)/shard_map/ppermute | solution.py:830
  370.6 20.1 %collective-permute-start.40 = (bf16[2,256,512]{2,1,0:T(8,128)(2,1)}, bf16[2,256,512]{2,1,0:T(8,128)(2,1)S(1)}, u32[]{:S(2)}, u32[]{:S(2)}) collective-permute-start(bf16[2,256,512]{2,1,0:T(8,128)(2,1)} %get-tuple-element.268), channel_id=1, source_target_pairs={{0,16},{16,0},{1,17},{17,1},{2,18},{18,2},{3,19},{19,3},{4,20},{20... | collective-permute-start | bytes 1572872 | tf_op jit(solution)/shard_map/ppermute | solution.py:830
  370.7 23.3 %collective-permute-start.41 = (bf16[2,256,512]{2,1,0:T(8,128)(2,1)}, bf16[2,256,512]{2,1,0:T(8,128)(2,1)S(1)}, u32[]{:S(2)}, u32[]{:S(2)}) collective-permute-start(bf16[2,256,512]{2,1,0:T(8,128)(2,1)} %get-tuple-element.269), channel_id=1, source_target_pairs={{0,8},{8,0},{1,9},{9,1},{2,10},{10,2},{3,11},{11,3},{4,12},{12,4},... | collective-permute-start | bytes 1572872 | tf_op jit(solution)/shard_map/ppermute | solution.py:830
  402.5 25.4 %collective-permute-start.43 = (bf16[2,5,256,128]{3,2,1,0:T(8,128)(2,1)S(1)}, bf16[2,5,256,128]{3,2,1,0:T(8,128)(2,1)S(1)}, u32[]{:S(2)}, u32[]{:S(2)}) collective-permute-start(bf16[2,5,256,128]{3,2,1,0:T(8,128)(2,1)S(1)} %pad_maximum_fusion.11), channel_id=1, source_target_pairs={{0,8},{8,0},{1,9},{9,1},{2,10},{10,2},{3,11},{11,3},{4,12},{12,4},... | collective-permute-start | bytes 1966088 | tf_op jit(solution)/shard_map/ppermute | solution.py:830
  406.0 21.9 %collective-permute-start.44 = (bf16[2,5,256,128]{3,2,1,0:T(8,128)(2,1)S(1)}, bf16[2,5,256,128]{3,2,1,0:T(8,128)(2,1)S(1)}, u32[]{:S(2)}, u32[]{:S(2)}) collective-permute-start(bf16[2,5,256,128]{3,2,1,0:T(8,128)(2,1)S(1)} %pad_maximum_fusion.12), channel_id=1, source_target_pairs={{0,16},{16,0},{1,17},{17,1},{2,18},{18,2},{3,19},{19,3},{4,20},{20... | collective-permute-start | bytes 1966088 | tf_op jit(solution)/shard_map/ppermute | solution.py:830
  428.0 21.6 %collective-permute-start.45 = (bf16[5,256,128]{2,1,0:T(8,128)(2,1)S(1)}, bf16[5,256,128]{2,1,0:T(8,128)(2,1)S(1)}, u32[]{:S(2)}, u32[]{:S(2)}) collective-permute-start(bf16[5,256,128]{2,1,0:T(8,128)(2,1)S(1)} %fusion.5), channel_id=1, source_target_pairs={{0,16},{16,0},{1,17},{17,1},{2,18},{18,2},{3,19},{19,3},{4,20},{20... | collective-permute-start | bytes 983048 | tf_op jit(solution)/shard_map/ppermute | solution.py:830
  498.4 33.4 %collective-permute-start.58 = (bf16[392,1024]{1,0:T(8,128)(2,1)}, bf16[392,1024]{1,0:T(8,128)(2,1)}, u32[]{:S(2)}, u32[]{:S(2)}) collective-permute-start(bf16[392,1024]{1,0:T(8,128)(2,1)} %get-tuple-element.327), channel_id=1, source_target_pairs={{1,0},{0,1},{5,2},{4,3},{3,4},{2,5},{7,6},{6,7},{9,8},{8,9},{13,10... | collective-permute-start | bytes 2408456 | tf_op jit(solution)/shard_map/ppermute | solution.py:886
  504.9 29.7 %collective-permute-start.64 = (f32[20,128]{1,0:T(8,128)S(1)}, f32[20,128]{1,0:T(8,128)S(1)}, u32[]{:S(2)}, u32[]{:S(2)}) collective-permute-start(f32[20,128]{1,0:T(8,128)S(1)} %fusion.37), channel_id=1, source_target_pairs={{0,3},{1,0},{2,1},{3,2},{4,7},{5,4},{6,5},{7,6},{8,11},{9,8},{10,9... | collective-permute-start | bytes 30728 | tf_op jit(solution)/shard_map/ppermute | solution.py:1084
  (100 other events, 1088.4 us)
Sparse Core Ops, SparseCore 0:
  95.2 107.1 all-gather.2
  411.3 41.5 reduce-scatter.1

commit v6 on v5

--- a/solution.py
+++ b/solution.py
@@ -491,34 +491,36 @@
     return d_heads, delta, (keep_a, keep_b), (send_a, send_b)
 
 
-def project_grad_kernel(bits_ref, t_ref, da_ref, db_ref, *refs):
-    cols = da_ref.shape[2]
-    grad = dot(t_ref[...], jnp.concatenate([da_ref[0], db_ref[0]], 1)).astype(BF)
+def project_grad_kernel(bits_ref, t_ref, *refs):
+    *d_refs, _, _, _, _ = refs
+    refs = refs[-4:]
+    cols = refs[0].shape[3]
+    grad = dot(t_ref[...], jnp.concatenate([ref[0] for ref in d_refs], 1)).astype(BF)
     for p in range(PAIR):
         put_halves(bits_ref, grad[:, p * cols : (p + 1) * cols], p, refs[2 * p], refs[2 * p + 1], (slice(None), 0))
 
 
-def project_grads(bits, turned, da, db):
+def project_grads(bits, turned, *pieces):
     width, seq = turned.shape
-    cols = da.shape[2]
-    piece = pl.BlockSpec((1, seq, cols), lambda i, bits: (i, 0, 0))
+    cols = sum(piece.shape[2] for piece in pieces) // PAIR
+    specs = [pl.BlockSpec((1, seq, piece.shape[2]), lambda i, bits: (i, 0, 0)) for piece in pieces]
     grad = pl.BlockSpec((2, 1, width // 4, cols), lambda i, bits: (0, i, 0, 0))
     keep_a, send_a, keep_b, send_b = call(
         project_grad_kernel,
         (3,),
-        [pl.BlockSpec((width, seq), lambda i, bits: (0, 0)), piece, piece],
+        [pl.BlockSpec((width, seq), lambda i, bits: (0, 0))] + specs,
         [grad] * 4,
         [shaped((2, 3, width // 4, cols))] * 4,
-        (bits, turned, da, db),
+        (bits, turned, *pieces),
         name="project_grads",
         prefetch=1,
     )
     return (keep_a, keep_b), (send_a, send_b)
 
 
-def project_back_kernel(a_ref, b_ref, c_ref, d_ref, qk_ref, v_ref, out_ref):
+def project_back_kernel(a_ref, c_ref, d_ref, qk_ref, v_ref, out_ref):
     total = None
-    for first, refs in ((0, (a_ref, b_ref)), (PAIR, (c_ref, d_ref))):
+    for first, refs in ((0, (a_ref,)), (PAIR, (c_ref, d_ref))):
         places = [first + p for p in range(PAIR)]
         left = [ref[i] for i in range(3) for ref in refs]
         right = [qk_ref[0, place, i] for i in range(2) for place in places] + [v_ref[0, place] for place in places]
@@ -534,7 +536,7 @@
     return call(
         project_back_kernel,
         (owners,),
-        [pl.BlockSpec((3, half, cols), lambda n: (0, which, 0)) for piece in pieces]
+        [pl.BlockSpec((3, half, piece.shape[2]), lambda n: (0, which, 0)) for piece in pieces]
         + [
             pl.BlockSpec((1, places, 2, cols, part), lambda n: (turned_owner(n), 0, 0, 0, 0)),
             pl.BlockSpec((1, places, cols, part), lambda n: (n, 0, 0, 0)),
@@ -991,17 +993,18 @@
     centred_two, scale_two = moments(hidden)
     second = (centred_two * scale_two * gains[1] + shift_all[1]).astype(BF)
     second_other = swap(second, "c")
-    swapped, second = together(swapped, second)
+    swapped, second, w_qk = together(swapped, second, w_qk)
     up_a = ordered(x, up_a[None], swapped[0][None], 0).reshape(4, PAIR, 2 * dims, units)
     up_b = ordered(y, up_b[None], swapped[1][None], 0).reshape(4, PAIR, 2 * dims, units)
     up_all = up_a, up_b
     targets, second, down_all = together(targets, second, down_all)
     near, far = sent(targets)
-    out_mine, act_mine, slope_mine = ffn_forward(place, second, up_all, down_all, up_shift, F32)
-    out_mine, near = together(out_mine, near)
-    out_other, act_other, slope_other = ffn_forward(place, after(second_other, near), up_all, down_all, up_shift, BF)
-    out_other, far = together(out_other, far)
-    output = hidden + (out_mine + swap(out_other, "c").astype(F32)) + shift_all[3]
+    out_other, act_other, slope_other = ffn_forward(place, second_other, up_all, down_all, up_shift, BF)
+    out_other, near = together(out_other, near)
+    out_swapped = swap(out_other, "c")
+    out_mine, act_mine, slope_mine = ffn_forward(place, after(second, near), up_all, down_all, up_shift, F32)
+    out_mine, far, out_swapped = together(out_mine, far, out_swapped)
+    output = hidden + (out_mine + out_swapped.astype(F32)) + shift_all[3]
     d_out = output - on_chip(teacher, near, far).astype(F32)
     d_ffn = d_out.astype(BF)
     d_ffn_other = swap(d_ffn, "c")
@@ -1036,18 +1039,17 @@
     one = scatter_start([jnp.concatenate(pair, 1) for pair in zip(sends, sends_o)])
     grad_one = list(zip(grad_one, grad_o))
     delta, grad_ff, grad_one = together(delta, grad_ff, grad_one)
-    back_c, sum_c = attend_backward(qkv, after(d_heads, back_b), lse, delta, 0, 2, 2, 256)
+    back_c, sum_c = attend_backward(qkv, after(d_heads, back_b), lse, delta, 0, 0, 4, 256)
     one, back_c = together(one, back_c)
     one_ends = scatter_middle(grad_one, one)
-    back_d, sum_d = attend_backward(qkv, after(d_heads, back_c), lse, delta, 0, 0, 2, 256)
-    one_ends, back_d = together(one_ends, back_d)
-    grad_two, sends = project_grads(bits, turned, back_d, back_c)
+    grad_two, sends = project_grads(bits, turned, back_c)
     two = scatter_start(sends)
-    pieces = (back_d, back_c, back_a, back_b)
+    one_ends, grad_two = together(one_ends, grad_two)
+    one = [part for part in scatter_end(grad_one, one, one_ends)]
+    early = [lax.ppermute(jnp.concatenate([one[p][:3], one[p][4:]]), "t", rings[PAIR + p]) for p in range(PAIR)]
+    pieces = (back_c, back_a, back_b)
     d_first_other = project_back(pieces, w_qk, after(w_vo, grad_two), 1)
     d_first_swapped = swap(d_first_other, "c")
-    one = scatter_end(grad_one, one, one_ends)
-    early = [lax.ppermute(jnp.concatenate([one[p][:3], one[p][4:]]), "t", rings[PAIR + p]) for p in range(PAIR)]
     two, d_first_other = together(two, d_first_other)
     two_ends = scatter_middle([[keep] for keep in grad_two], two)
     d_first = project_back(pieces, w_qk, after(w_vo, d_first_other), 0)
@@ -1056,10 +1058,10 @@
     *d_inputs, sums_one = norm_backward(d_first, d_first_swapped, inputs, d_hidden, gains[0], True)
     early, sums_one = together(early, sums_one)
     grad_near, grad_far = sent_back(*d_inputs)
-    small = (sum_a, sum_b, sum_c, sum_d, up_sum, sums_one)
+    small = (sum_a, sum_b, sum_c, up_sum, sums_one)
     small, d_inputs = together(small, d_inputs)
     two_ends, grad_near, out_near, out_far = together(two_ends, grad_near, out_near, out_far)
-    sum_a, sum_b, sum_c, sum_d, up_sum, sums_one = small
+    sum_a, sum_b, sum_c, up_sum, sums_one = small
     two = scatter_end([[keep] for keep in grad_two], two, two_ends)
     late = lax.ppermute(jnp.concatenate([two[1], one[1][3:4]]), "t", rings[1])
 
@@ -1069,7 +1071,7 @@
     grad_attn = sum((part.astype(F32) for part in (*early, late)), grad_attn).reshape(4, 2, dims, cols)
     grad_attn = ordered(c, chosen(grad_attn, c, 1), swap(chosen(grad_attn, 1 - c, 1), "c"), 2)
 
-    heads_sum = jnp.concatenate([sum_d, sum_c, sum_a, sum_b], 2).reshape(3, steps, 4, lane)
+    heads_sum = jnp.concatenate([sum_c, sum_a, sum_b], 2).reshape(3, steps, 4, lane)
     heads_sum = placed(jnp.stack([heads_sum[0], heads_sum[2]]), 1)
     heads_sum = jnp.pad(heads_sum, ((0, 0), (0, 0), (0, 0), (0, dims - lane))).reshape(2 * steps, 4 * dims)
     own = jnp.concatenate([heads_sum, up_sum])

time: 554 us -> 551 us (level)
    ppermute x42, waiting for transfers between devices: 61.8 us -> 52.4 us  [swap(): return lax.ppermute(value, axis, [(0, 1), (1, 0)])]
    ppermute x42, starting transfers between devices: 54.8 us -> 49.1 us  [swap(): return lax.ppermute(value, axis, [(0, 1), (1, 0)])]
    pallas_call x24 -> x23, Pallas kernels: 267 us -> 265 us  [call(): pl.pallas_call(body, grid_spec=pltpu.PrefetchScalarGridSpec(num_scalar_pr...]
  transfers between devices with their start and end apart: 67 -> 67, of which waited for: 21 -> 21; matrix products, arithmetic and copies ran while one was open for 9% -> 10% of each run, Pallas kernels for 43% -> 43%
where the time goes in v6:
time: 551 us; the launch traced here: 544 us
  Pallas kernels  265 us (48%)
  waiting for transfers between devices  96.4 us (17%)
  starting transfers between devices  91.5 us (17%)
  other arithmetic  50.4 us (9%)
  local copies, waits for them, and re-layouts  24.9 us (5%)
  between operations  15.7 us (3%)
    pallas_call x23, Pallas kernels, call(): pl.pallas_call(body, grid_spec=pltpu.PrefetchScalarGridSpec(num_scalar_pr...  265 us
    ppermute x42, waiting for transfers between devices, swap(): return lax.ppermute(value, axis, [(0, 1), (1, 0)])  52.4 us
    ppermute x42, starting transfers between devices, swap(): return lax.ppermute(value, axis, [(0, 1), (1, 0)])  49.1 us
    ppermute x9, waiting for transfers between devices, ring_gather(): lax.ppermute(value, 't', rings[-j % steps])  24.4 us
    ppermute x3, starting transfers between devices, clip_local(): lax.ppermute(sums, 't', rings[away])  19.4 us
    ppermute x2, waiting for transfers between devices, sent(): lax.ppermute(pair[1], every, second_way)  14.6 us
    ppermute x9, starting transfers between devices, ring_gather(): lax.ppermute(value, 't', rings[-j % steps])  11.2 us
  transfers between devices with their start and end apart: 67, of which 21 were waited for; matrix products, arithmetic and copies ran while one was open for 10% of the time, Pallas kernels for 43%

profile of v6, /device:TPU:0, one launch (start us, length us, event | category | flops | bytes accessed | tf_op | source)
XLA Modules:
  0.0 544.1 jit_solution(1665226918208539163)
XLA Ops:
  33.0 4.5 collective-permute-done.1
  37.5 15.2 %collective-permute-done.2 = bf16[512,256]{1,0:T(8,128)(2,1)S(1)} collective-permute-done((bf16[512,256]{1,0:T(8,128)(2,1)S(1)}, bf16[512,256]{1,0:T(8,128)(2,1)S(1)}, u32[]{:S(2)}, u32[]{:S(2)}) %collective-permute-start.2) | collective-permute-done | bytes 262176 | tf_op jit(solution)/shard_map/ppermute | solution.py:897
  58.9 9.9 %collective-permute-done.4 = bf16[4,256,256]{2,1,0:T(8,128)(2,1)S(1)} collective-permute-done((bf16[4,256,256]{2,1,0:T(8,128)(2,1)}, bf16[4,256,256]{2,1,0:T(8,128)(2,1)S(1)}, u32[]{:S(2)}, u32[]{:S(2)}) %collective-permute-start.4) | collective-permute-done | bytes 524320 | tf_op jit(solution)/shard_map/ppermute | solution.py:832
  85.3 9.9 %collective-permute-done.16 = bf16[392,1024]{1,0:T(8,128)(2,1)S(1)} collective-permute-done((bf16[392,1024]{1,0:T(8,128)(2,1)}, bf16[392,1024]{1,0:T(8,128)(2,1)S(1)}, u32[]{:S(2)}, u32[]{:S(2)}) %collective-permute-start.16) | collective-permute-done | bytes 802848 | tf_op jit(solution)/shard_map/ppermute | solution.py:882
  106.6 11.9 %project.1 = (bf16[2,3,4,64,1568]{4,3,2,1,0:T(8,128)(2,1)}, bf16[1024,1568]{1,0:T(8,128)(2,1)}) custom-call(s32[2]{0:T(128)} %pad_add_fusion.bits_ref, bf16[784,1024]{1,0:T(8,128)(2,1)} %copy-done.15, bf16[784,1024]{1,0:T(8,128)(2,1)} %collective-permute-done.20.xb_ref, bf16[2,4,256,256]{3,2,1,0:T(8,128)(2,1)} %copy-done.10, ...), custom_call_target="tpu_custom_call" | custom-call | flops 1000 | bytes 1000 | tf_op jit(solution)/shard_map/project/pallas_call | solution.py:194
  118.6 16.2 %attend.2 = (bf16[8,64,1568]{2,1,0:T(8,128)(2,1)}, bf16[1568,512]{1,0:T(8,128)(2,1)}, f32[8,64,1568]{2,1,0:T(8,128)}, f32[8,1,1568]{2,1,0:T(1,128)}) custom-call(bf16[2,3,4,64,1568]{4,3,2,1,0:T(8,128)(2,1)} %get-tuple-element.190.q_ref.k_ref.v_ref, bf16[2,3,4,64,1568]{4,3,2,1,0:T(8,128)(2,1)} %get-tuple-element.190.q_ref.k_ref.v_ref, ...), custom_call_target="tpu_custom_call" | custom-call | flops 1000 | bytes 1000 | tf_op jit(solution)/shard_map/attend/pallas_call | solution.py:194
  136.9 16.3 %attend.3 = (bf16[8,64,1568]{2,1,0:T(8,128)(2,1)}, bf16[1568,512]{1,0:T(8,128)(2,1)}, f32[8,64,1568]{2,1,0:T(8,128)}, f32[8,1,1568]{2,1,0:T(1,128)}) custom-call(bf16[2,3,4,64,1568]{4,3,2,1,0:T(8,128)(2,1)} %get-tuple-element.190.q_ref.k_ref.v_ref, ...), custom_call_target="tpu_custom_call", output_to_operand_aliasing={{0}: (3, {}), {1}: (4, {}), {2}: (5, {}), {3}: (6, {})} | custom-call | flops 1000 | bytes 1000 | tf_op jit(solution)/shard_map/attend/pallas_call | solution.py:194
  163.4 4.1 mix.3
  175.6 24.8 %collective-permute-done.24 = bf16[2,2,256,512]{3,2,1,0:T(8,128)(2,1)} collective-permute-done((bf16[2,2,256,512]{3,2,1,0:T(8,128)(2,1)S(1)}, bf16[2,2,256,512]{3,2,1,0:T(8,128)(2,1)}, u32[]{:S(2)}, u32[]{:S(2)}) %collective-permute-start.24) | collective-permute-done | bytes 1048608 | tf_op jit(solution)/shard_map/ppermute | solution.py:832
  201.9 4.0 all-gather.3.cloned.1.call-done
  212.8 15.1 %ffn.2 = (bf16[784,1024]{1,0:T(8,128)(2,1)}, bf16[784,2048]{1,0:T(8,128)(2,1)}, bf16[784,2048]{1,0:T(8,128)(2,1)}) custom-call(s32[1]{0:T(128)} %bitcast.51.place_ref, bf16[784,1024]{1,0:T(8,128)(2,1)} %collective-permute-done.26.x_ref.xb_ref, bf16[4,2,256,512]{3,2,1,0:T(8,128)(2,1)} %bitcast.223, bf16[4,2,256,512]{3,2,1,0:T(8,128)(2,1)} %bitcast.227, ...), custom_call_target="tpu_custom_call" | custom-call | flops 1000 | bytes 1000 | tf_op jit(solution)/shard_map/ffn/pallas_call | solution.py:194
  231.7 15.5 %ffn.3 = (f32[784,1024]{1,0:T(8,128)}, bf16[784,2048]{1,0:T(8,128)(2,1)}, bf16[784,2048]{1,0:T(8,128)(2,1)}) custom-call(s32[1]{0:T(128)} %bitcast.51.place_ref, bf16[784,1024]{1,0:T(8,128)(2,1)} %add_convert_fusion.x_ref.xa_ref, bf16[4,2,256,512]{3,2,1,0:T(8,128)(2,1)} %bitcast.224, bf16[4,2,256,512]{3,2,1,0:T(8,128)(2,1)} %bitcast.228, ...), custom_call_target="tpu_custom_call" | custom-call | flops 1000 | bytes 1000 | tf_op jit(solution)/shard_map/ffn/pallas_call | solution.py:194
  247.3 4.7 collective-permute-done.28
  253.1 5.6 %fusion.46 = (bf16[784,1024]{1,0:T(8,128)(2,1)S(1)}, f32[784,1024]{1,0:T(8,128)}, bf16[784,1024]{1,0:T(8,128)(2,1)S(1)}) fusion(bf16[392,1024]{1,0:T(8,128)(2,1)} %collective-permute-done.28, bf16[392,1024]{1,0:T(8,128)(2,1)S(1)} %broadcast_select_fusion.2, f32[1024]{0:T(1024)S(1)} %bitcast.253, f32[784,1024]{1,0:T(8,128)S(1)} %get-tuple-element.367.x_ref, ...), kind=kLoop, calls=%fused_computation.219 | loop fusion | flops 8830976 | bytes 16060416 | tf_op jit(solution)/shard_map/convert_element_type | solution.py:1009
  259.9 13.7 %ffn_backward.2 = (f32[784,1024]{1,0:T(8,128)}, bf16[784,2048]{1,0:T(8,128)(2,1)}, f32[4,1,512]{2,1,0:T(1,128)}) custom-call(s32[1]{0:T(128)} %bitcast.51.place_ref, bf16[784,1024]{1,0:T(8,128)(2,1)} %copy-done.7, bf16[4,4,256,512]{3,2,1,0:T(8,128)(2,1)} %bitcast.221, bf16[4,2,256,512]{3,2,1,0:T(8,128)(2,1)} %bitcast.225, ...), custom_call_target="tpu_custom_call" | custom-call | flops 1000 | bytes 1000 | tf_op jit(solution)/shard_map/ffn_backward/pallas_call | solution.py:194
  274.8 13.4 %ffn_backward.3 = (bf16[784,1024]{1,0:T(8,128)(2,1)}, bf16[784,2048]{1,0:T(8,128)(2,1)}, f32[4,1,512]{2,1,0:T(1,128)}) custom-call(s32[1]{0:T(128)} %bitcast.51.place_ref, bf16[784,1024]{1,0:T(8,128)(2,1)} %copy-done.14, bf16[4,4,256,512]{3,2,1,0:T(8,128)(2,1)} %bitcast.222, bf16[4,2,256,512]{3,2,1,0:T(8,128)(2,1)} %bitcast.226, ...), custom_call_target="tpu_custom_call" | custom-call | flops 1000 | bytes 1000 | tf_op jit(solution)/shard_map/ffn_backward/pallas_call | solution.py:194
  288.2 14.4 %ffn_grad.2 = (bf16[2,2,256,512]{3,2,1,0:T(8,128)(2,1)}, bf16[2,2,256,512]{3,2,1,0:T(8,128)(2,1)}, bf16[2,2,256,512]{3,2,1,0:T(8,128)(2,1)}, bf16[2,2,256,512]{3,2,1,0:T(8,128)(2,1)}) custom-call(s32[2]{0:T(128)} %pad_add_fusion.bits_ref, bf16[784,1024]{1,0:T(8,128)(2,1)} %copy-done.7, bf16[784,1024]{1,0:T(8,128)(2,1)} %copy-done.14, ...), custom_call_target="tpu_custom_call" | custom-call | flops 1000 | bytes 1000 | tf_op jit(solution)/shard_map/ffn_grad/pallas_call | solution.py:194
  303.8 9.4 %norm_backward.2 = (f32[784,1024]{1,0:T(8,128)}, bf16[784,1024]{1,0:T(8,128)(2,1)}, f32[8,1024]{1,0:T(8,128)}) custom-call(f32[784,1024]{1,0:T(8,128)} %get-tuple-element.238.da_ref, bf16[784,1024]{1,0:T(8,128)(2,1)} %copy-done.29, f32[784,1024]{1,0:T(8,128)} %copy-done, f32[784,1024]{1,0:T(8,128)} %get-tuple-element.365.rest_ref, f32[1,1024]{1,0:T(1,128)} %copy-done.57), custom_call_target="tpu_custom_call" | custom-call | flops 1000 | bytes 1000 | tf_op jit(solution)/shard_map/norm_backward/pallas_call | solution.py:194
  316.7 14.3 %ffn_grad.3 = (bf16[2,2,256,512]{3,2,1,0:T(8,128)(2,1)}, bf16[2,2,256,512]{3,2,1,0:T(8,128)(2,1)}, bf16[2,2,256,512]{3,2,1,0:T(8,128)(2,1)}, bf16[2,2,256,512]{3,2,1,0:T(8,128)(2,1)}) custom-call(s32[2]{0:T(128)} %pad_add_fusion.bits_ref, bf16[784,1024]{1,0:T(8,128)(2,1)} %add_convert_fusion.x_ref.xa_ref, ...), custom_call_target="tpu_custom_call" | custom-call | flops 1000 | bytes 1000 | tf_op jit(solution)/shard_map/ffn_grad/pallas_call | solution.py:194
  334.4 9.1 %mix_back.1 = (bf16[8,64,1568]{2,1,0:T(8,128)(2,1)}, f32[8,1,1568]{2,1,0:T(1,128)}, bf16[2,2,256,128]{3,2,1,0:T(8,128)(2,1)}, bf16[2,2,256,128]{3,2,1,0:T(8,128)...) custom-call(s32[2]{0:T(128)} %pad_add_fusion.bits_ref, ...), custom_call_target="tpu_custom_call" | custom-call | flops 1000 | bytes 1000 | tf_op jit(solution)/shard_map/mix_back/pallas_call | solution.py:194
  343.4 16.3 %attend_backward.3 = (bf16[3,1568,128]{2,1,0:T(8,128)(2,1)}, f32[3,1,128]{2,1,0:T(1,128)}) custom-call(bf16[2,3,4,64,1568]{4,3,2,1,0:T(8,128)(2,1)} %get-tuple-element.190.q_ref.k_ref.v_ref, bf16[2,3,4,64,1568]{4,3,2,1,0:T(8,128)(2,1)} %get-tuple-element.190.q_ref.k_ref.v_ref, bf16[2,3,4,64,1568]{4,3,2,1,0:T(8,128)(2,1)} %get-tuple-element.190.q_ref.k_ref.v_ref, ...), custom_call_target="tpu_custom_call" | custom-call | flops 1000 | bytes 1000 | tf_op jit(solution)/shard_map/attend_backward/pallas_call | solution.py:194
  364.4 4.0 add_middle.1
  372.5 16.6 %attend_backward.4 = (bf16[3,1568,128]{2,1,0:T(8,128)(2,1)}, f32[3,1,128]{2,1,0:T(1,128)}) custom-call(bf16[2,3,4,64,1568]{4,3,2,1,0:T(8,128)(2,1)} %get-tuple-element.190.q_ref.k_ref.v_ref, bf16[2,3,4,64,1568]{4,3,2,1,0:T(8,128)(2,1)} %get-tuple-element.190.q_ref.k_ref.v_ref, bf16[2,3,4,64,1568]{4,3,2,1,0:T(8,128)(2,1)} %get-tuple-element.190.q_ref.k_ref.v_ref, ...), custom_call_target="tpu_custom_call" | custom-call | flops 1000 | bytes 1000 | tf_op jit(solution)/shard_map/attend_backward/pallas_call | solution.py:194
  389.2 4.5 collective-permute-done.40.refs_8_
  396.4 7.4 %project_grads.2 = (bf16[2,3,256,128]{3,2,1,0:T(8,128)(2,1)}, bf16[2,3,256,128]{3,2,1,0:T(8,128)(2,1)}, bf16[2,3,256,128]{3,2,1,0:T(8,128)(2,1)}, bf16[2,3,256,128]{3,2,1,0:T(8,128)(2,1)}) custom-call(s32[2]{0:T(128)} %pad_add_fusion.bits_ref, bf16[1024,1568]{1,0:T(8,128)(2,1)} %get-tuple-element.278.t_ref, ...), custom_call_target="tpu_custom_call" | custom-call | flops 1000 | bytes 1000 | tf_op jit(solution)/shard_map/project_grads/pallas_call | solution.py:194
  408.0 5.0 add_end.1
  413.1 30.8 %attend_backward.5 = (bf16[3,1568,256]{2,1,0:T(8,128)(2,1)}, f32[3,1,256]{2,1,0:T(1,128)}) custom-call(bf16[2,3,4,64,1568]{4,3,2,1,0:T(8,128)(2,1)} %get-tuple-element.190.q_ref.k_ref.v_ref, bf16[2,3,4,64,1568]{4,3,2,1,0:T(8,128)(2,1)} %get-tuple-element.190.q_ref.k_ref.v_ref, bf16[2,3,4,64,1568]{4,3,2,1,0:T(8,128)(2,1)} %get-tuple-element.190.q_ref.k_ref.v_ref, ...), custom_call_target="tpu_custom_call" | custom-call | flops 1000 | bytes 1000 | tf_op jit(solution)/shard_map/attend_backward/pallas_call | solution.py:194
  446.6 7.3 %project_grads.3 = (bf16[2,3,256,128]{3,2,1,0:T(8,128)(2,1)}, bf16[2,3,256,128]{3,2,1,0:T(8,128)(2,1)}, bf16[2,3,256,128]{3,2,1,0:T(8,128)(2,1)}, bf16[2,3,256,128]{3,2,1,0:T(8,128)(2,1)}) custom-call(s32[2]{0:T(128)} %pad_add_fusion.bits_ref, bf16[1024,1568]{1,0:T(8,128)(2,1)} %get-tuple-element.278.t_ref, ...), custom_call_target="tpu_custom_call" | custom-call | flops 1000 | bytes 1000 | tf_op jit(solution)/shard_map/project_grads/pallas_call | solution.py:194
  454.7 6.7 %project_back.2 = f32[784,1024]{1,0:T(8,128)} custom-call(bf16[3,1568,256]{2,1,0:T(8,128)(2,1)} %get-tuple-element.297.refs_0_.a_ref, bf16[3,1568,128]{2,1,0:T(8,128)(2,1)} %get-tuple-element.271.refs_0_.c_ref, bf16[3,1568,128]{2,1,0:T(8,128)(2,1)} %get-tuple-element.279.refs_1_.d_ref, bf16[4,4,2,128,256]{4,3,2,1,0:T(8,128)(2,1)} %bitcast.231, ...), custom_call_target="tpu_custom_call" | custom-call | flops 1000 | bytes 1000 | tf_op jit(solution)/shard_map/project_back/pallas_call | solution.py:194
  466.2 6.9 %project_back.3.da_ref = f32[784,1024]{1,0:T(8,128)} custom-call(bf16[3,1568,256]{2,1,0:T(8,128)(2,1)} %get-tuple-element.297.refs_0_.a_ref, bf16[3,1568,128]{2,1,0:T(8,128)(2,1)} %get-tuple-element.271.refs_0_.c_ref, bf16[3,1568,128]{2,1,0:T(8,128)(2,1)} %get-tuple-element.279.refs_1_.d_ref, bf16[4,4,2,128,256]{4,3,2,1,0:T(8,128)(2,1)} %bitcast.232, ...), custom_call_target="tpu_custom_call" | custom-call | flops 1000 | bytes 1000 | tf_op jit(solution)/shard_map/project_back/pallas_call | solution.py:194
  474.0 7.4 %norm_backward.3 = (bf16[392,1024]{1,0:T(8,128)(2,1)}, bf16[392,1024]{1,0:T(8,128)(2,1)}, f32[8,1024]{1,0:T(8,128)}) custom-call(f32[784,1024]{1,0:T(8,128)} %project_back.3.da_ref, f32[784,1024]{1,0:T(8,128)} %collective-permute-done.51.db_ref, f32[784,1024]{1,0:T(8,128)} %fusion.45.x_ref, f32[784,1024]{1,0:T(8,128)} %get-tuple-element.311.rest_ref, ...), custom_call_target="tpu_custom_call" | custom-call | flops 1000 | bytes 1000 | tf_op jit(solution)/shard_map/norm_backward/pallas_call | solution.py:194
  501.6 18.8 %collective-permute-start.64 = (f32[20,128]{1,0:T(8,128)S(1)}, f32[20,128]{1,0:T(8,128)S(1)}, u32[]{:S(2)}, u32[]{:S(2)}) collective-permute-start(f32[20,128]{1,0:T(8,128)S(1)} %fusion.37), channel_id=1, source_target_pairs={{0,3},{1,0},{2,1},{3,2},{4,7},{5,4},{6,5},{7,6},{8,11},{9,8},{10,9... | collective-permute-start | bytes 30728 | tf_op jit(solution)/shard_map/ppermute | solution.py:1086
  (413 shorter events, 164.6 us)
Async XLA Ops:
  7.2 198.7 %all-gather.3.cloned.1.call-start = ((), (), s32[]{:S(2)}) async-start(), calls=%async_computation.2 | async-start | bytes 4456448 | tf_op jit(solution)/shard_map/all_gather | solution.py:969
  30.5 22.2 %collective-permute-start.2 = (bf16[512,256]{1,0:T(8,128)(2,1)S(1)}, bf16[512,256]{1,0:T(8,128)(2,1)S(1)}, u32[]{:S(2)}, u32[]{:S(2)}) collective-permute-start(bf16[512,256]{1,0:T(8,128)(2,1)S(1)} %pad_maximum_fusion.18), channel_id=1, source_target_pairs={{0,2},{1,3},{2,0},{3,1},{4,6},{5,7},{6,4},{7,5},{8,10},{9,11},{10,... | collective-permute-start | bytes 786440 | tf_op jit(solution)/shard_map/ppermute | solution.py:897
  31.1 21.6 %collective-permute-start.3 = (bf16[512,256]{1,0:T(8,128)(2,1)S(1)}, bf16[512,256]{1,0:T(8,128)(2,1)S(1)}, u32[]{:S(2)}, u32[]{:S(2)}) collective-permute-start(bf16[512,256]{1,0:T(8,128)(2,1)S(1)} %pad_maximum_fusion.18), channel_id=1, source_target_pairs={{0,1},{1,2},{2,3},{3,0},{4,5},{5,6},{6,7},{7,4},{8,9},{9,10},{10,1... | collective-permute-start | bytes 786440 | tf_op jit(solution)/shard_map/ppermute | solution.py:897
  69.7 25.4 %collective-permute-start.14 = (bf16[2,4,256,256]{3,2,1,0:T(8,128)(2,1)S(1)}, bf16[2,4,256,256]{3,2,1,0:T(8,128)(2,1)}, u32[]{:S(2)}, u32[]{:S(2)}) collective-permute-start(bf16[2,4,256,256]{3,2,1,0:T(8,128)(2,1)S(1)} %pad_maximum_fusion.7.qk_ref), channel_id=1, source_target_pairs={{0,8},{8,0},{1,9},{9,1},{2,10},{10,2},{3,11},{11,3},{4,12},{12,4},... | collective-permute-start | bytes 3145736 | tf_op jit(solution)/shard_map/ppermute | solution.py:832
  71.5 23.6 %collective-permute-start.15 = (bf16[2,4,256,256]{3,2,1,0:T(8,128)(2,1)S(1)}, bf16[2,4,256,256]{3,2,1,0:T(8,128)(2,1)}, u32[]{:S(2)}, u32[]{:S(2)}) collective-permute-start(bf16[2,4,256,256]{3,2,1,0:T(8,128)(2,1)S(1)} %pad_maximum_fusion.8.v_ref), channel_id=1, source_target_pairs={{0,16},{16,0},{1,17},{17,1},{2,18},{18,2},{3,19},{19,3},{4,20},{20... | collective-permute-start | bytes 3145736 | tf_op jit(solution)/shard_map/ppermute | solution.py:832
  74.1 21.0 %collective-permute-start.16 = (bf16[392,1024]{1,0:T(8,128)(2,1)}, bf16[392,1024]{1,0:T(8,128)(2,1)S(1)}, u32[]{:S(2)}, u32[]{:S(2)}) collective-permute-start(bf16[392,1024]{1,0:T(8,128)(2,1)} %get-tuple-element.383), channel_id=1, source_target_pairs={{0,1},{1,0},{2,5},{3,4},{4,3},{5,2},{6,7},{7,6},{8,9},{9,8},{10,13... | collective-permute-start | bytes 2408456 | tf_op jit(solution)/shard_map/ppermute | solution.py:882
  95.1 378.7 %reduce-scatter.2.cloned.1.call-start = ((), (), s32[]{:S(2)}) async-start(), calls=%async_computation.1 | async-start | bytes 2621440 | tf_op jit(solution)/shard_map/reduce_scatter | solution.py:1037
  101.4 33.4 %collective-permute-start.17 = (bf16[256,512]{1,0:T(8,128)(2,1)S(1)}, bf16[256,512]{1,0:T(8,128)(2,1)S(1)}, u32[]{:S(2)}, u32[]{:S(2)}) collective-permute-start(bf16[256,512]{1,0:T(8,128)(2,1)S(1)} %get-tuple-element.185), channel_id=1, source_target_pairs={{0,3},{1,0},{2,1},{3,2},{4,7},{5,4},{6,5},{7,6},{8,11},{9,8},{10,9... | collective-permute-start | bytes 786440 | tf_op jit(solution)/shard_map/ppermute | solution.py:897
  101.5 33.3 %collective-permute-start.18 = (bf16[256,512]{1,0:T(8,128)(2,1)S(1)}, bf16[256,512]{1,0:T(8,128)(2,1)S(1)}, u32[]{:S(2)}, u32[]{:S(2)}) collective-permute-start(bf16[256,512]{1,0:T(8,128)(2,1)S(1)} %get-tuple-element.185), channel_id=1, source_target_pairs={{0,2},{1,3},{2,0},{3,1},{4,6},{5,7},{6,4},{7,5},{8,10},{9,11},{10,... | collective-permute-start | bytes 786440 | tf_op jit(solution)/shard_map/ppermute | solution.py:897
  104.4 30.4 %collective-permute-start.19 = (bf16[256,512]{1,0:T(8,128)(2,1)S(1)}, bf16[256,512]{1,0:T(8,128)(2,1)S(1)}, u32[]{:S(2)}, u32[]{:S(2)}) collective-permute-start(bf16[256,512]{1,0:T(8,128)(2,1)S(1)} %get-tuple-element.185), channel_id=1, source_target_pairs={{0,1},{1,2},{2,3},{3,0},{4,5},{5,6},{6,7},{7,4},{8,9},{9,10},{10,1... | collective-permute-start | bytes 786440 | tf_op jit(solution)/shard_map/ppermute | solution.py:897
  134.9 21.3 %collective-permute-start.21 = (bf16[2,256,512]{2,1,0:T(8,128)(2,1)S(1)}, bf16[2,256,512]{2,1,0:T(8,128)(2,1)S(1)}, u32[]{:S(2)}, u32[]{:S(2)}) collective-permute-start(bf16[2,256,512]{2,1,0:T(8,128)(2,1)S(1)} %pad_maximum_fusion.16), channel_id=1, source_target_pairs={{0,16},{16,0},{1,17},{17,1},{2,18},{18,2},{3,19},{19,3},{4,20},{20... | collective-permute-start | bytes 1572872 | tf_op jit(solution)/shard_map/ppermute | solution.py:832
  136.4 19.8 %collective-permute-start.22 = (bf16[2,256,512]{2,1,0:T(8,128)(2,1)S(1)}, bf16[2,256,512]{2,1,0:T(8,128)(2,1)S(1)}, u32[]{:S(2)}, u32[]{:S(2)}) collective-permute-start(bf16[2,256,512]{2,1,0:T(8,128)(2,1)S(1)} %pad_maximum_fusion.17), channel_id=1, source_target_pairs={{0,8},{8,0},{1,9},{9,1},{2,10},{10,2},{3,11},{11,3},{4,12},{12,4},... | collective-permute-start | bytes 1572872 | tf_op jit(solution)/shard_map/ppermute | solution.py:832
  159.8 40.7 %collective-permute-start.24 = (bf16[2,2,256,512]{3,2,1,0:T(8,128)(2,1)S(1)}, bf16[2,2,256,512]{3,2,1,0:T(8,128)(2,1)}, u32[]{:S(2)}, u32[]{:S(2)}) collective-permute-start(bf16[2,2,256,512]{3,2,1,0:T(8,128)(2,1)S(1)} %pad_maximum_fusion.9), channel_id=1, source_target_pairs={{0,8},{8,0},{1,9},{9,1},{2,10},{10,2},{3,11},{11,3},{4,12},{12,4},... | collective-permute-start | bytes 3145736 | tf_op jit(solution)/shard_map/ppermute | solution.py:832
  162.8 39.1 %collective-permute-start.25 = (bf16[2,2,256,512]{3,2,1,0:T(8,128)(2,1)}, bf16[2,2,256,512]{3,2,1,0:T(8,128)(2,1)}, u32[]{:S(2)}, u32[]{:S(2)}) collective-permute-start(bf16[2,2,256,512]{3,2,1,0:T(8,128)(2,1)} %pad_maximum_fusion.10), channel_id=1, source_target_pairs={{0,16},{16,0},{1,17},{17,1},{2,18},{18,2},{3,19},{19,3},{4,20},{20... | collective-permute-start | bytes 3145736 | tf_op jit(solution)/shard_map/ppermute | solution.py:832
  172.4 40.4 %collective-permute-start.26 = (bf16[784,1024]{1,0:T(8,128)(2,1)}, bf16[784,1024]{1,0:T(8,128)(2,1)}, u32[]{:S(2)}, u32[]{:S(2)}) collective-permute-start(bf16[784,1024]{1,0:T(8,128)(2,1)} %add_convert_fusion.x_ref.xa_ref), channel_id=1, source_target_pairs={{0,4},{4,0},{1,5},{5,1},{2,6},{6,2},{3,7},{7,3},{8,12},{12,8},{9,1... | collective-permute-start | bytes 4816904 | tf_op jit(solution)/shard_map/ppermute | solution.py:832
  205.9 22.0 %collective-permute-start.27 = (bf16[392,1024]{1,0:T(8,128)(2,1)}, bf16[392,1024]{1,0:T(8,128)(2,1)S(1)}, u32[]{:S(2)}, u32[]{:S(2)}) collective-permute-start(bf16[392,1024]{1,0:T(8,128)(2,1)} %get-tuple-element.218), channel_id=1, source_target_pairs={{2,4},{3,5},{4,2},{5,3},{10,12},{11,13},{12,10},{13,11},{18,20},{1... | collective-permute-start | bytes 2408456 | tf_op jit(solution)/shard_map/ppermute | solution.py:882
  227.9 24.1 %collective-permute-start.29 = (bf16[784,1024]{1,0:T(8,128)(2,1)}, bf16[784,1024]{1,0:T(8,128)(2,1)S(1)}, u32[]{:S(2)}, u32[]{:S(2)}) collective-permute-start(bf16[784,1024]{1,0:T(8,128)(2,1)} %get-tuple-element.223), channel_id=1, source_target_pairs={{0,4},{4,0},{1,5},{5,1},{2,6},{6,2},{3,7},{7,3},{8,12},{12,8},{9,1... | collective-permute-start | bytes 4816904 | tf_op jit(solution)/shard_map/ppermute | solution.py:832
  231.1 20.9 %collective-permute-start.28 = (bf16[392,1024]{1,0:T(8,128)(2,1)S(1)}, bf16[392,1024]{1,0:T(8,128)(2,1)}, u32[]{:S(2)}, u32[]{:S(2)}) collective-permute-start(bf16[392,1024]{1,0:T(8,128)(2,1)S(1)} %copy-done.33), channel_id=1, source_target_pairs={{0,1},{1,0},{2,5},{3,4},{4,3},{5,2},{6,7},{7,6},{8,9},{9,8},{10,13... | collective-permute-start | bytes 2408456 | tf_op jit(solution)/shard_map/ppermute | solution.py:882
  313.2 20.7 %collective-permute-start.32 = (bf16[784,1024]{1,0:T(8,128)(2,1)}, bf16[784,1024]{1,0:T(8,128)(2,1)}, u32[]{:S(2)}, u32[]{:S(2)}) collective-permute-start(bf16[784,1024]{1,0:T(8,128)(2,1)} %get-tuple-element.243.da_ref), channel_id=1, source_target_pairs={{0,4},{4,0},{1,5},{5,1},{2,6},{6,2},{3,7},{7,3},{8,12},{12,8},{9,1... | collective-permute-start | bytes 4816904 | tf_op jit(solution)/shard_map/ppermute | solution.py:832
  313.8 18.8 %collective-permute-start.37 = (bf16[392,1024]{1,0:T(8,128)(2,1)S(1)}, bf16[392,1024]{1,0:T(8,128)(2,1)S(1)}, u32[]{:S(2)}, u32[]{:S(2)}) collective-permute-start(bf16[392,1024]{1,0:T(8,128)(2,1)S(1)} %get-tuple-element.382), channel_id=1, source_target_pairs={{4,2},{5,3},{2,4},{3,5},{12,10},{13,11},{10,12},{11,13},{20,18},{2... | collective-permute-start | bytes 2408456 | tf_op jit(solution)/shard_map/ppermute | solution.py:888
  314.5 45.2 %collective-permute-start.35 = (bf16[2,2,256,512]{3,2,1,0:T(8,128)(2,1)}, bf16[2,2,256,512]{3,2,1,0:T(8,128)(2,1)S(1)}, u32[]{:S(2)}, u32[]{:S(2)}) collective-permute-start(bf16[2,2,256,512]{3,2,1,0:T(8,128)(2,1)} %get-tuple-element.255), channel_id=1, source_target_pairs={{0,8},{8,0},{1,9},{9,1},{2,10},{10,2},{3,11},{11,3},{4,12},{12,4},... | collective-permute-start | bytes 3145736 | tf_op jit(solution)/shard_map/ppermute | solution.py:832
  314.7 45.1 %collective-permute-start.36 = (bf16[2,2,256,512]{3,2,1,0:T(8,128)(2,1)}, bf16[2,2,256,512]{3,2,1,0:T(8,128)(2,1)S(1)}, u32[]{:S(2)}, u32[]{:S(2)}) collective-permute-start(bf16[2,2,256,512]{3,2,1,0:T(8,128)(2,1)} %get-tuple-element.256), channel_id=1, source_target_pairs={{0,16},{16,0},{1,17},{17,1},{2,18},{18,2},{3,19},{19,3},{4,20},{20... | collective-permute-start | bytes 3145736 | tf_op jit(solution)/shard_map/ppermute | solution.py:832
  331.0 32.1 %collective-permute-start.33 = (bf16[2,2,256,512]{3,2,1,0:T(8,128)(2,1)}, bf16[2,2,256,512]{3,2,1,0:T(8,128)(2,1)S(1)}, u32[]{:S(2)}, u32[]{:S(2)}) collective-permute-start(bf16[2,2,256,512]{3,2,1,0:T(8,128)(2,1)} %get-tuple-element.253), channel_id=1, source_target_pairs={{0,8},{8,0},{1,9},{9,1},{2,10},{10,2},{3,11},{11,3},{4,12},{12,4},... | collective-permute-start | bytes 3145736 | tf_op jit(solution)/shard_map/ppermute | solution.py:832
  333.5 29.6 %collective-permute-start.34 = (bf16[2,2,256,512]{3,2,1,0:T(8,128)(2,1)}, bf16[2,2,256,512]{3,2,1,0:T(8,128)(2,1)S(1)}, u32[]{:S(2)}, u32[]{:S(2)}) collective-permute-start(bf16[2,2,256,512]{3,2,1,0:T(8,128)(2,1)} %get-tuple-element.254), channel_id=1, source_target_pairs={{0,16},{16,0},{1,17},{17,1},{2,18},{18,2},{3,19},{19,3},{4,20},{20... | collective-permute-start | bytes 3145736 | tf_op jit(solution)/shard_map/ppermute | solution.py:832
  333.9 55.2 %collective-permute-start.42 = (bf16[392,1024]{1,0:T(8,128)(2,1)S(1)}, bf16[392,1024]{1,0:T(8,128)(2,1)S(1)}, u32[]{:S(2)}, u32[]{:S(2)}) collective-permute-start(bf16[392,1024]{1,0:T(8,128)(2,1)S(1)} %get-tuple-element.381), channel_id=1, source_target_pairs={{1,0},{0,1},{5,2},{4,3},{3,4},{2,5},{7,6},{6,7},{9,8},{8,9},{13,10... | collective-permute-start | bytes 2408456 | tf_op jit(solution)/shard_map/ppermute | solution.py:888
  368.4 20.7 %collective-permute-start.38 = (bf16[2,256,512]{2,1,0:T(8,128)(2,1)}, bf16[2,256,512]{2,1,0:T(8,128)(2,1)S(1)}, u32[]{:S(2)}, u32[]{:S(2)}) collective-permute-start(bf16[2,256,512]{2,1,0:T(8,128)(2,1)} %get-tuple-element.267), channel_id=1, source_target_pairs={{0,16},{16,0},{1,17},{17,1},{2,18},{18,2},{3,19},{19,3},{4,20},{20... | collective-permute-start | bytes 1572872 | tf_op jit(solution)/shard_map/ppermute | solution.py:832
  372.0 21.7 %collective-permute-start.40 = (bf16[2,256,512]{2,1,0:T(8,128)(2,1)}, bf16[2,256,512]{2,1,0:T(8,128)(2,1)S(1)}, u32[]{:S(2)}, u32[]{:S(2)}) collective-permute-start(bf16[2,256,512]{2,1,0:T(8,128)(2,1)} %get-tuple-element.269), channel_id=1, source_target_pairs={{0,16},{16,0},{1,17},{17,1},{2,18},{18,2},{3,19},{19,3},{4,20},{20... | collective-permute-start | bytes 1572872 | tf_op jit(solution)/shard_map/ppermute | solution.py:832
  372.4 24.0 %collective-permute-start.41 = (bf16[2,256,512]{2,1,0:T(8,128)(2,1)}, bf16[2,256,512]{2,1,0:T(8,128)(2,1)S(1)}, u32[]{:S(2)}, u32[]{:S(2)}) collective-permute-start(bf16[2,256,512]{2,1,0:T(8,128)(2,1)} %get-tuple-element.270), channel_id=1, source_target_pairs={{0,8},{8,0},{1,9},{9,1},{2,10},{10,2},{3,11},{11,3},{4,12},{12,4},... | collective-permute-start | bytes 1572872 | tf_op jit(solution)/shard_map/ppermute | solution.py:832
  404.9 39.2 %collective-permute-start.43 = (bf16[2,5,256,128]{3,2,1,0:T(8,128)(2,1)S(1)}, bf16[2,5,256,128]{3,2,1,0:T(8,128)(2,1)S(1)}, u32[]{:S(2)}, u32[]{:S(2)}) collective-permute-start(bf16[2,5,256,128]{3,2,1,0:T(8,128)(2,1)S(1)} %pad_maximum_fusion.11), channel_id=1, source_target_pairs={{0,8},{8,0},{1,9},{9,1},{2,10},{10,2},{3,11},{11,3},{4,12},{12,4},... | collective-permute-start | bytes 1966088 | tf_op jit(solution)/shard_map/ppermute | solution.py:832
  407.6 36.5 %collective-permute-start.44 = (bf16[2,5,256,128]{3,2,1,0:T(8,128)(2,1)S(1)}, bf16[2,5,256,128]{3,2,1,0:T(8,128)(2,1)S(1)}, u32[]{:S(2)}, u32[]{:S(2)}) collective-permute-start(bf16[2,5,256,128]{3,2,1,0:T(8,128)(2,1)S(1)} %pad_maximum_fusion.12), channel_id=1, source_target_pairs={{0,16},{16,0},{1,17},{17,1},{2,18},{18,2},{3,19},{19,3},{4,20},{20... | collective-permute-start | bytes 1966088 | tf_op jit(solution)/shard_map/ppermute | solution.py:832
  496.0 32.8 %collective-permute-start.58 = (bf16[392,1024]{1,0:T(8,128)(2,1)}, bf16[392,1024]{1,0:T(8,128)(2,1)}, u32[]{:S(2)}, u32[]{:S(2)}) collective-permute-start(bf16[392,1024]{1,0:T(8,128)(2,1)} %get-tuple-element.326), channel_id=1, source_target_pairs={{1,0},{0,1},{5,2},{4,3},{3,4},{2,5},{7,6},{6,7},{9,8},{8,9},{13,10... | collective-permute-start | bytes 2408456 | tf_op jit(solution)/shard_map/ppermute | solution.py:888
  501.6 29.9 %collective-permute-start.64 = (f32[20,128]{1,0:T(8,128)S(1)}, f32[20,128]{1,0:T(8,128)S(1)}, u32[]{:S(2)}, u32[]{:S(2)}) collective-permute-start(f32[20,128]{1,0:T(8,128)S(1)} %fusion.37), channel_id=1, source_target_pairs={{0,3},{1,0},{2,1},{3,2},{4,7},{5,4},{6,5},{7,6},{8,11},{9,8},{10,9... | collective-permute-start | bytes 30728 | tf_op jit(solution)/shard_map/ppermute | solution.py:1086
  (100 other events, 1134.4 us)
Sparse Core Ops, SparseCore 0:
  95.3 110.5 all-gather.2
  413.2 41.2 reduce-scatter.1

commit v7 on v6

--- a/solution.py
+++ b/solution.py
@@ -932,6 +932,10 @@
     attn = jnp.concatenate([jnp.swapaxes(w_qkv, 1, 2), w_out[None]]).reshape(4, 2, cols, dims)
     mine, other = chosen(attn, c, 1).reshape(4 * cols, dims), chosen(attn, 1 - c, 1).reshape(4 * cols, dims)
     attn_piece = ordered(c, mine, swap(other, "c"), 1)
+    attn_rows = ring_gather(attn_piece)
+    attn_rows, w_up, w_down, norm_gain, shifts, bias_qv, up_bias, clips, teacher = together(
+        attn_rows, w_up, w_down, norm_gain, shifts, bias_qv, up_bias, clips, teacher
+    )
     ff = jnp.stack([w_up, w_down.T]).reshape(2, dims, 2, units)
     ff_piece = ordered(c, chosen(ff, c, 2), swap(chosen(ff, 1 - c, 2), "c"), 1)
 
@@ -950,8 +954,7 @@
     up_shift = placed(tails[:, 2:3], 0)
 
     whole = ("y", "x", "t")
-    attn_rows = together(*ring_gather(attn_piece))
-    near, far = to_chip(after(clips, attn_rows))
+    near, far = to_chip(clips)
     attn_rows = (attn_piece, *attn_rows)
     qk_rows = jnp.stack([part[: 2 * cols] for part in attn_rows])
     vo_rows = jnp.stack([part[2 * cols :] for part in attn_rows])

time: 551 us -> 553 us (level)
    ppermute x42, starting transfers between devices: 49.1 us -> 38.4 us  [swap(): return lax.ppermute(value, axis, [(0, 1), (1, 0)])]
    ppermute x9, starting transfers between devices: 11.2 us -> 19.4 us  [ring_gather(): lax.ppermute(value, 't', rings[-j % steps])]
  transfers between devices with their start and end apart: 67 -> 67, of which waited for: 21 -> 20; matrix products, arithmetic and copies ran while one was open for 10% -> 10% of each run, Pallas kernels for 43% -> 43%
where the time goes in v7:
time: 553 us; the launch traced here: 546 us
  Pallas kernels  265 us (48%)
  waiting for transfers between devices  98.4 us (18%)
  starting transfers between devices  90.3 us (16%)
  other arithmetic  52.6 us (10%)
  local copies, waits for them, and re-layouts  24.2 us (4%)
  between operations  15.7 us (3%)
    pallas_call x23, Pallas kernels, call(): pl.pallas_call(body, grid_spec=pltpu.PrefetchScalarGridSpec(num_scalar_pr...  265 us
    ppermute x42, waiting for transfers between devices, swap(): return lax.ppermute(value, axis, [(0, 1), (1, 0)])  53.2 us
    ppermute x42, starting transfers between devices, swap(): return lax.ppermute(value, axis, [(0, 1), (1, 0)])  38.4 us
    ppermute x9, waiting for transfers between devices, ring_gather(): lax.ppermute(value, 't', rings[-j % steps])  24.4 us
    ppermute x3, starting transfers between devices, clip_local(): lax.ppermute(sums, 't', rings[away])  19.7 us
    ppermute x9, starting transfers between devices, ring_gather(): lax.ppermute(value, 't', rings[-j % steps])  19.4 us
    ppermute x2, waiting for transfers between devices, sent(): lax.ppermute(pair[1], every, second_way)  16 us
  transfers between devices with their start and end apart: 67, of which 20 were waited for; matrix products, arithmetic and copies ran while one was open for 10% of the time, Pallas kernels for 43%

profile of v7, /device:TPU:0, one launch (start us, length us, event | category | flops | bytes accessed | tf_op | source)
XLA Modules:
  0.0 546.3 jit_solution(11802553600916540805)
XLA Ops:
  10.9 5.0 collective-permute-start.1
  17.0 5.6 %collective-permute-done.1 = bf16[512,256]{1,0:T(8,128)(2,1)S(1)} collective-permute-done((bf16[512,256]{1,0:T(8,128)(2,1)S(1)}, bf16[512,256]{1,0:T(8,128)(2,1)S(1)}, u32[]{:S(2)}, u32[]{:S(2)}) %collective-permute-start.1) | collective-permute-done | bytes 262176 | tf_op jit(solution)/shard_map/ppermute | solution.py:897
  22.6 15.9 %collective-permute-done.2 = bf16[512,256]{1,0:T(8,128)(2,1)S(1)} collective-permute-done((bf16[512,256]{1,0:T(8,128)(2,1)S(1)}, bf16[512,256]{1,0:T(8,128)(2,1)S(1)}, u32[]{:S(2)}, u32[]{:S(2)}) %collective-permute-start.2) | collective-permute-done | bytes 262176 | tf_op jit(solution)/shard_map/ppermute | solution.py:897
  49.1 10.6 %collective-permute-done.8 = bf16[16,256]{1,0:T(8,128)(2,1)S(1)} collective-permute-done((bf16[16,256]{1,0:T(8,128)(2,1)S(1)}, bf16[16,256]{1,0:T(8,128)(2,1)S(1)}, u32[]{:S(2)}, u32[]{:S(2)}) %collective-permute-start.8) | collective-permute-done | bytes 8224 | tf_op jit(solution)/shard_map/ppermute | solution.py:832
  67.9 6.7 %collective-permute-start.12 = (bf16[10,1024]{1,0:T(8,128)(2,1)S(1)}, bf16[10,1024]{1,0:T(8,128)(2,1)S(1)}, u32[]{:S(2)}, u32[]{:S(2)}) collective-permute-start(bf16[10,1024]{1,0:T(8,128)(2,1)S(1)} %fusion.29), channel_id=1, source_target_pairs={{0,1},{1,2},{2,3},{3,0},{4,5},{5,6},{6,7},{7,4},{8,9},{9,10},{10,1... | collective-permute-start | bytes 61448 | tf_op jit(solution)/shard_map/ppermute | solution.py:897
  91.1 11.6 %collective-permute-done.16 = bf16[392,1024]{1,0:T(8,128)(2,1)S(1)} collective-permute-done((bf16[392,1024]{1,0:T(8,128)(2,1)}, bf16[392,1024]{1,0:T(8,128)(2,1)S(1)}, u32[]{:S(2)}, u32[]{:S(2)}) %collective-permute-start.16) | collective-permute-done | bytes 802848 | tf_op jit(solution)/shard_map/ppermute | solution.py:882
  111.4 11.9 %project.1 = (bf16[2,3,4,64,1568]{4,3,2,1,0:T(8,128)(2,1)}, bf16[1024,1568]{1,0:T(8,128)(2,1)}) custom-call(s32[2]{0:T(128)} %pad_add_fusion.bits_ref, bf16[784,1024]{1,0:T(8,128)(2,1)} %copy-done.15, bf16[784,1024]{1,0:T(8,128)(2,1)} %collective-permute-done.20.xb_ref, bf16[2,4,256,256]{3,2,1,0:T(8,128)(2,1)} %copy-done.10, ...), custom_call_target="tpu_custom_call" | custom-call | flops 1000 | bytes 1000 | tf_op jit(solution)/shard_map/project/pallas_call | solution.py:194
  123.4 16.2 %attend.2 = (bf16[8,64,1568]{2,1,0:T(8,128)(2,1)}, bf16[1568,512]{1,0:T(8,128)(2,1)}, f32[8,64,1568]{2,1,0:T(8,128)}, f32[8,1,1568]{2,1,0:T(1,128)}) custom-call(bf16[2,3,4,64,1568]{4,3,2,1,0:T(8,128)(2,1)} %get-tuple-element.204.q_ref.k_ref.v_ref, bf16[2,3,4,64,1568]{4,3,2,1,0:T(8,128)(2,1)} %get-tuple-element.204.q_ref.k_ref.v_ref, ...), custom_call_target="tpu_custom_call" | custom-call | flops 1000 | bytes 1000 | tf_op jit(solution)/shard_map/attend/pallas_call | solution.py:194
  141.9 16.3 %attend.3 = (bf16[8,64,1568]{2,1,0:T(8,128)(2,1)}, bf16[1568,512]{1,0:T(8,128)(2,1)}, f32[8,64,1568]{2,1,0:T(8,128)}, f32[8,1,1568]{2,1,0:T(1,128)}) custom-call(bf16[2,3,4,64,1568]{4,3,2,1,0:T(8,128)(2,1)} %get-tuple-element.204.q_ref.k_ref.v_ref, ...), custom_call_target="tpu_custom_call", output_to_operand_aliasing={{0}: (3, {}), {1}: (4, {}), {2}: (5, {}), {3}: (6, {})} | custom-call | flops 1000 | bytes 1000 | tf_op jit(solution)/shard_map/attend/pallas_call | solution.py:194
  168.2 4.1 mix.3
  180.3 23.9 %collective-permute-done.24 = bf16[2,2,256,512]{3,2,1,0:T(8,128)(2,1)} collective-permute-done((bf16[2,2,256,512]{3,2,1,0:T(8,128)(2,1)S(1)}, bf16[2,2,256,512]{3,2,1,0:T(8,128)(2,1)}, u32[]{:S(2)}, u32[]{:S(2)}) %collective-permute-start.24) | collective-permute-done | bytes 1048608 | tf_op jit(solution)/shard_map/ppermute | solution.py:832
  215.1 15.1 %ffn.2 = (bf16[784,1024]{1,0:T(8,128)(2,1)}, bf16[784,2048]{1,0:T(8,128)(2,1)}, bf16[784,2048]{1,0:T(8,128)(2,1)}) custom-call(s32[1]{0:T(128)} %bitcast.50.place_ref, bf16[784,1024]{1,0:T(8,128)(2,1)} %collective-permute-done.26.x_ref.xb_ref, bf16[4,2,256,512]{3,2,1,0:T(8,128)(2,1)} %bitcast.221, bf16[4,2,256,512]{3,2,1,0:T(8,128)(2,1)} %bitcast.225, ...), custom_call_target="tpu_custom_call" | custom-call | flops 1000 | bytes 1000 | tf_op jit(solution)/shard_map/ffn/pallas_call | solution.py:194
  234.1 15.5 %ffn.3 = (f32[784,1024]{1,0:T(8,128)}, bf16[784,2048]{1,0:T(8,128)(2,1)}, bf16[784,2048]{1,0:T(8,128)(2,1)}) custom-call(s32[1]{0:T(128)} %bitcast.50.place_ref, bf16[784,1024]{1,0:T(8,128)(2,1)} %add_convert_fusion.x_ref.xa_ref, bf16[4,2,256,512]{3,2,1,0:T(8,128)(2,1)} %bitcast.222, bf16[4,2,256,512]{3,2,1,0:T(8,128)(2,1)} %bitcast.226, ...), custom_call_target="tpu_custom_call" | custom-call | flops 1000 | bytes 1000 | tf_op jit(solution)/shard_map/ffn/pallas_call | solution.py:194
  249.7 4.5 collective-permute-done.28
  255.4 5.5 %fusion.46 = (bf16[784,1024]{1,0:T(8,128)(2,1)S(1)}, f32[784,1024]{1,0:T(8,128)}, bf16[784,1024]{1,0:T(8,128)(2,1)S(1)}) fusion(bf16[392,1024]{1,0:T(8,128)(2,1)} %collective-permute-done.28, bf16[392,1024]{1,0:T(8,128)(2,1)S(1)} %broadcast_select_fusion.2, f32[1024]{0:T(1024)S(1)} %bitcast.251, f32[784,1024]{1,0:T(8,128)S(1)} %get-tuple-element.381.x_ref, ...), kind=kLoop, calls=%fused_computation.219 | loop fusion | flops 8830976 | bytes 16060416 | tf_op jit(solution)/shard_map/convert_element_type | solution.py:1012
  262.1 13.7 %ffn_backward.2 = (f32[784,1024]{1,0:T(8,128)}, bf16[784,2048]{1,0:T(8,128)(2,1)}, f32[4,1,512]{2,1,0:T(1,128)}) custom-call(s32[1]{0:T(128)} %bitcast.50.place_ref, bf16[784,1024]{1,0:T(8,128)(2,1)} %copy-done.7, bf16[4,4,256,512]{3,2,1,0:T(8,128)(2,1)} %bitcast.219, bf16[4,2,256,512]{3,2,1,0:T(8,128)(2,1)} %bitcast.223, ...), custom_call_target="tpu_custom_call" | custom-call | flops 1000 | bytes 1000 | tf_op jit(solution)/shard_map/ffn_backward/pallas_call | solution.py:194
  277.0 13.4 %ffn_backward.3 = (bf16[784,1024]{1,0:T(8,128)(2,1)}, bf16[784,2048]{1,0:T(8,128)(2,1)}, f32[4,1,512]{2,1,0:T(1,128)}) custom-call(s32[1]{0:T(128)} %bitcast.50.place_ref, bf16[784,1024]{1,0:T(8,128)(2,1)} %copy-done.14, bf16[4,4,256,512]{3,2,1,0:T(8,128)(2,1)} %bitcast.220, bf16[4,2,256,512]{3,2,1,0:T(8,128)(2,1)} %bitcast.224, ...), custom_call_target="tpu_custom_call" | custom-call | flops 1000 | bytes 1000 | tf_op jit(solution)/shard_map/ffn_backward/pallas_call | solution.py:194
  290.4 14.4 %ffn_grad.2 = (bf16[2,2,256,512]{3,2,1,0:T(8,128)(2,1)}, bf16[2,2,256,512]{3,2,1,0:T(8,128)(2,1)}, bf16[2,2,256,512]{3,2,1,0:T(8,128)(2,1)}, bf16[2,2,256,512]{3,2,1,0:T(8,128)(2,1)}) custom-call(s32[2]{0:T(128)} %pad_add_fusion.bits_ref, bf16[784,1024]{1,0:T(8,128)(2,1)} %copy-done.7, bf16[784,1024]{1,0:T(8,128)(2,1)} %copy-done.14, ...), custom_call_target="tpu_custom_call" | custom-call | flops 1000 | bytes 1000 | tf_op jit(solution)/shard_map/ffn_grad/pallas_call | solution.py:194
  305.9 9.4 %norm_backward.2 = (f32[784,1024]{1,0:T(8,128)}, bf16[784,1024]{1,0:T(8,128)(2,1)}, f32[8,1024]{1,0:T(8,128)}) custom-call(f32[784,1024]{1,0:T(8,128)} %get-tuple-element.252.da_ref, bf16[784,1024]{1,0:T(8,128)(2,1)} %copy-done.29, f32[784,1024]{1,0:T(8,128)} %copy-done, f32[784,1024]{1,0:T(8,128)} %get-tuple-element.379.rest_ref, f32[1,1024]{1,0:T(1,128)} %copy-done.61), custom_call_target="tpu_custom_call" | custom-call | flops 1000 | bytes 1000 | tf_op jit(solution)/shard_map/norm_backward/pallas_call | solution.py:194
  319.0 14.3 %ffn_grad.3 = (bf16[2,2,256,512]{3,2,1,0:T(8,128)(2,1)}, bf16[2,2,256,512]{3,2,1,0:T(8,128)(2,1)}, bf16[2,2,256,512]{3,2,1,0:T(8,128)(2,1)}, bf16[2,2,256,512]{3,2,1,0:T(8,128)(2,1)}) custom-call(s32[2]{0:T(128)} %pad_add_fusion.bits_ref, bf16[784,1024]{1,0:T(8,128)(2,1)} %add_convert_fusion.x_ref.xa_ref, ...), custom_call_target="tpu_custom_call" | custom-call | flops 1000 | bytes 1000 | tf_op jit(solution)/shard_map/ffn_grad/pallas_call | solution.py:194
  336.0 9.0 %mix_back.1 = (bf16[8,64,1568]{2,1,0:T(8,128)(2,1)}, f32[8,1,1568]{2,1,0:T(1,128)}, bf16[2,2,256,128]{3,2,1,0:T(8,128)(2,1)}, bf16[2,2,256,128]{3,2,1,0:T(8,128)...) custom-call(s32[2]{0:T(128)} %pad_add_fusion.bits_ref, ...), custom_call_target="tpu_custom_call" | custom-call | flops 1000 | bytes 1000 | tf_op jit(solution)/shard_map/mix_back/pallas_call | solution.py:194
  345.1 16.3 %attend_backward.3 = (bf16[3,1568,128]{2,1,0:T(8,128)(2,1)}, f32[3,1,128]{2,1,0:T(1,128)}) custom-call(bf16[2,3,4,64,1568]{4,3,2,1,0:T(8,128)(2,1)} %get-tuple-element.204.q_ref.k_ref.v_ref, bf16[2,3,4,64,1568]{4,3,2,1,0:T(8,128)(2,1)} %get-tuple-element.204.q_ref.k_ref.v_ref, bf16[2,3,4,64,1568]{4,3,2,1,0:T(8,128)(2,1)} %get-tuple-element.204.q_ref.k_ref.v_ref, ...), custom_call_target="tpu_custom_call" | custom-call | flops 1000 | bytes 1000 | tf_op jit(solution)/shard_map/attend_backward/pallas_call | solution.py:194
  374.8 16.6 %attend_backward.4 = (bf16[3,1568,128]{2,1,0:T(8,128)(2,1)}, f32[3,1,128]{2,1,0:T(1,128)}) custom-call(bf16[2,3,4,64,1568]{4,3,2,1,0:T(8,128)(2,1)} %get-tuple-element.204.q_ref.k_ref.v_ref, bf16[2,3,4,64,1568]{4,3,2,1,0:T(8,128)(2,1)} %get-tuple-element.204.q_ref.k_ref.v_ref, bf16[2,3,4,64,1568]{4,3,2,1,0:T(8,128)(2,1)} %get-tuple-element.204.q_ref.k_ref.v_ref, ...), custom_call_target="tpu_custom_call" | custom-call | flops 1000 | bytes 1000 | tf_op jit(solution)/shard_map/attend_backward/pallas_call | solution.py:194
  391.4 4.5 collective-permute-done.40.refs_8_
  398.7 7.4 %project_grads.2 = (bf16[2,3,256,128]{3,2,1,0:T(8,128)(2,1)}, bf16[2,3,256,128]{3,2,1,0:T(8,128)(2,1)}, bf16[2,3,256,128]{3,2,1,0:T(8,128)(2,1)}, bf16[2,3,256,128]{3,2,1,0:T(8,128)(2,1)}) custom-call(s32[2]{0:T(128)} %pad_add_fusion.bits_ref, bf16[1024,1568]{1,0:T(8,128)(2,1)} %get-tuple-element.292.t_ref, ...), custom_call_target="tpu_custom_call" | custom-call | flops 1000 | bytes 1000 | tf_op jit(solution)/shard_map/project_grads/pallas_call | solution.py:194
  409.6 5.0 add_end.1
  414.8 30.8 %attend_backward.5 = (bf16[3,1568,256]{2,1,0:T(8,128)(2,1)}, f32[3,1,256]{2,1,0:T(1,128)}) custom-call(bf16[2,3,4,64,1568]{4,3,2,1,0:T(8,128)(2,1)} %get-tuple-element.204.q_ref.k_ref.v_ref, bf16[2,3,4,64,1568]{4,3,2,1,0:T(8,128)(2,1)} %get-tuple-element.204.q_ref.k_ref.v_ref, bf16[2,3,4,64,1568]{4,3,2,1,0:T(8,128)(2,1)} %get-tuple-element.204.q_ref.k_ref.v_ref, ...), custom_call_target="tpu_custom_call" | custom-call | flops 1000 | bytes 1000 | tf_op jit(solution)/shard_map/attend_backward/pallas_call | solution.py:194
  448.8 7.3 %project_grads.3 = (bf16[2,3,256,128]{3,2,1,0:T(8,128)(2,1)}, bf16[2,3,256,128]{3,2,1,0:T(8,128)(2,1)}, bf16[2,3,256,128]{3,2,1,0:T(8,128)(2,1)}, bf16[2,3,256,128]{3,2,1,0:T(8,128)(2,1)}) custom-call(s32[2]{0:T(128)} %pad_add_fusion.bits_ref, bf16[1024,1568]{1,0:T(8,128)(2,1)} %get-tuple-element.292.t_ref, ...), custom_call_target="tpu_custom_call" | custom-call | flops 1000 | bytes 1000 | tf_op jit(solution)/shard_map/project_grads/pallas_call | solution.py:194
  456.2 6.7 %project_back.2 = f32[784,1024]{1,0:T(8,128)} custom-call(bf16[3,1568,256]{2,1,0:T(8,128)(2,1)} %get-tuple-element.311.refs_0_.a_ref, bf16[3,1568,128]{2,1,0:T(8,128)(2,1)} %get-tuple-element.285.refs_0_.c_ref, bf16[3,1568,128]{2,1,0:T(8,128)(2,1)} %get-tuple-element.293.refs_1_.d_ref, bf16[4,4,2,128,256]{4,3,2,1,0:T(8,128)(2,1)} %bitcast.229, ...), custom_call_target="tpu_custom_call" | custom-call | flops 1000 | bytes 1000 | tf_op jit(solution)/shard_map/project_back/pallas_call | solution.py:194
  468.2 6.9 %project_back.3.da_ref = f32[784,1024]{1,0:T(8,128)} custom-call(bf16[3,1568,256]{2,1,0:T(8,128)(2,1)} %get-tuple-element.311.refs_0_.a_ref, bf16[3,1568,128]{2,1,0:T(8,128)(2,1)} %get-tuple-element.285.refs_0_.c_ref, bf16[3,1568,128]{2,1,0:T(8,128)(2,1)} %get-tuple-element.293.refs_1_.d_ref, bf16[4,4,2,128,256]{4,3,2,1,0:T(8,128)(2,1)} %bitcast.230, ...), custom_call_target="tpu_custom_call" | custom-call | flops 1000 | bytes 1000 | tf_op jit(solution)/shard_map/project_back/pallas_call | solution.py:194
  476.1 7.3 %norm_backward.3 = (bf16[392,1024]{1,0:T(8,128)(2,1)}, bf16[392,1024]{1,0:T(8,128)(2,1)}, f32[8,1024]{1,0:T(8,128)}) custom-call(f32[784,1024]{1,0:T(8,128)} %project_back.3.da_ref, f32[784,1024]{1,0:T(8,128)} %collective-permute-done.51.db_ref, f32[784,1024]{1,0:T(8,128)} %fusion.45.x_ref, f32[784,1024]{1,0:T(8,128)} %get-tuple-element.325.rest_ref, ...), custom_call_target="tpu_custom_call" | custom-call | flops 1000 | bytes 1000 | tf_op jit(solution)/shard_map/norm_backward/pallas_call | solution.py:194
  503.8 19.1 %collective-permute-start.64 = (f32[20,128]{1,0:T(8,128)S(1)}, f32[20,128]{1,0:T(8,128)S(1)}, u32[]{:S(2)}, u32[]{:S(2)}) collective-permute-start(f32[20,128]{1,0:T(8,128)S(1)} %fusion.37), channel_id=1, source_target_pairs={{0,3},{1,0},{2,1},{3,2},{4,7},{5,4},{6,5},{7,6},{8,11},{9,8},{10,9... | collective-permute-start | bytes 30728 | tf_op jit(solution)/shard_map/ppermute | solution.py:1089
  (421 shorter events, 159.9 us)
Async XLA Ops:
  7.2 201.0 %all-gather.3.cloned.1.call-start = ((), (), s32[]{:S(2)}) async-start(), calls=%async_computation.2 | async-start | bytes 4456448 | tf_op jit(solution)/shard_map/all_gather | solution.py:972
  15.9 22.6 %collective-permute-start.2 = (bf16[512,256]{1,0:T(8,128)(2,1)S(1)}, bf16[512,256]{1,0:T(8,128)(2,1)S(1)}, u32[]{:S(2)}, u32[]{:S(2)}) collective-permute-start(bf16[512,256]{1,0:T(8,128)(2,1)S(1)} %pad_maximum_fusion.18), channel_id=1, source_target_pairs={{0,2},{1,3},{2,0},{3,1},{4,6},{5,7},{6,4},{7,5},{8,10},{9,11},{10,... | collective-permute-start | bytes 786440 | tf_op jit(solution)/shard_map/ppermute | solution.py:897
  15.9 22.6 %collective-permute-start.3 = (bf16[512,256]{1,0:T(8,128)(2,1)S(1)}, bf16[512,256]{1,0:T(8,128)(2,1)S(1)}, u32[]{:S(2)}, u32[]{:S(2)}) collective-permute-start(bf16[512,256]{1,0:T(8,128)(2,1)S(1)} %pad_maximum_fusion.18), channel_id=1, source_target_pairs={{0,1},{1,2},{2,3},{3,0},{4,5},{5,6},{6,7},{7,4},{8,9},{9,10},{10,1... | collective-permute-start | bytes 786440 | tf_op jit(solution)/shard_map/ppermute | solution.py:897
  42.9 34.2 %collective-permute-start.4 = (bf16[4,256,256]{2,1,0:T(8,128)(2,1)}, bf16[4,256,256]{2,1,0:T(8,128)(2,1)}, u32[]{:S(2)}, u32[]{:S(2)}) collective-permute-start(bf16[4,256,256]{2,1,0:T(8,128)(2,1)} %pad_maximum_fusion.14), channel_id=1, source_target_pairs={{0,16},{16,0},{1,17},{17,1},{2,18},{18,2},{3,19},{19,3},{4,20},{20... | collective-permute-start | bytes 1572872 | tf_op jit(solution)/shard_map/ppermute | solution.py:832
  45.3 31.8 %collective-permute-start.5 = (bf16[4,256,256]{2,1,0:T(8,128)(2,1)}, bf16[4,256,256]{2,1,0:T(8,128)(2,1)}, u32[]{:S(2)}, u32[]{:S(2)}) collective-permute-start(bf16[4,256,256]{2,1,0:T(8,128)(2,1)} %pad_maximum_fusion.15), channel_id=1, source_target_pairs={{0,8},{8,0},{1,9},{9,1},{2,10},{10,2},{3,11},{11,3},{4,12},{12,4},... | collective-permute-start | bytes 1572872 | tf_op jit(solution)/shard_map/ppermute | solution.py:832
  48.4 28.7 %collective-permute-start.6 = (bf16[392,1024]{1,0:T(8,128)(2,1)S(1)}, bf16[392,1024]{1,0:T(8,128)(2,1)S(1)}, u32[]{:S(2)}, u32[]{:S(2)}) collective-permute-start(bf16[392,1024]{1,0:T(8,128)(2,1)S(1)} %get-tuple-element.398), channel_id=1, source_target_pairs={{2,4},{3,5},{4,2},{5,3},{10,12},{11,13},{12,10},{13,11},{18,20},{1... | collective-permute-start | bytes 2408456 | tf_op jit(solution)/shard_map/ppermute | solution.py:882
  78.7 23.9 %collective-permute-start.14 = (bf16[2,4,256,256]{3,2,1,0:T(8,128)(2,1)S(1)}, bf16[2,4,256,256]{3,2,1,0:T(8,128)(2,1)}, u32[]{:S(2)}, u32[]{:S(2)}) collective-permute-start(bf16[2,4,256,256]{3,2,1,0:T(8,128)(2,1)S(1)} %pad_maximum_fusion.7.qk_ref), channel_id=1, source_target_pairs={{0,8},{8,0},{1,9},{9,1},{2,10},{10,2},{3,11},{11,3},{4,12},{12,4},... | collective-permute-start | bytes 3145736 | tf_op jit(solution)/shard_map/ppermute | solution.py:832
  81.5 21.2 %collective-permute-start.15 = (bf16[2,4,256,256]{3,2,1,0:T(8,128)(2,1)S(1)}, bf16[2,4,256,256]{3,2,1,0:T(8,128)(2,1)}, u32[]{:S(2)}, u32[]{:S(2)}) collective-permute-start(bf16[2,4,256,256]{3,2,1,0:T(8,128)(2,1)S(1)} %pad_maximum_fusion.8.v_ref), channel_id=1, source_target_pairs={{0,16},{16,0},{1,17},{17,1},{2,18},{18,2},{3,19},{19,3},{4,20},{20... | collective-permute-start | bytes 3145736 | tf_op jit(solution)/shard_map/ppermute | solution.py:832
  102.8 373.3 %reduce-scatter.2.cloned.1.call-start = ((), (), s32[]{:S(2)}) async-start(), calls=%async_computation.1 | async-start | bytes 2621440 | tf_op jit(solution)/shard_map/reduce_scatter | solution.py:1040
  105.9 33.7 %collective-permute-start.17 = (bf16[256,512]{1,0:T(8,128)(2,1)S(1)}, bf16[256,512]{1,0:T(8,128)(2,1)S(1)}, u32[]{:S(2)}, u32[]{:S(2)}) collective-permute-start(bf16[256,512]{1,0:T(8,128)(2,1)S(1)} %get-tuple-element.199), channel_id=1, source_target_pairs={{0,3},{1,0},{2,1},{3,2},{4,7},{5,4},{6,5},{7,6},{8,11},{9,8},{10,9... | collective-permute-start | bytes 786440 | tf_op jit(solution)/shard_map/ppermute | solution.py:897
  106.8 32.7 %collective-permute-start.18 = (bf16[256,512]{1,0:T(8,128)(2,1)S(1)}, bf16[256,512]{1,0:T(8,128)(2,1)S(1)}, u32[]{:S(2)}, u32[]{:S(2)}) collective-permute-start(bf16[256,512]{1,0:T(8,128)(2,1)S(1)} %get-tuple-element.199), channel_id=1, source_target_pairs={{0,2},{1,3},{2,0},{3,1},{4,6},{5,7},{6,4},{7,5},{8,10},{9,11},{10,... | collective-permute-start | bytes 786440 | tf_op jit(solution)/shard_map/ppermute | solution.py:897
  108.1 31.5 %collective-permute-start.19 = (bf16[256,512]{1,0:T(8,128)(2,1)S(1)}, bf16[256,512]{1,0:T(8,128)(2,1)S(1)}, u32[]{:S(2)}, u32[]{:S(2)}) collective-permute-start(bf16[256,512]{1,0:T(8,128)(2,1)S(1)} %get-tuple-element.199), channel_id=1, source_target_pairs={{0,1},{1,2},{2,3},{3,0},{4,5},{5,6},{6,7},{7,4},{8,9},{9,10},{10,1... | collective-permute-start | bytes 786440 | tf_op jit(solution)/shard_map/ppermute | solution.py:897
  139.6 21.5 %collective-permute-start.21 = (bf16[2,256,512]{2,1,0:T(8,128)(2,1)S(1)}, bf16[2,256,512]{2,1,0:T(8,128)(2,1)S(1)}, u32[]{:S(2)}, u32[]{:S(2)}) collective-permute-start(bf16[2,256,512]{2,1,0:T(8,128)(2,1)S(1)} %pad_maximum_fusion.16), channel_id=1, source_target_pairs={{0,16},{16,0},{1,17},{17,1},{2,18},{18,2},{3,19},{19,3},{4,20},{20... | collective-permute-start | bytes 1572872 | tf_op jit(solution)/shard_map/ppermute | solution.py:832
  164.7 39.5 %collective-permute-start.24 = (bf16[2,2,256,512]{3,2,1,0:T(8,128)(2,1)S(1)}, bf16[2,2,256,512]{3,2,1,0:T(8,128)(2,1)}, u32[]{:S(2)}, u32[]{:S(2)}) collective-permute-start(bf16[2,2,256,512]{3,2,1,0:T(8,128)(2,1)S(1)} %pad_maximum_fusion.9), channel_id=1, source_target_pairs={{0,8},{8,0},{1,9},{9,1},{2,10},{10,2},{3,11},{11,3},{4,12},{12,4},... | collective-permute-start | bytes 3145736 | tf_op jit(solution)/shard_map/ppermute | solution.py:832
  167.7 36.6 %collective-permute-start.25 = (bf16[2,2,256,512]{3,2,1,0:T(8,128)(2,1)}, bf16[2,2,256,512]{3,2,1,0:T(8,128)(2,1)}, u32[]{:S(2)}, u32[]{:S(2)}) collective-permute-start(bf16[2,2,256,512]{3,2,1,0:T(8,128)(2,1)} %pad_maximum_fusion.10), channel_id=1, source_target_pairs={{0,16},{16,0},{1,17},{17,1},{2,18},{18,2},{3,19},{19,3},{4,20},{20... | collective-permute-start | bytes 3145736 | tf_op jit(solution)/shard_map/ppermute | solution.py:832
  177.1 38.0 %collective-permute-start.26 = (bf16[784,1024]{1,0:T(8,128)(2,1)}, bf16[784,1024]{1,0:T(8,128)(2,1)}, u32[]{:S(2)}, u32[]{:S(2)}) collective-permute-start(bf16[784,1024]{1,0:T(8,128)(2,1)} %add_convert_fusion.x_ref.xa_ref), channel_id=1, source_target_pairs={{0,4},{4,0},{1,5},{5,1},{2,6},{6,2},{3,7},{7,3},{8,12},{12,8},{9,1... | collective-permute-start | bytes 4816904 | tf_op jit(solution)/shard_map/ppermute | solution.py:832
  208.1 22.1 %collective-permute-start.27 = (bf16[392,1024]{1,0:T(8,128)(2,1)}, bf16[392,1024]{1,0:T(8,128)(2,1)S(1)}, u32[]{:S(2)}, u32[]{:S(2)}) collective-permute-start(bf16[392,1024]{1,0:T(8,128)(2,1)} %get-tuple-element.232), channel_id=1, source_target_pairs={{2,4},{3,5},{4,2},{5,3},{10,12},{11,13},{12,10},{13,11},{18,20},{1... | collective-permute-start | bytes 2408456 | tf_op jit(solution)/shard_map/ppermute | solution.py:882
  230.2 24.0 %collective-permute-start.29 = (bf16[784,1024]{1,0:T(8,128)(2,1)}, bf16[784,1024]{1,0:T(8,128)(2,1)S(1)}, u32[]{:S(2)}, u32[]{:S(2)}) collective-permute-start(bf16[784,1024]{1,0:T(8,128)(2,1)} %get-tuple-element.237), channel_id=1, source_target_pairs={{0,4},{4,0},{1,5},{5,1},{2,6},{6,2},{3,7},{7,3},{8,12},{12,8},{9,1... | collective-permute-start | bytes 4816904 | tf_op jit(solution)/shard_map/ppermute | solution.py:832
  233.3 20.9 %collective-permute-start.28 = (bf16[392,1024]{1,0:T(8,128)(2,1)S(1)}, bf16[392,1024]{1,0:T(8,128)(2,1)}, u32[]{:S(2)}, u32[]{:S(2)}) collective-permute-start(bf16[392,1024]{1,0:T(8,128)(2,1)S(1)} %copy-done.35), channel_id=1, source_target_pairs={{0,1},{1,0},{2,5},{3,4},{4,3},{5,2},{6,7},{7,6},{8,9},{9,8},{10,13... | collective-permute-start | bytes 2408456 | tf_op jit(solution)/shard_map/ppermute | solution.py:882
  315.3 20.6 %collective-permute-start.32 = (bf16[784,1024]{1,0:T(8,128)(2,1)}, bf16[784,1024]{1,0:T(8,128)(2,1)}, u32[]{:S(2)}, u32[]{:S(2)}) collective-permute-start(bf16[784,1024]{1,0:T(8,128)(2,1)} %get-tuple-element.257.da_ref), channel_id=1, source_target_pairs={{0,4},{4,0},{1,5},{5,1},{2,6},{6,2},{3,7},{7,3},{8,12},{12,8},{9,1... | collective-permute-start | bytes 4816904 | tf_op jit(solution)/shard_map/ppermute | solution.py:832
  316.7 44.7 %collective-permute-start.35 = (bf16[2,2,256,512]{3,2,1,0:T(8,128)(2,1)}, bf16[2,2,256,512]{3,2,1,0:T(8,128)(2,1)S(1)}, u32[]{:S(2)}, u32[]{:S(2)}) collective-permute-start(bf16[2,2,256,512]{3,2,1,0:T(8,128)(2,1)} %get-tuple-element.269), channel_id=1, source_target_pairs={{0,8},{8,0},{1,9},{9,1},{2,10},{10,2},{3,11},{11,3},{4,12},{12,4},... | collective-permute-start | bytes 3145736 | tf_op jit(solution)/shard_map/ppermute | solution.py:832
  316.7 44.6 %collective-permute-start.36 = (bf16[2,2,256,512]{3,2,1,0:T(8,128)(2,1)}, bf16[2,2,256,512]{3,2,1,0:T(8,128)(2,1)S(1)}, u32[]{:S(2)}, u32[]{:S(2)}) collective-permute-start(bf16[2,2,256,512]{3,2,1,0:T(8,128)(2,1)} %get-tuple-element.270), channel_id=1, source_target_pairs={{0,16},{16,0},{1,17},{17,1},{2,18},{18,2},{3,19},{19,3},{4,20},{20... | collective-permute-start | bytes 3145736 | tf_op jit(solution)/shard_map/ppermute | solution.py:832
  333.2 31.8 %collective-permute-start.33 = (bf16[2,2,256,512]{3,2,1,0:T(8,128)(2,1)}, bf16[2,2,256,512]{3,2,1,0:T(8,128)(2,1)S(1)}, u32[]{:S(2)}, u32[]{:S(2)}) collective-permute-start(bf16[2,2,256,512]{3,2,1,0:T(8,128)(2,1)} %get-tuple-element.267), channel_id=1, source_target_pairs={{0,8},{8,0},{1,9},{9,1},{2,10},{10,2},{3,11},{11,3},{4,12},{12,4},... | collective-permute-start | bytes 3145736 | tf_op jit(solution)/shard_map/ppermute | solution.py:832
  335.6 29.8 %collective-permute-start.34 = (bf16[2,2,256,512]{3,2,1,0:T(8,128)(2,1)}, bf16[2,2,256,512]{3,2,1,0:T(8,128)(2,1)S(1)}, u32[]{:S(2)}, u32[]{:S(2)}) collective-permute-start(bf16[2,2,256,512]{3,2,1,0:T(8,128)(2,1)} %get-tuple-element.268), channel_id=1, source_target_pairs={{0,16},{16,0},{1,17},{17,1},{2,18},{18,2},{3,19},{19,3},{4,20},{20... | collective-permute-start | bytes 3145736 | tf_op jit(solution)/shard_map/ppermute | solution.py:832
  336.0 55.4 %collective-permute-start.42 = (bf16[392,1024]{1,0:T(8,128)(2,1)S(1)}, bf16[392,1024]{1,0:T(8,128)(2,1)S(1)}, u32[]{:S(2)}, u32[]{:S(2)}) collective-permute-start(bf16[392,1024]{1,0:T(8,128)(2,1)S(1)} %get-tuple-element.395), channel_id=1, source_target_pairs={{1,0},{0,1},{5,2},{4,3},{3,4},{2,5},{7,6},{6,7},{9,8},{8,9},{13,10... | collective-permute-start | bytes 2408456 | tf_op jit(solution)/shard_map/ppermute | solution.py:888
  370.4 21.0 %collective-permute-start.38 = (bf16[2,256,512]{2,1,0:T(8,128)(2,1)}, bf16[2,256,512]{2,1,0:T(8,128)(2,1)S(1)}, u32[]{:S(2)}, u32[]{:S(2)}) collective-permute-start(bf16[2,256,512]{2,1,0:T(8,128)(2,1)} %get-tuple-element.281), channel_id=1, source_target_pairs={{0,16},{16,0},{1,17},{17,1},{2,18},{18,2},{3,19},{19,3},{4,20},{20... | collective-permute-start | bytes 1572872 | tf_op jit(solution)/shard_map/ppermute | solution.py:832
  374.1 21.9 %collective-permute-start.40 = (bf16[2,256,512]{2,1,0:T(8,128)(2,1)}, bf16[2,256,512]{2,1,0:T(8,128)(2,1)S(1)}, u32[]{:S(2)}, u32[]{:S(2)}) collective-permute-start(bf16[2,256,512]{2,1,0:T(8,128)(2,1)} %get-tuple-element.283), channel_id=1, source_target_pairs={{0,16},{16,0},{1,17},{17,1},{2,18},{18,2},{3,19},{19,3},{4,20},{20... | collective-permute-start | bytes 1572872 | tf_op jit(solution)/shard_map/ppermute | solution.py:832
  374.4 24.3 %collective-permute-start.41 = (bf16[2,256,512]{2,1,0:T(8,128)(2,1)}, bf16[2,256,512]{2,1,0:T(8,128)(2,1)S(1)}, u32[]{:S(2)}, u32[]{:S(2)}) collective-permute-start(bf16[2,256,512]{2,1,0:T(8,128)(2,1)} %get-tuple-element.284), channel_id=1, source_target_pairs={{0,8},{8,0},{1,9},{9,1},{2,10},{10,2},{3,11},{11,3},{4,12},{12,4},... | collective-permute-start | bytes 1572872 | tf_op jit(solution)/shard_map/ppermute | solution.py:832
  407.2 38.5 %collective-permute-start.43 = (bf16[2,5,256,128]{3,2,1,0:T(8,128)(2,1)S(1)}, bf16[2,5,256,128]{3,2,1,0:T(8,128)(2,1)S(1)}, u32[]{:S(2)}, u32[]{:S(2)}) collective-permute-start(bf16[2,5,256,128]{3,2,1,0:T(8,128)(2,1)S(1)} %pad_maximum_fusion.11), channel_id=1, source_target_pairs={{0,8},{8,0},{1,9},{9,1},{2,10},{10,2},{3,11},{11,3},{4,12},{12,4},... | collective-permute-start | bytes 1966088 | tf_op jit(solution)/shard_map/ppermute | solution.py:832
  409.4 36.4 %collective-permute-start.44 = (bf16[2,5,256,128]{3,2,1,0:T(8,128)(2,1)S(1)}, bf16[2,5,256,128]{3,2,1,0:T(8,128)(2,1)S(1)}, u32[]{:S(2)}, u32[]{:S(2)}) collective-permute-start(bf16[2,5,256,128]{3,2,1,0:T(8,128)(2,1)S(1)} %pad_maximum_fusion.12), channel_id=1, source_target_pairs={{0,16},{16,0},{1,17},{17,1},{2,18},{18,2},{3,19},{19,3},{4,20},{20... | collective-permute-start | bytes 1966088 | tf_op jit(solution)/shard_map/ppermute | solution.py:832
  498.0 33.3 %collective-permute-start.58 = (bf16[392,1024]{1,0:T(8,128)(2,1)}, bf16[392,1024]{1,0:T(8,128)(2,1)}, u32[]{:S(2)}, u32[]{:S(2)}) collective-permute-start(bf16[392,1024]{1,0:T(8,128)(2,1)} %get-tuple-element.340), channel_id=1, source_target_pairs={{1,0},{0,1},{5,2},{4,3},{3,4},{2,5},{7,6},{6,7},{9,8},{8,9},{13,10... | collective-permute-start | bytes 2408456 | tf_op jit(solution)/shard_map/ppermute | solution.py:888
  503.8 30.2 %collective-permute-start.64 = (f32[20,128]{1,0:T(8,128)S(1)}, f32[20,128]{1,0:T(8,128)S(1)}, u32[]{:S(2)}, u32[]{:S(2)}) collective-permute-start(f32[20,128]{1,0:T(8,128)S(1)} %fusion.37), channel_id=1, source_target_pairs={{0,3},{1,0},{2,1},{3,2},{4,7},{5,4},{6,5},{7,6},{8,11},{9,8},{10,9... | collective-permute-start | bytes 30728 | tf_op jit(solution)/shard_map/ppermute | solution.py:1089
  (104 other events, 1200.8 us)
Sparse Core Ops, SparseCore 0:
  102.9 105.1 all-gather.2
  414.8 41.8 reduce-scatter.1
